TPU v7x, 512 devices: a whole 4x4x16 slice. The times are simulated.
512 devices in a mesh: member: 32 (over z_hi, y, core), tensor: 16 (over x, z_lo).
Axes of the slice: x: 4, y: 4, z: 16 (z_hi: 4, z_lo: 4; z = z_hi * 4 + z_lo), core: 2. Of those that a mesh axis runs over, the one named last changes fastest.
Arguments:
- features: bfloat16 [6144, 16384], P('member', 'tensor'), may hold values from -6 to 6
- down_weight: bfloat16 [5120, 16384], P('member', 'tensor'), may hold values from -0.09375 to 0.09375
- member_left: bfloat16 [1024, 5120], P('member'), may hold values from -6 to 6
- member_right: bfloat16 [1024, 16384], P('member', 'tensor'), may hold values from -6 to 6
- probe: float32 [5120], P('tensor'), may hold values from -16 to 16
- payoff: float32 [1024], replicated, may hold values from 0.5 to 2
- opponent: int32 [1024], replicated, may hold values from 0 to 1023, each once
Outputs:
- mixed: bfloat16 [6144, 5120], P('member', 'tensor')
- weight_step: float32 [5120, 16384], P('member', 'tensor')
Inputs may be any that keep to these rules, and one draw needn't show every extreme that they name: Each member index appears exactly once as an opponent.
All inputs are finite; a program needn't handle non-finite values.
Results may differ from a plain program's by a relative error of at most 0.017.
Values may be sent and summed in bfloat16 or wider, within the bound.
No kernel may reach another device: no remote copies, remote signals or barrier semaphores. Data moves between devices by JAX's collectives and lax.ppermute only.
A program may use at most 64 MiB of HBM per device.

v0:
```python
import jax
import jax.numpy as jnp
from jax import lax
from jax.sharding import PartitionSpec as P

D = 5120
FF = 16384


def per_device(features, down_weight, member_left, member_right, probe, payoff, opponent):
    rows, width = features.shape
    members = member_right.shape[0]
    tokens = rows // members
    population = payoff.shape[0]
    spread = 1.0 / jnp.sqrt(jnp.float32(FF))
    inner = jnp.einsum(
        "mtf,mf->mt",
        features.reshape(members, tokens, width),
        member_right,
        preferred_element_type=jnp.float32,
    )
    lowrank = (spread * inner)[:, :, None] * member_left.astype(jnp.float32)[:, None, :]
    base = lax.dot_general(
        features,
        lax.all_gather(down_weight, "member", axis=0, tiled=True),
        (((1,), (1,)), ((), ())),
        preferred_element_type=jnp.float32,
    )
    partial_term = (base + lowrank.reshape(rows, D)).astype(jnp.bfloat16)
    total = lax.psum_scatter(
        partial_term.astype(jnp.float32), "tensor", scatter_dimension=1, tiled=True
    )
    mixed = total.astype(jnp.bfloat16)
    dots_part = jnp.sum(total * probe[None, :], axis=1)
    scale = 0.5 / jnp.sqrt(jnp.float32(D))
    dots = lax.psum(dots_part, "tensor")
    own_score = jnp.mean(jnp.tanh(scale * dots).reshape(members, tokens), axis=1)
    score = lax.all_gather(own_score, "member", axis=0, tiled=True)
    labels = jnp.arange(population, dtype=jnp.int32)
    matches = opponent[:, None] == labels[None, :]
    rival = jnp.sum(jnp.where(matches, score[None, :], 0.0), axis=1)
    fitness = payoff * (score - rival)
    pieces = lax.all_to_all(member_left, "member", split_axis=1, concat_axis=0, tiled=True)
    scaled = (fitness[:, None] * pieces.astype(jnp.float32)).astype(jnp.bfloat16)
    term = lax.dot_general(
        scaled,
        lax.all_gather(member_right, "member", axis=0, tiled=True),
        (((0,), (0,)), ((), ())),
        preferred_element_type=jnp.float32,
    )
    weight_step = term / jnp.sqrt(jnp.float32(population))
    return (mixed, weight_step)


def solution(mesh):
    in_specs = (
        P("member", "tensor"),
        P("member", "tensor"),
        P("member", None),
        P("member", "tensor"),
        P("tensor"),
        P(),
        P(),
    )
    out_specs = (P("member", "tensor"), P("member", "tensor"))
    return jax.shard_map(
        per_device, mesh=mesh, in_specs=in_specs, out_specs=out_specs, check_vma=False
    )
```

profile of v0, /device:TPU:24, one launch (start us, length us, event | category | flops | bytes accessed | tf_op | source)
XLA Modules:
  0.0 461.7 jit_solution(7408774594237088251)
XLA Ops:
  7.2 0.0 all-gather.3.cloned.1.call-start
  7.2 0.7 all-gather.3.cloned.1.call-update
  7.9 0.0 reduce-scatter.4.cloned.1.call-start
  7.9 3.9 mul.53
  11.9 0.0 copy-start
  11.9 0.0 copy-start.2
  11.9 5.1 %mul.54 = f32[192,5120]{1,0:T(8,128)} reshape(f32[32,6,5120]{2,1,0:T(8,128)} %mul.53) | data formatting | bytes 7864320 | tf_op jit(solution)/shard_map/mul | solution.py:22
  17.0 0.0 copy-done
  17.0 0.1 reshape.25
  17.1 0.0 copy-done.2
  17.2 0.4 fusion.3
  17.6 0.1 mul.51
  17.7 156.5 %all-gather.3.cloned.1.call-done = bf16[5120,1024]{1,0:T(8,128)(2,1)} async-done(((bf16[160,1024]{1,0:T(8,128)(2,1)}), bf16[5120,1024]{1,0:T(8,128)(2,1)}) %all-gather.3.cloned.1.call-update) | async-done | bytes 10485776 | tf_op jit(solution)/shard_map/all_gather | solution.py:25
  174.2 10.6 %fusion.1 = f32[192,5120]{1,0:T(8,128)} fusion(bf16[192,1024]{1,0:T(8,128)(2,1)S(1)} %copy-done, bf16[5120,1024]{1,0:T(8,128)(2,1)} %all-gather.3.cloned.1.call-done, f32[192,5120]{1,0:T(8,128)} %mul.54, f32[192]{0:T(256)S(1)} %mul.51), kind=kOutput, calls=%fused_computation.2 | convolution fusion | flops 2017198080 | bytes 18744064 | tf_op jit(solution)/shard_map/dot_general | solution.py:23
  184.7 5.6 %copy.14 = f32[192,5120]{0,1:T(8,128)} copy(f32[192,5120]{1,0:T(8,128)} %fusion.1) | data formatting | bytes 7864320
  190.3 0.0 copy-start.1
  190.3 0.0 copy-start.5
  190.3 0.0 copy-start.3
  190.3 0.0 copy-start.4
  190.4 0.0 reduce-scatter.4.cloned.1.call-update
  190.4 0.0 all-gather.5.cloned.1.call-start
  190.4 0.7 all-gather.5.cloned.1.call-update
  191.1 0.2 copy-done.1
  191.3 0.6 all_to_all.10
  192.0 1.1 copy.11
  193.1 12.6 %all-to-all-start = ((bf16[32,32,160]{2,0,1:T(8,128)(2,1)}), bf16[32,32,160]{2,0,1:T(8,128)(2,1)S(1)}, u32[]{:S(2)}, u32[]{:S(2)}) async-start(bf16[32,32,160]{2,0,1:T(8,128)(2,1)} %copy.11), calls=%async_computation | async-start | bytes 1048576 | tf_op jit(solution)/shard_map/all_to_all | solution.py:43
  205.7 1.3 dynamic-slice
  207.6 118.6 %reduce-scatter.4.cloned.1.call-done = f32[320,192]{1,0:T(8,128)} async-done(((f32[5120,192]{1,0:T(8,128)}), f32[320,192]{1,0:T(8,128)}) %reduce-scatter.4.cloned.1.call-update) | async-done | bytes 245776
  326.2 1.1 copy.15
  327.3 0.0 copy-done.5
  327.3 0.7 multiply_reduce_fusion
  328.0 42.7 %psum.7 = f32[192]{0:T(256)S(1)} all-reduce(f32[192]{0:T(256)S(1)} %get-tuple-element.2), channel_id=1, replica_groups=mesh['member'=32,'tensor'=16] {'tensor'}, use_global_device_ids=true, to_apply=%region_2.0 | all-reduce | flops 192 | bytes 1536 | tf_op jit(solution)/shard_map/psum | solution.py:36
  370.7 0.1 reshape.26
  370.8 0.1 reduce_sum.28
  370.9 0.1 multiply_dynamic-update-slice_fusion
  371.1 80.2 %all-reduce = f32[1024]{0:T(1024)S(1)} all-reduce(f32[1024]{0:T(1024)S(1)} %multiply_dynamic-update-slice_fusion), channel_id=1, replica_groups=mesh['member'=32,'tensor'=16] {'member'}, use_global_device_ids=true, to_apply=%add | all-reduce | flops 1024 | bytes 8192
  451.2 0.0 copy-done.3
  451.2 0.7 select_reduce_fusion
  451.9 0.0 copy-done.4
  451.9 0.0 all-to-all-done
  451.9 0.2 fusion.2
  452.1 0.0 all-gather.5.cloned.1.call-done
  452.2 3.0 convolution_multiply_fusion
  (4 shorter events, 0.0 us)
Async XLA Ops:
  7.2 167.0 %all-gather.3.cloned.1.call-start = ((), (), s32[]{:S(2)}) async-start(), calls=%async_computation.2 | async-start | bytes 10813440 | tf_op jit(solution)/shard_map/all_gather | solution.py:25
  7.9 318.3 %reduce-scatter.4.cloned.1.call-start = ((), (), s32[]{:S(2)}) async-start(), calls=%async_computation.4 | async-start | bytes 5570560
  11.9 5.1 %copy-start = (bf16[192,1024]{1,0:T(8,128)(2,1)S(1)}, bf16[192,1024]{1,0:T(8,128)(2,1)}, u32[]{:S(2)}) copy-start(bf16[192,1024]{1,0:T(8,128)(2,1)} %param.7) | copy-start | bytes 1179652
  11.9 5.3 %copy-start.2 = (bf16[32,1024]{1,0:T(8,128)(2,1)S(1)}, bf16[32,1024]{1,0:T(8,128)(2,1)}, u32[]{:S(2)}) copy-start(bf16[32,1024]{1,0:T(8,128)(2,1)} %param.10) | copy-start | bytes 196612
  190.3 1.0 copy-start.1
  190.3 137.0 %copy-start.5 = (f32[320]{0:T(512)S(1)}, f32[320]{0:T(512)}, u32[]{:S(2)}) copy-start(f32[320]{0:T(512)} %param.11) | copy-start | bytes 3844
  190.3 260.9 %copy-start.3 = (s32[1024]{0:T(1024)S(1)}, s32[1024]{0:T(1024)}, u32[]{:S(2)}) copy-start(s32[1024]{0:T(1024)} %param.13) | copy-start | bytes 12292
  190.3 261.6 %copy-start.4 = (f32[1024]{0:T(1024)S(1)}, f32[1024]{0:T(1024)}, u32[]{:S(2)}) copy-start(f32[1024]{0:T(1024)} %param.12) | copy-start | bytes 12292
  190.4 261.8 %all-gather.5.cloned.1.call-start = ((), (), s32[]{:S(2)}) async-start(), calls=%async_computation.3 | async-start | bytes 2162688 | tf_op jit(solution)/shard_map/all_gather | solution.py:47
  193.1 258.9 %all-to-all-start = ((bf16[32,32,160]{2,0,1:T(8,128)(2,1)}), bf16[32,32,160]{2,0,1:T(8,128)(2,1)S(1)}, u32[]{:S(2)}, u32[]{:S(2)}) async-start(bf16[32,32,160]{2,0,1:T(8,128)(2,1)} %copy.11), calls=%async_computation | async-start | bytes 1048576 | tf_op jit(solution)/shard_map/all_to_all | solution.py:43
Sparse Core Ops, SparseCore 0:
  11.1 162.9 all-gather.2
  190.5 135.6 reduce-scatter.3
  329.3 76.0 all-gather.4
where the time goes:
time: 470 us; the launch traced here: 462 us
  waiting for transfers between devices  276 us (59%)
  blocking collectives  123 us (26%)
  local copies, waits for them, and re-layouts  19.4 us (4%)
  between operations  14.5 us (3%)
  matrix products  14 us (3%)
  starting transfers between devices  12.8 us (3%)
    all_gather x1, waiting for transfers between devices, per_device(): lax.all_gather(down_weight, 'member', axis=0, tiled=True)  156 us
    unnamed x4, waiting for transfers between devices  120 us
    unnamed x1, blocking collectives  80.2 us
    psum x1, blocking collectives, per_device(): dots = lax.psum(dots_part, 'tensor')  42.7 us
    all_to_all x1, starting transfers between devices, per_device(): lax.all_to_all(member_left, 'member', split_axis=1, concat_axis=0, tiled=...  12.6 us
    dot_general x1, matrix products, per_device(): lax.dot_general(features, lax.all_gather(down_weight, 'member', axis=0, t...  10.6 us
  transfers between devices with their start and end apart: 4, of which 2 were waited for; matrix products, arithmetic and copies ran while one was open for 3% of the time, Pallas kernels for 0%

commit v1 on v0

v1 whole, which is shorter than its diff:
```python
import jax
import jax.numpy as jnp
from jax import lax
from jax.sharding import Mesh, PartitionSpec as P

D = 5120
FF = 16384
AXES = ("zh", "y", "c", "x", "zl")
SIZES = (4, 4, 2, 4, 4)


def place(*index):
    at = 0
    for i, size in zip(index, SIZES):
        at = at * size + i
    return at


def ring(step):
    return [(i, (i + step) % 4) for i in range(4)]


def swapped(flip):
    return [
        (place(zh, y, c, x, zl), place(x, zl, c ^ flip, zh, y))
        for zh in range(4) for y in range(4) for c in range(2) for x in range(4) for zl in range(4)
    ]


def turned(flip):
    return [
        ((y * 2 + c) * 4 + zl, (zl * 2 + (c ^ flip)) * 4 + y)
        for y in range(4) for c in range(2) for zl in range(4)
    ]


def move(value, axis, step):
    return lax.ppermute(value, axis, ring(step))


def per_device(features, down_weight, member_left, member_right, probe, payoff, opponent):
    f32, bf16 = jnp.float32, jnp.bfloat16
    rows, width = features.shape
    members = member_right.shape[0]
    tokens = rows // members
    population = payoff.shape[0]
    block = down_weight.shape[0]
    cols = probe.shape[0]
    spread = 1.0 / jnp.sqrt(f32(FF))
    zh, y, c, x, zl = (lax.axis_index(a) for a in AXES)
    first = c == 0

    own = jnp.concatenate([down_weight, member_right], axis=0)
    cut = own.shape[0] // 2
    before = move(own, "zh", 1)
    after = move(own, "zh", -1)
    gathered = lax.all_gather(features, ("y", "c"), axis=0, tiled=True)
    far = jnp.concatenate([move(before[:cut], "zh", 1), move(after[cut:], "zh", -1)], axis=0)

    left_cols = lax.dynamic_slice(member_left, (0, (x * 4 + zl) * cols), (members, cols)).astype(f32)
    payload = jnp.concatenate([left_cols, probe[None, :]], axis=0)
    mine = jnp.where(first, payload[:, :block], payload[:, block:])
    other = jnp.where(first, payload[:, block:], payload[:, :block])
    mine = lax.ppermute(mine, AXES, swapped(0))
    other = lax.ppermute(other, AXES, swapped(1))
    left_mine = mine[:members].astype(bf16)
    left_other = other[:members].astype(bf16)
    left_pair = jnp.where(
        first, jnp.concatenate([left_mine, left_other], 0), jnp.concatenate([left_other, left_mine], 0)
    )
    left_all = lax.all_gather(left_pair, ("x", "zl"), axis=0, tiled=True)

    direction = jnp.sum(down_weight.astype(f32) * mine[members][:, None], axis=0)
    direction = lax.psum(lax.psum(direction, ("y", "c")), "zh")
    wide = features.astype(f32)
    along = jnp.sum(wide * direction[None, :], axis=1)
    inner = jnp.sum(
        wide.reshape(members, tokens, width) * member_right.astype(f32)[:, None, :], axis=2
    ).reshape(rows)
    left_dot = jnp.sum(left_cols * probe[None, :], axis=1)
    sums = jnp.concatenate([along, inner, left_dot])
    sums = lax.psum(lax.psum(sums, "x"), "zl")
    along, inner, left_dot = sums[:rows], spread * sums[rows : 2 * rows], sums[2 * rows :]
    dots = along + inner * jnp.repeat(left_dot, tokens)
    scale = 0.5 / jnp.sqrt(f32(D))
    own_score = jnp.mean(jnp.tanh(scale * dots).reshape(members, tokens), axis=1)
    score = lax.dynamic_update_slice(
        jnp.zeros((population,), f32), own_score, (((zh * 4 + y) * 2 + c) * members,)
    )
    score = lax.psum(lax.psum(score, ("y", "c")), "zh")
    labels = jnp.arange(population, dtype=jnp.int32)
    rival = jnp.sum(jnp.where(opponent[:, None] == labels[None, :], score[None, :], 0.0), axis=1)
    fitness = payoff * (score - rival)

    stack = jnp.stack([own, after, far, before])
    parts = []
    for k in range(4):
        weight = lax.dynamic_index_in_dim(stack, lax.rem(x + k + 4 - zh, 4), 0, keepdims=False)[:block]
        part = lax.dot_general(
            weight, gathered, (((1,), (1,)), ((), ())), preferred_element_type=f32
        ).astype(bf16)
        parts.append(part if k == 0 else move(part, "x", k))
    total = sum(p.astype(f32) for p in parts).astype(bf16)
    span = 2 * rows
    parts = []
    for k in range(4):
        part = lax.dynamic_slice(total, (0, lax.rem(zl + k, 4) * span), (block, span))
        parts.append(part if k == 0 else move(part, "zl", k))
    total = sum(p.astype(f32) for p in parts).astype(bf16)
    low, high = total[:, :rows], total[:, rows:]
    same = lax.ppermute(jnp.where(first, low, high), ("y", "c", "zl"), turned(0))
    cross = lax.ppermute(jnp.where(first, high, low), ("y", "c", "zl"), turned(1))
    total = jnp.where(
        first, jnp.concatenate([same, cross], 0), jnp.concatenate([cross, same], 0)
    ).astype(f32).T
    lowrank = inner.reshape(members, tokens)[:, :, None] * left_cols[:, None, :]
    mixed = (total + lowrank.reshape(rows, cols)).astype(bf16)

    rights = jnp.roll(stack[:, block:], zh, axis=0)
    right_all = lax.all_gather(rights, ("y", "c"), axis=0, tiled=False)
    scaled = (fitness[:, None] * left_all.astype(f32)).astype(bf16)
    scaled = scaled.reshape(4, 8, members, block).transpose(1, 0, 2, 3).reshape(population, block)
    term = lax.dot_general(
        scaled, right_all.reshape(population, width), (((0,), (0,)), ((), ())),
        preferred_element_type=f32,
    )
    return mixed, term / jnp.sqrt(f32(population))


def solution(mesh):
    fine = Mesh(mesh.devices.reshape(SIZES), AXES)
    member, tensor = ("zh", "y", "c"), ("x", "zl")
    in_specs = (
        P(member, tensor), P(member, tensor), P(member, None), P(member, tensor), P(tensor), P(), P(),
    )
    out_specs = (P(member, tensor), P(member, tensor))
    return jax.shard_map(
        per_device, mesh=fine, in_specs=in_specs, out_specs=out_specs, check_vma=False
    )
```

time: 470 us -> 270 us (0.57)
  waiting for transfers between devices: 276 us -> 37.9 us
  starting transfers between devices: 12.8 us -> 57.2 us
  local copies, waits for them, and re-layouts: 19.4 us -> 5.96 us
  blocking collectives: 123 us -> 134 us
    all_gather x2, waiting for transfers between devices: 156 us -> 0.04 us  [the longest x1 0.02 us: per_device(): right_all = lax.all_gather(rights, ('y', 'c'), axis=0, tiled=False)]
    unnamed x4 -> x2, waiting for transfers between devices: 120 us -> 0.7 us
    unnamed x1 -> x0, blocking collectives: 80.2 us -> none
    ppermute x0 -> x14, starting transfers between devices: none -> 57.1 us  [the longest x10 39.9 us: move(): return lax.ppermute(value, axis, ring(step))]
    psum x1 -> x6, blocking collectives: 42.7 us -> 88.4 us  [the longest x2 40.3 us: per_device(): direction = lax.psum(lax.psum(direction, ('y', 'c')), 'zh')]
    all_gather x0 -> x1, blocking collectives: none -> 45.4 us  [per_device(): left_all = lax.all_gather(left_pair, ('x', 'zl'), axis=0, tiled=True)]
    ppermute x0 -> x14, waiting for transfers between devices: none -> 37.2 us  [the longest x10 20.5 us: move(): return lax.ppermute(value, axis, ring(step))]
    all_to_all x1 -> x0, starting transfers between devices: 12.6 us -> none  [per_device(): lax.all_to_all(member_left, 'member', split_axis=1, concat_axis=0, tiled=...]
  transfers between devices with their start and end apart: 4 -> 16, of which waited for: 2 -> 7; matrix products, arithmetic and copies ran while one was open for 3% -> 8% of each run, Pallas kernels for 0% -> 0%
where the time goes in v1:
time: 270 us; the launch traced here: 266 us
  blocking collectives  134 us (50%)
  starting transfers between devices  57.2 us (21%)
  waiting for transfers between devices  37.9 us (14%)
  between operations  14.6 us (5%)
  matrix products  9.77 us (4%)
  other arithmetic  6.35 us (2%)
  local copies, waits for them, and re-layouts  5.96 us (2%)
    all_gather x1, blocking collectives, per_device(): left_all = lax.all_gather(left_pair, ('x', 'zl'), axis=0, tiled=True)  45.4 us
    psum x2, blocking collectives, per_device(): direction = lax.psum(lax.psum(direction, ('y', 'c')), 'zh')  40.3 us
    ppermute x10, starting transfers between devices, move(): return lax.ppermute(value, axis, ring(step))  39.9 us
    psum x2, blocking collectives, per_device(): score = lax.psum(lax.psum(score, ('y', 'c')), 'zh')  24.2 us
    psum x2, blocking collectives, per_device(): sums = lax.psum(lax.psum(sums, 'x'), 'zl')  23.8 us
    ppermute x10, waiting for transfers between devices, move(): return lax.ppermute(value, axis, ring(step))  20.5 us
    ppermute x1, waiting for transfers between devices, per_device(): other = lax.ppermute(other, AXES, swapped(1))  11.9 us
    dot_general x4, matrix products, per_device(): lax.dot_general(weight, gathered, (((1,), (1,)), ((), ())), preferred_ele...  6.81 us
  transfers between devices with their start and end apart: 16, of which 7 were waited for; matrix products, arithmetic and copies ran while one was open for 8% of the time, Pallas kernels for 0%

profile of v1, /device:TPU:24, one launch (start us, length us, event | category | flops | bytes accessed | tf_op | source)
XLA Modules:
  0.0 265.5 jit_solution(8847667842412016814)
XLA Ops:
  7.2 0.7 all-gather.4.cloned.1.call-update
  8.0 1.0 constant_dynamic-update-slice_fusion.1
  9.0 0.8 constant_dynamic-update-slice_fusion
  9.8 9.1 %collective-permute-start.1 = (bf16[192,1024]{1,0:T(8,128)(2,1)S(1)}, bf16[192,1024]{1,0:T(8,128)(2,1)}, u32[]{:S(2)}, u32[]{:S(2)}) collective-permute-start(bf16[192,1024]{1,0:T(8,128)(2,1)S(1)} %constant_dynamic-update-slice_fusion), channel_id=1, source_target_pairs={{0,128},{128,256},{256,384},{384,0},{1,129},{129,257},{257,385},{3... | collective-permute-start | bytes 1179656 | tf_op jit(solution)/shard_map/ppermute | solution.py:38
  18.9 5.6 %collective-permute-start = (bf16[192,1024]{1,0:T(8,128)(2,1)S(1)}, bf16[192,1024]{1,0:T(8,128)(2,1)}, u32[]{:S(2)}, u32[]{:S(2)}) collective-permute-start(bf16[192,1024]{1,0:T(8,128)(2,1)S(1)} %constant_dynamic-update-slice_fusion), channel_id=1, source_target_pairs={{0,384},{128,0},{256,128},{384,256},{1,385},{129,1},{257,129},{385... | collective-permute-start | bytes 1179656 | tf_op jit(solution)/shard_map/ppermute | solution.py:38
  24.5 0.7 broadcast_in_dim.12
  25.2 0.8 dynamic-slice_convert_fusion
  26.1 3.5 %collective-permute-start.12 = (f32[33,160]{1,0:T(8,128)S(1)}, f32[33,160]{1,0:T(8,128)S(1)}, u32[]{:S(2)}, u32[]{:S(2)}) collective-permute-start(f32[33,160]{1,0:T(8,128)S(1)} %fusion.9), channel_id=1, source_target_pairs={{0,0},{1,32},{2,64},{3,96},{4,128},{5,160},{6,192},{7,224},{8,256}... | collective-permute-start | bytes 63368 | tf_op jit(solution)/shard_map/ppermute | solution.py:64
  29.7 5.1 %collective-permute-start.13 = (bf16[33,160]{1,0:T(8,128)(2,1)S(1)}, bf16[33,160]{1,0:T(8,128)(2,1)S(1)}, u32[]{:S(2)}, u32[]{:S(2)}) collective-permute-start(bf16[33,160]{1,0:T(8,128)(2,1)S(1)} %fusion.10), channel_id=1, source_target_pairs={{0,16},{1,48},{2,80},{3,112},{4,144},{5,176},{6,208},{7,240},{8,27... | collective-permute-start | bytes 31688 | tf_op jit(solution)/shard_map/ppermute | solution.py:65
  34.8 1.0 multiply_reduce_fusion.1
  36.4 11.9 %collective-permute-done.13 = bf16[33,160]{1,0:T(8,128)(2,1)S(1)} collective-permute-done((bf16[33,160]{1,0:T(8,128)(2,1)S(1)}, bf16[33,160]{1,0:T(8,128)(2,1)S(1)}, u32[]{:S(2)}, u32[]{:S(2)}) %collective-permute-start.13) | collective-permute-done | bytes 10592 | tf_op jit(solution)/shard_map/ppermute | solution.py:65
  48.3 4.1 %collective-permute-done.12 = f32[33,160]{1,0:T(8,128)S(1)} collective-permute-done((f32[33,160]{1,0:T(8,128)S(1)}, f32[33,160]{1,0:T(8,128)S(1)}, u32[]{:S(2)}, u32[]{:S(2)}) %collective-permute-start.12) | collective-permute-done | bytes 21152 | tf_op jit(solution)/shard_map/ppermute | solution.py:64
  52.6 26.5 %psum.42 = f32[1024]{0:T(1024)S(1)} all-reduce(f32[1024]{0:T(1024)S(1)} %multiply_reduce_fusion), channel_id=1, replica_groups=mesh['zh'=4,'y'=4,'c'=2,'x'=4,'zl'=4] {'y','c'}, use_global_device_ids=true, to_apply=%region_1.2 | all-reduce | flops 1024 | bytes 8192 | tf_op jit(solution)/shard_map/psum | solution.py:74
  79.2 13.8 %psum.43 = f32[1024]{0:T(1024)S(1)} all-reduce(f32[1024]{0:T(1024)S(1)} %psum.42), channel_id=1, replica_groups=mesh['zh'=4,'y'=4,'c'=2,'x'=4,'zl'=4] {'zh'}, use_global_device_ids=true, to_apply=%region_2.3 | all-reduce | flops 1024 | bytes 8192 | tf_op jit(solution)/shard_map/psum | solution.py:74
  92.9 0.2 fusion.2
  93.3 11.0 %psum.44 = f32[416]{0:T(512)S(1)} all-reduce(f32[416]{0:T(512)S(1)} %pad_maximum_fusion.2), channel_id=1, replica_groups=mesh['zh'=4,'y'=4,'c'=2,'x'=4,'zl'=4] {'x'}, use_global_device_ids=true, to_apply=%region_6.7 | all-reduce | flops 416 | bytes 3328 | tf_op jit(solution)/shard_map/psum | solution.py:82
  104.2 12.8 %psum.45 = f32[416]{0:T(512)S(1)} all-reduce(f32[416]{0:T(512)S(1)} %psum.44), channel_id=1, replica_groups=mesh['zh'=4,'y'=4,'c'=2,'x'=4,'zl'=4] {'zl'}, use_global_device_ids=true, to_apply=%region_7.8 | all-reduce | flops 416 | bytes 3328 | tf_op jit(solution)/shard_map/psum | solution.py:82
  117.4 0.9 slice.95
  118.3 7.2 %collective-permute-start.3 = (bf16[96,1024]{1,0:T(8,128)(2,1)S(1)}, bf16[96,1024]{1,0:T(8,128)(2,1)S(1)}, u32[]{:S(2)}, u32[]{:S(2)}) collective-permute-start(bf16[96,1024]{1,0:T(8,128)(2,1)S(1)} %slice.95), channel_id=1, source_target_pairs={{0,384},{128,0},{256,128},{384,256},{1,385},{129,1},{257,129},{385... | collective-permute-start | bytes 589832 | tf_op jit(solution)/shard_map/ppermute | solution.py:38
  125.6 0.9 slice.94
  126.5 2.5 collective-permute-start.2
  129.1 7.3 %collective-permute-done.3 = bf16[96,1024]{1,0:T(8,128)(2,1)S(1)} collective-permute-done((bf16[96,1024]{1,0:T(8,128)(2,1)S(1)}, bf16[96,1024]{1,0:T(8,128)(2,1)S(1)}, u32[]{:S(2)}, u32[]{:S(2)}) %collective-permute-start.3) | collective-permute-done | bytes 196640 | tf_op jit(solution)/shard_map/ppermute | solution.py:38
  136.4 6.9 %collective-permute-done.2 = bf16[96,1024]{1,0:T(8,128)(2,1)S(1)} collective-permute-done((bf16[96,1024]{1,0:T(8,128)(2,1)S(1)}, bf16[96,1024]{1,0:T(8,128)(2,1)S(1)}, u32[]{:S(2)}, u32[]{:S(2)}) %collective-permute-start.2) | collective-permute-done | bytes 196640 | tf_op jit(solution)/shard_map/ppermute | solution.py:38
  143.3 1.3 pad_maximum_fusion
  144.7 0.8 fusion.7
  145.8 10.0 %psum.46 = f32[1024]{0:T(1024)S(1)} all-reduce(f32[1024]{0:T(1024)S(1)} %multiply_dynamic-update-slice_fusion), channel_id=1, replica_groups=mesh['zh'=4,'y'=4,'c'=2,'x'=4,'zl'=4] {'y','c'}, use_global_device_ids=true, to_apply=%region_9.10 | all-reduce | flops 1024 | bytes 8192 | tf_op jit(solution)/shard_map/psum | solution.py:90
  155.8 14.2 %psum.47 = f32[1024]{0:T(1024)S(1)} all-reduce(f32[1024]{0:T(1024)S(1)} %psum.46), channel_id=1, replica_groups=mesh['zh'=4,'y'=4,'c'=2,'x'=4,'zl'=4] {'zh'}, use_global_device_ids=true, to_apply=%region_10.11 | all-reduce | flops 1024 | bytes 8192 | tf_op jit(solution)/shard_map/psum | solution.py:90
  170.0 0.7 select_reduce_fusion
  170.8 3.2 %convolution_convert_fusion = bf16[160,1536]{1,0:T(8,128)(2,1)S(1)} fusion(bf16[1536,1024]{1,0:T(8,128)(2,1)} %all-gather.4.cloned.1.call-done, bf16[4,192,1024]{2,1,0:T(8,128)(2,1)S(1)} %pad_maximum_fusion, s32[]{:T(128)S(6)} %select_n.93), kind=kOutput, calls=%fused_computation.2 | convolution fusion | flops 503562240 | bytes 3964932 | tf_op jit(solution)/shard_map/dot_general | solution.py:99
  174.0 1.9 collective-permute-start.6
  175.9 1.2 convolution_convert_fusion.1
  177.2 3.0 %collective-permute-start.5 = (bf16[160,1536]{1,0:T(8,128)(2,1)S(1)}, bf16[160,1536]{1,0:T(8,128)(2,1)S(1)}, u32[]{:S(2)}, u32[]{:S(2)}) collective-permute-start(bf16[160,1536]{1,0:T(8,128)(2,1)S(1)} %convolution_convert_fusion.1), channel_id=1, source_target_pairs={{0,8},{4,12},{8,0},{12,4},{1,9},{5,13},{9,1},{13,5},{2,10},{6,14},... | collective-permute-start | bytes 1474568 | tf_op jit(solution)/shard_map/ppermute | solution.py:38
  180.1 1.2 convolution_convert_fusion.2
  181.3 2.9 %collective-permute-start.4 = (bf16[160,1536]{1,0:T(8,128)(2,1)S(1)}, bf16[160,1536]{1,0:T(8,128)(2,1)S(1)}, u32[]{:S(2)}, u32[]{:S(2)}) collective-permute-start(bf16[160,1536]{1,0:T(8,128)(2,1)S(1)} %convolution_convert_fusion.2), channel_id=1, source_target_pairs={{0,4},{4,8},{8,12},{12,0},{1,5},{5,9},{9,13},{13,1},{2,6},{6,10},{... | collective-permute-start | bytes 1474568 | tf_op jit(solution)/shard_map/ppermute | solution.py:38
  184.2 45.4 %all_gather.13 = bf16[1024,160]{1,0:T(8,128)(2,1)S(1)} all-gather(bf16[64,160]{1,0:T(8,128)(2,1)S(1)} %maximum_select_fusion.1), channel_id=1, replica_groups=mesh['zh'=4,'y'=4,'c'=2,'x'=4,'zl'=4] {'x','zl'}, dimensions={0}, use_global_device_ids=true | all-gather | bytes 348160 | tf_op jit(solution)/shard_map/all_gather | solution.py:71
  229.6 1.2 fusion
  230.8 0.3 add_convert_fusion
  231.2 1.9 collective-permute-start.9
  233.1 3.8 %collective-permute-start.8 = (bf16[160,384]{1,0:T(8,128)(2,1)S(1)}, bf16[160,384]{1,0:T(8,128)(2,1)S(1)}, u32[]{:S(2)}, u32[]{:S(2)}) collective-permute-start(bf16[160,384]{1,0:T(8,128)(2,1)S(1)} %get-tuple-element.14), channel_id=1, source_target_pairs={{0,2},{1,3},{2,0},{3,1},{4,6},{5,7},{6,4},{7,5},{8,10},{9,11},{10,... | collective-permute-start | bytes 368648 | tf_op jit(solution)/shard_map/ppermute | solution.py:38
  236.9 2.0 collective-permute-start.7
  239.0 0.2 multiply_convert_fusion
  239.2 1.6 collective-permute-done.8
  240.8 4.7 %collective-permute-done.7 = bf16[160,384]{1,0:T(8,128)(2,1)S(1)} collective-permute-done((bf16[160,384]{1,0:T(8,128)(2,1)S(1)}, bf16[160,384]{1,0:T(8,128)(2,1)S(1)}, u32[]{:S(2)}, u32[]{:S(2)}) %collective-permute-start.7) | collective-permute-done | bytes 122912 | tf_op jit(solution)/shard_map/ppermute | solution.py:38
  245.7 1.9 collective-permute-start.11
  247.6 6.6 %collective-permute-start.10 = (bf16[160,192]{1,0:T(8,128)(2,1)S(1)}, bf16[160,192]{1,0:T(8,128)(2,1)S(1)}, u32[]{:S(2)}, u32[]{:S(2)}) collective-permute-start(bf16[160,192]{1,0:T(8,128)(2,1)S(1)} %get-tuple-element.15), channel_id=1, source_target_pairs={{0,0},{1,32},{2,64},{3,96},{16,16},{17,48},{18,80},{19,112},{32,1}... | collective-permute-start | bytes 184328 | tf_op jit(solution)/shard_map/ppermute | solution.py:111
  254.3 3.0 %fusion.1 = f32[160,1024]{1,0:T(8,128)} fusion(bf16[8,4,32,1024]{3,2,1,0:T(8,128)(2,1)} %bitcast.38, bf16[4,8,32,160]{3,2,1,0:T(8,128)(2,1)S(1)} %bitcast.39), kind=kOutput, calls=%fused_computation.9 | convolution fusion | flops 335708160 | bytes 3080192 | tf_op jit(solution)/shard_map/dot_general | solution.py:123
  257.3 0.6 collective-permute-done.10
  257.9 0.8 copy.20
  (54 shorter events, 2.0 us)
Async XLA Ops:
  7.2 28.9 %copy-start.3 = (bf16[32,1024]{1,0:T(8,128)(2,1)S(1)}, bf16[32,1024]{1,0:T(8,128)(2,1)}, u32[]{:S(2)}) copy-start(bf16[32,1024]{1,0:T(8,128)(2,1)} %param.10) | copy-start | bytes 196612
  7.2 163.6 %all-gather.4.cloned.1.call-start = ((), (), s32[]{:S(2)}) async-start(), calls=%async_computation | async-start | bytes 3538944 | tf_op jit(solution)/shard_map/all_gather | solution.py:57
  7.9 246.4 %all-gather.6.cloned.1.call-start = ((), (), s32[]{:S(2)}) async-start(), calls=%async_computation.1 | async-start | bytes 2359296 | tf_op jit(solution)/shard_map/all_gather | solution.py:120
  9.8 115.8 %collective-permute-start.1 = (bf16[192,1024]{1,0:T(8,128)(2,1)S(1)}, bf16[192,1024]{1,0:T(8,128)(2,1)}, u32[]{:S(2)}, u32[]{:S(2)}) collective-permute-start(bf16[192,1024]{1,0:T(8,128)(2,1)S(1)} %constant_dynamic-update-slice_fusion), channel_id=1, source_target_pairs={{0,128},{128,256},{256,384},{384,0},{1,129},{129,257},{257,385},{3... | collective-permute-start | bytes 1179656 | tf_op jit(solution)/shard_map/ppermute | solution.py:38
  18.9 98.5 %collective-permute-start = (bf16[192,1024]{1,0:T(8,128)(2,1)S(1)}, bf16[192,1024]{1,0:T(8,128)(2,1)}, u32[]{:S(2)}, u32[]{:S(2)}) collective-permute-start(bf16[192,1024]{1,0:T(8,128)(2,1)S(1)} %constant_dynamic-update-slice_fusion), channel_id=1, source_target_pairs={{0,384},{128,0},{256,128},{384,256},{1,385},{129,1},{257,129},{385... | collective-permute-start | bytes 1179656 | tf_op jit(solution)/shard_map/ppermute | solution.py:38
  26.1 26.4 %collective-permute-start.12 = (f32[33,160]{1,0:T(8,128)S(1)}, f32[33,160]{1,0:T(8,128)S(1)}, u32[]{:S(2)}, u32[]{:S(2)}) collective-permute-start(f32[33,160]{1,0:T(8,128)S(1)} %fusion.9), channel_id=1, source_target_pairs={{0,0},{1,32},{2,64},{3,96},{4,128},{5,160},{6,192},{7,224},{8,256}... | collective-permute-start | bytes 63368 | tf_op jit(solution)/shard_map/ppermute | solution.py:64
  29.7 18.7 %collective-permute-start.13 = (bf16[33,160]{1,0:T(8,128)(2,1)S(1)}, bf16[33,160]{1,0:T(8,128)(2,1)S(1)}, u32[]{:S(2)}, u32[]{:S(2)}) collective-permute-start(bf16[33,160]{1,0:T(8,128)(2,1)S(1)} %fusion.10), channel_id=1, source_target_pairs={{0,16},{1,48},{2,80},{3,112},{4,144},{5,176},{6,208},{7,240},{8,27... | collective-permute-start | bytes 31688 | tf_op jit(solution)/shard_map/ppermute | solution.py:65
  35.8 16.6 %copy-start.2 = (bf16[160,1024]{1,0:T(8,128)(2,1)S(1)}, bf16[160,1024]{1,0:T(8,128)(2,1)}, u32[]{:S(2)}) copy-start(bf16[160,1024]{1,0:T(8,128)(2,1)} %param.8) | copy-start | bytes 983044
  35.9 57.0 %copy-start.1 = (bf16[192,1024]{1,0:T(8,128)(2,1)S(1)}, bf16[192,1024]{1,0:T(8,128)(2,1)}, u32[]{:S(2)}) copy-start(bf16[192,1024]{1,0:T(8,128)(2,1)} %param.7) | copy-start | bytes 1179652
  48.3 96.3 %copy-start.4 = (bf16[33,160]{1,0:T(8,128)(2,1)}, bf16[33,160]{1,0:T(8,128)(2,1)S(1)}, u32[]{:S(2)}) copy-start(bf16[33,160]{1,0:T(8,128)(2,1)S(1)} %collective-permute-done.13) | copy-start | bytes 31684
  118.3 18.0 %collective-permute-start.3 = (bf16[96,1024]{1,0:T(8,128)(2,1)S(1)}, bf16[96,1024]{1,0:T(8,128)(2,1)S(1)}, u32[]{:S(2)}, u32[]{:S(2)}) collective-permute-start(bf16[96,1024]{1,0:T(8,128)(2,1)S(1)} %slice.95), channel_id=1, source_target_pairs={{0,384},{128,0},{256,128},{384,256},{1,385},{129,1},{257,129},{385... | collective-permute-start | bytes 589832 | tf_op jit(solution)/shard_map/ppermute | solution.py:38
  126.5 16.7 %collective-permute-start.2 = (bf16[96,1024]{1,0:T(8,128)(2,1)S(1)}, bf16[96,1024]{1,0:T(8,128)(2,1)S(1)}, u32[]{:S(2)}, u32[]{:S(2)}) collective-permute-start(bf16[96,1024]{1,0:T(8,128)(2,1)S(1)} %slice.94), channel_id=1, source_target_pairs={{0,128},{128,256},{256,384},{384,0},{1,129},{129,257},{257,385},{3... | collective-permute-start | bytes 589832 | tf_op jit(solution)/shard_map/ppermute | solution.py:38
  143.3 26.8 %copy-start.5 = (s32[1024]{0:T(1024)S(1)}, s32[1024]{0:T(1024)}, u32[]{:S(2)}) copy-start(s32[1024]{0:T(1024)} %param.13) | copy-start | bytes 12292
  143.3 27.4 %copy-start.6 = (f32[1024]{0:T(1024)S(1)}, f32[1024]{0:T(1024)}, u32[]{:S(2)}) copy-start(f32[1024]{0:T(1024)} %param.12) | copy-start | bytes 12292
  170.8 5.2 %copy-start = (bf16[1536,1024]{1,0:T(8,128)(2,1)S(1)}, bf16[1536,1024]{1,0:T(8,128)(2,1)}, u32[]{:S(2)}) copy-start(bf16[1536,1024]{1,0:T(8,128)(2,1)} %all-gather.4.cloned.1.call-done) | copy-start | bytes 9437188
  174.0 56.8 %collective-permute-start.6 = (bf16[160,1536]{1,0:T(8,128)(2,1)S(1)}, bf16[160,1536]{1,0:T(8,128)(2,1)S(1)}, u32[]{:S(2)}, u32[]{:S(2)}) collective-permute-start(bf16[160,1536]{1,0:T(8,128)(2,1)S(1)} %convolution_convert_fusion), channel_id=1, source_target_pairs={{0,12},{4,0},{8,4},{12,8},{1,13},{5,1},{9,5},{13,9},{2,14},{6,2},{... | collective-permute-start | bytes 1474568 | tf_op jit(solution)/shard_map/ppermute | solution.py:38
  177.1 7.1 %slice-start = ((bf16[33,160]{1,0:T(8,128)(2,1)}), bf16[32,160]{1,0:T(8,128)(2,1)S(1)}, s32[]{:S(2)}) async-start(bf16[33,160]{1,0:T(8,128)(2,1)} %copy-done.4), calls=%async_computation.2 | async-start | bytes 32768 | tf_op jit(solution)/shard_map/slice | solution.py:67
  177.2 53.7 %collective-permute-start.5 = (bf16[160,1536]{1,0:T(8,128)(2,1)S(1)}, bf16[160,1536]{1,0:T(8,128)(2,1)S(1)}, u32[]{:S(2)}, u32[]{:S(2)}) collective-permute-start(bf16[160,1536]{1,0:T(8,128)(2,1)S(1)} %convolution_convert_fusion.1), channel_id=1, source_target_pairs={{0,8},{4,12},{8,0},{12,4},{1,9},{5,13},{9,1},{13,5},{2,10},{6,14},... | collective-permute-start | bytes 1474568 | tf_op jit(solution)/shard_map/ppermute | solution.py:38
  181.3 49.5 %collective-permute-start.4 = (bf16[160,1536]{1,0:T(8,128)(2,1)S(1)}, bf16[160,1536]{1,0:T(8,128)(2,1)S(1)}, u32[]{:S(2)}, u32[]{:S(2)}) collective-permute-start(bf16[160,1536]{1,0:T(8,128)(2,1)S(1)} %convolution_convert_fusion.2), channel_id=1, source_target_pairs={{0,4},{4,8},{8,12},{12,0},{1,5},{5,9},{9,13},{13,1},{2,6},{6,10},{... | collective-permute-start | bytes 1474568 | tf_op jit(solution)/shard_map/ppermute | solution.py:38
  231.2 8.0 %collective-permute-start.9 = (bf16[160,384]{1,0:T(8,128)(2,1)S(1)}, bf16[160,384]{1,0:T(8,128)(2,1)S(1)}, u32[]{:S(2)}, u32[]{:S(2)}) collective-permute-start(bf16[160,384]{1,0:T(8,128)(2,1)S(1)} %get-tuple-element.13), channel_id=1, source_target_pairs={{0,3},{1,0},{2,1},{3,2},{4,7},{5,4},{6,5},{7,6},{8,11},{9,8},{10,9... | collective-permute-start | bytes 368648 | tf_op jit(solution)/shard_map/ppermute | solution.py:38
  233.1 7.7 %collective-permute-start.8 = (bf16[160,384]{1,0:T(8,128)(2,1)S(1)}, bf16[160,384]{1,0:T(8,128)(2,1)S(1)}, u32[]{:S(2)}, u32[]{:S(2)}) collective-permute-start(bf16[160,384]{1,0:T(8,128)(2,1)S(1)} %get-tuple-element.14), channel_id=1, source_target_pairs={{0,2},{1,3},{2,0},{3,1},{4,6},{5,7},{6,4},{7,5},{8,10},{9,11},{10,... | collective-permute-start | bytes 368648 | tf_op jit(solution)/shard_map/ppermute | solution.py:38
  236.9 8.6 %collective-permute-start.7 = (bf16[160,384]{1,0:T(8,128)(2,1)S(1)}, bf16[160,384]{1,0:T(8,128)(2,1)S(1)}, u32[]{:S(2)}, u32[]{:S(2)}) collective-permute-start(bf16[160,384]{1,0:T(8,128)(2,1)S(1)} %get-tuple-element.12), channel_id=1, source_target_pairs={{0,1},{1,2},{2,3},{3,0},{4,5},{5,6},{6,7},{7,4},{8,9},{9,10},{10,1... | collective-permute-start | bytes 368648 | tf_op jit(solution)/shard_map/ppermute | solution.py:38
  245.7 11.6 %collective-permute-start.11 = (bf16[160,192]{1,0:T(8,128)(2,1)S(1)}, bf16[160,192]{1,0:T(8,128)(2,1)S(1)}, u32[]{:S(2)}, u32[]{:S(2)}) collective-permute-start(bf16[160,192]{1,0:T(8,128)(2,1)S(1)} %get-tuple-element.16), channel_id=1, source_target_pairs={{0,16},{1,48},{2,80},{3,112},{16,0},{17,32},{18,64},{19,96},{32,17... | collective-permute-start | bytes 184328 | tf_op jit(solution)/shard_map/ppermute | solution.py:112
  247.6 10.2 %collective-permute-start.10 = (bf16[160,192]{1,0:T(8,128)(2,1)S(1)}, bf16[160,192]{1,0:T(8,128)(2,1)S(1)}, u32[]{:S(2)}, u32[]{:S(2)}) collective-permute-start(bf16[160,192]{1,0:T(8,128)(2,1)S(1)} %get-tuple-element.15), channel_id=1, source_target_pairs={{0,0},{1,32},{2,64},{3,96},{16,16},{17,48},{18,80},{19,112},{32,1}... | collective-permute-start | bytes 184328 | tf_op jit(solution)/shard_map/ppermute | solution.py:111
Sparse Core Ops, SparseCore 0:
  10.1 39.0 all-gather.3
  145.6 26.4 all-gather.5

commit v2 on v1

v2 whole, which is shorter than its diff:
```python
import jax
import jax.numpy as jnp
from jax import lax
from jax.sharding import Mesh, PartitionSpec as P

D = 5120
FF = 16384
AXES = ("zh", "y", "c", "x", "zl")
SIZES = (4, 4, 2, 4, 4)


def place(*index):
    at = 0
    for i, size in zip(index, SIZES):
        at = at * size + i
    return at


def ring(step):
    return [(i, (i + step) % 4) for i in range(4)]


def swapped(flip):
    return [
        (place(zh, y, c, x, zl), place(x, zl, c ^ flip, zh, y))
        for zh in range(4) for y in range(4) for c in range(2) for x in range(4) for zl in range(4)
    ]


def turned(flip):
    return [
        ((y * 2 + c) * 4 + zl, (zl * 2 + (c ^ flip)) * 4 + y)
        for y in range(4) for c in range(2) for zl in range(4)
    ]


def move(value, axis, step):
    return lax.ppermute(value, axis, ring(step))


def added(value, axis):
    return value + move(value, axis, 1) + move(value, axis, -1) + move(value, axis, 2)


def around(value, axis, index):
    stack = jnp.stack([value, move(value, axis, -1), move(value, axis, 2), move(value, axis, 1)])
    return jnp.roll(stack, index, axis=0)


def in_three(value):
    terms = []
    for _ in range(3):
        term = lax.reduce_precision(value, 8, 7)
        terms.append(term.astype(jnp.bfloat16))
        value = value - term
    return jnp.stack(terms)


def per_device(features, down_weight, member_left, member_right, probe, payoff, opponent):
    f32, bf16 = jnp.float32, jnp.bfloat16
    rows, width = features.shape
    members = member_right.shape[0]
    tokens = rows // members
    population = payoff.shape[0]
    block = down_weight.shape[0]
    cols = probe.shape[0]
    spread = 1.0 / jnp.sqrt(f32(FF))
    zh, y, c, x, zl = (lax.axis_index(a) for a in AXES)
    first = c == 0
    group = 8

    gathered = lax.all_gather(features, ("y", "c"), axis=0, tiled=True)

    lead = (block + members) // 2
    chunks = []
    for own in (down_weight[:lead], jnp.concatenate([down_weight[lead:], member_right], axis=0)):
        cut = own.shape[0] // 2
        before = move(own, "zh", 1)
        after = move(own, "zh", -1)
        far = [move(before[:cut], "zh", 1), move(after[cut:], "zh", -1)]
        chunks.append(jnp.concatenate([own, after] + far + [before], axis=0).reshape(4, lead, width))
    weights = [chunks[0], chunks[1][:, : block - lead]]
    rights = chunks[1][:, block - lead :]

    probes = around(probe, "x", x)
    probes = jnp.where(first, probes[:, :block], probes[:, block:])
    probes = lax.ppermute(probes, ("y", "c", "zl"), turned(0))
    probes = in_three(jnp.roll(probes, -zh, axis=0))
    direction = 0.0
    for weight, start in zip(weights, (0, lead)):
        part = probes[:, :, start : start + weight.shape[1]].reshape(3, -1)
        direction += lax.dot_general(
            part, weight.reshape(-1, width), (((1,), (0,)), ((), ())), preferred_element_type=f32
        ).sum(0)

    left_cols = lax.dynamic_slice(member_left, (0, (x * 4 + zl) * cols), (members, cols))
    mine = jnp.where(first, left_cols[:, :block], left_cols[:, block:])
    other = jnp.where(first, left_cols[:, block:], left_cols[:, :block])
    mine = lax.ppermute(mine, AXES, swapped(0))
    other = lax.ppermute(other, AXES, swapped(1))
    left_all = jnp.where(
        first, jnp.concatenate([mine, other], 0), jnp.concatenate([other, mine], 0)
    )
    left_all = around(around(left_all, "x", x), "zl", zl)

    left_cols = left_cols.astype(f32)
    along = lax.dot_general(
        in_three(direction), gathered, (((1,), (1,)), ((), ())), preferred_element_type=f32
    ).sum(0)
    inner = jnp.sum(
        features.astype(f32).reshape(members, tokens, width) * member_right.astype(f32)[:, None, :],
        axis=2,
    ).reshape(rows)
    left_dot = jnp.sum(left_cols * probe[None, :], axis=1)
    here = y * 2 + c
    inner = lax.dynamic_update_slice(jnp.zeros((group * rows,), f32), inner, (here * rows,))
    left_dot = lax.dynamic_update_slice(
        jnp.zeros((group * members,), f32), left_dot, (here * members,)
    )
    sums = jnp.concatenate([along, inner, left_dot])
    sums = sums + lax.ppermute(sums, "c", [(0, 1), (1, 0)])
    sums = added(added(added(sums, "y"), "x"), "zl")
    along, inner, left_dot = jnp.split(sums, [group * rows, 2 * group * rows])
    inner = spread * inner
    dots = along + inner * jnp.repeat(left_dot, tokens)
    scale = 0.5 / jnp.sqrt(f32(D))
    score = jnp.mean(jnp.tanh(scale * dots).reshape(group * members, tokens), axis=1)
    score = around(score, "zh", zh).reshape(population)
    labels = jnp.arange(population, dtype=jnp.int32)
    rival = jnp.sum(jnp.where(opponent[:, None] == labels[None, :], score[None, :], 0.0), axis=1)
    fitness = payoff * (score - rival)

    totals = []
    for weight in weights:
        parts = []
        for k in range(4):
            part = lax.dynamic_index_in_dim(weight, lax.rem(x + k + 4 - zh, 4), 0, keepdims=False)
            part = lax.dot_general(
                part, gathered, (((1,), (1,)), ((), ())), preferred_element_type=f32
            ).astype(bf16)
            parts.append(part if k == 0 else move(part, "x", k))
        totals.append(sum(p.astype(f32) for p in parts).astype(bf16))
    total = jnp.concatenate(totals, axis=0)
    span = 2 * rows
    parts = []
    for k in range(4):
        part = lax.dynamic_slice(total, (0, lax.rem(zl + k, 4) * span), (block, span))
        parts.append(part if k == 0 else move(part, "zl", k))
    total = sum(p.astype(f32) for p in parts).astype(bf16)
    low, high = total[:, :rows], total[:, rows:]
    same = lax.ppermute(jnp.where(first, low, high), ("y", "c", "zl"), turned(0))
    cross = lax.ppermute(jnp.where(first, high, low), ("y", "c", "zl"), turned(1))
    total = jnp.where(
        first, jnp.concatenate([same, cross], 0), jnp.concatenate([cross, same], 0)
    ).astype(f32).T
    own_inner = lax.dynamic_slice(inner, (here * rows,), (rows,))
    lowrank = own_inner.reshape(members, tokens)[:, :, None] * left_cols[:, None, :]
    mixed = (total + lowrank.reshape(rows, cols)).astype(bf16)

    right_all = lax.all_gather(jnp.roll(rights, zh, axis=0), ("y", "c"), axis=0, tiled=False)
    scaled = left_all.reshape(4, 4, 2, members, block).transpose(0, 2, 1, 3, 4).astype(f32)
    fitness = fitness.reshape(4, 4, 2, members).transpose(1, 2, 0, 3)
    scaled = (fitness[..., None] * scaled).astype(bf16).reshape(population, block)
    term = lax.dot_general(
        scaled, right_all.reshape(population, width), (((0,), (0,)), ((), ())),
        preferred_element_type=f32,
    )
    return mixed, term / jnp.sqrt(f32(population))


def solution(mesh):
    fine = Mesh(mesh.devices.reshape(SIZES), AXES)
    member, tensor = ("zh", "y", "c"), ("x", "zl")
    in_specs = (
        P(member, tensor), P(member, tensor), P(member, None), P(member, tensor), P(tensor), P(), P(),
    )
    out_specs = (P(member, tensor), P(member, tensor))
    return jax.shard_map(
        per_device, mesh=fine, in_specs=in_specs, out_specs=out_specs, check_vma=False
    )
```

time: 270 us -> 316 us (1.17)
  blocking collectives: 134 us -> 0 us
  starting transfers between devices: 57.2 us -> 178 us
  waiting for transfers between devices: 37.9 us -> 63.3 us
  local copies, waits for them, and re-layouts: 5.96 us -> 21.1 us
  matrix products: 9.77 us -> 23.8 us
    ppermute x10 -> x38, starting transfers between devices: 39.9 us -> 156 us  [move(): return lax.ppermute(value, axis, ring(step))]
    psum x6 -> x0, blocking collectives: 88.4 us -> none  [the longest x2 40.3 us: per_device(): direction = lax.psum(lax.psum(direction, ('y', 'c')), 'zh')]
    all_gather x1 -> x0, blocking collectives: 45.4 us -> none  [per_device(): left_all = lax.all_gather(left_pair, ('x', 'zl'), axis=0, tiled=True)]
    ppermute x10 -> x38, waiting for transfers between devices: 20.5 us -> 50.2 us  [move(): return lax.ppermute(value, axis, ring(step))]
    dot_general x4 -> x11, matrix products: 6.81 us -> 20.8 us  [the longest x8 19.3 us: per_device(): lax.dot_general(part, gathered, (((1,), (1,)), ((), ())), preferred_eleme...]
    ppermute x0 -> x2, starting transfers between devices: none -> 8.16 us  [the longest x1 6.24 us: per_device(): probes = lax.ppermute(probes, ('y', 'c', 'zl'), turned(0))]
    ppermute x1, waiting for transfers between devices: 11.9 us -> 4.05 us  [per_device(): other = lax.ppermute(other, AXES, swapped(1))]
    ppermute x0 -> x2, waiting for transfers between devices: none -> 7.64 us  [the longest x1 7.64 us: per_device(): probes = lax.ppermute(probes, ('y', 'c', 'zl'), turned(0))]
  transfers between devices with their start and end apart: 16 -> 46, of which waited for: 7 -> 18; matrix products, arithmetic and copies ran while one was open for 8% -> 16% of each run, Pallas kernels for 0% -> 0%
where the time goes in v2:
time: 316 us; the launch traced here: 310 us
  starting transfers between devices  178 us (56%)
  waiting for transfers between devices  63.3 us (20%)
  matrix products  23.8 us (8%)
  local copies, waits for them, and re-layouts  21.1 us (7%)
  between operations  15.2 us (5%)
  other arithmetic  7.8 us (2%)
    ppermute x38, starting transfers between devices, move(): return lax.ppermute(value, axis, ring(step))  156 us
    ppermute x38, waiting for transfers between devices, move(): return lax.ppermute(value, axis, ring(step))  50.2 us
    dot_general x8, matrix products, per_device(): lax.dot_general(part, gathered, (((1,), (1,)), ((), ())), preferred_eleme...  19.3 us
    unnamed x40, local copies, waits for them, and re-layouts  8 us
    ppermute x1, waiting for transfers between devices, per_device(): probes = lax.ppermute(probes, ('y', 'c', 'zl'), turned(0))  7.64 us
  transfers between devices with their start and end apart: 46, of which 18 were waited for; matrix products, arithmetic and copies ran while one was open for 16% of the time, Pallas kernels for 0%

profile of v2, /device:TPU:24, one launch (start us, length us, event | category | flops | bytes accessed | tf_op | source)
XLA Modules:
  0.0 309.6 jit_solution(6981247276600123655)
XLA Ops:
  8.9 12.7 %collective-permute-start = (bf16[96,1024]{1,0:T(8,128)(2,1)}, bf16[96,1024]{1,0:T(8,128)(2,1)}, u32[]{:S(2)}, u32[]{:S(2)}) collective-permute-start(bf16[96,1024]{1,0:T(8,128)(2,1)} %get-tuple-element.25), channel_id=1, source_target_pairs={{0,384},{128,0},{256,128},{384,256},{1,385},{129,1},{257,129},{385... | collective-permute-start | bytes 589832 | tf_op jit(solution)/shard_map/ppermute | solution.py:38
  23.6 4.7 %collective-permute-start.19 = (f32[320]{0:T(512)}, f32[320]{0:T(512)S(1)}, u32[]{:S(2)}, u32[]{:S(2)}) collective-permute-start(f32[320]{0:T(512)} %param.11), channel_id=1, source_target_pairs={{0,12},{4,0},{8,4},{12,8},{1,13},{5,1},{9,5},{13,9},{2,14},{6,2},{... | collective-permute-start | bytes 3848 | tf_op jit(solution)/shard_map/ppermute | solution.py:38
  28.3 2.7 collective-permute-start.20
  31.0 2.8 collective-permute-start.21
  42.5 7.8 %collective-permute-start.7 = (bf16[96,1024]{1,0:T(8,128)(2,1)}, bf16[96,1024]{1,0:T(8,128)(2,1)S(1)}, u32[]{:S(2)}, u32[]{:S(2)}) collective-permute-start(bf16[96,1024]{1,0:T(8,128)(2,1)} %pad_maximum_fusion), channel_id=1, source_target_pairs={{0,384},{128,0},{256,128},{384,256},{1,385},{129,1},{257,129},{385... | collective-permute-start | bytes 589832 | tf_op jit(solution)/shard_map/ppermute | solution.py:38
  50.3 3.5 %collective-permute-start.36 = (bf16[32,160]{1,0:T(8,128)(2,1)S(1)}, bf16[32,160]{1,0:T(8,128)(2,1)S(1)}, u32[]{:S(2)}, u32[]{:S(2)}) collective-permute-start(bf16[32,160]{1,0:T(8,128)(2,1)S(1)} %get-tuple-element.22), channel_id=1, source_target_pairs={{0,0},{1,32},{2,64},{3,96},{4,128},{5,160},{6,192},{7,224},{8,256}... | collective-permute-start | bytes 30728 | tf_op jit(solution)/shard_map/ppermute | solution.py:99
  54.0 6.2 %collective-permute-start.22 = (f32[4,160]{1,0:T(4,128)S(1)}, f32[4,160]{1,0:T(4,128)S(1)}, u32[]{:S(2)}, u32[]{:S(2)}) collective-permute-start(f32[4,160]{1,0:T(4,128)S(1)} %fusion.49), channel_id=1, source_target_pairs={{0,0},{1,32},{2,64},{3,96},{16,16},{17,48},{18,80},{19,112},{32,1}... | collective-permute-start | bytes 7688 | tf_op jit(solution)/shard_map/ppermute | solution.py:87
  61.1 7.6 %collective-permute-done.22 = f32[4,160]{1,0:T(4,128)S(1)} collective-permute-done((f32[4,160]{1,0:T(4,128)S(1)}, f32[4,160]{1,0:T(4,128)S(1)}, u32[]{:S(2)}, u32[]{:S(2)}) %collective-permute-start.22) | collective-permute-done | bytes 2592 | tf_op jit(solution)/shard_map/ppermute | solution.py:87
  70.7 3.3 %collective-permute-start.8 = (bf16[96,1024]{1,0:T(8,128)(2,1)}, bf16[96,1024]{1,0:T(8,128)(2,1)S(1)}, u32[]{:S(2)}, u32[]{:S(2)}) collective-permute-start(bf16[96,1024]{1,0:T(8,128)(2,1)} %pad_maximum_fusion), channel_id=1, source_target_pairs={{0,128},{128,256},{256,384},{384,0},{1,129},{129,257},{257,385},{3... | collective-permute-start | bytes 589832 | tf_op jit(solution)/shard_map/ppermute | solution.py:38
  74.1 4.1 %collective-permute-done.37 = bf16[32,160]{1,0:T(8,128)(2,1)S(1)} collective-permute-done((bf16[32,160]{1,0:T(8,128)(2,1)S(1)}, bf16[32,160]{1,0:T(8,128)(2,1)S(1)}, u32[]{:S(2)}, u32[]{:S(2)}) %collective-permute-start.37) | collective-permute-done | bytes 10272 | tf_op jit(solution)/shard_map/ppermute | solution.py:100
  78.1 17.1 %collective-permute-start.38 = (bf16[64,160]{1,0:T(8,128)(2,1)S(1)}, bf16[64,160]{1,0:T(8,128)(2,1)S(1)}, u32[]{:S(2)}, u32[]{:S(2)}) collective-permute-start(bf16[64,160]{1,0:T(8,128)(2,1)S(1)} %maximum_select_fusion.2), channel_id=1, source_target_pairs={{0,12},{4,0},{8,4},{12,8},{1,13},{5,1},{9,5},{13,9},{2,14},{6,2},{... | collective-permute-start | bytes 61448 | tf_op jit(solution)/shard_map/ppermute | solution.py:38
  96.8 3.7 %collective-permute-start.39 = (bf16[64,160]{1,0:T(8,128)(2,1)S(1)}, bf16[64,160]{1,0:T(8,128)(2,1)S(1)}, u32[]{:S(2)}, u32[]{:S(2)}) collective-permute-start(bf16[64,160]{1,0:T(8,128)(2,1)S(1)} %maximum_select_fusion.2), channel_id=1, source_target_pairs={{0,8},{4,12},{8,0},{12,4},{1,9},{5,13},{9,1},{13,5},{2,10},{6,14},... | collective-permute-start | bytes 61448 | tf_op jit(solution)/shard_map/ppermute | solution.py:38
  100.5 3.6 %collective-permute-done.39 = bf16[64,160]{1,0:T(8,128)(2,1)S(1)} collective-permute-done((bf16[64,160]{1,0:T(8,128)(2,1)S(1)}, bf16[64,160]{1,0:T(8,128)(2,1)S(1)}, u32[]{:S(2)}, u32[]{:S(2)}) %collective-permute-start.39) | collective-permute-done | bytes 20512 | tf_op jit(solution)/shard_map/ppermute | solution.py:38
  104.1 2.8 collective-permute-start.40
  106.9 4.5 %collective-permute-done.40 = bf16[64,160]{1,0:T(8,128)(2,1)S(1)} collective-permute-done((bf16[64,160]{1,0:T(8,128)(2,1)S(1)}, bf16[64,160]{1,0:T(8,128)(2,1)S(1)}, u32[]{:S(2)}, u32[]{:S(2)}) %collective-permute-start.40) | collective-permute-done | bytes 20512 | tf_op jit(solution)/shard_map/ppermute | solution.py:38
  114.2 4.8 %collective-permute-done.41 = bf16[4,64,160]{2,1,0:T(8,128)(2,1)S(1)} collective-permute-done((bf16[4,64,160]{2,1,0:T(8,128)(2,1)S(1)}, bf16[4,64,160]{2,1,0:T(8,128)(2,1)S(1)}, u32[]{:S(2)}, u32[]{:S(2)}) %collective-permute-start.41) | collective-permute-done | bytes 81952 | tf_op jit(solution)/shard_map/ppermute | solution.py:38
  121.6 5.6 %collective-permute-done.42 = bf16[4,64,160]{2,1,0:T(8,128)(2,1)S(1)} collective-permute-done((bf16[4,64,160]{2,1,0:T(8,128)(2,1)S(1)}, bf16[4,64,160]{2,1,0:T(8,128)(2,1)S(1)}, u32[]{:S(2)}, u32[]{:S(2)}) %collective-permute-start.42) | collective-permute-done | bytes 81952 | tf_op jit(solution)/shard_map/ppermute | solution.py:38
  127.2 2.4 collective-permute-start.43
  130.2 5.6 %collective-permute-done.43 = bf16[4,64,160]{2,1,0:T(8,128)(2,1)S(1)} collective-permute-done((bf16[4,64,160]{2,1,0:T(8,128)(2,1)S(1)}, bf16[4,64,160]{2,1,0:T(8,128)(2,1)S(1)}, u32[]{:S(2)}, u32[]{:S(2)}) %collective-permute-start.43) | collective-permute-done | bytes 81952 | tf_op jit(solution)/shard_map/ppermute | solution.py:38
  142.0 9.0 %collective-permute-start.2 = (bf16[48,1024]{1,0:T(8,128)(2,1)S(1)}, bf16[48,1024]{1,0:T(8,128)(2,1)S(1)}, u32[]{:S(2)}, u32[]{:S(2)}) collective-permute-start(bf16[48,1024]{1,0:T(8,128)(2,1)S(1)} %slice.66), channel_id=1, source_target_pairs={{0,128},{128,256},{256,384},{384,0},{1,129},{129,257},{257,385},{3... | collective-permute-start | bytes 294920 | tf_op jit(solution)/shard_map/ppermute | solution.py:38
  153.8 7.8 %collective-permute-start.9 = (bf16[48,1024]{1,0:T(8,128)(2,1)S(1)}, bf16[48,1024]{1,0:T(8,128)(2,1)S(1)}, u32[]{:S(2)}, u32[]{:S(2)}) collective-permute-start(bf16[48,1024]{1,0:T(8,128)(2,1)S(1)} %slice.68), channel_id=1, source_target_pairs={{0,128},{128,256},{256,384},{384,0},{1,129},{129,257},{257,385},{3... | collective-permute-start | bytes 294920 | tf_op jit(solution)/shard_map/ppermute | solution.py:38
  166.0 6.7 %collective-permute-done.10 = bf16[48,1024]{1,0:T(8,128)(2,1)S(1)} collective-permute-done((bf16[48,1024]{1,0:T(8,128)(2,1)S(1)}, bf16[48,1024]{1,0:T(8,128)(2,1)S(1)}, u32[]{:S(2)}, u32[]{:S(2)}) %collective-permute-start.10) | collective-permute-done | bytes 98336 | tf_op jit(solution)/shard_map/ppermute | solution.py:38
  176.1 3.9 %convolution_convert_fusion = bf16[96,1536]{1,0:T(8,128)(2,1)} fusion(bf16[1536,1024]{1,0:T(8,128)(2,1)} %all-gather.4.cloned.1.call-done, bf16[4,96,1024]{2,1,0:T(8,128)(2,1)} %bitcast.95, s32[]{:T(128)S(6)} %select_n.163), kind=kOutput, calls=%fused_computation.2 | convolution fusion | flops 302137344 | bytes 3637252 | tf_op jit(solution)/shard_map/dot_general | solution.py:138
  180.0 3.8 %collective-permute-start.6 = (bf16[96,1536]{1,0:T(8,128)(2,1)}, bf16[96,1536]{1,0:T(8,128)(2,1)}, u32[]{:S(2)}, u32[]{:S(2)}) collective-permute-start(bf16[96,1536]{1,0:T(8,128)(2,1)} %convolution_convert_fusion), channel_id=1, source_target_pairs={{0,12},{4,0},{8,4},{12,8},{1,13},{5,1},{9,5},{13,9},{2,14},{6,2},{... | collective-permute-start | bytes 884744 | tf_op jit(solution)/shard_map/ppermute | solution.py:38
  183.8 2.7 convolution_convert_fusion.1
  191.3 2.8 convolution_convert_fusion.2
  194.1 2.6 collective-permute-start.26
  198.7 5.1 %collective-permute-start.24 = (f32[3328]{0:T(1024)S(1)}, f32[3328]{0:T(1024)S(1)}, u32[]{:S(2)}, u32[]{:S(2)}) collective-permute-start(f32[3328]{0:T(1024)S(1)} %fusion.75), channel_id=1, source_target_pairs={{0,32},{32,64},{64,96},{96,0},{1,33},{33,65},{65,97},{97,1},{2,34}... | collective-permute-start | bytes 39944 | tf_op jit(solution)/shard_map/ppermute | solution.py:38
  205.6 5.5 %collective-permute-start.29 = (f32[3328]{0:T(1024)S(1)}, f32[3328]{0:T(1024)S(1)}, u32[]{:S(2)}, u32[]{:S(2)}) collective-permute-start(f32[3328]{0:T(1024)S(1)} %add_add_fusion.2), channel_id=1, source_target_pairs={{0,8},{4,12},{8,0},{12,4},{1,9},{5,13},{9,1},{13,5},{2,10},{6,14},... | collective-permute-start | bytes 39944 | tf_op jit(solution)/shard_map/ppermute | solution.py:38
  211.1 3.1 collective-permute-start.28
  214.2 2.8 collective-permute-start.27
  218.7 2.3 collective-permute-done.27
  223.0 5.1 %collective-permute-start.31 = (f32[3328]{0:T(1024)S(1)}, f32[3328]{0:T(1024)S(1)}, u32[]{:S(2)}, u32[]{:S(2)}) collective-permute-start(f32[3328]{0:T(1024)S(1)} %add_add_fusion.1), channel_id=1, source_target_pairs={{0,3},{1,0},{2,1},{3,2},{4,7},{5,4},{6,5},{7,6},{8,11},{9,8},{10,9... | collective-permute-start | bytes 39944 | tf_op jit(solution)/shard_map/ppermute | solution.py:38
  231.8 3.7 %collective-permute-done.30 = f32[3328]{0:T(1024)S(1)} collective-permute-done((f32[3328]{0:T(1024)S(1)}, f32[3328]{0:T(1024)S(1)}, u32[]{:S(2)}, u32[]{:S(2)}) %collective-permute-start.30) | collective-permute-done | bytes 13344 | tf_op jit(solution)/shard_map/ppermute | solution.py:38
  240.2 7.1 %collective-permute-start.34 = (f32[256]{0:T(256)S(1)}, f32[256]{0:T(256)S(1)}, u32[]{:S(2)}, u32[]{:S(2)}) collective-permute-start(f32[256]{0:T(256)S(1)} %broadcast_multiply_fusion), channel_id=1, source_target_pairs={{0,256},{128,384},{256,0},{384,128},{1,257},{129,385},{257,1},{385... | collective-permute-start | bytes 3080 | tf_op jit(solution)/shard_map/ppermute | solution.py:38
  247.2 6.3 %collective-permute-start.35 = (f32[256]{0:T(256)S(1)}, f32[256]{0:T(256)S(1)}, u32[]{:S(2)}, u32[]{:S(2)}) collective-permute-start(f32[256]{0:T(256)S(1)} %broadcast_multiply_fusion), channel_id=1, source_target_pairs={{0,128},{128,256},{256,384},{384,0},{1,129},{129,257},{257,385},{3... | collective-permute-start | bytes 3080 | tf_op jit(solution)/shard_map/ppermute | solution.py:38
  255.7 2.9 collective-permute-start.12
  258.6 2.8 collective-permute-start.11
  262.3 3.7 %collective-permute-start.4 = (bf16[96,1536]{1,0:T(8,128)(2,1)}, bf16[96,1536]{1,0:T(8,128)(2,1)S(1)}, u32[]{:S(2)}, u32[]{:S(2)}) collective-permute-start(bf16[96,1536]{1,0:T(8,128)(2,1)} %convolution_convert_fusion.2), channel_id=1, source_target_pairs={{0,4},{4,8},{8,12},{12,0},{1,5},{5,9},{9,13},{13,1},{2,6},{6,10},{... | collective-permute-start | bytes 884744 | tf_op jit(solution)/shard_map/ppermute | solution.py:38
  267.1 3.5 %collective-permute-done.11 = bf16[64,1536]{1,0:T(8,128)(2,1)} collective-permute-done((bf16[64,1536]{1,0:T(8,128)(2,1)}, bf16[64,1536]{1,0:T(8,128)(2,1)}, u32[]{:S(2)}, u32[]{:S(2)}) %collective-permute-start.11) | collective-permute-done | bytes 196640 | tf_op jit(solution)/shard_map/ppermute | solution.py:38
  270.6 2.3 add_convert_fusion
  273.6 2.3 fusion.4
  276.0 2.4 collective-permute-start.16
  280.3 3.4 %collective-permute-start.14 = (bf16[160,384]{1,0:T(8,128)(2,1)S(1)}, bf16[160,384]{1,0:T(8,128)(2,1)S(1)}, u32[]{:S(2)}, u32[]{:S(2)}) collective-permute-start(bf16[160,384]{1,0:T(8,128)(2,1)S(1)} %get-tuple-element.18), channel_id=1, source_target_pairs={{0,1},{1,2},{2,3},{3,0},{4,5},{5,6},{6,7},{7,4},{8,9},{9,10},{10,1... | collective-permute-start | bytes 368648 | tf_op jit(solution)/shard_map/ppermute | solution.py:38
  284.0 3.4 %collective-permute-done.15 = bf16[160,384]{1,0:T(8,128)(2,1)S(1)} collective-permute-done((bf16[160,384]{1,0:T(8,128)(2,1)S(1)}, bf16[160,384]{1,0:T(8,128)(2,1)S(1)}, u32[]{:S(2)}, u32[]{:S(2)}) %collective-permute-start.15) | collective-permute-done | bytes 122912 | tf_op jit(solution)/shard_map/ppermute | solution.py:38
  289.2 2.4 collective-permute-start.18
  291.5 6.0 %collective-permute-start.17 = (bf16[160,192]{1,0:T(8,128)(2,1)S(1)}, bf16[160,192]{1,0:T(8,128)(2,1)S(1)}, u32[]{:S(2)}, u32[]{:S(2)}) collective-permute-start(bf16[160,192]{1,0:T(8,128)(2,1)S(1)} %get-tuple-element.27), channel_id=1, source_target_pairs={{0,0},{1,32},{2,64},{3,96},{16,16},{17,48},{18,80},{19,112},{32,1}... | collective-permute-start | bytes 184328 | tf_op jit(solution)/shard_map/ppermute | solution.py:151
  297.6 3.0 convolution_multiply_fusion
  (168 shorter events, 70.6 us)
Async XLA Ops:
  7.2 168.9 %all-gather.4.cloned.1.call-start = ((), (), s32[]{:S(2)}) async-start(), calls=%async_computation | async-start | bytes 3538944 | tf_op jit(solution)/shard_map/all_gather | solution.py:72
  8.9 142.0 %collective-permute-start = (bf16[96,1024]{1,0:T(8,128)(2,1)}, bf16[96,1024]{1,0:T(8,128)(2,1)}, u32[]{:S(2)}, u32[]{:S(2)}) collective-permute-start(bf16[96,1024]{1,0:T(8,128)(2,1)} %get-tuple-element.25), channel_id=1, source_target_pairs={{0,384},{128,0},{256,128},{384,256},{1,385},{129,1},{257,129},{385... | collective-permute-start | bytes 589832 | tf_op jit(solution)/shard_map/ppermute | solution.py:38
  21.7 119.4 %collective-permute-start.1 = (bf16[96,1024]{1,0:T(8,128)(2,1)}, bf16[96,1024]{1,0:T(8,128)(2,1)}, u32[]{:S(2)}, u32[]{:S(2)}) collective-permute-start(bf16[96,1024]{1,0:T(8,128)(2,1)} %get-tuple-element.25), channel_id=1, source_target_pairs={{0,128},{128,256},{256,384},{384,0},{1,129},{129,257},{257,385},{3... | collective-permute-start | bytes 589832 | tf_op jit(solution)/shard_map/ppermute | solution.py:38
  23.6 18.9 %collective-permute-start.19 = (f32[320]{0:T(512)}, f32[320]{0:T(512)S(1)}, u32[]{:S(2)}, u32[]{:S(2)}) collective-permute-start(f32[320]{0:T(512)} %param.11), channel_id=1, source_target_pairs={{0,12},{4,0},{8,4},{12,8},{1,13},{5,1},{9,5},{13,9},{2,14},{6,2},{... | collective-permute-start | bytes 3848 | tf_op jit(solution)/shard_map/ppermute | solution.py:38
  28.3 22.1 %collective-permute-start.20 = (f32[320]{0:T(512)}, f32[320]{0:T(512)S(1)}, u32[]{:S(2)}, u32[]{:S(2)}) collective-permute-start(f32[320]{0:T(512)} %param.11), channel_id=1, source_target_pairs={{0,8},{4,12},{8,0},{12,4},{1,9},{5,13},{9,1},{13,5},{2,10},{6,14},... | collective-permute-start | bytes 3848 | tf_op jit(solution)/shard_map/ppermute | solution.py:38
  31.0 22.9 %collective-permute-start.21 = (f32[320]{0:T(512)}, f32[320]{0:T(512)S(1)}, u32[]{:S(2)}, u32[]{:S(2)}) collective-permute-start(f32[320]{0:T(512)} %param.11), channel_id=1, source_target_pairs={{0,4},{4,8},{8,12},{12,0},{1,5},{5,9},{9,13},{13,1},{2,6},{6,10},{... | collective-permute-start | bytes 3848 | tf_op jit(solution)/shard_map/ppermute | solution.py:38
  33.8 263.8 %all-gather.6.cloned.1.call-start = ((), (), s32[]{:S(2)}) async-start(), calls=%async_computation.1 | async-start | bytes 2359296 | tf_op jit(solution)/shard_map/all_gather | solution.py:160
  42.5 119.2 %collective-permute-start.7 = (bf16[96,1024]{1,0:T(8,128)(2,1)}, bf16[96,1024]{1,0:T(8,128)(2,1)S(1)}, u32[]{:S(2)}, u32[]{:S(2)}) collective-permute-start(bf16[96,1024]{1,0:T(8,128)(2,1)} %pad_maximum_fusion), channel_id=1, source_target_pairs={{0,384},{128,0},{256,128},{384,256},{1,385},{129,1},{257,129},{385... | collective-permute-start | bytes 589832 | tf_op jit(solution)/shard_map/ppermute | solution.py:38
  50.3 20.4 %collective-permute-start.36 = (bf16[32,160]{1,0:T(8,128)(2,1)S(1)}, bf16[32,160]{1,0:T(8,128)(2,1)S(1)}, u32[]{:S(2)}, u32[]{:S(2)}) collective-permute-start(bf16[32,160]{1,0:T(8,128)(2,1)S(1)} %get-tuple-element.22), channel_id=1, source_target_pairs={{0,0},{1,32},{2,64},{3,96},{4,128},{5,160},{6,192},{7,224},{8,256}... | collective-permute-start | bytes 30728 | tf_op jit(solution)/shard_map/ppermute | solution.py:99
  54.0 14.7 %collective-permute-start.22 = (f32[4,160]{1,0:T(4,128)S(1)}, f32[4,160]{1,0:T(4,128)S(1)}, u32[]{:S(2)}, u32[]{:S(2)}) collective-permute-start(f32[4,160]{1,0:T(4,128)S(1)} %fusion.49), channel_id=1, source_target_pairs={{0,0},{1,32},{2,64},{3,96},{16,16},{17,48},{18,80},{19,112},{32,1}... | collective-permute-start | bytes 7688 | tf_op jit(solution)/shard_map/ppermute | solution.py:87
  60.3 104.3 %copy-start.5 = (bf16[384,1024]{1,0:T(8,128)(2,1)S(1)}, bf16[384,1024]{1,0:T(8,128)(2,1)}, u32[]{:S(2)}) copy-start(bf16[384,1024]{1,0:T(8,128)(2,1)} %constant_dynamic-update-slice_fusion.9) | copy-start | bytes 2359300
  68.7 9.4 %collective-permute-start.37 = (bf16[32,160]{1,0:T(8,128)(2,1)S(1)}, bf16[32,160]{1,0:T(8,128)(2,1)S(1)}, u32[]{:S(2)}, u32[]{:S(2)}) collective-permute-start(bf16[32,160]{1,0:T(8,128)(2,1)S(1)} %get-tuple-element.21), channel_id=1, source_target_pairs={{0,16},{1,48},{2,80},{3,112},{4,144},{5,176},{6,208},{7,240},{8,27... | collective-permute-start | bytes 30728 | tf_op jit(solution)/shard_map/ppermute | solution.py:100
  70.7 83.1 %collective-permute-start.8 = (bf16[96,1024]{1,0:T(8,128)(2,1)}, bf16[96,1024]{1,0:T(8,128)(2,1)S(1)}, u32[]{:S(2)}, u32[]{:S(2)}) collective-permute-start(bf16[96,1024]{1,0:T(8,128)(2,1)} %pad_maximum_fusion), channel_id=1, source_target_pairs={{0,128},{128,256},{256,384},{384,0},{1,129},{129,257},{257,385},{3... | collective-permute-start | bytes 589832 | tf_op jit(solution)/shard_map/ppermute | solution.py:38
  78.1 18.7 %collective-permute-start.38 = (bf16[64,160]{1,0:T(8,128)(2,1)S(1)}, bf16[64,160]{1,0:T(8,128)(2,1)S(1)}, u32[]{:S(2)}, u32[]{:S(2)}) collective-permute-start(bf16[64,160]{1,0:T(8,128)(2,1)S(1)} %maximum_select_fusion.2), channel_id=1, source_target_pairs={{0,12},{4,0},{8,4},{12,8},{1,13},{5,1},{9,5},{13,9},{2,14},{6,2},{... | collective-permute-start | bytes 61448 | tf_op jit(solution)/shard_map/ppermute | solution.py:38
  96.8 7.3 %collective-permute-start.39 = (bf16[64,160]{1,0:T(8,128)(2,1)S(1)}, bf16[64,160]{1,0:T(8,128)(2,1)S(1)}, u32[]{:S(2)}, u32[]{:S(2)}) collective-permute-start(bf16[64,160]{1,0:T(8,128)(2,1)S(1)} %maximum_select_fusion.2), channel_id=1, source_target_pairs={{0,8},{4,12},{8,0},{12,4},{1,9},{5,13},{9,1},{13,5},{2,10},{6,14},... | collective-permute-start | bytes 61448 | tf_op jit(solution)/shard_map/ppermute | solution.py:38
  104.1 7.3 %collective-permute-start.40 = (bf16[64,160]{1,0:T(8,128)(2,1)S(1)}, bf16[64,160]{1,0:T(8,128)(2,1)S(1)}, u32[]{:S(2)}, u32[]{:S(2)}) collective-permute-start(bf16[64,160]{1,0:T(8,128)(2,1)S(1)} %maximum_select_fusion.2), channel_id=1, source_target_pairs={{0,4},{4,8},{8,12},{12,0},{1,5},{5,9},{9,13},{13,1},{2,6},{6,10},{... | collective-permute-start | bytes 61448 | tf_op jit(solution)/shard_map/ppermute | solution.py:38
  112.2 6.8 %collective-permute-start.41 = (bf16[4,64,160]{2,1,0:T(8,128)(2,1)S(1)}, bf16[4,64,160]{2,1,0:T(8,128)(2,1)S(1)}, u32[]{:S(2)}, u32[]{:S(2)}) collective-permute-start(bf16[4,64,160]{2,1,0:T(8,128)(2,1)S(1)} %get-tuple-element.15), channel_id=1, source_target_pairs={{0,3},{1,0},{2,1},{3,2},{4,7},{5,4},{6,5},{7,6},{8,11},{9,8},{10,9... | collective-permute-start | bytes 245768 | tf_op jit(solution)/shard_map/ppermute | solution.py:38
  119.0 8.2 %collective-permute-start.42 = (bf16[4,64,160]{2,1,0:T(8,128)(2,1)S(1)}, bf16[4,64,160]{2,1,0:T(8,128)(2,1)S(1)}, u32[]{:S(2)}, u32[]{:S(2)}) collective-permute-start(bf16[4,64,160]{2,1,0:T(8,128)(2,1)S(1)} %get-tuple-element.15), channel_id=1, source_target_pairs={{0,2},{1,3},{2,0},{3,1},{4,6},{5,7},{6,4},{7,5},{8,10},{9,11},{10,... | collective-permute-start | bytes 245768 | tf_op jit(solution)/shard_map/ppermute | solution.py:38
  127.2 8.6 %collective-permute-start.43 = (bf16[4,64,160]{2,1,0:T(8,128)(2,1)S(1)}, bf16[4,64,160]{2,1,0:T(8,128)(2,1)S(1)}, u32[]{:S(2)}, u32[]{:S(2)}) collective-permute-start(bf16[4,64,160]{2,1,0:T(8,128)(2,1)S(1)} %get-tuple-element.15), channel_id=1, source_target_pairs={{0,1},{1,2},{2,3},{3,0},{4,5},{5,6},{6,7},{7,4},{8,9},{9,10},{10,1... | collective-permute-start | bytes 245768 | tf_op jit(solution)/shard_map/ppermute | solution.py:38
  142.0 31.6 %collective-permute-start.2 = (bf16[48,1024]{1,0:T(8,128)(2,1)S(1)}, bf16[48,1024]{1,0:T(8,128)(2,1)S(1)}, u32[]{:S(2)}, u32[]{:S(2)}) collective-permute-start(bf16[48,1024]{1,0:T(8,128)(2,1)S(1)} %slice.66), channel_id=1, source_target_pairs={{0,128},{128,256},{256,384},{384,0},{1,129},{129,257},{257,385},{3... | collective-permute-start | bytes 294920 | tf_op jit(solution)/shard_map/ppermute | solution.py:38
  151.9 21.7 %collective-permute-start.3 = (bf16[48,1024]{1,0:T(8,128)(2,1)S(1)}, bf16[48,1024]{1,0:T(8,128)(2,1)S(1)}, u32[]{:S(2)}, u32[]{:S(2)}) collective-permute-start(bf16[48,1024]{1,0:T(8,128)(2,1)S(1)} %slice.67), channel_id=1, source_target_pairs={{0,384},{128,0},{256,128},{384,256},{1,385},{129,1},{257,129},{385... | collective-permute-start | bytes 294920 | tf_op jit(solution)/shard_map/ppermute | solution.py:38
  153.8 12.2 %collective-permute-start.9 = (bf16[48,1024]{1,0:T(8,128)(2,1)S(1)}, bf16[48,1024]{1,0:T(8,128)(2,1)S(1)}, u32[]{:S(2)}, u32[]{:S(2)}) collective-permute-start(bf16[48,1024]{1,0:T(8,128)(2,1)S(1)} %slice.68), channel_id=1, source_target_pairs={{0,128},{128,256},{256,384},{384,0},{1,129},{129,257},{257,385},{3... | collective-permute-start | bytes 294920 | tf_op jit(solution)/shard_map/ppermute | solution.py:38
  161.7 11.0 %collective-permute-start.10 = (bf16[48,1024]{1,0:T(8,128)(2,1)S(1)}, bf16[48,1024]{1,0:T(8,128)(2,1)S(1)}, u32[]{:S(2)}, u32[]{:S(2)}) collective-permute-start(bf16[48,1024]{1,0:T(8,128)(2,1)S(1)} %slice.69), channel_id=1, source_target_pairs={{0,384},{128,0},{256,128},{384,256},{1,385},{129,1},{257,129},{385... | collective-permute-start | bytes 294920 | tf_op jit(solution)/shard_map/ppermute | solution.py:38
  180.0 92.9 %collective-permute-start.6 = (bf16[96,1536]{1,0:T(8,128)(2,1)}, bf16[96,1536]{1,0:T(8,128)(2,1)}, u32[]{:S(2)}, u32[]{:S(2)}) collective-permute-start(bf16[96,1536]{1,0:T(8,128)(2,1)} %convolution_convert_fusion), channel_id=1, source_target_pairs={{0,12},{4,0},{8,4},{12,8},{1,13},{5,1},{9,5},{13,9},{2,14},{6,2},{... | collective-permute-start | bytes 884744 | tf_op jit(solution)/shard_map/ppermute | solution.py:38
  186.5 86.4 %collective-permute-start.5 = (bf16[96,1536]{1,0:T(8,128)(2,1)}, bf16[96,1536]{1,0:T(8,128)(2,1)}, u32[]{:S(2)}, u32[]{:S(2)}) collective-permute-start(bf16[96,1536]{1,0:T(8,128)(2,1)} %convolution_convert_fusion.1), channel_id=1, source_target_pairs={{0,8},{4,12},{8,0},{12,4},{1,9},{5,13},{9,1},{13,5},{2,10},{6,14},... | collective-permute-start | bytes 884744 | tf_op jit(solution)/shard_map/ppermute | solution.py:38
  189.4 4.7 %collective-permute-start.23 = (f32[3328]{0:T(1024)S(1)}, f32[3328]{0:T(1024)S(1)}, u32[]{:S(2)}, u32[]{:S(2)}) collective-permute-start(f32[3328]{0:T(1024)S(1)} %pad_maximum_fusion.1), channel_id=1, source_target_pairs={{0,16},{16,0},{1,17},{17,1},{2,18},{18,2},{3,19},{19,3},{4,20},{20... | collective-permute-start | bytes 39944 | tf_op jit(solution)/shard_map/ppermute | solution.py:121
  194.1 11.5 %collective-permute-start.26 = (f32[3328]{0:T(1024)S(1)}, f32[3328]{0:T(1024)S(1)}, u32[]{:S(2)}, u32[]{:S(2)}) collective-permute-start(f32[3328]{0:T(1024)S(1)} %fusion.75), channel_id=1, source_target_pairs={{0,64},{32,96},{64,0},{96,32},{1,65},{33,97},{65,1},{97,33},{2,66}... | collective-permute-start | bytes 39944 | tf_op jit(solution)/shard_map/ppermute | solution.py:38
  196.8 8.9 %collective-permute-start.25 = (f32[3328]{0:T(1024)S(1)}, f32[3328]{0:T(1024)S(1)}, u32[]{:S(2)}, u32[]{:S(2)}) collective-permute-start(f32[3328]{0:T(1024)S(1)} %fusion.75), channel_id=1, source_target_pairs={{0,96},{32,0},{64,32},{96,64},{1,97},{33,1},{65,33},{97,65},{2,98}... | collective-permute-start | bytes 39944 | tf_op jit(solution)/shard_map/ppermute | solution.py:38
  198.7 6.9 %collective-permute-start.24 = (f32[3328]{0:T(1024)S(1)}, f32[3328]{0:T(1024)S(1)}, u32[]{:S(2)}, u32[]{:S(2)}) collective-permute-start(f32[3328]{0:T(1024)S(1)} %fusion.75), channel_id=1, source_target_pairs={{0,32},{32,64},{64,96},{96,0},{1,33},{33,65},{65,97},{97,1},{2,34}... | collective-permute-start | bytes 39944 | tf_op jit(solution)/shard_map/ppermute | solution.py:38
  205.6 56.5 %copy-start.8 = (f32[1024]{0:T(1024)S(1)}, f32[1024]{0:T(1024)}, u32[]{:S(2)}) copy-start(f32[1024]{0:T(1024)} %param.12) | copy-start | bytes 12292
  205.6 13.1 %collective-permute-start.29 = (f32[3328]{0:T(1024)S(1)}, f32[3328]{0:T(1024)S(1)}, u32[]{:S(2)}, u32[]{:S(2)}) collective-permute-start(f32[3328]{0:T(1024)S(1)} %add_add_fusion.2), channel_id=1, source_target_pairs={{0,8},{4,12},{8,0},{12,4},{1,9},{5,13},{9,1},{13,5},{2,10},{6,14},... | collective-permute-start | bytes 39944 | tf_op jit(solution)/shard_map/ppermute | solution.py:38
  211.1 7.6 %collective-permute-start.28 = (f32[3328]{0:T(1024)S(1)}, f32[3328]{0:T(1024)S(1)}, u32[]{:S(2)}, u32[]{:S(2)}) collective-permute-start(f32[3328]{0:T(1024)S(1)} %add_add_fusion.2), channel_id=1, source_target_pairs={{0,12},{4,0},{8,4},{12,8},{1,13},{5,1},{9,5},{13,9},{2,14},{6,2},{... | collective-permute-start | bytes 39944 | tf_op jit(solution)/shard_map/ppermute | solution.py:38
  214.2 6.8 %collective-permute-start.27 = (f32[3328]{0:T(1024)S(1)}, f32[3328]{0:T(1024)S(1)}, u32[]{:S(2)}, u32[]{:S(2)}) collective-permute-start(f32[3328]{0:T(1024)S(1)} %add_add_fusion.2), channel_id=1, source_target_pairs={{0,4},{4,8},{8,12},{12,0},{1,5},{5,9},{9,13},{13,1},{2,6},{6,10},{... | collective-permute-start | bytes 39944 | tf_op jit(solution)/shard_map/ppermute | solution.py:38
  221.0 10.7 %collective-permute-start.32 = (f32[3328]{0:T(1024)S(1)}, f32[3328]{0:T(1024)S(1)}, u32[]{:S(2)}, u32[]{:S(2)}) collective-permute-start(f32[3328]{0:T(1024)S(1)} %add_add_fusion.1), channel_id=1, source_target_pairs={{0,2},{1,3},{2,0},{3,1},{4,6},{5,7},{6,4},{7,5},{8,10},{9,11},{10,... | collective-permute-start | bytes 39944 | tf_op jit(solution)/shard_map/ppermute | solution.py:38
  223.0 8.8 %collective-permute-start.31 = (f32[3328]{0:T(1024)S(1)}, f32[3328]{0:T(1024)S(1)}, u32[]{:S(2)}, u32[]{:S(2)}) collective-permute-start(f32[3328]{0:T(1024)S(1)} %add_add_fusion.1), channel_id=1, source_target_pairs={{0,3},{1,0},{2,1},{3,2},{4,7},{5,4},{6,5},{7,6},{8,11},{9,8},{10,9... | collective-permute-start | bytes 39944 | tf_op jit(solution)/shard_map/ppermute | solution.py:38
  228.1 7.4 %collective-permute-start.30 = (f32[3328]{0:T(1024)S(1)}, f32[3328]{0:T(1024)S(1)}, u32[]{:S(2)}, u32[]{:S(2)}) collective-permute-start(f32[3328]{0:T(1024)S(1)} %add_add_fusion.1), channel_id=1, source_target_pairs={{0,1},{1,2},{2,3},{3,0},{4,5},{5,6},{6,7},{7,4},{8,9},{9,10},{10,1... | collective-permute-start | bytes 39944 | tf_op jit(solution)/shard_map/ppermute | solution.py:38
  238.3 15.4 %collective-permute-start.33 = (f32[256]{0:T(256)S(1)}, f32[256]{0:T(256)S(1)}, u32[]{:S(2)}, u32[]{:S(2)}) collective-permute-start(f32[256]{0:T(256)S(1)} %broadcast_multiply_fusion), channel_id=1, source_target_pairs={{0,384},{128,0},{256,128},{384,256},{1,385},{129,1},{257,129},{385... | collective-permute-start | bytes 3080 | tf_op jit(solution)/shard_map/ppermute | solution.py:38
  240.2 15.5 %collective-permute-start.34 = (f32[256]{0:T(256)S(1)}, f32[256]{0:T(256)S(1)}, u32[]{:S(2)}, u32[]{:S(2)}) collective-permute-start(f32[256]{0:T(256)S(1)} %broadcast_multiply_fusion), channel_id=1, source_target_pairs={{0,256},{128,384},{256,0},{384,128},{1,257},{129,385},{257,1},{385... | collective-permute-start | bytes 3080 | tf_op jit(solution)/shard_map/ppermute | solution.py:38
  247.2 11.4 %collective-permute-start.35 = (f32[256]{0:T(256)S(1)}, f32[256]{0:T(256)S(1)}, u32[]{:S(2)}, u32[]{:S(2)}) collective-permute-start(f32[256]{0:T(256)S(1)} %broadcast_multiply_fusion), channel_id=1, source_target_pairs={{0,128},{128,256},{256,384},{384,0},{1,129},{129,257},{257,385},{3... | collective-permute-start | bytes 3080 | tf_op jit(solution)/shard_map/ppermute | solution.py:38
  253.6 8.6 %collective-permute-start.13 = (bf16[64,1536]{1,0:T(8,128)(2,1)}, bf16[64,1536]{1,0:T(8,128)(2,1)}, u32[]{:S(2)}, u32[]{:S(2)}) collective-permute-start(bf16[64,1536]{1,0:T(8,128)(2,1)} %convolution_convert_fusion.4), channel_id=1, source_target_pairs={{0,12},{4,0},{8,4},{12,8},{1,13},{5,1},{9,5},{13,9},{2,14},{6,2},{... | collective-permute-start | bytes 589832 | tf_op jit(solution)/shard_map/ppermute | solution.py:38
  255.7 11.5 %collective-permute-start.12 = (bf16[64,1536]{1,0:T(8,128)(2,1)}, bf16[64,1536]{1,0:T(8,128)(2,1)}, u32[]{:S(2)}, u32[]{:S(2)}) collective-permute-start(bf16[64,1536]{1,0:T(8,128)(2,1)} %convolution_convert_fusion.5), channel_id=1, source_target_pairs={{0,8},{4,12},{8,0},{12,4},{1,9},{5,13},{9,1},{13,5},{2,10},{6,14},... | collective-permute-start | bytes 589832 | tf_op jit(solution)/shard_map/ppermute | solution.py:38
  258.6 11.9 %collective-permute-start.11 = (bf16[64,1536]{1,0:T(8,128)(2,1)}, bf16[64,1536]{1,0:T(8,128)(2,1)}, u32[]{:S(2)}, u32[]{:S(2)}) collective-permute-start(bf16[64,1536]{1,0:T(8,128)(2,1)} %convolution_convert_fusion.6), channel_id=1, source_target_pairs={{0,4},{4,8},{8,12},{12,0},{1,5},{5,9},{9,13},{13,1},{2,6},{6,10},{... | collective-permute-start | bytes 589832 | tf_op jit(solution)/shard_map/ppermute | solution.py:38
  262.3 11.3 %collective-permute-start.4 = (bf16[96,1536]{1,0:T(8,128)(2,1)}, bf16[96,1536]{1,0:T(8,128)(2,1)S(1)}, u32[]{:S(2)}, u32[]{:S(2)}) collective-permute-start(bf16[96,1536]{1,0:T(8,128)(2,1)} %convolution_convert_fusion.2), channel_id=1, source_target_pairs={{0,4},{4,8},{8,12},{12,0},{1,5},{5,9},{9,13},{13,1},{2,6},{6,10},{... | collective-permute-start | bytes 884744 | tf_op jit(solution)/shard_map/ppermute | solution.py:38
  276.0 8.0 %collective-permute-start.16 = (bf16[160,384]{1,0:T(8,128)(2,1)S(1)}, bf16[160,384]{1,0:T(8,128)(2,1)S(1)}, u32[]{:S(2)}, u32[]{:S(2)}) collective-permute-start(bf16[160,384]{1,0:T(8,128)(2,1)S(1)} %get-tuple-element.20), channel_id=1, source_target_pairs={{0,3},{1,0},{2,1},{3,2},{4,7},{5,4},{6,5},{7,6},{8,11},{9,8},{10,9... | collective-permute-start | bytes 368648 | tf_op jit(solution)/shard_map/ppermute | solution.py:38
  278.4 9.0 %collective-permute-start.15 = (bf16[160,384]{1,0:T(8,128)(2,1)S(1)}, bf16[160,384]{1,0:T(8,128)(2,1)S(1)}, u32[]{:S(2)}, u32[]{:S(2)}) collective-permute-start(bf16[160,384]{1,0:T(8,128)(2,1)S(1)} %get-tuple-element.19), channel_id=1, source_target_pairs={{0,2},{1,3},{2,0},{3,1},{4,6},{5,7},{6,4},{7,5},{8,10},{9,11},{10,... | collective-permute-start | bytes 368648 | tf_op jit(solution)/shard_map/ppermute | solution.py:38
  280.3 8.6 %collective-permute-start.14 = (bf16[160,384]{1,0:T(8,128)(2,1)S(1)}, bf16[160,384]{1,0:T(8,128)(2,1)S(1)}, u32[]{:S(2)}, u32[]{:S(2)}) collective-permute-start(bf16[160,384]{1,0:T(8,128)(2,1)S(1)} %get-tuple-element.18), channel_id=1, source_target_pairs={{0,1},{1,2},{2,3},{3,0},{4,5},{5,6},{6,7},{7,4},{8,9},{9,10},{10,1... | collective-permute-start | bytes 368648 | tf_op jit(solution)/shard_map/ppermute | solution.py:38
  289.2 11.4 %collective-permute-start.18 = (bf16[160,192]{1,0:T(8,128)(2,1)S(1)}, bf16[160,192]{1,0:T(8,128)(2,1)S(1)}, u32[]{:S(2)}, u32[]{:S(2)}) collective-permute-start(bf16[160,192]{1,0:T(8,128)(2,1)S(1)} %get-tuple-element.28), channel_id=1, source_target_pairs={{0,16},{1,48},{2,80},{3,112},{16,0},{17,32},{18,64},{19,96},{32,17... | collective-permute-start | bytes 184328 | tf_op jit(solution)/shard_map/ppermute | solution.py:152
  291.5 10.4 %collective-permute-start.17 = (bf16[160,192]{1,0:T(8,128)(2,1)S(1)}, bf16[160,192]{1,0:T(8,128)(2,1)S(1)}, u32[]{:S(2)}, u32[]{:S(2)}) collective-permute-start(bf16[160,192]{1,0:T(8,128)(2,1)S(1)} %get-tuple-element.27), channel_id=1, source_target_pairs={{0,0},{1,32},{2,64},{3,96},{16,16},{17,48},{18,80},{19,112},{32,1}... | collective-permute-start | bytes 184328 | tf_op jit(solution)/shard_map/ppermute | solution.py:151
  (7 other events, 160.8 us)
Sparse Core Ops, SparseCore 0:
  33.9 32.9 all-gather.3
  176.1 25.7 all-gather.5

commit v3 on v1

v3 whole, which is shorter than its diff:
```python
import jax
import jax.numpy as jnp
from jax import lax
from jax.sharding import Mesh, PartitionSpec as P

D = 5120
FF = 16384
AXES = ("zh", "y", "c", "x", "zl")
SIZES = (4, 4, 2, 4, 4)


def place(*index):
    at = 0
    for i, size in zip(index, SIZES):
        at = at * size + i
    return at


def ring(step):
    return [(i, (i + step) % 4) for i in range(4)]


def swapped(flip):
    return [
        (place(zh, y, c, x, zl), place(x, zl, c ^ flip, zh, y))
        for zh in range(4) for y in range(4) for c in range(2) for x in range(4) for zl in range(4)
    ]


def turned(flip):
    return [
        ((y * 2 + c) * 4 + zl, (zl * 2 + (c ^ flip)) * 4 + y)
        for y in range(4) for c in range(2) for zl in range(4)
    ]


def move(value, axis, step):
    return lax.ppermute(value, axis, ring(step))


def pairs(step):
    return [(i, i ^ step) for i in range(4)]


def added(value, axis):
    value = value + lax.ppermute(value, axis, pairs(1))
    return value + lax.ppermute(value, axis, pairs(3))


def joined(value, axis, index):
    for step, later in ((1, index % 2 == 1), (3, index >= 2)):
        got = lax.ppermute(value, axis, pairs(step))
        value = jnp.concatenate([jnp.where(later, got, value), jnp.where(later, value, got)], axis=0)
    return value


def in_three(value):
    terms = []
    for _ in range(3):
        term = lax.reduce_precision(value, 8, 7)
        terms.append(term.astype(jnp.bfloat16))
        value = value - term
    return jnp.stack(terms)


def pack(along, inner, left_dot):
    last = in_three(left_dot).reshape(1, -1)
    last = jnp.pad(last, ((0, 1), (0, along.shape[0] - last.shape[1])))
    return jnp.concatenate([in_three(along), in_three(inner), last], axis=0)


def unpack(rows, few):
    return rows[:3].sum(0), rows[3:6].sum(0), rows[6, : 3 * few].reshape(3, few).sum(0)


def per_device(features, down_weight, member_left, member_right, probe, payoff, opponent):
    f32, bf16 = jnp.float32, jnp.bfloat16
    rows, width = features.shape
    members = member_right.shape[0]
    tokens = rows // members
    population = payoff.shape[0]
    block = down_weight.shape[0]
    cols = probe.shape[0]
    spread = 1.0 / jnp.sqrt(f32(FF))
    zh, y, c, x, zl = (lax.axis_index(a) for a in AXES)
    first = c == 0
    group = 8
    few, many = group * members, group * rows
    here = y * 2 + c

    gathered = lax.all_gather(features, ("y", "c"), axis=0, tiled=True)

    def around_z(own):
        cut = own.shape[0] // 2
        before = move(own, "zh", 1)
        after = move(own, "zh", -1)
        far = [move(before[:cut], "zh", 1), move(after[cut:], "zh", -1)]
        both = jnp.concatenate([own, after] + far + [before], axis=0).reshape(4, *own.shape)
        return both, before, after

    def products(weight):
        part = lax.dot_general(
            weight.reshape(-1, width), gathered, (((1,), (1,)), ((), ())),
            preferred_element_type=f32,
        ).astype(bf16).reshape(4, -1, many)
        return [
            lax.dynamic_index_in_dim(part, lax.rem(x + k + 4 - zh, 4), 0, keepdims=False)
            for k in range(4)
        ]

    def over_x(parts, extra):
        parts = [jnp.concatenate([p, extra], axis=0) for p in parts]
        return [parts[0]] + [move(parts[k], "x", k) for k in (1, 2, 3)]

    left_cols = lax.dynamic_slice(member_left, (0, (x * 4 + zl) * cols), (members, cols)).astype(f32)
    payload = jnp.concatenate([left_cols, probe[None, :]], axis=0)
    mine = jnp.where(first, payload[:, :block], payload[:, block:])
    other = jnp.where(first, left_cols[:, block:], left_cols[:, :block])
    mine = lax.ppermute(mine, AXES, swapped(0))
    other = lax.ppermute(other, AXES, swapped(1))

    lead = 112
    weight_one, before, after = around_z(down_weight[:lead])

    direction = jnp.sum(down_weight.astype(f32) * mine[members][:, None], axis=0)
    inner = jnp.sum(
        features.astype(f32).reshape(members, tokens, width) * member_right.astype(f32)[:, None, :],
        axis=2,
    ).reshape(rows)
    left_dot = jnp.sum(left_cols * probe[None, :], axis=1)
    inner = lax.dynamic_update_slice(jnp.zeros((many,), f32), inner, (here * rows,))
    left_dot = lax.dynamic_update_slice(jnp.zeros((few,), f32), left_dot, (here * members,))
    early = jnp.concatenate([direction, inner, left_dot])
    early, _, _ = lax.optimization_barrier((early, before, after))
    early = early + lax.ppermute(early, "c", [(0, 1), (1, 0)])
    early = added(early, "y")
    direction, inner, left_dot = jnp.split(early, [width, width + many])

    direction = jnp.pad(in_three(direction), ((0, 5), (0, 0)))
    rest = block - lead
    two, _, _ = around_z(jnp.concatenate([down_weight[lead:], member_right, direction], axis=0))
    weight_two, rights, direction = jnp.split(two, [rest, rest + members], axis=1)

    mine, other = mine[:members], other
    lefts = jnp.where(first, jnp.concatenate([mine, other], 0), jnp.concatenate([other, mine], 0))
    lefts = jnp.pad(lefts.astype(bf16), ((0, 0), (0, 192 - block))).reshape(8, many)
    parts = over_x(products(weight_one), lefts)
    weight_two, parts[1] = lax.optimization_barrier((weight_two, parts[1]))
    total_one = sum(p[:lead].astype(f32) for p in parts).astype(bf16)
    lefts = jnp.stack([parts[k][lead:] for k in (0, 3, 2, 1)])

    along = lax.dot_general(
        in_three(direction.astype(f32).sum((0, 1))), gathered, (((1,), (1,)), ((), ())),
        preferred_element_type=f32,
    ).sum(0)
    parts = over_x(products(weight_two), pack(along, inner, left_dot))
    total_two = sum(p.astype(f32) for p in parts)
    lefts, total_two = lax.optimization_barrier((lefts, total_two))
    lefts = joined(jnp.roll(lefts, x, axis=0).reshape(-1, many), "zl", zl)
    sums = pack(*unpack(total_two[rest:], few)).reshape(-1, 2 * rows)
    total = jnp.concatenate([total_one, total_two[:rest].astype(bf16)], axis=0)
    span = 2 * rows
    parts = []
    for k in range(4):
        part = lax.dynamic_slice(total, (0, lax.rem(zl + k, 4) * span), (block, span))
        part = jnp.concatenate([part, sums], axis=0)
        parts.append(part if k == 0 else move(part, "zl", k))
    total = sum(p.astype(f32) for p in parts)
    along, inner, left_dot = unpack(total[block:].reshape(-1, many), few)
    total = total[:block].astype(bf16)

    inner = spread * inner
    dots = along + inner * jnp.repeat(left_dot, tokens)
    scale = 0.5 / jnp.sqrt(f32(D))
    score = jnp.mean(jnp.tanh(scale * dots).reshape(few, tokens), axis=1)
    score = joined(score, "zh", zh)
    labels = jnp.arange(population, dtype=jnp.int32)
    rival = jnp.sum(jnp.where(opponent[:, None] == labels[None, :], score[None, :], 0.0), axis=1)
    fitness = payoff * (score - rival)

    low, high = total[:, :rows], total[:, rows:]
    same = lax.ppermute(jnp.where(first, low, high), ("y", "c", "zl"), turned(0))
    cross = lax.ppermute(jnp.where(first, high, low), ("y", "c", "zl"), turned(1))
    total = jnp.where(
        first, jnp.concatenate([same, cross], 0), jnp.concatenate([cross, same], 0)
    ).astype(f32).T
    inner = lax.dynamic_slice(inner, (here * rows,), (rows,))
    lowrank = inner.reshape(members, tokens)[:, :, None] * left_cols[:, None, :]
    mixed = (total + lowrank.reshape(rows, cols)).astype(bf16)

    right_all = lax.all_gather(jnp.roll(rights, zh, axis=0), ("y", "c"), axis=0, tiled=False)
    scaled = lefts.reshape(4, 4, 2, members, 192)[..., :block].transpose(0, 2, 1, 3, 4).astype(f32)
    fitness = fitness.reshape(4, 4, 2, members).transpose(1, 2, 0, 3)
    scaled = (fitness[..., None] * scaled).astype(bf16).reshape(population, block)
    term = lax.dot_general(
        scaled, right_all.reshape(population, width), (((0,), (0,)), ((), ())),
        preferred_element_type=f32,
    )
    return mixed, term / jnp.sqrt(f32(population))


def solution(mesh):
    fine = Mesh(mesh.devices.reshape(SIZES), AXES)
    member, tensor = ("zh", "y", "c"), ("x", "zl")
    in_specs = (
        P(member, tensor), P(member, tensor), P(member, None), P(member, tensor), P(tensor), P(), P(),
    )
    out_specs = (P(member, tensor), P(member, tensor))
    return jax.shard_map(
        per_device, mesh=fine, in_specs=in_specs, out_specs=out_specs, check_vma=False
    )
```

time: 270 us -> 240 us (0.89); the launches traced: 266 us -> 238 us
  blocking collectives: 134 us -> 0 us
  starting transfers between devices: 57.2 us -> 133 us
  waiting for transfers between devices: 37.9 us -> 63.6 us
  local copies, waits for them, and re-layouts: 5.96 us -> 9.62 us
    psum x6 -> x0, blocking collectives: 88.4 us -> none  [the longest x2 40.3 us: per_device(): direction = lax.psum(lax.psum(direction, ('y', 'c')), 'zh')]
    all_gather x1 -> x0, blocking collectives: 45.4 us -> none  [per_device(): left_all = lax.all_gather(left_pair, ('x', 'zl'), axis=0, tiled=True)]
    ppermute x10 -> x17, starting transfers between devices: 39.9 us -> 78.9 us  [move(): return lax.ppermute(value, axis, ring(step))]
    ppermute x0 -> x7, starting transfers between devices: none -> 26.6 us  [the longest x4 19.3 us: joined(): got = lax.ppermute(value, axis, pairs(step))]
    ppermute x10 -> x17, waiting for transfers between devices: 20.5 us -> 35.8 us  [move(): return lax.ppermute(value, axis, ring(step))]
    ppermute x1, waiting for transfers between devices: 11.9 us -> 0.01 us  [per_device(): other = lax.ppermute(other, AXES, swapped(1))]
    ppermute x0 -> x7, waiting for transfers between devices: none -> 8.12 us  [the longest x1 4.84 us: added(): return value + lax.ppermute(value, axis, pairs(3))]
    ppermute x1, waiting for transfers between devices: 4.14 us -> 12 us  [per_device(): mine = lax.ppermute(mine, AXES, swapped(0))]
  transfers between devices with their start and end apart: 16 -> 30, of which waited for: 7 -> 11; matrix products, arithmetic and copies ran while one was open for 8% -> 10% of each run, Pallas kernels for 0% -> 0%
where the time goes in v3:
time: 240 us; the launch traced here: 238 us
  starting transfers between devices  133 us (55%)
  waiting for transfers between devices  63.6 us (26%)
  between operations  15.3 us (6%)
  local copies, waits for them, and re-layouts  9.62 us (4%)
  matrix products  8.59 us (4%)
  other arithmetic  8.5 us (4%)
    ppermute x17, starting transfers between devices, move(): return lax.ppermute(value, axis, ring(step))  78.9 us
    ppermute x17, waiting for transfers between devices, move(): return lax.ppermute(value, axis, ring(step))  35.8 us
    ppermute x4, starting transfers between devices, joined(): got = lax.ppermute(value, axis, pairs(step))  19.3 us
    ppermute x1, starting transfers between devices, per_device(): other = lax.ppermute(other, AXES, swapped(1))  12.8 us
    ppermute x1, waiting for transfers between devices, per_device(): mine = lax.ppermute(mine, AXES, swapped(0))  12 us
    ppermute x1, starting transfers between devices, per_device(): lax.ppermute(jnp.where(first, low, high), ('y', 'c', 'zl'), turned(0))  8.85 us
    ppermute x1, waiting for transfers between devices, per_device(): lax.ppermute(jnp.where(first, high, low), ('y', 'c', 'zl'), turned(1))  6.91 us
    ppermute x1, waiting for transfers between devices, added(): return value + lax.ppermute(value, axis, pairs(3))  4.84 us
  transfers between devices with their start and end apart: 30, of which 11 were waited for; matrix products, arithmetic and copies ran while one was open for 10% of the time, Pallas kernels for 0%

profile of v3, /device:TPU:24, one launch (start us, length us, event | category | flops | bytes accessed | tf_op | source)
XLA Modules:
  0.0 238.3 jit_solution(3793774325392080849)
XLA Ops:
  8.0 1.8 constant_dynamic-update-slice_fusion.4
  9.7 12.7 %collective-permute-start = (bf16[112,1024]{1,0:T(8,128)(2,1)}, bf16[112,1024]{1,0:T(8,128)(2,1)S(1)}, u32[]{:S(2)}, u32[]{:S(2)}) collective-permute-start(bf16[112,1024]{1,0:T(8,128)(2,1)} %get-tuple-element.38), channel_id=1, source_target_pairs={{0,384},{128,0},{256,128},{384,256},{1,385},{129,1},{257,129},{385... | collective-permute-start | bytes 688136 | tf_op jit(solution)/shard_map/ppermute | solution.py:38
  22.5 1.9 collective-permute-start.1
  26.0 3.5 %collective-permute-start.4 = (f32[33,160]{1,0:T(8,128)S(1)}, f32[33,160]{1,0:T(8,128)S(1)}, u32[]{:S(2)}, u32[]{:S(2)}) collective-permute-start(f32[33,160]{1,0:T(8,128)S(1)} %fusion.14), channel_id=1, source_target_pairs={{0,0},{1,32},{2,64},{3,96},{4,128},{5,160},{6,192},{7,224},{8,256}... | collective-permute-start | bytes 63368 | tf_op jit(solution)/shard_map/ppermute | solution.py:119
  30.8 1.0 multiply_reduce_fusion.2
  32.3 12.0 %collective-permute-done.4 = f32[33,160]{1,0:T(8,128)S(1)} collective-permute-done((f32[33,160]{1,0:T(8,128)S(1)}, f32[33,160]{1,0:T(8,128)S(1)}, u32[]{:S(2)}, u32[]{:S(2)}) %collective-permute-start.4) | collective-permute-done | bytes 21152 | tf_op jit(solution)/shard_map/ppermute | solution.py:119
  44.5 1.9 collective-permute-start.5
  46.5 12.8 %collective-permute-start.12 = (bf16[32,160]{1,0:T(8,128)(2,1)S(1)}, bf16[32,160]{1,0:T(8,128)(2,1)S(1)}, u32[]{:S(2)}, u32[]{:S(2)}) collective-permute-start(bf16[32,160]{1,0:T(8,128)(2,1)S(1)} %slice_select_fusion), channel_id=1, source_target_pairs={{0,16},{1,48},{2,80},{3,112},{4,144},{5,176},{6,208},{7,240},{8,27... | collective-permute-start | bytes 30728 | tf_op jit(solution)/shard_map/ppermute | solution.py:120
  59.8 3.4 %collective-permute-start.6 = (f32[2816]{0:T(1024)S(1)}, f32[2816]{0:T(1024)S(1)}, u32[]{:S(2)}, u32[]{:S(2)}) collective-permute-start(f32[2816]{0:T(1024)S(1)} %add.167), channel_id=1, source_target_pairs={{0,32},{32,0},{64,96},{96,64},{1,33},{33,1},{65,97},{97,65},{2,34}... | collective-permute-start | bytes 33800 | tf_op jit(solution)/shard_map/ppermute | solution.py:46
  63.5 5.8 %collective-permute-start.2 = (bf16[56,1024]{1,0:T(8,128)(2,1)S(1)}, bf16[56,1024]{1,0:T(8,128)(2,1)S(1)}, u32[]{:S(2)}, u32[]{:S(2)}) collective-permute-start(bf16[56,1024]{1,0:T(8,128)(2,1)S(1)} %slice.135), channel_id=1, source_target_pairs={{0,128},{128,256},{256,384},{384,0},{1,129},{129,257},{257,385},{3... | collective-permute-start | bytes 344072 | tf_op jit(solution)/shard_map/ppermute | solution.py:38
  69.4 4.7 %collective-permute-start.3 = (bf16[56,1024]{1,0:T(8,128)(2,1)S(1)}, bf16[56,1024]{1,0:T(8,128)(2,1)S(1)}, u32[]{:S(2)}, u32[]{:S(2)}) collective-permute-start(bf16[56,1024]{1,0:T(8,128)(2,1)S(1)} %slice.136), channel_id=1, source_target_pairs={{0,384},{128,0},{256,128},{384,256},{1,385},{129,1},{257,129},{385... | collective-permute-start | bytes 344072 | tf_op jit(solution)/shard_map/ppermute | solution.py:38
  74.1 1.9 collective-permute-start.7
  76.1 4.8 %collective-permute-done.7 = f32[2816]{0:T(1024)S(1)} collective-permute-done((f32[2816]{0:T(1024)S(1)}, f32[2816]{0:T(1024)S(1)}, u32[]{:S(2)}, u32[]{:S(2)}) %collective-permute-start.7) | collective-permute-done | bytes 11296 | tf_op jit(solution)/shard_map/ppermute | solution.py:47
  81.1 9.9 %collective-permute-start.9 = (bf16[88,1024]{1,0:T(8,128)(2,1)S(1)}, bf16[88,1024]{1,0:T(8,128)(2,1)S(1)}, u32[]{:S(2)}, u32[]{:S(2)}) collective-permute-start(bf16[88,1024]{1,0:T(8,128)(2,1)S(1)} %pad_maximum_fusion.9), channel_id=1, source_target_pairs={{0,128},{128,256},{256,384},{384,0},{1,129},{129,257},{257,385},{3... | collective-permute-start | bytes 540680 | tf_op jit(solution)/shard_map/ppermute | solution.py:38
  91.0 1.9 collective-permute-start.8
  93.1 6.8 %collective-permute-done.9 = bf16[88,1024]{1,0:T(8,128)(2,1)S(1)} collective-permute-done((bf16[88,1024]{1,0:T(8,128)(2,1)S(1)}, bf16[88,1024]{1,0:T(8,128)(2,1)S(1)}, u32[]{:S(2)}, u32[]{:S(2)}) %collective-permute-start.9) | collective-permute-done | bytes 180256 | tf_op jit(solution)/shard_map/ppermute | solution.py:38
  99.9 10.7 %collective-permute-start.10 = (bf16[44,1024]{1,0:T(8,128)(2,1)S(1)}, bf16[44,1024]{1,0:T(8,128)(2,1)S(1)}, u32[]{:S(2)}, u32[]{:S(2)}) collective-permute-start(bf16[44,1024]{1,0:T(8,128)(2,1)S(1)} %slice.140), channel_id=1, source_target_pairs={{0,128},{128,256},{256,384},{384,0},{1,129},{129,257},{257,385},{3... | collective-permute-start | bytes 270344 | tf_op jit(solution)/shard_map/ppermute | solution.py:38
  110.6 3.1 %collective-permute-done.8 = bf16[88,1024]{1,0:T(8,128)(2,1)S(1)} collective-permute-done((bf16[88,1024]{1,0:T(8,128)(2,1)S(1)}, bf16[88,1024]{1,0:T(8,128)(2,1)S(1)}, u32[]{:S(2)}, u32[]{:S(2)}) %collective-permute-start.8) | collective-permute-done | bytes 180256 | tf_op jit(solution)/shard_map/ppermute | solution.py:38
  113.7 2.2 collective-permute-start.11
  116.0 11.1 %collective-permute-done.11 = bf16[44,1024]{1,0:T(8,128)(2,1)S(1)} collective-permute-done((bf16[44,1024]{1,0:T(8,128)(2,1)S(1)}, bf16[44,1024]{1,0:T(8,128)(2,1)S(1)}, u32[]{:S(2)}, u32[]{:S(2)}) %collective-permute-start.11) | collective-permute-done | bytes 90144 | tf_op jit(solution)/shard_map/ppermute | solution.py:38
  128.5 3.5 %convolution_convert_fusion = bf16[448,1536]{1,0:T(8,128)(2,1)S(1)} fusion(bf16[448,1024]{1,0:T(8,128)(2,1)S(1)} %constant_dynamic-update-slice_fusion, bf16[1536,1024]{1,0:T(8,128)(2,1)} %all-gather.4.cloned.1.call-done), kind=kOutput, calls=%fused_computation.2 | convolution fusion | flops 1409974272 | bytes 5439488 | tf_op jit(solution)/shard_map/dot_general | solution.py:102
  132.1 1.0 pad_maximum_fusion
  133.1 2.2 collective-permute-start.13
  135.3 6.3 %collective-permute-start.14 = (bf16[120,1536]{1,0:T(8,128)(2,1)}, bf16[120,1536]{1,0:T(8,128)(2,1)S(1)}, u32[]{:S(2)}, u32[]{:S(2)}) collective-permute-start(bf16[120,1536]{1,0:T(8,128)(2,1)} %get-tuple-element.49), channel_id=1, source_target_pairs={{0,8},{4,12},{8,0},{12,4},{1,9},{5,13},{9,1},{13,5},{2,10},{6,14},... | collective-permute-start | bytes 1105928 | tf_op jit(solution)/shard_map/ppermute | solution.py:38
  141.6 1.9 collective-permute-start.15
  144.5 9.7 %collective-permute-done.13 = bf16[120,1536]{1,0:T(8,128)(2,1)S(1)} collective-permute-done((bf16[120,1536]{1,0:T(8,128)(2,1)S(1)}, bf16[120,1536]{1,0:T(8,128)(2,1)S(1)}, u32[]{:S(2)}, u32[]{:S(2)}) %collective-permute-start.13) | collective-permute-done | bytes 368672 | tf_op jit(solution)/shard_map/ppermute | solution.py:38
  154.3 1.2 convolution_convert_fusion.1
  155.9 1.9 collective-permute-start.16
  157.9 2.9 %collective-permute-start.17 = (bf16[56,1536]{1,0:T(8,128)(2,1)S(1)}, bf16[56,1536]{1,0:T(8,128)(2,1)}, u32[]{:S(2)}, u32[]{:S(2)}) collective-permute-start(bf16[56,1536]{1,0:T(8,128)(2,1)S(1)} %concatenate.104), channel_id=1, source_target_pairs={{0,8},{4,12},{8,0},{12,4},{1,9},{5,13},{9,1},{13,5},{2,10},{6,14},... | collective-permute-start | bytes 516104 | tf_op jit(solution)/shard_map/ppermute | solution.py:38
  160.8 1.4 concatenate.105
  162.2 4.1 %collective-permute-start.18 = (bf16[56,1536]{1,0:T(8,128)(2,1)}, bf16[56,1536]{1,0:T(8,128)(2,1)S(1)}, u32[]{:S(2)}, u32[]{:S(2)}) collective-permute-start(bf16[56,1536]{1,0:T(8,128)(2,1)} %concatenate.105), channel_id=1, source_target_pairs={{0,12},{4,0},{8,4},{12,8},{1,13},{5,1},{9,5},{13,9},{2,14},{6,2},{... | collective-permute-start | bytes 516104 | tf_op jit(solution)/shard_map/ppermute | solution.py:38
  166.4 1.2 fusion.3
  168.4 2.4 %collective-permute-done.18 = bf16[56,1536]{1,0:T(8,128)(2,1)S(1)} collective-permute-done((bf16[56,1536]{1,0:T(8,128)(2,1)}, bf16[56,1536]{1,0:T(8,128)(2,1)S(1)}, u32[]{:S(2)}, u32[]{:S(2)}) %collective-permute-start.18) | collective-permute-done | bytes 172064 | tf_op jit(solution)/shard_map/ppermute | solution.py:38
  170.8 1.1 convert_add_fusion.1
  172.3 4.7 %collective-permute-start.26 = (bf16[32,1536]{1,0:T(8,128)(2,1)S(1)}, bf16[32,1536]{1,0:T(8,128)(2,1)S(1)}, u32[]{:S(2)}, u32[]{:S(2)}) collective-permute-start(bf16[32,1536]{1,0:T(8,128)(2,1)S(1)} %fusion.11), channel_id=1, source_target_pairs={{0,1},{1,0},{2,3},{3,2},{4,5},{5,4},{6,7},{7,6},{8,9},{9,8},{10,11... | collective-permute-start | bytes 294920 | tf_op jit(solution)/shard_map/ppermute | solution.py:52
  177.1 1.9 collective-permute-start.19
  179.1 1.9 collective-permute-start.20
  181.0 5.7 %collective-permute-start.21 = (bf16[192,384]{1,0:T(8,128)(2,1)S(1)}, bf16[192,384]{1,0:T(8,128)(2,1)S(1)}, u32[]{:S(2)}, u32[]{:S(2)}) collective-permute-start(bf16[192,384]{1,0:T(8,128)(2,1)S(1)} %get-tuple-element.47), channel_id=1, source_target_pairs={{0,3},{1,0},{2,1},{3,2},{4,7},{5,4},{6,5},{7,6},{8,11},{9,8},{10,9... | collective-permute-start | bytes 442376 | tf_op jit(solution)/shard_map/ppermute | solution.py:38
  186.8 2.5 %collective-permute-start.27 = (bf16[64,1536]{1,0:T(8,128)(2,1)S(1)}, bf16[64,1536]{1,0:T(8,128)(2,1)S(1)}, u32[]{:S(2)}, u32[]{:S(2)}) collective-permute-start(bf16[64,1536]{1,0:T(8,128)(2,1)S(1)} %pad_maximum_fusion.8), channel_id=1, source_target_pairs={{0,3},{1,2},{2,1},{3,0},{4,7},{5,6},{6,5},{7,4},{8,11},{9,10},{10,... | collective-permute-start | bytes 589832 | tf_op jit(solution)/shard_map/ppermute | solution.py:52
  189.3 1.4 collective-permute-done.20
  190.7 1.2 collective-permute-done.21
  192.7 6.0 %collective-permute-start.24 = (f32[256]{0:T(256)S(1)}, f32[256]{0:T(256)S(1)}, u32[]{:S(2)}, u32[]{:S(2)}) collective-permute-start(f32[256]{0:T(256)S(1)} %broadcast_multiply_fusion), channel_id=1, source_target_pairs={{0,128},{128,0},{256,384},{384,256},{1,129},{129,1},{257,385},{385... | collective-permute-start | bytes 3080 | tf_op jit(solution)/shard_map/ppermute | solution.py:52
  198.8 3.3 %collective-permute-done.24 = f32[256]{0:T(256)S(1)} collective-permute-done((f32[256]{0:T(256)S(1)}, f32[256]{0:T(256)S(1)}, u32[]{:S(2)}, u32[]{:S(2)}) %collective-permute-start.24) | collective-permute-done | bytes 1056 | tf_op jit(solution)/shard_map/ppermute | solution.py:52
  202.0 6.2 %collective-permute-start.25 = (f32[512]{0:T(512)S(1)}, f32[512]{0:T(512)S(1)}, u32[]{:S(2)}, u32[]{:S(2)}) collective-permute-start(f32[512]{0:T(512)S(1)} %pad_maximum_fusion.14), channel_id=1, source_target_pairs={{0,384},{128,256},{256,128},{384,0},{1,385},{129,257},{257,129},{3... | collective-permute-start | bytes 6152 | tf_op jit(solution)/shard_map/ppermute | solution.py:52
  208.3 8.9 %collective-permute-start.22 = (bf16[160,192]{1,0:T(8,128)(2,1)S(1)}, bf16[160,192]{1,0:T(8,128)(2,1)S(1)}, u32[]{:S(2)}, u32[]{:S(2)}) collective-permute-start(bf16[160,192]{1,0:T(8,128)(2,1)S(1)} %get-tuple-element.43), channel_id=1, source_target_pairs={{0,0},{1,32},{2,64},{3,96},{16,16},{17,48},{18,80},{19,112},{32,1}... | collective-permute-start | bytes 184328 | tf_op jit(solution)/shard_map/ppermute | solution.py:182
  217.2 1.9 collective-permute-start.23
  220.0 6.9 %collective-permute-done.23 = bf16[160,192]{1,0:T(8,128)(2,1)S(1)} collective-permute-done((bf16[160,192]{1,0:T(8,128)(2,1)S(1)}, bf16[160,192]{1,0:T(8,128)(2,1)S(1)}, u32[]{:S(2)}, u32[]{:S(2)}) %collective-permute-start.23) | collective-permute-done | bytes 61472 | tf_op jit(solution)/shard_map/ppermute | solution.py:183
  228.5 3.0 %convolution_multiply_fusion = f32[160,1024]{1,0:T(8,128)} fusion(bf16[1024,160]{1,0:T(8,128)(2,1)S(1)} %bitcast.68, bf16[1024,1024]{1,0:T(8,128)(2,1)} %bitcast.67), kind=kOutput, calls=%fused_computation.4 | convolution fusion | flops 335708160 | bytes 3080192 | tf_op jit(solution)/shard_map/dot_general | solution.py:195
  (156 shorter events, 12.5 us)
Async XLA Ops:
  7.2 23.4 %copy-start.1 = (bf16[192,1024]{1,0:T(8,128)(2,1)S(1)}, bf16[192,1024]{1,0:T(8,128)(2,1)}, u32[]{:S(2)}) copy-start(bf16[192,1024]{1,0:T(8,128)(2,1)} %param.7) | copy-start | bytes 1179652
  7.2 37.2 %copy-start.2 = (bf16[160,1024]{1,0:T(8,128)(2,1)S(1)}, bf16[160,1024]{1,0:T(8,128)(2,1)}, u32[]{:S(2)}) copy-start(bf16[160,1024]{1,0:T(8,128)(2,1)} %param.8) | copy-start | bytes 983044
  7.2 23.6 %copy-start.5 = (f32[320]{0:T(512)S(1)}, f32[320]{0:T(512)}, u32[]{:S(2)}) copy-start(f32[320]{0:T(512)} %param.11) | copy-start | bytes 3844
  7.2 121.3 %all-gather.4.cloned.1.call-start = ((), (), s32[]{:S(2)}) async-start(), calls=%async_computation | async-start | bytes 3538944 | tf_op jit(solution)/shard_map/all_gather | solution.py:91
  7.9 220.6 %all-gather.6.cloned.1.call-start = ((), (), s32[]{:S(2)}) async-start(), calls=%async_computation.1 | async-start | bytes 2359296 | tf_op jit(solution)/shard_map/all_gather | solution.py:191
  9.7 34.8 %collective-permute-start = (bf16[112,1024]{1,0:T(8,128)(2,1)}, bf16[112,1024]{1,0:T(8,128)(2,1)S(1)}, u32[]{:S(2)}, u32[]{:S(2)}) collective-permute-start(bf16[112,1024]{1,0:T(8,128)(2,1)} %get-tuple-element.38), channel_id=1, source_target_pairs={{0,384},{128,0},{256,128},{384,256},{1,385},{129,1},{257,129},{385... | collective-permute-start | bytes 688136 | tf_op jit(solution)/shard_map/ppermute | solution.py:38
  22.5 22.0 %collective-permute-start.1 = (bf16[112,1024]{1,0:T(8,128)(2,1)}, bf16[112,1024]{1,0:T(8,128)(2,1)S(1)}, u32[]{:S(2)}, u32[]{:S(2)}) collective-permute-start(bf16[112,1024]{1,0:T(8,128)(2,1)} %get-tuple-element.38), channel_id=1, source_target_pairs={{0,128},{128,256},{256,384},{384,0},{1,129},{129,257},{257,385},{3... | collective-permute-start | bytes 688136 | tf_op jit(solution)/shard_map/ppermute | solution.py:38
  26.0 18.3 %collective-permute-start.4 = (f32[33,160]{1,0:T(8,128)S(1)}, f32[33,160]{1,0:T(8,128)S(1)}, u32[]{:S(2)}, u32[]{:S(2)}) collective-permute-start(f32[33,160]{1,0:T(8,128)S(1)} %fusion.14), channel_id=1, source_target_pairs={{0,0},{1,32},{2,64},{3,96},{4,128},{5,160},{6,192},{7,224},{8,256}... | collective-permute-start | bytes 63368 | tf_op jit(solution)/shard_map/ppermute | solution.py:119
  30.5 50.6 %copy-start.3 = (bf16[32,1024]{1,0:T(8,128)(2,1)S(1)}, bf16[32,1024]{1,0:T(8,128)(2,1)}, u32[]{:S(2)}) copy-start(bf16[32,1024]{1,0:T(8,128)(2,1)} %param.10) | copy-start | bytes 196612
  30.8 45.3 %copy-start.4 = (bf16[448,1024]{1,0:T(8,128)(2,1)S(1)}, bf16[448,1024]{1,0:T(8,128)(2,1)}, u32[]{:S(2)}) copy-start(bf16[448,1024]{1,0:T(8,128)(2,1)} %get-tuple-element.37) | copy-start | bytes 2752516
  44.5 15.3 %collective-permute-start.5 = (f32[2816]{0:T(1024)S(1)}, f32[2816]{0:T(1024)S(1)}, u32[]{:S(2)}, u32[]{:S(2)}) collective-permute-start(f32[2816]{0:T(1024)S(1)} %pad_maximum_fusion.12), channel_id=1, source_target_pairs={{0,16},{16,0},{1,17},{17,1},{2,18},{18,2},{3,19},{19,3},{4,20},{20... | collective-permute-start | bytes 33800 | tf_op jit(solution)/shard_map/ppermute | solution.py:135
  46.5 16.8 %collective-permute-start.12 = (bf16[32,160]{1,0:T(8,128)(2,1)S(1)}, bf16[32,160]{1,0:T(8,128)(2,1)S(1)}, u32[]{:S(2)}, u32[]{:S(2)}) collective-permute-start(bf16[32,160]{1,0:T(8,128)(2,1)S(1)} %slice_select_fusion), channel_id=1, source_target_pairs={{0,16},{1,48},{2,80},{3,112},{4,144},{5,176},{6,208},{7,240},{8,27... | collective-permute-start | bytes 30728 | tf_op jit(solution)/shard_map/ppermute | solution.py:120
  59.8 14.3 %collective-permute-start.6 = (f32[2816]{0:T(1024)S(1)}, f32[2816]{0:T(1024)S(1)}, u32[]{:S(2)}, u32[]{:S(2)}) collective-permute-start(f32[2816]{0:T(1024)S(1)} %add.167), channel_id=1, source_target_pairs={{0,32},{32,0},{64,96},{96,64},{1,33},{33,1},{65,97},{97,65},{2,34}... | collective-permute-start | bytes 33800 | tf_op jit(solution)/shard_map/ppermute | solution.py:46
  63.5 29.5 %collective-permute-start.2 = (bf16[56,1024]{1,0:T(8,128)(2,1)S(1)}, bf16[56,1024]{1,0:T(8,128)(2,1)S(1)}, u32[]{:S(2)}, u32[]{:S(2)}) collective-permute-start(bf16[56,1024]{1,0:T(8,128)(2,1)S(1)} %slice.135), channel_id=1, source_target_pairs={{0,128},{128,256},{256,384},{384,0},{1,129},{129,257},{257,385},{3... | collective-permute-start | bytes 344072 | tf_op jit(solution)/shard_map/ppermute | solution.py:38
  69.4 23.7 %collective-permute-start.3 = (bf16[56,1024]{1,0:T(8,128)(2,1)S(1)}, bf16[56,1024]{1,0:T(8,128)(2,1)S(1)}, u32[]{:S(2)}, u32[]{:S(2)}) collective-permute-start(bf16[56,1024]{1,0:T(8,128)(2,1)S(1)} %slice.136), channel_id=1, source_target_pairs={{0,384},{128,0},{256,128},{384,256},{1,385},{129,1},{257,129},{385... | collective-permute-start | bytes 344072 | tf_op jit(solution)/shard_map/ppermute | solution.py:38
  74.1 6.8 %collective-permute-start.7 = (f32[2816]{0:T(1024)S(1)}, f32[2816]{0:T(1024)S(1)}, u32[]{:S(2)}, u32[]{:S(2)}) collective-permute-start(f32[2816]{0:T(1024)S(1)} %add.168), channel_id=1, source_target_pairs={{0,96},{32,64},{64,32},{96,0},{1,97},{33,65},{65,33},{97,1},{2,98}... | collective-permute-start | bytes 33800 | tf_op jit(solution)/shard_map/ppermute | solution.py:47
  81.1 18.8 %collective-permute-start.9 = (bf16[88,1024]{1,0:T(8,128)(2,1)S(1)}, bf16[88,1024]{1,0:T(8,128)(2,1)S(1)}, u32[]{:S(2)}, u32[]{:S(2)}) collective-permute-start(bf16[88,1024]{1,0:T(8,128)(2,1)S(1)} %pad_maximum_fusion.9), channel_id=1, source_target_pairs={{0,128},{128,256},{256,384},{384,0},{1,129},{129,257},{257,385},{3... | collective-permute-start | bytes 540680 | tf_op jit(solution)/shard_map/ppermute | solution.py:38
  91.0 22.7 %collective-permute-start.8 = (bf16[88,1024]{1,0:T(8,128)(2,1)S(1)}, bf16[88,1024]{1,0:T(8,128)(2,1)S(1)}, u32[]{:S(2)}, u32[]{:S(2)}) collective-permute-start(bf16[88,1024]{1,0:T(8,128)(2,1)S(1)} %pad_maximum_fusion.9), channel_id=1, source_target_pairs={{0,384},{128,0},{256,128},{384,256},{1,385},{129,1},{257,129},{385... | collective-permute-start | bytes 540680 | tf_op jit(solution)/shard_map/ppermute | solution.py:38
  99.9 16.1 %collective-permute-start.10 = (bf16[44,1024]{1,0:T(8,128)(2,1)S(1)}, bf16[44,1024]{1,0:T(8,128)(2,1)S(1)}, u32[]{:S(2)}, u32[]{:S(2)}) collective-permute-start(bf16[44,1024]{1,0:T(8,128)(2,1)S(1)} %slice.140), channel_id=1, source_target_pairs={{0,128},{128,256},{256,384},{384,0},{1,129},{129,257},{257,385},{3... | collective-permute-start | bytes 270344 | tf_op jit(solution)/shard_map/ppermute | solution.py:38
  113.7 13.4 %collective-permute-start.11 = (bf16[44,1024]{1,0:T(8,128)(2,1)S(1)}, bf16[44,1024]{1,0:T(8,128)(2,1)S(1)}, u32[]{:S(2)}, u32[]{:S(2)}) collective-permute-start(bf16[44,1024]{1,0:T(8,128)(2,1)S(1)} %slice.141), channel_id=1, source_target_pairs={{0,384},{128,0},{256,128},{384,256},{1,385},{129,1},{257,129},{385... | collective-permute-start | bytes 270344 | tf_op jit(solution)/shard_map/ppermute | solution.py:38
  132.0 11.5 %copy-start = (bf16[1536,1024]{1,0:T(8,128)(2,1)S(1)}, bf16[1536,1024]{1,0:T(8,128)(2,1)}, u32[]{:S(2)}) copy-start(bf16[1536,1024]{1,0:T(8,128)(2,1)} %all-gather.4.cloned.1.call-done) | copy-start | bytes 9437188
  133.1 21.2 %collective-permute-start.13 = (bf16[120,1536]{1,0:T(8,128)(2,1)S(1)}, bf16[120,1536]{1,0:T(8,128)(2,1)S(1)}, u32[]{:S(2)}, u32[]{:S(2)}) collective-permute-start(bf16[120,1536]{1,0:T(8,128)(2,1)S(1)} %get-tuple-element.50), channel_id=1, source_target_pairs={{0,4},{4,8},{8,12},{12,0},{1,5},{5,9},{9,13},{13,1},{2,6},{6,10},{... | collective-permute-start | bytes 1105928 | tf_op jit(solution)/shard_map/ppermute | solution.py:38
  135.3 31.1 %collective-permute-start.14 = (bf16[120,1536]{1,0:T(8,128)(2,1)}, bf16[120,1536]{1,0:T(8,128)(2,1)S(1)}, u32[]{:S(2)}, u32[]{:S(2)}) collective-permute-start(bf16[120,1536]{1,0:T(8,128)(2,1)} %get-tuple-element.49), channel_id=1, source_target_pairs={{0,8},{4,12},{8,0},{12,4},{1,9},{5,13},{9,1},{13,5},{2,10},{6,14},... | collective-permute-start | bytes 1105928 | tf_op jit(solution)/shard_map/ppermute | solution.py:38
  141.6 24.8 %collective-permute-start.15 = (bf16[120,1536]{1,0:T(8,128)(2,1)}, bf16[120,1536]{1,0:T(8,128)(2,1)}, u32[]{:S(2)}, u32[]{:S(2)}) collective-permute-start(bf16[120,1536]{1,0:T(8,128)(2,1)} %get-tuple-element.48), channel_id=1, source_target_pairs={{0,12},{4,0},{8,4},{12,8},{1,13},{5,1},{9,5},{13,9},{2,14},{6,2},{... | collective-permute-start | bytes 1105928 | tf_op jit(solution)/shard_map/ppermute | solution.py:38
  155.9 12.5 %collective-permute-start.16 = (bf16[56,1536]{1,0:T(8,128)(2,1)S(1)}, bf16[56,1536]{1,0:T(8,128)(2,1)}, u32[]{:S(2)}, u32[]{:S(2)}) collective-permute-start(bf16[56,1536]{1,0:T(8,128)(2,1)S(1)} %concatenate.103), channel_id=1, source_target_pairs={{0,4},{4,8},{8,12},{12,0},{1,5},{5,9},{9,13},{13,1},{2,6},{6,10},{... | collective-permute-start | bytes 516104 | tf_op jit(solution)/shard_map/ppermute | solution.py:38
  157.9 10.4 %collective-permute-start.17 = (bf16[56,1536]{1,0:T(8,128)(2,1)S(1)}, bf16[56,1536]{1,0:T(8,128)(2,1)}, u32[]{:S(2)}, u32[]{:S(2)}) collective-permute-start(bf16[56,1536]{1,0:T(8,128)(2,1)S(1)} %concatenate.104), channel_id=1, source_target_pairs={{0,8},{4,12},{8,0},{12,4},{1,9},{5,13},{9,1},{13,5},{2,10},{6,14},... | collective-permute-start | bytes 516104 | tf_op jit(solution)/shard_map/ppermute | solution.py:38
  162.2 8.6 %collective-permute-start.18 = (bf16[56,1536]{1,0:T(8,128)(2,1)}, bf16[56,1536]{1,0:T(8,128)(2,1)S(1)}, u32[]{:S(2)}, u32[]{:S(2)}) collective-permute-start(bf16[56,1536]{1,0:T(8,128)(2,1)} %concatenate.105), channel_id=1, source_target_pairs={{0,12},{4,0},{8,4},{12,8},{1,13},{5,1},{9,5},{13,9},{2,14},{6,2},{... | collective-permute-start | bytes 516104 | tf_op jit(solution)/shard_map/ppermute | solution.py:38
  171.9 47.3 %copy-start.6 = (s32[1024]{0:T(1024)S(1)}, s32[1024]{0:T(1024)}, u32[]{:S(2)}) copy-start(s32[1024]{0:T(1024)} %param.13) | copy-start | bytes 12292
  171.9 47.9 %copy-start.7 = (f32[1024]{0:T(1024)S(1)}, f32[1024]{0:T(1024)}, u32[]{:S(2)}) copy-start(f32[1024]{0:T(1024)} %param.12) | copy-start | bytes 12292
  172.3 14.4 %collective-permute-start.26 = (bf16[32,1536]{1,0:T(8,128)(2,1)S(1)}, bf16[32,1536]{1,0:T(8,128)(2,1)S(1)}, u32[]{:S(2)}, u32[]{:S(2)}) collective-permute-start(bf16[32,1536]{1,0:T(8,128)(2,1)S(1)} %fusion.11), channel_id=1, source_target_pairs={{0,1},{1,0},{2,3},{3,2},{4,5},{5,4},{6,7},{7,6},{8,9},{9,8},{10,11... | collective-permute-start | bytes 294920 | tf_op jit(solution)/shard_map/ppermute | solution.py:52
  177.1 12.2 %collective-permute-start.19 = (bf16[192,384]{1,0:T(8,128)(2,1)S(1)}, bf16[192,384]{1,0:T(8,128)(2,1)S(1)}, u32[]{:S(2)}, u32[]{:S(2)}) collective-permute-start(bf16[192,384]{1,0:T(8,128)(2,1)S(1)} %get-tuple-element.45), channel_id=1, source_target_pairs={{0,1},{1,2},{2,3},{3,0},{4,5},{5,6},{6,7},{7,4},{8,9},{9,10},{10,1... | collective-permute-start | bytes 442376 | tf_op jit(solution)/shard_map/ppermute | solution.py:38
  179.1 11.7 %collective-permute-start.20 = (bf16[192,384]{1,0:T(8,128)(2,1)S(1)}, bf16[192,384]{1,0:T(8,128)(2,1)S(1)}, u32[]{:S(2)}, u32[]{:S(2)}) collective-permute-start(bf16[192,384]{1,0:T(8,128)(2,1)S(1)} %get-tuple-element.46), channel_id=1, source_target_pairs={{0,2},{1,3},{2,0},{3,1},{4,6},{5,7},{6,4},{7,5},{8,10},{9,11},{10,... | collective-permute-start | bytes 442376 | tf_op jit(solution)/shard_map/ppermute | solution.py:38
  181.0 10.9 %collective-permute-start.21 = (bf16[192,384]{1,0:T(8,128)(2,1)S(1)}, bf16[192,384]{1,0:T(8,128)(2,1)S(1)}, u32[]{:S(2)}, u32[]{:S(2)}) collective-permute-start(bf16[192,384]{1,0:T(8,128)(2,1)S(1)} %get-tuple-element.47), channel_id=1, source_target_pairs={{0,3},{1,0},{2,1},{3,2},{4,7},{5,4},{6,5},{7,6},{8,11},{9,8},{10,9... | collective-permute-start | bytes 442376 | tf_op jit(solution)/shard_map/ppermute | solution.py:38
  186.8 40.9 %collective-permute-start.27 = (bf16[64,1536]{1,0:T(8,128)(2,1)S(1)}, bf16[64,1536]{1,0:T(8,128)(2,1)S(1)}, u32[]{:S(2)}, u32[]{:S(2)}) collective-permute-start(bf16[64,1536]{1,0:T(8,128)(2,1)S(1)} %pad_maximum_fusion.8), channel_id=1, source_target_pairs={{0,3},{1,2},{2,1},{3,0},{4,7},{5,6},{6,5},{7,4},{8,11},{9,10},{10,... | collective-permute-start | bytes 589832 | tf_op jit(solution)/shard_map/ppermute | solution.py:52
  192.7 9.4 %collective-permute-start.24 = (f32[256]{0:T(256)S(1)}, f32[256]{0:T(256)S(1)}, u32[]{:S(2)}, u32[]{:S(2)}) collective-permute-start(f32[256]{0:T(256)S(1)} %broadcast_multiply_fusion), channel_id=1, source_target_pairs={{0,128},{128,0},{256,384},{384,256},{1,129},{129,1},{257,385},{385... | collective-permute-start | bytes 3080 | tf_op jit(solution)/shard_map/ppermute | solution.py:52
  202.0 17.1 %collective-permute-start.25 = (f32[512]{0:T(512)S(1)}, f32[512]{0:T(512)S(1)}, u32[]{:S(2)}, u32[]{:S(2)}) collective-permute-start(f32[512]{0:T(512)S(1)} %pad_maximum_fusion.14), channel_id=1, source_target_pairs={{0,384},{128,256},{256,128},{384,0},{1,385},{129,257},{257,129},{3... | collective-permute-start | bytes 6152 | tf_op jit(solution)/shard_map/ppermute | solution.py:52
  208.3 11.6 %collective-permute-start.22 = (bf16[160,192]{1,0:T(8,128)(2,1)S(1)}, bf16[160,192]{1,0:T(8,128)(2,1)S(1)}, u32[]{:S(2)}, u32[]{:S(2)}) collective-permute-start(bf16[160,192]{1,0:T(8,128)(2,1)S(1)} %get-tuple-element.43), channel_id=1, source_target_pairs={{0,0},{1,32},{2,64},{3,96},{16,16},{17,48},{18,80},{19,112},{32,1}... | collective-permute-start | bytes 184328 | tf_op jit(solution)/shard_map/ppermute | solution.py:182
  217.2 9.7 %collective-permute-start.23 = (bf16[160,192]{1,0:T(8,128)(2,1)S(1)}, bf16[160,192]{1,0:T(8,128)(2,1)S(1)}, u32[]{:S(2)}, u32[]{:S(2)}) collective-permute-start(bf16[160,192]{1,0:T(8,128)(2,1)S(1)} %get-tuple-element.44), channel_id=1, source_target_pairs={{0,16},{1,48},{2,80},{3,112},{16,0},{17,32},{18,64},{19,96},{32,17... | collective-permute-start | bytes 184328 | tf_op jit(solution)/shard_map/ppermute | solution.py:183
Sparse Core Ops, SparseCore 0:
  10.2 39.3 all-gather.3
  128.6 28.9 all-gather.5

commit v4 on v2

v4 whole, which is shorter than its diff:
```python
import jax
import jax.numpy as jnp
from jax import lax
from jax.sharding import Mesh, PartitionSpec as P

D = 5120
FF = 16384
AXES = ("zh", "y", "c", "x", "zl")
SIZES = (4, 4, 2, 4, 4)


def place(*index):
    at = 0
    for i, size in zip(index, SIZES):
        at = at * size + i
    return at


def ring(step):
    return [(i, (i + step) % 4) for i in range(4)]


def swapped(flip):
    return [
        (place(zh, y, c, x, zl), place(x, zl, c ^ flip, zh, y))
        for zh in range(4) for y in range(4) for c in range(2) for x in range(4) for zl in range(4)
    ]


def turned(flip):
    return [
        ((y * 2 + c) * 4 + zl, (zl * 2 + (c ^ flip)) * 4 + y)
        for y in range(4) for c in range(2) for zl in range(4)
    ]


def move(value, axis, step):
    return lax.ppermute(value, axis, ring(step))


def pairs(step):
    return [(i, i ^ step) for i in range(4)]


def joined(value, axis, index):
    for step, later in ((1, index % 2 == 1), (3, index >= 2)):
        got = lax.ppermute(value, axis, pairs(step))
        value = jnp.concatenate([jnp.where(later, got, value), jnp.where(later, value, got)], axis=0)
    return value


def in_three(value):
    terms = []
    for _ in range(3):
        term = lax.reduce_precision(value, 8, 7)
        terms.append(term.astype(jnp.bfloat16))
        value = value - term
    return jnp.stack(terms)


def placed(value, index, count):
    size = value.shape[0]
    return lax.dynamic_update_slice(jnp.zeros((size * count,), value.dtype), value, (index * size,))


def per_device(features, down_weight, member_left, member_right, probe, payoff, opponent):
    f32, bf16 = jnp.float32, jnp.bfloat16
    rows, width = features.shape
    members = member_right.shape[0]
    tokens = rows // members
    population = payoff.shape[0]
    block = down_weight.shape[0]
    cols = probe.shape[0]
    spread = 1.0 / jnp.sqrt(f32(FF))
    zh, y, c, x, zl = (lax.axis_index(a) for a in AXES)
    first = c == 0
    group = 8
    few, many = group * members, group * rows
    here = y * 2 + c

    gathered = lax.all_gather(features, ("y", "c"), axis=0, tiled=True)

    own = jnp.concatenate([down_weight, member_right], axis=0)
    cut = own.shape[0] // 2
    before = move(own, "zh", 1)
    after = move(own, "zh", -1)
    far = [move(before[:cut], "zh", 1), move(after[cut:], "zh", -1)]
    stack = jnp.concatenate([own, after] + far + [before], axis=0).reshape(4, *own.shape)
    weight, rights = stack[:, :block], stack[:, block:]

    probes = lax.psum(placed(probe, x, 4), "x").reshape(4, cols)
    probes = jnp.where(first, probes[:, :block], probes[:, block:])
    probes = lax.ppermute(probes, ("y", "c", "zl"), turned(0))

    left_cols = lax.dynamic_slice(member_left, (0, (x * 4 + zl) * cols), (members, cols))
    mine = jnp.where(first, left_cols[:, :block], left_cols[:, block:])
    other = jnp.where(first, left_cols[:, block:], left_cols[:, :block])
    mine = lax.ppermute(mine, AXES, swapped(0))
    other = lax.ppermute(other, AXES, swapped(1))
    lefts = jnp.where(first, jnp.concatenate([mine, other], 0), jnp.concatenate([other, mine], 0))
    lefts = jnp.pad(lefts, ((0, 0), (0, 192 - block))).reshape(8, many)
    left_cols = left_cols.astype(f32)

    part = lax.dot_general(
        weight.reshape(-1, width), gathered, (((1,), (1,)), ((), ())), preferred_element_type=f32
    ).astype(bf16).reshape(4, block, many)
    parts = []
    for k in range(4):
        one = lax.dynamic_index_in_dim(part, lax.rem(x + k + 4 - zh, 4), 0, keepdims=False)
        one = jnp.concatenate([one, lefts], axis=0)
        parts.append(one if k == 0 else move(one, "x", k))
    total = sum(p[:block].astype(f32) for p in parts).astype(bf16)
    lefts = jnp.stack([parts[k][block:] for k in (0, 3, 2, 1)])
    lefts, total = lax.optimization_barrier((lefts, total))
    lefts = joined(jnp.roll(lefts, x, axis=0).reshape(-1, many), "zl", zl)

    probes = in_three(jnp.roll(probes, -zh, axis=0)).reshape(3, -1)
    direction = lax.dot_general(
        probes, weight.reshape(-1, width), (((1,), (0,)), ((), ())), preferred_element_type=f32
    ).sum(0)
    along = lax.dot_general(
        in_three(direction), gathered, (((1,), (1,)), ((), ())), preferred_element_type=f32
    ).sum(0)
    inner = jnp.sum(
        features.astype(f32).reshape(members, tokens, width) * member_right.astype(f32)[:, None, :],
        axis=2,
    ).reshape(rows)
    left_dot = jnp.sum(left_cols * probe[None, :], axis=1)
    sums = jnp.concatenate([along, placed(inner, here, group), placed(left_dot, here, group)])
    for axis in ("c", "y", "x", "zl"):
        sums = lax.psum(sums, axis)
    along, inner, left_dot = jnp.split(sums, [many, 2 * many])
    inner = spread * inner
    dots = along + inner * jnp.repeat(left_dot, tokens)
    scale = 0.5 / jnp.sqrt(f32(D))
    score = jnp.mean(jnp.tanh(scale * dots).reshape(few, tokens), axis=1)
    score = lax.psum(placed(score, zh, 4), "zh")
    labels = jnp.arange(population, dtype=jnp.int32)
    rival = jnp.sum(jnp.where(opponent[:, None] == labels[None, :], score[None, :], 0.0), axis=1)
    fitness = payoff * (score - rival)

    span = 2 * rows
    parts = []
    for k in range(4):
        part = lax.dynamic_slice(total, (0, lax.rem(zl + k, 4) * span), (block, span))
        parts.append(part if k == 0 else move(part, "zl", k))
    total = sum(p.astype(f32) for p in parts).astype(bf16)

    low, high = total[:, :rows], total[:, rows:]
    same = lax.ppermute(jnp.where(first, low, high), ("y", "c", "zl"), turned(0))
    cross = lax.ppermute(jnp.where(first, high, low), ("y", "c", "zl"), turned(1))
    total = jnp.where(
        first, jnp.concatenate([same, cross], 0), jnp.concatenate([cross, same], 0)
    ).astype(f32).T
    inner = lax.dynamic_slice(inner, (here * rows,), (rows,))
    lowrank = inner.reshape(members, tokens)[:, :, None] * left_cols[:, None, :]
    mixed = (total + lowrank.reshape(rows, cols)).astype(bf16)

    right_all = lax.all_gather(jnp.roll(rights, zh, axis=0), ("y", "c"), axis=0, tiled=False)
    scaled = lefts.reshape(4, 4, 2, members, 192)[..., :block].transpose(0, 2, 1, 3, 4).astype(f32)
    fitness = fitness.reshape(4, 4, 2, members).transpose(1, 2, 0, 3)
    scaled = (fitness[..., None] * scaled).astype(bf16).reshape(population, block)
    term = lax.dot_general(
        scaled, right_all.reshape(population, width), (((0,), (0,)), ((), ())),
        preferred_element_type=f32,
    )
    return mixed, term / jnp.sqrt(f32(population))


def solution(mesh):
    fine = Mesh(mesh.devices.reshape(SIZES), AXES)
    member, tensor = ("zh", "y", "c"), ("x", "zl")
    in_specs = (
        P(member, tensor), P(member, tensor), P(member, None), P(member, tensor), P(tensor), P(), P(),
    )
    out_specs = (P(member, tensor), P(member, tensor))
    return jax.shard_map(
        per_device, mesh=fine, in_specs=in_specs, out_specs=out_specs, check_vma=False
    )
```

time: 316 us -> 248 us (0.78)
  the two profiles are of different devices: /device:TPU:24 before, /device:TPU:33 now
where the time goes in v4:
time: 248 us; the launch traced here: 246 us
  starting transfers between devices  89.2 us (36%)
  blocking collectives  69.9 us (28%)
  waiting for transfers between devices  41 us (17%)
  between operations  14.8 us (6%)
  local copies, waits for them, and re-layouts  13.7 us (6%)
  matrix products  9.82 us (4%)
  other arithmetic  7.95 us (3%)
    psum x4, blocking collectives, per_device(): sums = lax.psum(sums, axis)  49.9 us
    ppermute x10, starting transfers between devices, move(): return lax.ppermute(value, axis, ring(step))  44.6 us
    ppermute x10, waiting for transfers between devices, move(): return lax.ppermute(value, axis, ring(step))  28.2 us
    ppermute x1, starting transfers between devices, per_device(): lax.ppermute(jnp.where(first, high, low), ('y', 'c', 'zl'), turned(1))  19.5 us
    psum x1, blocking collectives, per_device(): score = lax.psum(placed(score, zh, 4), 'zh')  10.7 us
    ppermute x2, starting transfers between devices, joined(): got = lax.ppermute(value, axis, pairs(step))  10.2 us
    psum x1, blocking collectives, per_device(): probes = lax.psum(placed(probe, x, 4), 'x').reshape(4, cols)  9.35 us
    ppermute x1, starting transfers between devices, per_device(): other = lax.ppermute(other, AXES, swapped(1))  6.27 us
  transfers between devices with their start and end apart: 19, of which 8 were waited for; matrix products, arithmetic and copies ran while one was open for 11% of the time, Pallas kernels for 0%

profile of v4, /device:TPU:33, one launch (start us, length us, event | category | flops | bytes accessed | tf_op | source)
XLA Modules:
  0.0 246.4 jit_solution(18047994870373829340)
XLA Ops:
  8.0 1.8 constant_dynamic-update-slice_fusion.1
  9.7 1.5 constant_dynamic-update-slice_fusion
  11.2 8.8 %collective-permute-start.3 = (bf16[192,1024]{1,0:T(8,128)(2,1)}, bf16[192,1024]{1,0:T(8,128)(2,1)}, u32[]{:S(2)}, u32[]{:S(2)}) collective-permute-start(bf16[192,1024]{1,0:T(8,128)(2,1)} %get-tuple-element.34), channel_id=1, source_target_pairs={{0,128},{128,256},{256,384},{384,0},{1,129},{129,257},{257,385},{3... | collective-permute-start | bytes 1179656 | tf_op jit(solution)/shard_map/ppermute | solution.py:38
  20.0 4.7 %collective-permute-start.2 = (bf16[192,1024]{1,0:T(8,128)(2,1)}, bf16[192,1024]{1,0:T(8,128)(2,1)}, u32[]{:S(2)}, u32[]{:S(2)}) collective-permute-start(bf16[192,1024]{1,0:T(8,128)(2,1)} %get-tuple-element.34), channel_id=1, source_target_pairs={{0,384},{128,0},{256,128},{384,256},{1,385},{129,1},{257,129},{385... | collective-permute-start | bytes 1179656 | tf_op jit(solution)/shard_map/ppermute | solution.py:38
  25.1 9.3 %psum.42 = f32[4,320]{1,0:T(4,128)S(1)} all-reduce(f32[4,320]{1,0:T(4,128)S(1)} %reshape.98), channel_id=1, replica_groups=mesh['zh'=4,'y'=4,'c'=2,'x'=4,'zl'=4] {'x'}, use_global_device_ids=true, to_apply=%region_0.0 | all-reduce | flops 1280 | bytes 10240 | tf_op jit(solution)/shard_map/psum | solution.py:91
  34.5 3.6 %collective-permute-start.14 = (f32[4,160]{1,0:T(4,128)S(1)}, f32[4,160]{1,0:T(4,128)S(1)}, u32[]{:S(2)}, u32[]{:S(2)}) collective-permute-start(f32[4,160]{1,0:T(4,128)S(1)} %slice_select_fusion), channel_id=1, source_target_pairs={{0,0},{1,32},{2,64},{3,96},{16,16},{17,48},{18,80},{19,112},{32,1}... | collective-permute-start | bytes 7688 | tf_op jit(solution)/shard_map/ppermute | solution.py:93
  38.2 0.9 broadcast_select_fusion.7
  39.1 2.5 %collective-permute-start = (bf16[32,160]{1,0:T(8,128)(2,1)S(1)}, bf16[32,160]{1,0:T(8,128)(2,1)S(1)}, u32[]{:S(2)}, u32[]{:S(2)}) collective-permute-start(bf16[32,160]{1,0:T(8,128)(2,1)S(1)} %get-tuple-element.28), channel_id=1, source_target_pairs={{0,0},{1,32},{2,64},{3,96},{4,128},{5,160},{6,192},{7,224},{8,256}... | collective-permute-start | bytes 30728 | tf_op jit(solution)/shard_map/ppermute | solution.py:98
  41.6 6.3 %collective-permute-start.1 = (bf16[32,160]{1,0:T(8,128)(2,1)S(1)}, bf16[32,160]{1,0:T(8,128)(2,1)S(1)}, u32[]{:S(2)}, u32[]{:S(2)}) collective-permute-start(bf16[32,160]{1,0:T(8,128)(2,1)S(1)} %get-tuple-element.29), channel_id=1, source_target_pairs={{0,16},{1,48},{2,80},{3,112},{4,144},{5,176},{6,208},{7,240},{8,27... | collective-permute-start | bytes 30728 | tf_op jit(solution)/shard_map/ppermute | solution.py:99
  48.1 0.8 dynamic-slice_convert_fusion
  49.0 1.2 multiply_reduce_fusion
  50.1 0.9 multiply_reduce_fusion.1
  51.3 0.9 copy.43
  52.6 3.3 %collective-permute-done.14 = f32[4,160]{1,0:T(4,128)S(1)} collective-permute-done((f32[4,160]{1,0:T(4,128)S(1)}, f32[4,160]{1,0:T(4,128)S(1)}, u32[]{:S(2)}, u32[]{:S(2)}) %collective-permute-start.14) | collective-permute-done | bytes 2592 | tf_op jit(solution)/shard_map/ppermute | solution.py:93
  56.0 0.9 slice.70
  56.9 8.3 %collective-permute-start.4 = (bf16[96,1024]{1,0:T(8,128)(2,1)S(1)}, bf16[96,1024]{1,0:T(8,128)(2,1)S(1)}, u32[]{:S(2)}, u32[]{:S(2)}) collective-permute-start(bf16[96,1024]{1,0:T(8,128)(2,1)S(1)} %slice.70), channel_id=1, source_target_pairs={{0,128},{128,256},{256,384},{384,0},{1,129},{129,257},{257,385},{3... | collective-permute-start | bytes 589832 | tf_op jit(solution)/shard_map/ppermute | solution.py:38
  65.5 0.9 slice.71
  66.4 7.5 %collective-permute-start.5 = (bf16[96,1024]{1,0:T(8,128)(2,1)S(1)}, bf16[96,1024]{1,0:T(8,128)(2,1)S(1)}, u32[]{:S(2)}, u32[]{:S(2)}) collective-permute-start(bf16[96,1024]{1,0:T(8,128)(2,1)S(1)} %slice.71), channel_id=1, source_target_pairs={{0,384},{128,0},{256,128},{384,256},{1,385},{129,1},{257,129},{385... | collective-permute-start | bytes 589832 | tf_op jit(solution)/shard_map/ppermute | solution.py:38
  74.0 1.0 constant_dynamic-update-slice_fusion.5
  75.0 12.5 %collective-permute-done.5 = bf16[96,1024]{1,0:T(8,128)(2,1)S(1)} collective-permute-done((bf16[96,1024]{1,0:T(8,128)(2,1)S(1)}, bf16[96,1024]{1,0:T(8,128)(2,1)S(1)}, u32[]{:S(2)}, u32[]{:S(2)}) %collective-permute-start.5) | collective-permute-done | bytes 196640 | tf_op jit(solution)/shard_map/ppermute | solution.py:38
  87.6 1.0 constant_dynamic-update-slice_fusion.2
  88.6 1.2 slice.72
  91.0 3.0 %convolution_reduce_fusion = f32[1536]{0:T(1024)S(1)} fusion(bf16[1536,1024]{1,0:T(8,128)(2,1)} %all-gather.4.cloned.1.call-done, bf16[1,1024]{1,0:T(2,128)(2,1)S(1)} %get-tuple-element.42, bf16[1,1024]{1,0:T(2,128)(2,1)S(1)} %get-tuple-element.43, bf16[1,1024]{1,0:T(2,128)(2,1)S(1)} %get-tuple-element.41), kind=kOutput, calls=%fused_computation.4 | convolution fusion | flops 9458688 | bytes 3158016 | tf_op jit(solution)/shard_map/dot_general | solution.py:121
  94.0 3.4 %psum.43 = f32[3328]{0:T(1024)S(1)} all-reduce(f32[3328]{0:T(1024)S(1)} %pad_maximum_fusion.6), channel_id=1, replica_groups=mesh['zh'=4,'y'=4,'c'=2,'x'=4,'zl'=4] {'c'}, use_global_device_ids=true, to_apply=%region_5.6 | all-reduce | flops 3328 | bytes 26624 | tf_op jit(solution)/shard_map/psum | solution.py:131
  97.4 16.6 %psum.44 = f32[3328]{0:T(1024)S(1)} all-reduce(f32[3328]{0:T(1024)S(1)} %psum.43), channel_id=1, replica_groups=mesh['zh'=4,'y'=4,'c'=2,'x'=4,'zl'=4] {'y'}, use_global_device_ids=true, to_apply=%region_6.7 | all-reduce | flops 3328 | bytes 26624 | tf_op jit(solution)/shard_map/psum | solution.py:131
  114.0 20.0 %psum.45 = f32[3328]{0:T(1024)S(1)} all-reduce(f32[3328]{0:T(1024)S(1)} %psum.44), channel_id=1, replica_groups=mesh['zh'=4,'y'=4,'c'=2,'x'=4,'zl'=4] {'x'}, use_global_device_ids=true, to_apply=%region_7.8 | all-reduce | flops 3328 | bytes 26624 | tf_op jit(solution)/shard_map/psum | solution.py:131
  134.1 9.9 %psum.46 = f32[3328]{0:T(1024)S(1)} all-reduce(f32[3328]{0:T(1024)S(1)} %psum.45), channel_id=1, replica_groups=mesh['zh'=4,'y'=4,'c'=2,'x'=4,'zl'=4] {'zl'}, use_global_device_ids=true, to_apply=%region_8.9 | all-reduce | flops 3328 | bytes 26624 | tf_op jit(solution)/shard_map/psum | solution.py:131
  144.5 10.7 %psum.47 = f32[1024]{0:T(1024)S(1)} all-reduce(f32[1024]{0:T(1024)S(1)} %multiply_dynamic-update-slice_fusion), channel_id=1, replica_groups=mesh['zh'=4,'y'=4,'c'=2,'x'=4,'zl'=4] {'zh'}, use_global_device_ids=true, to_apply=%region_10.11 | all-reduce | flops 1024 | bytes 8192 | tf_op jit(solution)/shard_map/psum | solution.py:137
  155.3 3.5 %convolution_convert_fusion = bf16[640,1536]{1,0:T(8,128)(2,1)S(1)} fusion(bf16[640,1024]{1,0:T(8,128)(2,1)} %bitcast.59, bf16[1536,1024]{1,0:T(8,128)(2,1)S(1)} %copy-done), kind=kOutput, calls=%fused_computation.2 | convolution fusion | flops 2014248960 | bytes 6422528 | tf_op jit(solution)/shard_map/dot_general | solution.py:104
  158.8 1.3 copy-done.1
  160.4 2.4 collective-permute-start.6
  163.6 3.1 %collective-permute-start.7 = (bf16[168,1536]{1,0:T(8,128)(2,1)S(1)}, bf16[168,1536]{1,0:T(8,128)(2,1)S(1)}, u32[]{:S(2)}, u32[]{:S(2)}) collective-permute-start(bf16[168,1536]{1,0:T(8,128)(2,1)S(1)} %get-tuple-element.37), channel_id=1, source_target_pairs={{0,8},{4,12},{8,0},{12,4},{1,9},{5,13},{9,1},{13,5},{2,10},{6,14},... | collective-permute-start | bytes 1548296 | tf_op jit(solution)/shard_map/ppermute | solution.py:38
  166.7 1.9 collective-permute-start.8
  168.7 1.5 collective-permute-done.6
  170.2 4.8 %collective-permute-done.7 = bf16[168,1536]{1,0:T(8,128)(2,1)S(1)} collective-permute-done((bf16[168,1536]{1,0:T(8,128)(2,1)S(1)}, bf16[168,1536]{1,0:T(8,128)(2,1)S(1)}, u32[]{:S(2)}, u32[]{:S(2)}) %collective-permute-start.7) | collective-permute-done | bytes 516128 | tf_op jit(solution)/shard_map/ppermute | solution.py:38
  175.0 5.4 %collective-permute-done.8 = bf16[168,1536]{1,0:T(8,128)(2,1)S(1)} collective-permute-done((bf16[168,1536]{1,0:T(8,128)(2,1)S(1)}, bf16[168,1536]{1,0:T(8,128)(2,1)S(1)}, u32[]{:S(2)}, u32[]{:S(2)}) %collective-permute-start.8) | collective-permute-done | bytes 516128 | tf_op jit(solution)/shard_map/ppermute | solution.py:38
  180.5 1.3 fusion.4
  181.9 5.5 %collective-permute-start.15 = (bf16[32,1536]{1,0:T(8,128)(2,1)S(1)}, bf16[32,1536]{1,0:T(8,128)(2,1)S(1)}, u32[]{:S(2)}, u32[]{:S(2)}) collective-permute-start(bf16[32,1536]{1,0:T(8,128)(2,1)S(1)} %fusion.8), channel_id=1, source_target_pairs={{0,1},{1,0},{2,3},{3,2},{4,5},{5,4},{6,7},{7,6},{8,9},{9,8},{10,11... | collective-permute-start | bytes 294920 | tf_op jit(solution)/shard_map/ppermute | solution.py:47
  187.4 1.9 collective-permute-start.9
  189.3 3.4 %collective-permute-start.11 = (bf16[160,384]{1,0:T(8,128)(2,1)S(1)}, bf16[160,384]{1,0:T(8,128)(2,1)S(1)}, u32[]{:S(2)}, u32[]{:S(2)}) collective-permute-start(bf16[160,384]{1,0:T(8,128)(2,1)S(1)} %get-tuple-element.22), channel_id=1, source_target_pairs={{0,3},{1,0},{2,1},{3,2},{4,7},{5,4},{6,5},{7,6},{8,11},{9,8},{10,9... | collective-permute-start | bytes 368648 | tf_op jit(solution)/shard_map/ppermute | solution.py:38
  192.7 2.5 %collective-permute-start.10 = (bf16[160,384]{1,0:T(8,128)(2,1)S(1)}, bf16[160,384]{1,0:T(8,128)(2,1)S(1)}, u32[]{:S(2)}, u32[]{:S(2)}) collective-permute-start(bf16[160,384]{1,0:T(8,128)(2,1)S(1)} %get-tuple-element.23), channel_id=1, source_target_pairs={{0,2},{1,3},{2,0},{3,1},{4,6},{5,7},{6,4},{7,5},{8,10},{9,11},{10,... | collective-permute-start | bytes 368648 | tf_op jit(solution)/shard_map/ppermute | solution.py:38
  195.4 3.9 %collective-permute-done.10 = bf16[160,384]{1,0:T(8,128)(2,1)S(1)} collective-permute-done((bf16[160,384]{1,0:T(8,128)(2,1)S(1)}, bf16[160,384]{1,0:T(8,128)(2,1)S(1)}, u32[]{:S(2)}, u32[]{:S(2)}) %collective-permute-start.10) | collective-permute-done | bytes 122912 | tf_op jit(solution)/shard_map/ppermute | solution.py:38
  199.5 2.4 collective-permute-start.12
  201.9 19.5 %collective-permute-start.13 = (bf16[160,192]{1,0:T(8,128)(2,1)S(1)}, bf16[160,192]{1,0:T(8,128)(2,1)S(1)}, u32[]{:S(2)}, u32[]{:S(2)}) collective-permute-start(bf16[160,192]{1,0:T(8,128)(2,1)S(1)} %get-tuple-element.33), channel_id=1, source_target_pairs={{0,16},{1,48},{2,80},{3,112},{16,0},{17,32},{18,64},{19,96},{32,17... | collective-permute-start | bytes 184328 | tf_op jit(solution)/shard_map/ppermute | solution.py:151
  221.4 4.8 %collective-permute-start.16 = (bf16[64,1536]{1,0:T(8,128)(2,1)S(1)}, bf16[64,1536]{1,0:T(8,128)(2,1)S(1)}, u32[]{:S(2)}, u32[]{:S(2)}) collective-permute-start(bf16[64,1536]{1,0:T(8,128)(2,1)S(1)} %pad_maximum_fusion.4), channel_id=1, source_target_pairs={{0,3},{1,2},{2,1},{3,0},{4,7},{5,6},{6,5},{7,4},{8,11},{9,10},{10,... | collective-permute-start | bytes 589832 | tf_op jit(solution)/shard_map/ppermute | solution.py:47
  226.2 5.4 %collective-permute-done.13 = bf16[160,192]{1,0:T(8,128)(2,1)S(1)} collective-permute-done((bf16[160,192]{1,0:T(8,128)(2,1)S(1)}, bf16[160,192]{1,0:T(8,128)(2,1)S(1)}, u32[]{:S(2)}, u32[]{:S(2)}) %collective-permute-start.13) | collective-permute-done | bytes 61472 | tf_op jit(solution)/shard_map/ppermute | solution.py:151
  232.4 3.4 %collective-permute-done.16 = bf16[64,1536]{1,0:T(8,128)(2,1)S(1)} collective-permute-done((bf16[64,1536]{1,0:T(8,128)(2,1)S(1)}, bf16[64,1536]{1,0:T(8,128)(2,1)S(1)}, u32[]{:S(2)}, u32[]{:S(2)}) %collective-permute-start.16) | collective-permute-done | bytes 196640 | tf_op jit(solution)/shard_map/ppermute | solution.py:47
  236.6 3.0 %convolution_multiply_fusion = f32[160,1024]{1,0:T(8,128)} fusion(bf16[1024,160]{1,0:T(8,128)(2,1)S(1)} %bitcast.56, bf16[1024,1024]{1,0:T(8,128)(2,1)} %bitcast.55), kind=kOutput, calls=%fused_computation.3 | convolution fusion | flops 335708160 | bytes 3080192 | tf_op jit(solution)/shard_map/dot_general | solution.py:163
  (86 shorter events, 7.1 us)
Async XLA Ops:
  7.2 40.7 %copy-start.3 = (bf16[32,1024]{1,0:T(8,128)(2,1)S(1)}, bf16[32,1024]{1,0:T(8,128)(2,1)}, u32[]{:S(2)}) copy-start(bf16[32,1024]{1,0:T(8,128)(2,1)} %param.10) | copy-start | bytes 196612
  7.2 17.5 %copy-start.4 = (f32[320]{0:T(512)S(1)}, f32[320]{0:T(512)}, u32[]{:S(2)}) copy-start(f32[320]{0:T(512)} %param.11) | copy-start | bytes 3844
  7.2 83.8 %all-gather.4.cloned.1.call-start = ((), (), s32[]{:S(2)}) async-start(), calls=%async_computation | async-start | bytes 3538944 | tf_op jit(solution)/shard_map/all_gather | solution.py:81
  7.9 228.7 %all-gather.6.cloned.1.call-start = ((), (), s32[]{:S(2)}) async-start(), calls=%async_computation.1 | async-start | bytes 2359296 | tf_op jit(solution)/shard_map/all_gather | solution.py:159
  11.2 44.7 %collective-permute-start.3 = (bf16[192,1024]{1,0:T(8,128)(2,1)}, bf16[192,1024]{1,0:T(8,128)(2,1)}, u32[]{:S(2)}, u32[]{:S(2)}) collective-permute-start(bf16[192,1024]{1,0:T(8,128)(2,1)} %get-tuple-element.34), channel_id=1, source_target_pairs={{0,128},{128,256},{256,384},{384,0},{1,129},{129,257},{257,385},{3... | collective-permute-start | bytes 1179656 | tf_op jit(solution)/shard_map/ppermute | solution.py:38
  20.0 45.5 %collective-permute-start.2 = (bf16[192,1024]{1,0:T(8,128)(2,1)}, bf16[192,1024]{1,0:T(8,128)(2,1)}, u32[]{:S(2)}, u32[]{:S(2)}) collective-permute-start(bf16[192,1024]{1,0:T(8,128)(2,1)} %get-tuple-element.34), channel_id=1, source_target_pairs={{0,384},{128,0},{256,128},{384,256},{1,385},{129,1},{257,129},{385... | collective-permute-start | bytes 1179656 | tf_op jit(solution)/shard_map/ppermute | solution.py:38
  34.5 21.3 %collective-permute-start.14 = (f32[4,160]{1,0:T(4,128)S(1)}, f32[4,160]{1,0:T(4,128)S(1)}, u32[]{:S(2)}, u32[]{:S(2)}) collective-permute-start(f32[4,160]{1,0:T(4,128)S(1)} %slice_select_fusion), channel_id=1, source_target_pairs={{0,0},{1,32},{2,64},{3,96},{16,16},{17,48},{18,80},{19,112},{32,1}... | collective-permute-start | bytes 7688 | tf_op jit(solution)/shard_map/ppermute | solution.py:93
  39.1 26.1 %collective-permute-start = (bf16[32,160]{1,0:T(8,128)(2,1)S(1)}, bf16[32,160]{1,0:T(8,128)(2,1)S(1)}, u32[]{:S(2)}, u32[]{:S(2)}) collective-permute-start(bf16[32,160]{1,0:T(8,128)(2,1)S(1)} %get-tuple-element.28), channel_id=1, source_target_pairs={{0,0},{1,32},{2,64},{3,96},{4,128},{5,160},{6,192},{7,224},{8,256}... | collective-permute-start | bytes 30728 | tf_op jit(solution)/shard_map/ppermute | solution.py:98
  41.6 23.6 %collective-permute-start.1 = (bf16[32,160]{1,0:T(8,128)(2,1)S(1)}, bf16[32,160]{1,0:T(8,128)(2,1)S(1)}, u32[]{:S(2)}, u32[]{:S(2)}) collective-permute-start(bf16[32,160]{1,0:T(8,128)(2,1)S(1)} %get-tuple-element.29), channel_id=1, source_target_pairs={{0,16},{1,48},{2,80},{3,112},{4,144},{5,176},{6,208},{7,240},{8,27... | collective-permute-start | bytes 30728 | tf_op jit(solution)/shard_map/ppermute | solution.py:99
  56.9 18.1 %collective-permute-start.4 = (bf16[96,1024]{1,0:T(8,128)(2,1)S(1)}, bf16[96,1024]{1,0:T(8,128)(2,1)S(1)}, u32[]{:S(2)}, u32[]{:S(2)}) collective-permute-start(bf16[96,1024]{1,0:T(8,128)(2,1)S(1)} %slice.70), channel_id=1, source_target_pairs={{0,128},{128,256},{256,384},{384,0},{1,129},{129,257},{257,385},{3... | collective-permute-start | bytes 589832 | tf_op jit(solution)/shard_map/ppermute | solution.py:38
  66.4 21.1 %collective-permute-start.5 = (bf16[96,1024]{1,0:T(8,128)(2,1)S(1)}, bf16[96,1024]{1,0:T(8,128)(2,1)S(1)}, u32[]{:S(2)}, u32[]{:S(2)}) collective-permute-start(bf16[96,1024]{1,0:T(8,128)(2,1)S(1)} %slice.71), channel_id=1, source_target_pairs={{0,384},{128,0},{256,128},{384,256},{1,385},{129,1},{257,129},{385... | collective-permute-start | bytes 589832 | tf_op jit(solution)/shard_map/ppermute | solution.py:38
  91.0 64.2 %copy-start = (bf16[1536,1024]{1,0:T(8,128)(2,1)S(1)}, bf16[1536,1024]{1,0:T(8,128)(2,1)}, u32[]{:S(2)}) copy-start(bf16[1536,1024]{1,0:T(8,128)(2,1)} %all-gather.4.cloned.1.call-done) | copy-start | bytes 9437188
  158.8 1.3 copy-start.1
  160.2 2.6 %copy-start.5 = (s32[1024]{0:T(1024)S(1)}, s32[1024]{0:T(1024)}, u32[]{:S(2)}) copy-start(s32[1024]{0:T(1024)} %param.13) | copy-start | bytes 12292
  160.2 3.2 %copy-start.6 = (f32[1024]{0:T(1024)S(1)}, f32[1024]{0:T(1024)}, u32[]{:S(2)}) copy-start(f32[1024]{0:T(1024)} %param.12) | copy-start | bytes 12292
  160.4 9.8 %collective-permute-start.6 = (bf16[168,1536]{1,0:T(8,128)(2,1)S(1)}, bf16[168,1536]{1,0:T(8,128)(2,1)S(1)}, u32[]{:S(2)}, u32[]{:S(2)}) collective-permute-start(bf16[168,1536]{1,0:T(8,128)(2,1)S(1)} %get-tuple-element.36), channel_id=1, source_target_pairs={{0,12},{4,0},{8,4},{12,8},{1,13},{5,1},{9,5},{13,9},{2,14},{6,2},{... | collective-permute-start | bytes 1548296 | tf_op jit(solution)/shard_map/ppermute | solution.py:38
  163.6 11.4 %collective-permute-start.7 = (bf16[168,1536]{1,0:T(8,128)(2,1)S(1)}, bf16[168,1536]{1,0:T(8,128)(2,1)S(1)}, u32[]{:S(2)}, u32[]{:S(2)}) collective-permute-start(bf16[168,1536]{1,0:T(8,128)(2,1)S(1)} %get-tuple-element.37), channel_id=1, source_target_pairs={{0,8},{4,12},{8,0},{12,4},{1,9},{5,13},{9,1},{13,5},{2,10},{6,14},... | collective-permute-start | bytes 1548296 | tf_op jit(solution)/shard_map/ppermute | solution.py:38
  166.7 13.8 %collective-permute-start.8 = (bf16[168,1536]{1,0:T(8,128)(2,1)S(1)}, bf16[168,1536]{1,0:T(8,128)(2,1)S(1)}, u32[]{:S(2)}, u32[]{:S(2)}) collective-permute-start(bf16[168,1536]{1,0:T(8,128)(2,1)S(1)} %get-tuple-element.38), channel_id=1, source_target_pairs={{0,4},{4,8},{8,12},{12,0},{1,5},{5,9},{9,13},{13,1},{2,6},{6,10},{... | collective-permute-start | bytes 1548296 | tf_op jit(solution)/shard_map/ppermute | solution.py:38
  181.8 49.8 %copy-start.2 = (f32[192,320]{0,1:T(8,128)S(1)}, f32[192,320]{0,1:T(8,128)}, u32[]{:S(2)}) copy-start(f32[192,320]{0,1:T(8,128)} %copy.43) | copy-start | bytes 737284
  181.9 13.4 %collective-permute-start.15 = (bf16[32,1536]{1,0:T(8,128)(2,1)S(1)}, bf16[32,1536]{1,0:T(8,128)(2,1)S(1)}, u32[]{:S(2)}, u32[]{:S(2)}) collective-permute-start(bf16[32,1536]{1,0:T(8,128)(2,1)S(1)} %fusion.8), channel_id=1, source_target_pairs={{0,1},{1,0},{2,3},{3,2},{4,5},{5,4},{6,7},{7,6},{8,9},{9,8},{10,11... | collective-permute-start | bytes 294920 | tf_op jit(solution)/shard_map/ppermute | solution.py:47
  187.4 7.9 %collective-permute-start.9 = (bf16[160,384]{1,0:T(8,128)(2,1)S(1)}, bf16[160,384]{1,0:T(8,128)(2,1)S(1)}, u32[]{:S(2)}, u32[]{:S(2)}) collective-permute-start(bf16[160,384]{1,0:T(8,128)(2,1)S(1)} %get-tuple-element.21), channel_id=1, source_target_pairs={{0,1},{1,2},{2,3},{3,0},{4,5},{5,6},{6,7},{7,4},{8,9},{9,10},{10,1... | collective-permute-start | bytes 368648 | tf_op jit(solution)/shard_map/ppermute | solution.py:38
  189.3 6.0 %collective-permute-start.11 = (bf16[160,384]{1,0:T(8,128)(2,1)S(1)}, bf16[160,384]{1,0:T(8,128)(2,1)S(1)}, u32[]{:S(2)}, u32[]{:S(2)}) collective-permute-start(bf16[160,384]{1,0:T(8,128)(2,1)S(1)} %get-tuple-element.22), channel_id=1, source_target_pairs={{0,3},{1,0},{2,1},{3,2},{4,7},{5,4},{6,5},{7,6},{8,11},{9,8},{10,9... | collective-permute-start | bytes 368648 | tf_op jit(solution)/shard_map/ppermute | solution.py:38
  192.7 6.6 %collective-permute-start.10 = (bf16[160,384]{1,0:T(8,128)(2,1)S(1)}, bf16[160,384]{1,0:T(8,128)(2,1)S(1)}, u32[]{:S(2)}, u32[]{:S(2)}) collective-permute-start(bf16[160,384]{1,0:T(8,128)(2,1)S(1)} %get-tuple-element.23), channel_id=1, source_target_pairs={{0,2},{1,3},{2,0},{3,1},{4,6},{5,7},{6,4},{7,5},{8,10},{9,11},{10,... | collective-permute-start | bytes 368648 | tf_op jit(solution)/shard_map/ppermute | solution.py:38
  199.5 26.7 %collective-permute-start.12 = (bf16[160,192]{1,0:T(8,128)(2,1)S(1)}, bf16[160,192]{1,0:T(8,128)(2,1)S(1)}, u32[]{:S(2)}, u32[]{:S(2)}) collective-permute-start(bf16[160,192]{1,0:T(8,128)(2,1)S(1)} %get-tuple-element.32), channel_id=1, source_target_pairs={{0,0},{1,32},{2,64},{3,96},{16,16},{17,48},{18,80},{19,112},{32,1}... | collective-permute-start | bytes 184328 | tf_op jit(solution)/shard_map/ppermute | solution.py:150
  201.9 29.7 %collective-permute-start.13 = (bf16[160,192]{1,0:T(8,128)(2,1)S(1)}, bf16[160,192]{1,0:T(8,128)(2,1)S(1)}, u32[]{:S(2)}, u32[]{:S(2)}) collective-permute-start(bf16[160,192]{1,0:T(8,128)(2,1)S(1)} %get-tuple-element.33), channel_id=1, source_target_pairs={{0,16},{1,48},{2,80},{3,112},{16,0},{17,32},{18,64},{19,96},{32,17... | collective-permute-start | bytes 184328 | tf_op jit(solution)/shard_map/ppermute | solution.py:151
  221.4 14.4 %collective-permute-start.16 = (bf16[64,1536]{1,0:T(8,128)(2,1)S(1)}, bf16[64,1536]{1,0:T(8,128)(2,1)S(1)}, u32[]{:S(2)}, u32[]{:S(2)}) collective-permute-start(bf16[64,1536]{1,0:T(8,128)(2,1)S(1)} %pad_maximum_fusion.4), channel_id=1, source_target_pairs={{0,3},{1,2},{2,1},{3,0},{4,7},{5,6},{6,5},{7,4},{8,11},{9,10},{10,... | collective-permute-start | bytes 589832 | tf_op jit(solution)/shard_map/ppermute | solution.py:47
Sparse Core Ops, SparseCore 0:
  10.1 39.9 all-gather.3
  91.1 37.0 all-gather.5

commit v5 on v4

--- a/solution.py
+++ b/solution.py
@@ -80,55 +80,89 @@
 
     gathered = lax.all_gather(features, ("y", "c"), axis=0, tiled=True)
 
-    own = jnp.concatenate([down_weight, member_right], axis=0)
-    cut = own.shape[0] // 2
-    before = move(own, "zh", 1)
-    after = move(own, "zh", -1)
-    far = [move(before[:cut], "zh", 1), move(after[cut:], "zh", -1)]
-    stack = jnp.concatenate([own, after] + far + [before], axis=0).reshape(4, *own.shape)
-    weight, rights = stack[:, :block], stack[:, block:]
-
-    probes = lax.psum(placed(probe, x, 4), "x").reshape(4, cols)
-    probes = jnp.where(first, probes[:, :block], probes[:, block:])
-    probes = lax.ppermute(probes, ("y", "c", "zl"), turned(0))
-
-    left_cols = lax.dynamic_slice(member_left, (0, (x * 4 + zl) * cols), (members, cols))
-    mine = jnp.where(first, left_cols[:, :block], left_cols[:, block:])
+    left_cols = lax.dynamic_slice(member_left, (0, (x * 4 + zl) * cols), (members, cols)).astype(f32)
+    payload = jnp.concatenate([left_cols, probe[None, :]], axis=0)
+    mine = jnp.where(first, payload[:, :block], payload[:, block:])
     other = jnp.where(first, left_cols[:, block:], left_cols[:, :block])
     mine = lax.ppermute(mine, AXES, swapped(0))
     other = lax.ppermute(other, AXES, swapped(1))
-    lefts = jnp.where(first, jnp.concatenate([mine, other], 0), jnp.concatenate([other, mine], 0))
-    lefts = jnp.pad(lefts, ((0, 0), (0, 192 - block))).reshape(8, many)
-    left_cols = left_cols.astype(f32)
-
-    part = lax.dot_general(
-        weight.reshape(-1, width), gathered, (((1,), (1,)), ((), ())), preferred_element_type=f32
-    ).astype(bf16).reshape(4, block, many)
-    parts = []
-    for k in range(4):
-        one = lax.dynamic_index_in_dim(part, lax.rem(x + k + 4 - zh, 4), 0, keepdims=False)
-        one = jnp.concatenate([one, lefts], axis=0)
-        parts.append(one if k == 0 else move(one, "x", k))
-    total = sum(p[:block].astype(f32) for p in parts).astype(bf16)
-    lefts = jnp.stack([parts[k][block:] for k in (0, 3, 2, 1)])
-    lefts, total = lax.optimization_barrier((lefts, total))
-    lefts = joined(jnp.roll(lefts, x, axis=0).reshape(-1, many), "zl", zl)
-
-    probes = in_three(jnp.roll(probes, -zh, axis=0)).reshape(3, -1)
-    direction = lax.dot_general(
-        probes, weight.reshape(-1, width), (((1,), (0,)), ((), ())), preferred_element_type=f32
-    ).sum(0)
-    along = lax.dot_general(
-        in_three(direction), gathered, (((1,), (1,)), ((), ())), preferred_element_type=f32
-    ).sum(0)
+
+    lead = 96
+    chunks = [down_weight[:lead], jnp.concatenate([down_weight[lead:], member_right], axis=0)]
+    chunks[1], mine, other = lax.optimization_barrier((chunks[1], mine, other))
+    cut = lead // 2
+    steps = [(move(own, "zh", 1), move(own, "zh", -1)) for own in chunks]
+
+    direction = jnp.sum(down_weight.astype(f32) * mine[members][:, None], axis=0)
     inner = jnp.sum(
         features.astype(f32).reshape(members, tokens, width) * member_right.astype(f32)[:, None, :],
         axis=2,
     ).reshape(rows)
     left_dot = jnp.sum(left_cols * probe[None, :], axis=1)
-    sums = jnp.concatenate([along, placed(inner, here, group), placed(left_dot, here, group)])
-    for axis in ("c", "y", "x", "zl"):
-        sums = lax.psum(sums, axis)
+    early = jnp.concatenate([direction, placed(inner, here, group), placed(left_dot, here, group)])
+    early = lax.psum(lax.psum(early, "c"), "y")
+
+    direction = jnp.pad(in_three(early[:width]), ((0, 5), (0, 0)))
+    (before, after), (before_two, after_two) = steps
+    low = move(jnp.concatenate([before[:cut], direction], axis=0), "zh", 1)
+    high = move(jnp.concatenate([after[cut:], direction], axis=0), "zh", -1)
+    low_two = move(jnp.concatenate([before_two[:cut], low[cut:]], axis=0), "zh", 1)
+    high_two = move(after_two[cut:], "zh", -1)
+    direction = sum(d.astype(f32) for d in (direction, low[cut:], high[cut:], low_two[cut:])).sum(0)
+    stacks = [
+        jnp.concatenate([own, late, one[:cut], two, soon], axis=0).reshape(4, lead, width)
+        for own, late, one, two, soon in (
+            (chunks[0], after, low, high[: lead - cut], before),
+            (chunks[1], after_two, low_two, high_two, before_two),
+        )
+    ]
+    rest = block - lead
+    weights, rights = [stacks[0], stacks[1][:, :rest]], stacks[1][:, rest:]
+
+    mine = mine[:members]
+    lefts = jnp.where(first, jnp.concatenate([mine, other], 0), jnp.concatenate([other, mine], 0))
+    lefts = jnp.pad(lefts.astype(bf16), ((0, 0), (0, 192 - block))).reshape(8, many)
+
+    def products(weight):
+        part = lax.dot_general(
+            weight.reshape(-1, width), gathered, (((1,), (1,)), ((), ())),
+            preferred_element_type=f32,
+        ).astype(bf16).reshape(4, -1, many)
+        return [
+            lax.dynamic_index_in_dim(part, lax.rem(x + k + 4 - zh, 4), 0, keepdims=False)
+            for k in range(4)
+        ]
+
+    ones = [jnp.concatenate([p, lefts], axis=0) for p in products(weights[0])]
+    ones = [ones[0]] + [move(ones[k], "x", k) for k in (1, 2, 3)]
+    weights[1], direction, ones[1] = lax.optimization_barrier((weights[1], direction, ones[1]))
+
+    along = lax.dot_general(
+        in_three(direction), gathered, (((1,), (1,)), ((), ())), preferred_element_type=f32
+    ).sum(0)
+    sums = lax.psum(jnp.concatenate([along, early[width:]]), "x")
+
+    twos = products(weights[1])
+    twos, sums = lax.optimization_barrier((twos, sums))
+    twos = [twos[0]] + [move(twos[k], "x", k) for k in (1, 2, 3)]
+    sums, twos[1] = lax.optimization_barrier((sums, twos[1]))
+    sums = lax.psum(sums, "zl")
+    total = jnp.concatenate([
+        sum(p[:lead].astype(f32) for p in ones).astype(bf16),
+        sum(p.astype(f32) for p in twos).astype(bf16),
+    ], axis=0)
+    lefts = jnp.stack([ones[k][lead:] for k in (0, 3, 2, 1)])
+    lefts, total = lax.optimization_barrier((lefts, total))
+    lefts = joined(jnp.roll(lefts, x, axis=0).reshape(-1, many), "zl", zl)
+
+    span = 2 * rows
+    parts = []
+    for k in range(4):
+        part = lax.dynamic_slice(total, (0, lax.rem(zl + k, 4) * span), (block, span))
+        parts.append(part if k == 0 else move(part, "zl", k))
+    sums, parts[1] = lax.optimization_barrier((sums, parts[1]))
+    total = sum(p.astype(f32) for p in parts).astype(bf16)
+
     along, inner, left_dot = jnp.split(sums, [many, 2 * many])
     inner = spread * inner
     dots = along + inner * jnp.repeat(left_dot, tokens)
@@ -138,13 +172,6 @@
     labels = jnp.arange(population, dtype=jnp.int32)
     rival = jnp.sum(jnp.where(opponent[:, None] == labels[None, :], score[None, :], 0.0), axis=1)
     fitness = payoff * (score - rival)
-
-    span = 2 * rows
-    parts = []
-    for k in range(4):
-        part = lax.dynamic_slice(total, (0, lax.rem(zl + k, 4) * span), (block, span))
-        parts.append(part if k == 0 else move(part, "zl", k))
-    total = sum(p.astype(f32) for p in parts).astype(bf16)
 
     low, high = total[:, :rows], total[:, rows:]
     same = lax.ppermute(jnp.where(first, low, high), ("y", "c", "zl"), turned(0))

time: 248 us -> 249 us (level)
  the two profiles are of different devices: /device:TPU:33 before, /device:TPU:24 now
where the time goes in v5:
time: 249 us; the launch traced here: 248 us
  starting transfers between devices  109 us (44%)
  blocking collectives  62.3 us (25%)
  waiting for transfers between devices  24.7 us (10%)
  local copies, waits for them, and re-layouts  18.8 us (8%)
  between operations  15.1 us (6%)
  matrix products  9.25 us (4%)
  other arithmetic  8.23 us (3%)
    ppermute x17, starting transfers between devices, move(): return lax.ppermute(value, axis, ring(step))  85.9 us
    psum x2, blocking collectives, per_device(): early = lax.psum(lax.psum(early, 'c'), 'y')  18.6 us
    psum x1, blocking collectives, per_device(): sums = lax.psum(sums, 'zl')  15.6 us
    psum x1, blocking collectives, per_device(): sums = lax.psum(jnp.concatenate([along, early[width:]]), 'x')  14.9 us
    psum x1, blocking collectives, per_device(): score = lax.psum(placed(score, zh, 4), 'zh')  13.1 us
    ppermute x17, waiting for transfers between devices, move(): return lax.ppermute(value, axis, ring(step))  12.4 us
    unnamed x39, local copies, waits for them, and re-layouts  6.56 us
    ppermute x2, starting transfers between devices, joined(): got = lax.ppermute(value, axis, pairs(step))  6.49 us
  transfers between devices with their start and end apart: 25, of which 6 were waited for; matrix products, arithmetic and copies ran while one was open for 12% of the time, Pallas kernels for 0%

profile of v5, /device:TPU:24, one launch (start us, length us, event | category | flops | bytes accessed | tf_op | source)
XLA Modules:
  0.0 247.7 jit_solution(4249656091453969956)
XLA Ops:
  8.0 1.7 constant_dynamic-update-slice_fusion.2
  9.7 9.1 %collective-permute-start.3 = (bf16[96,1024]{1,0:T(8,128)(2,1)}, bf16[96,1024]{1,0:T(8,128)(2,1)}, u32[]{:S(2)}, u32[]{:S(2)}) collective-permute-start(bf16[96,1024]{1,0:T(8,128)(2,1)} %get-tuple-element.57), channel_id=1, source_target_pairs={{0,128},{128,256},{256,384},{384,0},{1,129},{129,257},{257,385},{3... | collective-permute-start | bytes 589832 | tf_op jit(solution)/shard_map/ppermute | solution.py:38
  18.8 5.6 %collective-permute-start.2 = (bf16[96,1024]{1,0:T(8,128)(2,1)}, bf16[96,1024]{1,0:T(8,128)(2,1)}, u32[]{:S(2)}, u32[]{:S(2)}) collective-permute-start(bf16[96,1024]{1,0:T(8,128)(2,1)} %get-tuple-element.57), channel_id=1, source_target_pairs={{0,384},{128,0},{256,128},{384,256},{1,385},{129,1},{257,129},{385... | collective-permute-start | bytes 589832 | tf_op jit(solution)/shard_map/ppermute | solution.py:38
  26.0 3.5 %collective-permute-start = (f32[33,160]{1,0:T(8,128)S(1)}, f32[33,160]{1,0:T(8,128)S(1)}, u32[]{:S(2)}, u32[]{:S(2)}) collective-permute-start(f32[33,160]{1,0:T(8,128)S(1)} %fusion.10), channel_id=1, source_target_pairs={{0,0},{1,32},{2,64},{3,96},{4,128},{5,160},{6,192},{7,224},{8,256}... | collective-permute-start | bytes 63368 | tf_op jit(solution)/shard_map/ppermute | solution.py:87
  29.6 5.1 %collective-permute-start.1 = (bf16[32,160]{1,0:T(8,128)(2,1)S(1)}, bf16[32,160]{1,0:T(8,128)(2,1)S(1)}, u32[]{:S(2)}, u32[]{:S(2)}) collective-permute-start(bf16[32,160]{1,0:T(8,128)(2,1)S(1)} %slice_select_fusion), channel_id=1, source_target_pairs={{0,16},{1,48},{2,80},{3,112},{4,144},{5,176},{6,208},{7,240},{8,27... | collective-permute-start | bytes 30728 | tf_op jit(solution)/shard_map/ppermute | solution.py:88
  34.7 1.0 mul.116
  36.0 1.0 multiply_reduce_fusion.2
  37.9 3.9 %collective-permute-done.1 = bf16[32,160]{1,0:T(8,128)(2,1)S(1)} collective-permute-done((bf16[32,160]{1,0:T(8,128)(2,1)S(1)}, bf16[32,160]{1,0:T(8,128)(2,1)S(1)}, u32[]{:S(2)}, u32[]{:S(2)}) %collective-permute-start.1) | collective-permute-done | bytes 10272 | tf_op jit(solution)/shard_map/ppermute | solution.py:88
  41.8 12.2 %collective-permute-start.9 = (bf16[96,1024]{1,0:T(8,128)(2,1)S(1)}, bf16[96,1024]{1,0:T(8,128)(2,1)S(1)}, u32[]{:S(2)}, u32[]{:S(2)}) collective-permute-start(bf16[96,1024]{1,0:T(8,128)(2,1)S(1)} %pad_maximum_fusion.5), channel_id=1, source_target_pairs={{0,128},{128,256},{256,384},{384,0},{1,129},{129,257},{257,385},{3... | collective-permute-start | bytes 589832 | tf_op jit(solution)/shard_map/ppermute | solution.py:38
  54.0 4.0 %collective-permute-start.8 = (bf16[96,1024]{1,0:T(8,128)(2,1)S(1)}, bf16[96,1024]{1,0:T(8,128)(2,1)S(1)}, u32[]{:S(2)}, u32[]{:S(2)}) collective-permute-start(bf16[96,1024]{1,0:T(8,128)(2,1)S(1)} %pad_maximum_fusion.5), channel_id=1, source_target_pairs={{0,384},{128,0},{256,128},{384,256},{1,385},{129,1},{257,129},{385... | collective-permute-start | bytes 589832 | tf_op jit(solution)/shard_map/ppermute | solution.py:38
  58.4 3.3 %psum.35 = f32[2816]{0:T(1024)S(1)} all-reduce(f32[2816]{0:T(1024)S(1)} %pad_maximum_fusion.13), channel_id=1, replica_groups=mesh['zh'=4,'y'=4,'c'=2,'x'=4,'zl'=4] {'c'}, use_global_device_ids=true, to_apply=%region_3.4 | all-reduce | flops 2816 | bytes 22528 | tf_op jit(solution)/shard_map/psum | solution.py:103
  61.7 15.3 %psum.36 = f32[2816]{0:T(1024)S(1)} all-reduce(f32[2816]{0:T(1024)S(1)} %psum.35), channel_id=1, replica_groups=mesh['zh'=4,'y'=4,'c'=2,'x'=4,'zl'=4] {'y'}, use_global_device_ids=true, to_apply=%region_4.5 | all-reduce | flops 2816 | bytes 22528 | tf_op jit(solution)/shard_map/psum | solution.py:103
  77.8 0.9 slice.129
  78.8 0.9 slice.132
  79.7 4.3 %collective-permute-start.4 = (bf16[56,1024]{1,0:T(8,128)(2,1)S(1)}, bf16[56,1024]{1,0:T(8,128)(2,1)S(1)}, u32[]{:S(2)}, u32[]{:S(2)}) collective-permute-start(bf16[56,1024]{1,0:T(8,128)(2,1)S(1)} %get-tuple-element.68), channel_id=1, source_target_pairs={{0,128},{128,256},{256,384},{384,0},{1,129},{129,257},{257,385},{3... | collective-permute-start | bytes 344072 | tf_op jit(solution)/shard_map/ppermute | solution.py:38
  83.9 5.5 %collective-permute-start.5 = (bf16[56,1024]{1,0:T(8,128)(2,1)S(1)}, bf16[56,1024]{1,0:T(8,128)(2,1)S(1)}, u32[]{:S(2)}, u32[]{:S(2)}) collective-permute-start(bf16[56,1024]{1,0:T(8,128)(2,1)S(1)} %get-tuple-element.67), channel_id=1, source_target_pairs={{0,384},{128,0},{256,128},{384,256},{1,385},{129,1},{257,129},{385... | collective-permute-start | bytes 344072 | tf_op jit(solution)/shard_map/ppermute | solution.py:38
  89.4 0.9 constant_dynamic-update-slice_fusion.1
  90.4 6.3 %collective-permute-start.11 = (bf16[48,1024]{1,0:T(8,128)(2,1)S(1)}, bf16[48,1024]{1,0:T(8,128)(2,1)S(1)}, u32[]{:S(2)}, u32[]{:S(2)}) collective-permute-start(bf16[48,1024]{1,0:T(8,128)(2,1)S(1)} %slice.139), channel_id=1, source_target_pairs={{0,384},{128,0},{256,128},{384,256},{1,385},{129,1},{257,129},{385... | collective-permute-start | bytes 294920 | tf_op jit(solution)/shard_map/ppermute | solution.py:38
  97.5 3.4 %collective-permute-start.10 = (bf16[56,1024]{1,0:T(8,128)(2,1)S(1)}, bf16[56,1024]{1,0:T(8,128)(2,1)S(1)}, u32[]{:S(2)}, u32[]{:S(2)}) collective-permute-start(bf16[56,1024]{1,0:T(8,128)(2,1)S(1)} %pad_maximum_fusion.9), channel_id=1, source_target_pairs={{0,128},{128,256},{256,384},{384,0},{1,129},{129,257},{257,385},{3... | collective-permute-start | bytes 344072 | tf_op jit(solution)/shard_map/ppermute | solution.py:38
  101.0 1.2 collective-permute-done.5
  102.2 1.0 constant_dynamic-update-slice_fusion
  103.2 10.4 %collective-permute-done.10 = bf16[56,1024]{1,0:T(8,128)(2,1)S(1)} collective-permute-done((bf16[56,1024]{1,0:T(8,128)(2,1)S(1)}, bf16[56,1024]{1,0:T(8,128)(2,1)S(1)}, u32[]{:S(2)}, u32[]{:S(2)}) %collective-permute-start.10) | collective-permute-done | bytes 114720 | tf_op jit(solution)/shard_map/ppermute | solution.py:38
  114.9 3.3 %convolution_convert_fusion = bf16[384,1536]{1,0:T(8,128)(2,1)S(1)} fusion(bf16[384,1024]{1,0:T(8,128)(2,1)S(1)} %constant_dynamic-update-slice_fusion, bf16[1536,1024]{1,0:T(8,128)(2,1)} %all-gather.4.cloned.1.call-done), kind=kOutput, calls=%fused_computation.2 | convolution fusion | flops 1208549376 | bytes 5111808 | tf_op jit(solution)/shard_map/dot_general | solution.py:127
  118.4 1.0 pad_maximum_fusion.2
  119.7 2.0 collective-permute-start.12
  122.4 1.9 slice.140
  124.3 1.0 slice.149
  126.9 5.1 %collective-permute-start.6 = (bf16[104,1536]{1,0:T(8,128)(2,1)}, bf16[104,1536]{1,0:T(8,128)(2,1)}, u32[]{:S(2)}, u32[]{:S(2)}) collective-permute-start(bf16[104,1536]{1,0:T(8,128)(2,1)} %get-tuple-element.62), channel_id=1, source_target_pairs={{0,12},{4,0},{8,4},{12,8},{1,13},{5,1},{9,5},{13,9},{2,14},{6,2},{... | collective-permute-start | bytes 958472 | tf_op jit(solution)/shard_map/ppermute | solution.py:38
  132.1 5.5 %collective-permute-start.7 = (bf16[104,1536]{1,0:T(8,128)(2,1)}, bf16[104,1536]{1,0:T(8,128)(2,1)}, u32[]{:S(2)}, u32[]{:S(2)}) collective-permute-start(bf16[104,1536]{1,0:T(8,128)(2,1)} %get-tuple-element.63), channel_id=1, source_target_pairs={{0,8},{4,12},{8,0},{12,4},{1,9},{5,13},{9,1},{13,5},{2,10},{6,14},... | collective-permute-start | bytes 958472 | tf_op jit(solution)/shard_map/ppermute | solution.py:38
  137.6 0.9 convolution_reduce_fusion
  138.6 14.9 %psum.37 = f32[3328]{0:T(1024)S(1)} all-reduce(f32[3328]{0:T(1024)S(1)} %pad_maximum_fusion.12), channel_id=1, replica_groups=mesh['zh'=4,'y'=4,'c'=2,'x'=4,'zl'=4] {'x'}, use_global_device_ids=true, to_apply=%region_7.8 | all-reduce | flops 3328 | bytes 26624 | tf_op jit(solution)/shard_map/psum | solution.py:143
  153.4 2.0 convolution_convert_fusion.1
  155.6 2.0 collective-permute-start.13
  157.6 4.0 %collective-permute-start.14 = (bf16[64,1536]{1,0:T(8,128)(2,1)S(1)}, bf16[64,1536]{1,0:T(8,128)(2,1)S(1)}, u32[]{:S(2)}, u32[]{:S(2)}) collective-permute-start(bf16[64,1536]{1,0:T(8,128)(2,1)S(1)} %get-tuple-element.29), channel_id=1, source_target_pairs={{0,8},{4,12},{8,0},{12,4},{1,9},{5,13},{9,1},{13,5},{2,10},{6,14},... | collective-permute-start | bytes 589832 | tf_op jit(solution)/shard_map/ppermute | solution.py:38
  161.6 3.3 %collective-permute-start.15 = (bf16[64,1536]{1,0:T(8,128)(2,1)S(1)}, bf16[64,1536]{1,0:T(8,128)(2,1)S(1)}, u32[]{:S(2)}, u32[]{:S(2)}) collective-permute-start(bf16[64,1536]{1,0:T(8,128)(2,1)S(1)} %get-tuple-element.30), channel_id=1, source_target_pairs={{0,12},{4,0},{8,4},{12,8},{1,13},{5,1},{9,5},{13,9},{2,14},{6,2},{... | collective-permute-start | bytes 589832 | tf_op jit(solution)/shard_map/ppermute | solution.py:38
  166.3 1.4 fusion.3
  169.5 3.7 %collective-permute-start.21 = (bf16[32,1536]{1,0:T(8,128)(2,1)S(1)}, bf16[32,1536]{1,0:T(8,128)(2,1)S(1)}, u32[]{:S(2)}, u32[]{:S(2)}) collective-permute-start(bf16[32,1536]{1,0:T(8,128)(2,1)S(1)} %fusion.7), channel_id=1, source_target_pairs={{0,1},{1,0},{2,3},{3,2},{4,5},{5,4},{6,7},{7,6},{8,9},{9,8},{10,11... | collective-permute-start | bytes 294920 | tf_op jit(solution)/shard_map/ppermute | solution.py:47
  173.2 2.2 collective-permute-start.16
  175.4 6.7 %collective-permute-start.17 = (bf16[160,384]{1,0:T(8,128)(2,1)S(1)}, bf16[160,384]{1,0:T(8,128)(2,1)S(1)}, u32[]{:S(2)}, u32[]{:S(2)}) collective-permute-start(bf16[160,384]{1,0:T(8,128)(2,1)S(1)} %get-tuple-element.53), channel_id=1, source_target_pairs={{0,2},{1,3},{2,0},{3,1},{4,6},{5,7},{6,4},{7,5},{8,10},{9,11},{10,... | collective-permute-start | bytes 368648 | tf_op jit(solution)/shard_map/ppermute | solution.py:38
  182.1 4.8 %collective-permute-start.18 = (bf16[160,384]{1,0:T(8,128)(2,1)S(1)}, bf16[160,384]{1,0:T(8,128)(2,1)S(1)}, u32[]{:S(2)}, u32[]{:S(2)}) collective-permute-start(bf16[160,384]{1,0:T(8,128)(2,1)S(1)} %get-tuple-element.52), channel_id=1, source_target_pairs={{0,3},{1,0},{2,1},{3,2},{4,7},{5,4},{6,5},{7,6},{8,11},{9,8},{10,9... | collective-permute-start | bytes 368648 | tf_op jit(solution)/shard_map/ppermute | solution.py:38
  186.9 15.6 %psum.38 = f32[3328]{0:T(1024)S(1)} all-reduce(f32[3328]{0:T(1024)S(1)} %psum.37), channel_id=1, replica_groups=mesh['zh'=4,'y'=4,'c'=2,'x'=4,'zl'=4] {'zl'}, use_global_device_ids=true, to_apply=%region_8.9 | all-reduce | flops 3328 | bytes 26624 | tf_op jit(solution)/shard_map/psum | solution.py:149
  202.6 2.8 %collective-permute-start.22 = (bf16[64,1536]{1,0:T(8,128)(2,1)S(1)}, bf16[64,1536]{1,0:T(8,128)(2,1)S(1)}, u32[]{:S(2)}, u32[]{:S(2)}) collective-permute-start(bf16[64,1536]{1,0:T(8,128)(2,1)S(1)} %pad_maximum_fusion.6), channel_id=1, source_target_pairs={{0,3},{1,2},{2,1},{3,0},{4,7},{5,6},{6,5},{7,4},{8,11},{9,10},{10,... | collective-permute-start | bytes 589832 | tf_op jit(solution)/shard_map/ppermute | solution.py:47
  206.1 13.1 %psum.39 = f32[1024]{0:T(1024)S(1)} all-reduce(f32[1024]{0:T(1024)S(1)} %multiply_dynamic-update-slice_fusion), channel_id=1, replica_groups=mesh['zh'=4,'y'=4,'c'=2,'x'=4,'zl'=4] {'zh'}, use_global_device_ids=true, to_apply=%region_10.11 | all-reduce | flops 1024 | bytes 8192 | tf_op jit(solution)/shard_map/psum | solution.py:171
  220.2 6.4 %collective-permute-start.19 = (bf16[160,192]{1,0:T(8,128)(2,1)S(1)}, bf16[160,192]{1,0:T(8,128)(2,1)S(1)}, u32[]{:S(2)}, u32[]{:S(2)}) collective-permute-start(bf16[160,192]{1,0:T(8,128)(2,1)S(1)} %get-tuple-element.60), channel_id=1, source_target_pairs={{0,0},{1,32},{2,64},{3,96},{16,16},{17,48},{18,80},{19,112},{32,1}... | collective-permute-start | bytes 184328 | tf_op jit(solution)/shard_map/ppermute | solution.py:177
  226.6 1.9 collective-permute-start.20
  228.6 2.0 collective-permute-done.19
  230.6 5.6 %collective-permute-done.20 = bf16[160,192]{1,0:T(8,128)(2,1)S(1)} collective-permute-done((bf16[160,192]{1,0:T(8,128)(2,1)S(1)}, bf16[160,192]{1,0:T(8,128)(2,1)S(1)}, u32[]{:S(2)}, u32[]{:S(2)}) %collective-permute-start.20) | collective-permute-done | bytes 61472 | tf_op jit(solution)/shard_map/ppermute | solution.py:178
  237.9 3.0 %convolution_multiply_fusion = f32[160,1024]{1,0:T(8,128)} fusion(bf16[1024,160]{1,0:T(8,128)(2,1)S(1)} %bitcast.54, bf16[1024,1024]{1,0:T(8,128)(2,1)} %bitcast.53), kind=kOutput, calls=%fused_computation.4 | convolution fusion | flops 335708160 | bytes 3080192 | tf_op jit(solution)/shard_map/dot_general | solution.py:190
  (136 shorter events, 16.0 us)
Async XLA Ops:
  7.2 28.7 %copy-start.1 = (bf16[192,1024]{1,0:T(8,128)(2,1)S(1)}, bf16[192,1024]{1,0:T(8,128)(2,1)}, u32[]{:S(2)}) copy-start(bf16[192,1024]{1,0:T(8,128)(2,1)} %param.7) | copy-start | bytes 1179652
  7.2 28.6 %slice-start = ((bf16[160,1024]{1,0:T(8,128)(2,1)}), bf16[64,1024]{1,0:T(8,128)(2,1)S(1)}, s32[]{:S(2)}) async-start(bf16[160,1024]{1,0:T(8,128)(2,1)} %param.8), calls=%async_computation.2 | async-start | bytes 262144 | tf_op jit(solution)/shard_map/slice | solution.py:91
  7.2 28.8 %copy-start.12 = (f32[320]{0:T(512)S(1)}, f32[320]{0:T(512)}, u32[]{:S(2)}) copy-start(f32[320]{0:T(512)} %param.11) | copy-start | bytes 3844
  7.2 28.6 %copy-start.6 = (bf16[32,1024]{1,0:T(8,128)(2,1)S(1)}, bf16[32,1024]{1,0:T(8,128)(2,1)}, u32[]{:S(2)}) copy-start(bf16[32,1024]{1,0:T(8,128)(2,1)} %param.10) | copy-start | bytes 196612
  7.2 107.7 %all-gather.4.cloned.1.call-start = ((), (), s32[]{:S(2)}) async-start(), calls=%async_computation | async-start | bytes 3538944 | tf_op jit(solution)/shard_map/all_gather | solution.py:81
  7.9 230.0 %all-gather.6.cloned.1.call-start = ((), (), s32[]{:S(2)}) async-start(), calls=%async_computation.1 | async-start | bytes 2359296 | tf_op jit(solution)/shard_map/all_gather | solution.py:186
  9.7 68.1 %collective-permute-start.3 = (bf16[96,1024]{1,0:T(8,128)(2,1)}, bf16[96,1024]{1,0:T(8,128)(2,1)}, u32[]{:S(2)}, u32[]{:S(2)}) collective-permute-start(bf16[96,1024]{1,0:T(8,128)(2,1)} %get-tuple-element.57), channel_id=1, source_target_pairs={{0,128},{128,256},{256,384},{384,0},{1,129},{129,257},{257,385},{3... | collective-permute-start | bytes 589832 | tf_op jit(solution)/shard_map/ppermute | solution.py:38
  18.8 59.9 %collective-permute-start.2 = (bf16[96,1024]{1,0:T(8,128)(2,1)}, bf16[96,1024]{1,0:T(8,128)(2,1)}, u32[]{:S(2)}, u32[]{:S(2)}) collective-permute-start(bf16[96,1024]{1,0:T(8,128)(2,1)} %get-tuple-element.57), channel_id=1, source_target_pairs={{0,384},{128,0},{256,128},{384,256},{1,385},{129,1},{257,129},{385... | collective-permute-start | bytes 589832 | tf_op jit(solution)/shard_map/ppermute | solution.py:38
  26.0 15.8 %collective-permute-start = (f32[33,160]{1,0:T(8,128)S(1)}, f32[33,160]{1,0:T(8,128)S(1)}, u32[]{:S(2)}, u32[]{:S(2)}) collective-permute-start(f32[33,160]{1,0:T(8,128)S(1)} %fusion.10), channel_id=1, source_target_pairs={{0,0},{1,32},{2,64},{3,96},{4,128},{5,160},{6,192},{7,224},{8,256}... | collective-permute-start | bytes 63368 | tf_op jit(solution)/shard_map/ppermute | solution.py:87
  29.6 12.3 %collective-permute-start.1 = (bf16[32,160]{1,0:T(8,128)(2,1)S(1)}, bf16[32,160]{1,0:T(8,128)(2,1)S(1)}, u32[]{:S(2)}, u32[]{:S(2)}) collective-permute-start(bf16[32,160]{1,0:T(8,128)(2,1)S(1)} %slice_select_fusion), channel_id=1, source_target_pairs={{0,16},{1,48},{2,80},{3,112},{4,144},{5,176},{6,208},{7,240},{8,27... | collective-permute-start | bytes 30728 | tf_op jit(solution)/shard_map/ppermute | solution.py:88
  35.7 22.6 %copy-start.2 = (bf16[160,1024]{1,0:T(8,128)(2,1)S(1)}, bf16[160,1024]{1,0:T(8,128)(2,1)}, u32[]{:S(2)}) copy-start(bf16[160,1024]{1,0:T(8,128)(2,1)} %param.8) | copy-start | bytes 983044
  36.0 53.4 %copy-start.11 = (bf16[384,1024]{1,0:T(8,128)(2,1)S(1)}, bf16[384,1024]{1,0:T(8,128)(2,1)}, u32[]{:S(2)}) copy-start(bf16[384,1024]{1,0:T(8,128)(2,1)} %get-tuple-element.56) | copy-start | bytes 2359300
  41.8 54.9 %collective-permute-start.9 = (bf16[96,1024]{1,0:T(8,128)(2,1)S(1)}, bf16[96,1024]{1,0:T(8,128)(2,1)S(1)}, u32[]{:S(2)}, u32[]{:S(2)}) collective-permute-start(bf16[96,1024]{1,0:T(8,128)(2,1)S(1)} %pad_maximum_fusion.5), channel_id=1, source_target_pairs={{0,128},{128,256},{256,384},{384,0},{1,129},{129,257},{257,385},{3... | collective-permute-start | bytes 589832 | tf_op jit(solution)/shard_map/ppermute | solution.py:38
  54.0 36.3 %collective-permute-start.8 = (bf16[96,1024]{1,0:T(8,128)(2,1)S(1)}, bf16[96,1024]{1,0:T(8,128)(2,1)S(1)}, u32[]{:S(2)}, u32[]{:S(2)}) collective-permute-start(bf16[96,1024]{1,0:T(8,128)(2,1)S(1)} %pad_maximum_fusion.5), channel_id=1, source_target_pairs={{0,384},{128,0},{256,128},{384,256},{1,385},{129,1},{257,129},{385... | collective-permute-start | bytes 589832 | tf_op jit(solution)/shard_map/ppermute | solution.py:38
  77.1 41.2 %copy-start.10 = (f32[2816]{0:T(1024)}, f32[2816]{0:T(1024)S(1)}, u32[]{:S(2)}) copy-start(f32[2816]{0:T(1024)S(1)} %psum.36) | copy-start | bytes 33796
  79.7 17.8 %collective-permute-start.4 = (bf16[56,1024]{1,0:T(8,128)(2,1)S(1)}, bf16[56,1024]{1,0:T(8,128)(2,1)S(1)}, u32[]{:S(2)}, u32[]{:S(2)}) collective-permute-start(bf16[56,1024]{1,0:T(8,128)(2,1)S(1)} %get-tuple-element.68), channel_id=1, source_target_pairs={{0,128},{128,256},{256,384},{384,0},{1,129},{129,257},{257,385},{3... | collective-permute-start | bytes 344072 | tf_op jit(solution)/shard_map/ppermute | solution.py:38
  83.9 18.3 %collective-permute-start.5 = (bf16[56,1024]{1,0:T(8,128)(2,1)S(1)}, bf16[56,1024]{1,0:T(8,128)(2,1)S(1)}, u32[]{:S(2)}, u32[]{:S(2)}) collective-permute-start(bf16[56,1024]{1,0:T(8,128)(2,1)S(1)} %get-tuple-element.67), channel_id=1, source_target_pairs={{0,384},{128,0},{256,128},{384,256},{1,385},{129,1},{257,129},{385... | collective-permute-start | bytes 344072 | tf_op jit(solution)/shard_map/ppermute | solution.py:38
  90.4 23.9 %collective-permute-start.11 = (bf16[48,1024]{1,0:T(8,128)(2,1)S(1)}, bf16[48,1024]{1,0:T(8,128)(2,1)S(1)}, u32[]{:S(2)}, u32[]{:S(2)}) collective-permute-start(bf16[48,1024]{1,0:T(8,128)(2,1)S(1)} %slice.139), channel_id=1, source_target_pairs={{0,384},{128,0},{256,128},{384,256},{1,385},{129,1},{257,129},{385... | collective-permute-start | bytes 294920 | tf_op jit(solution)/shard_map/ppermute | solution.py:38
  96.7 21.5 %copy-start.4 = (bf16[96,1024]{1,0:T(8,128)(2,1)}, bf16[96,1024]{1,0:T(8,128)(2,1)S(1)}, u32[]{:S(2)}) copy-start(bf16[96,1024]{1,0:T(8,128)(2,1)S(1)} %collective-permute-done.9) | copy-start | bytes 589828
  97.5 20.8 %copy-start.7 = (bf16[56,1024]{1,0:T(8,128)(2,1)}, bf16[56,1024]{1,0:T(8,128)(2,1)S(1)}, u32[]{:S(2)}) copy-start(bf16[56,1024]{1,0:T(8,128)(2,1)S(1)} %collective-permute-done.4) | copy-start | bytes 344068
  97.5 16.1 %collective-permute-start.10 = (bf16[56,1024]{1,0:T(8,128)(2,1)S(1)}, bf16[56,1024]{1,0:T(8,128)(2,1)S(1)}, u32[]{:S(2)}, u32[]{:S(2)}) collective-permute-start(bf16[56,1024]{1,0:T(8,128)(2,1)S(1)} %pad_maximum_fusion.9), channel_id=1, source_target_pairs={{0,128},{128,256},{256,384},{384,0},{1,129},{129,257},{257,385},{3... | collective-permute-start | bytes 344072 | tf_op jit(solution)/shard_map/ppermute | solution.py:38
  102.2 16.1 %copy-start.8 = (bf16[56,1024]{1,0:T(8,128)(2,1)}, bf16[56,1024]{1,0:T(8,128)(2,1)S(1)}, u32[]{:S(2)}) copy-start(bf16[56,1024]{1,0:T(8,128)(2,1)S(1)} %collective-permute-done.5) | copy-start | bytes 344068
  113.6 4.7 %copy-start.9 = (bf16[56,1024]{1,0:T(8,128)(2,1)}, bf16[56,1024]{1,0:T(8,128)(2,1)S(1)}, u32[]{:S(2)}) copy-start(bf16[56,1024]{1,0:T(8,128)(2,1)S(1)} %collective-permute-done.10) | copy-start | bytes 344068
  118.3 1.4 copy-start.3
  118.3 3.4 %copy-start.5 = (bf16[96,1024]{1,0:T(8,128)(2,1)S(1)}, bf16[96,1024]{1,0:T(8,128)(2,1)}, u32[]{:S(2)}) copy-start(bf16[96,1024]{1,0:T(8,128)(2,1)} %copy-done.4) | copy-start | bytes 589828
  118.3 19.3 %copy-start = (bf16[1536,1024]{1,0:T(8,128)(2,1)S(1)}, bf16[1536,1024]{1,0:T(8,128)(2,1)}, u32[]{:S(2)}) copy-start(bf16[1536,1024]{1,0:T(8,128)(2,1)} %all-gather.4.cloned.1.call-done) | copy-start | bytes 9437188
  119.7 18.9 %slice-start.1 = ((f32[2816]{0:T(1024)}), f32[1792]{0:T(1024)S(1)}, s32[]{:S(2)}) async-start(f32[2816]{0:T(1024)} %copy-done.10), calls=%async_computation.3 | async-start | bytes 16384 | tf_op jit(solution)/shard_map/slice | solution.py:143
  119.7 17.9 %collective-permute-start.12 = (bf16[104,1536]{1,0:T(8,128)(2,1)}, bf16[104,1536]{1,0:T(8,128)(2,1)}, u32[]{:S(2)}, u32[]{:S(2)}) collective-permute-start(bf16[104,1536]{1,0:T(8,128)(2,1)} %get-tuple-element.64), channel_id=1, source_target_pairs={{0,4},{4,8},{8,12},{12,0},{1,5},{5,9},{9,13},{13,1},{2,6},{6,10},{... | collective-permute-start | bytes 958472 | tf_op jit(solution)/shard_map/ppermute | solution.py:38
  126.9 39.4 %collective-permute-start.6 = (bf16[104,1536]{1,0:T(8,128)(2,1)}, bf16[104,1536]{1,0:T(8,128)(2,1)}, u32[]{:S(2)}, u32[]{:S(2)}) collective-permute-start(bf16[104,1536]{1,0:T(8,128)(2,1)} %get-tuple-element.62), channel_id=1, source_target_pairs={{0,12},{4,0},{8,4},{12,8},{1,13},{5,1},{9,5},{13,9},{2,14},{6,2},{... | collective-permute-start | bytes 958472 | tf_op jit(solution)/shard_map/ppermute | solution.py:38
  132.1 33.5 %collective-permute-start.7 = (bf16[104,1536]{1,0:T(8,128)(2,1)}, bf16[104,1536]{1,0:T(8,128)(2,1)}, u32[]{:S(2)}, u32[]{:S(2)}) collective-permute-start(bf16[104,1536]{1,0:T(8,128)(2,1)} %get-tuple-element.63), channel_id=1, source_target_pairs={{0,8},{4,12},{8,0},{12,4},{1,9},{5,13},{9,1},{13,5},{2,10},{6,14},... | collective-permute-start | bytes 958472 | tf_op jit(solution)/shard_map/ppermute | solution.py:38
  155.6 63.6 %copy-start.13 = (s32[1024]{0:T(1024)S(1)}, s32[1024]{0:T(1024)}, u32[]{:S(2)}) copy-start(s32[1024]{0:T(1024)} %param.13) | copy-start | bytes 12292
  155.6 64.3 %copy-start.14 = (f32[1024]{0:T(1024)S(1)}, f32[1024]{0:T(1024)}, u32[]{:S(2)}) copy-start(f32[1024]{0:T(1024)} %param.12) | copy-start | bytes 12292
  155.6 12.9 %collective-permute-start.13 = (bf16[64,1536]{1,0:T(8,128)(2,1)S(1)}, bf16[64,1536]{1,0:T(8,128)(2,1)S(1)}, u32[]{:S(2)}, u32[]{:S(2)}) collective-permute-start(bf16[64,1536]{1,0:T(8,128)(2,1)S(1)} %get-tuple-element.27), channel_id=1, source_target_pairs={{0,4},{4,8},{8,12},{12,0},{1,5},{5,9},{9,13},{13,1},{2,6},{6,10},{... | collective-permute-start | bytes 589832 | tf_op jit(solution)/shard_map/ppermute | solution.py:38
  157.6 10.9 %collective-permute-start.14 = (bf16[64,1536]{1,0:T(8,128)(2,1)S(1)}, bf16[64,1536]{1,0:T(8,128)(2,1)S(1)}, u32[]{:S(2)}, u32[]{:S(2)}) collective-permute-start(bf16[64,1536]{1,0:T(8,128)(2,1)S(1)} %get-tuple-element.29), channel_id=1, source_target_pairs={{0,8},{4,12},{8,0},{12,4},{1,9},{5,13},{9,1},{13,5},{2,10},{6,14},... | collective-permute-start | bytes 589832 | tf_op jit(solution)/shard_map/ppermute | solution.py:38
  161.6 7.6 %collective-permute-start.15 = (bf16[64,1536]{1,0:T(8,128)(2,1)S(1)}, bf16[64,1536]{1,0:T(8,128)(2,1)S(1)}, u32[]{:S(2)}, u32[]{:S(2)}) collective-permute-start(bf16[64,1536]{1,0:T(8,128)(2,1)S(1)} %get-tuple-element.30), channel_id=1, source_target_pairs={{0,12},{4,0},{8,4},{12,8},{1,13},{5,1},{9,5},{13,9},{2,14},{6,2},{... | collective-permute-start | bytes 589832 | tf_op jit(solution)/shard_map/ppermute | solution.py:38
  169.5 33.1 %collective-permute-start.21 = (bf16[32,1536]{1,0:T(8,128)(2,1)S(1)}, bf16[32,1536]{1,0:T(8,128)(2,1)S(1)}, u32[]{:S(2)}, u32[]{:S(2)}) collective-permute-start(bf16[32,1536]{1,0:T(8,128)(2,1)S(1)} %fusion.7), channel_id=1, source_target_pairs={{0,1},{1,0},{2,3},{3,2},{4,5},{5,4},{6,7},{7,6},{8,9},{9,8},{10,11... | collective-permute-start | bytes 294920 | tf_op jit(solution)/shard_map/ppermute | solution.py:47
  173.2 32.2 %collective-permute-start.16 = (bf16[160,384]{1,0:T(8,128)(2,1)S(1)}, bf16[160,384]{1,0:T(8,128)(2,1)S(1)}, u32[]{:S(2)}, u32[]{:S(2)}) collective-permute-start(bf16[160,384]{1,0:T(8,128)(2,1)S(1)} %get-tuple-element.51), channel_id=1, source_target_pairs={{0,1},{1,2},{2,3},{3,0},{4,5},{5,6},{6,7},{7,4},{8,9},{9,10},{10,1... | collective-permute-start | bytes 368648 | tf_op jit(solution)/shard_map/ppermute | solution.py:38
  175.4 44.6 %collective-permute-start.17 = (bf16[160,384]{1,0:T(8,128)(2,1)S(1)}, bf16[160,384]{1,0:T(8,128)(2,1)S(1)}, u32[]{:S(2)}, u32[]{:S(2)}) collective-permute-start(bf16[160,384]{1,0:T(8,128)(2,1)S(1)} %get-tuple-element.53), channel_id=1, source_target_pairs={{0,2},{1,3},{2,0},{3,1},{4,6},{5,7},{6,4},{7,5},{8,10},{9,11},{10,... | collective-permute-start | bytes 368648 | tf_op jit(solution)/shard_map/ppermute | solution.py:38
  182.1 37.9 %collective-permute-start.18 = (bf16[160,384]{1,0:T(8,128)(2,1)S(1)}, bf16[160,384]{1,0:T(8,128)(2,1)S(1)}, u32[]{:S(2)}, u32[]{:S(2)}) collective-permute-start(bf16[160,384]{1,0:T(8,128)(2,1)S(1)} %get-tuple-element.52), channel_id=1, source_target_pairs={{0,3},{1,0},{2,1},{3,2},{4,7},{5,4},{6,5},{7,6},{8,11},{9,8},{10,9... | collective-permute-start | bytes 368648 | tf_op jit(solution)/shard_map/ppermute | solution.py:38
  202.6 34.5 %collective-permute-start.22 = (bf16[64,1536]{1,0:T(8,128)(2,1)S(1)}, bf16[64,1536]{1,0:T(8,128)(2,1)S(1)}, u32[]{:S(2)}, u32[]{:S(2)}) collective-permute-start(bf16[64,1536]{1,0:T(8,128)(2,1)S(1)} %pad_maximum_fusion.6), channel_id=1, source_target_pairs={{0,3},{1,2},{2,1},{3,0},{4,7},{5,6},{6,5},{7,4},{8,11},{9,10},{10,... | collective-permute-start | bytes 589832 | tf_op jit(solution)/shard_map/ppermute | solution.py:47
  220.2 10.4 %collective-permute-start.19 = (bf16[160,192]{1,0:T(8,128)(2,1)S(1)}, bf16[160,192]{1,0:T(8,128)(2,1)S(1)}, u32[]{:S(2)}, u32[]{:S(2)}) collective-permute-start(bf16[160,192]{1,0:T(8,128)(2,1)S(1)} %get-tuple-element.60), channel_id=1, source_target_pairs={{0,0},{1,32},{2,64},{3,96},{16,16},{17,48},{18,80},{19,112},{32,1}... | collective-permute-start | bytes 184328 | tf_op jit(solution)/shard_map/ppermute | solution.py:177
  226.6 9.7 %collective-permute-start.20 = (bf16[160,192]{1,0:T(8,128)(2,1)S(1)}, bf16[160,192]{1,0:T(8,128)(2,1)S(1)}, u32[]{:S(2)}, u32[]{:S(2)}) collective-permute-start(bf16[160,192]{1,0:T(8,128)(2,1)S(1)} %get-tuple-element.61), channel_id=1, source_target_pairs={{0,16},{1,48},{2,80},{3,112},{16,0},{17,32},{18,64},{19,96},{32,17... | collective-permute-start | bytes 184328 | tf_op jit(solution)/shard_map/ppermute | solution.py:178
Sparse Core Ops, SparseCore 0:
  10.2 38.5 all-gather.3
  126.2 30.2 all-gather.5

commit v6 on v1

v6 whole, which is shorter than its diff:
```python
import jax
import jax.numpy as jnp
from jax import lax
from jax.sharding import Mesh, PartitionSpec as P

D = 5120
FF = 16384
AXES = ("zh", "y", "c", "x", "zl")
SIZES = (4, 4, 2, 4, 4)


def place(*index):
    at = 0
    for i, size in zip(index, SIZES):
        at = at * size + i
    return at


def ring(step):
    return [(i, (i + step) % 4) for i in range(4)]


def swapped(flip):
    return [
        (place(zh, y, c, x, zl), place(x, zl, c ^ flip, zh, y))
        for zh in range(4) for y in range(4) for c in range(2) for x in range(4) for zl in range(4)
    ]


def turned():
    return [(y * 4 + zl, zl * 4 + y) for y in range(4) for zl in range(4)]


def move(value, axis, step):
    return lax.ppermute(value, axis, ring(step))


def pairs(step):
    return [(i, i ^ step) for i in range(4)]


def joined(value, axis, index):
    for step, later in ((1, index % 2 == 1), (3, index >= 2)):
        got = lax.ppermute(value, axis, pairs(step))
        value = jnp.concatenate([jnp.where(later, got, value), jnp.where(later, value, got)], axis=0)
    return value


def placed(value, index, count):
    size = value.shape[0]
    return lax.dynamic_update_slice(jnp.zeros((size * count,), value.dtype), value, (index * size,))


def per_device(features, down_weight, member_left, member_right, probe, payoff, opponent):
    f32, bf16 = jnp.float32, jnp.bfloat16
    rows, width = features.shape
    members = member_right.shape[0]
    tokens = rows // members
    population = payoff.shape[0]
    block = down_weight.shape[0]
    cols = probe.shape[0]
    spread = 1.0 / jnp.sqrt(f32(FF))
    zh, y, c, x, zl = (lax.axis_index(a) for a in AXES)
    first = c == 0
    here = y * 2 + c

    own = jnp.concatenate([down_weight, member_right], axis=0)
    stack = lax.all_gather(own, ("zh", "c"), axis=0, tiled=True).reshape(4, 2, -1, width)
    weight = stack[:, :, :block].reshape(-1, width)
    rights = lax.all_gather(stack[:, :, block:], "y", axis=0, tiled=False)

    around = [features] + [move(features, "y", -j) for j in (1, 2, 3)]

    left_cols = lax.dynamic_slice(member_left, (0, (x * 4 + zl) * cols), (members, cols)).astype(f32)
    payload = jnp.concatenate([left_cols, probe[None, :]], axis=0)
    mine = jnp.where(first, payload[:, :block], payload[:, block:])
    other = jnp.where(first, left_cols[:, block:], left_cols[:, :block])
    mine = lax.ppermute(mine, AXES, swapped(0))
    other = lax.ppermute(other, AXES, swapped(1))

    direction = jnp.sum(down_weight.astype(f32) * mine[members][:, None], axis=0)
    direction = lax.psum(lax.psum(direction, ("y", "c")), "zh")
    wide = features.astype(f32)
    along = jnp.sum(wide * direction[None, :], axis=1)
    inner = jnp.sum(
        wide.reshape(members, tokens, width) * member_right.astype(f32)[:, None, :], axis=2
    ).reshape(rows)
    left_dot = jnp.sum(left_cols * probe[None, :], axis=1)
    sums = lax.psum(lax.psum(jnp.concatenate([along, inner, left_dot]), "x"), "zl")
    along, inner, left_dot = jnp.split(sums, [rows, 2 * rows])
    inner = spread * inner
    dots = along + inner * jnp.repeat(left_dot, tokens)
    scale = 0.5 / jnp.sqrt(f32(D))
    own_score = jnp.mean(jnp.tanh(scale * dots).reshape(members, tokens), axis=1)

    many = 4 * rows
    mine = mine[:members]
    lefts = jnp.where(first, jnp.concatenate([mine, other], 0), jnp.concatenate([other, mine], 0))
    lefts = jnp.pad(lefts.astype(bf16), ((0, 0), (0, 192 - block))).reshape(-1, many)
    part = lax.dot_general(
        weight, jnp.concatenate(around, axis=0), (((1,), (1,)), ((), ())),
        preferred_element_type=f32,
    ).astype(bf16).reshape(4, cols, many)
    parts = []
    for k in range(4):
        one = lax.dynamic_index_in_dim(part, lax.rem(x + k, 4), 0, keepdims=False)
        one = jnp.concatenate([one, lefts], axis=0)
        parts.append(one if k == 0 else move(one, "x", k))
    own_score, parts[1] = lax.optimization_barrier((own_score, parts[1]))
    score = lax.psum(placed(own_score, here, 8), ("y", "c"))
    total = sum(p[:cols].astype(f32) for p in parts).astype(bf16)
    lefts = jnp.stack([parts[k][cols:] for k in (0, 3, 2, 1)])
    lefts, total = lax.optimization_barrier((lefts, total))
    lefts = joined(jnp.roll(lefts, x, axis=0).reshape(-1, many), "zl", zl)

    total = total.T.reshape(4, rows, cols)
    parts = []
    for k in range(4):
        one = lax.dynamic_index_in_dim(total, lax.rem(zl + k + 4 - y, 4), 0, keepdims=False)
        parts.append(one if k == 0 else move(one, "zl", k))
    score, parts[1] = lax.optimization_barrier((score, parts[1]))
    score = lax.psum(placed(score, zh, 4), "zh")
    total = sum(p.astype(f32) for p in parts).astype(bf16)

    total = lax.ppermute(total, ("y", "zl"), turned()).astype(f32)
    lowrank = inner.reshape(members, tokens)[:, :, None] * left_cols[:, None, :]
    mixed = (total + lowrank.reshape(rows, cols)).astype(bf16)

    labels = jnp.arange(population, dtype=jnp.int32)
    rival = jnp.sum(jnp.where(opponent[:, None] == labels[None, :], score[None, :], 0.0), axis=1)
    fitness = payoff * (score - rival)
    fitness = fitness.reshape(4, 4, -1).transpose(1, 0, 2).reshape(population, 1)
    scaled = lefts.reshape(population, 192)[:, :block].astype(f32)
    scaled = (fitness * scaled).astype(bf16)
    term = lax.dot_general(
        scaled, rights.reshape(population, width), (((0,), (0,)), ((), ())),
        preferred_element_type=f32,
    )
    return mixed, term / jnp.sqrt(f32(population))


def solution(mesh):
    fine = Mesh(mesh.devices.reshape(SIZES), AXES)
    member, tensor = ("zh", "y", "c"), ("x", "zl")
    in_specs = (
        P(member, tensor), P(member, tensor), P(member, None), P(member, tensor), P(tensor), P(), P(),
    )
    out_specs = (P(member, tensor), P(member, tensor))
    return jax.shard_map(
        per_device, mesh=fine, in_specs=in_specs, out_specs=out_specs, check_vma=False
    )
```

time: 270 us -> 221 us (0.82)
  blocking collectives: 134 us -> 109 us
  waiting for transfers between devices: 37.9 us -> 18.7 us
  starting transfers between devices: 57.2 us -> 49.4 us
  matrix products: 9.77 us -> 6.73 us
    all_gather x1 -> x0, blocking collectives: 45.4 us -> none  [per_device(): left_all = lax.all_gather(left_pair, ('x', 'zl'), axis=0, tiled=True)]
    ppermute x1, waiting for transfers between devices: 11.9 us -> 0.01 us  [per_device(): other = lax.ppermute(other, AXES, swapped(1))]
    psum x4, blocking collectives: 48 us -> 59.4 us  [the longest x1 18 us: per_device(): lax.psum(jnp.concatenate([along, inner, left_dot]), 'x')]
    psum x2, blocking collectives: 40.3 us -> 50 us  [per_device(): direction = lax.psum(lax.psum(direction, ('y', 'c')), 'zh')]
    ppermute x10 -> x9, starting transfers between devices: 39.9 us -> 30.9 us  [move(): return lax.ppermute(value, axis, ring(step))]
    ppermute x10 -> x9, waiting for transfers between devices: 20.5 us -> 13.4 us  [move(): return lax.ppermute(value, axis, ring(step))]
    dot_general x5 -> x2, matrix products: 9.77 us -> 6.73 us  [the longest x1 3.48 us: per_device(): lax.dot_general(weight, jnp.concatenate(around, axis=0), (((1,), (1,)), (...]
    ppermute x2 -> x3, starting transfers between devices: 8.56 us -> 11 us  [the longest x2 6.23 us: joined(): got = lax.ppermute(value, axis, pairs(step))]
  transfers between devices with their start and end apart: 16 -> 16, of which waited for: 7 -> 3; matrix products, arithmetic and copies ran while one was open for 8% -> 7% of each run, Pallas kernels for 0% -> 0%
where the time goes in v6:
time: 221 us; the launch traced here: 216 us
  blocking collectives  109 us (49%)
  starting transfers between devices  49.4 us (22%)
  waiting for transfers between devices  18.7 us (8%)
  between operations  14.6 us (7%)
  other arithmetic  8.85 us (4%)
  local copies, waits for them, and re-layouts  8.54 us (4%)
  matrix products  6.73 us (3%)
    psum x2, blocking collectives, per_device(): direction = lax.psum(lax.psum(direction, ('y', 'c')), 'zh')  50 us
    ppermute x9, starting transfers between devices, move(): return lax.ppermute(value, axis, ring(step))  30.9 us
    psum x1, blocking collectives, per_device(): lax.psum(jnp.concatenate([along, inner, left_dot]), 'x')  18 us
    psum x1, blocking collectives, per_device(): lax.psum(lax.psum(jnp.concatenate([along, inner, left_dot]), 'x'), 'zl')  15.9 us
    psum x1, blocking collectives, per_device(): score = lax.psum(placed(score, zh, 4), 'zh')  15.3 us
    ppermute x9, waiting for transfers between devices, move(): return lax.ppermute(value, axis, ring(step))  13.4 us
    psum x1, blocking collectives, per_device(): score = lax.psum(placed(own_score, here, 8), ('y', 'c'))  10.3 us
    ppermute x2, starting transfers between devices, joined(): got = lax.ppermute(value, axis, pairs(step))  6.23 us
  transfers between devices with their start and end apart: 16, of which 3 were waited for; matrix products, arithmetic and copies ran while one was open for 7% of the time, Pallas kernels for 0%

profile of v6, /device:TPU:24, one launch (start us, length us, event | category | flops | bytes accessed | tf_op | source)
XLA Modules:
  0.0 216.3 jit_solution(11431462381977817755)
XLA Ops:
  7.2 1.8 pad_maximum_fusion.3
  9.1 7.6 %collective-permute-start.4 = (bf16[192,1024]{1,0:T(8,128)(2,1)}, bf16[192,1024]{1,0:T(8,128)(2,1)}, u32[]{:S(2)}, u32[]{:S(2)}) collective-permute-start(bf16[192,1024]{1,0:T(8,128)(2,1)} %param.7), channel_id=1, source_target_pairs={{0,32},{32,64},{64,96},{96,0},{1,33},{33,65},{65,97},{97,1},{2,34}... | collective-permute-start | bytes 1179656 | tf_op jit(solution)/shard_map/ppermute | solution.py:35
  16.7 1.9 collective-permute-start.3
  18.7 2.8 %collective-permute-start.2 = (bf16[192,1024]{1,0:T(8,128)(2,1)}, bf16[192,1024]{1,0:T(8,128)(2,1)}, u32[]{:S(2)}, u32[]{:S(2)}) collective-permute-start(bf16[192,1024]{1,0:T(8,128)(2,1)} %param.7), channel_id=1, source_target_pairs={{0,96},{32,0},{64,32},{96,64},{1,97},{33,1},{65,33},{97,65},{2,98}... | collective-permute-start | bytes 1179656 | tf_op jit(solution)/shard_map/ppermute | solution.py:35
  21.5 0.8 dynamic-slice_convert_fusion
  22.4 4.1 %collective-permute-start.1 = (bf16[32,160]{1,0:T(8,128)(2,1)S(1)}, bf16[32,160]{1,0:T(8,128)(2,1)S(1)}, u32[]{:S(2)}, u32[]{:S(2)}) collective-permute-start(bf16[32,160]{1,0:T(8,128)(2,1)S(1)} %slice_select_fusion), channel_id=1, source_target_pairs={{0,16},{1,48},{2,80},{3,112},{4,144},{5,176},{6,208},{7,240},{8,27... | collective-permute-start | bytes 30728 | tf_op jit(solution)/shard_map/ppermute | solution.py:79
  26.5 0.7 broadcast_in_dim.14
  27.3 3.3 %collective-permute-start = (f32[33,160]{1,0:T(8,128)S(1)}, f32[33,160]{1,0:T(8,128)S(1)}, u32[]{:S(2)}, u32[]{:S(2)}) collective-permute-start(f32[33,160]{1,0:T(8,128)S(1)} %fusion.20), channel_id=1, source_target_pairs={{0,0},{1,32},{2,64},{3,96},{4,128},{5,160},{6,192},{7,224},{8,256}... | collective-permute-start | bytes 63368 | tf_op jit(solution)/shard_map/ppermute | solution.py:78
  30.6 1.0 multiply_reduce_fusion.1
  31.8 0.1 mul.116
  31.9 0.1 mul.117
  32.0 5.2 %collective-permute-done = f32[33,160]{1,0:T(8,128)S(1)} collective-permute-done((f32[33,160]{1,0:T(8,128)S(1)}, f32[33,160]{1,0:T(8,128)S(1)}, u32[]{:S(2)}, u32[]{:S(2)}) %collective-permute-start) | collective-permute-done | bytes 21152 | tf_op jit(solution)/shard_map/ppermute | solution.py:78
  37.3 0.1 multiply_reduce_fusion
  37.4 12.4 %psum.42 = f32[1024]{0:T(1024)S(1)} all-reduce(f32[1024]{0:T(1024)S(1)} %multiply_reduce_fusion), channel_id=1, replica_groups=mesh['zh'=4,'y'=4,'c'=2,'x'=4,'zl'=4] {'y','c'}, use_global_device_ids=true, to_apply=%region_1.2 | all-reduce | flops 1024 | bytes 8192 | tf_op jit(solution)/shard_map/psum | solution.py:82
  49.8 37.6 %psum.43 = f32[1024]{0:T(1024)S(1)} all-reduce(f32[1024]{0:T(1024)S(1)} %psum.42), channel_id=1, replica_groups=mesh['zh'=4,'y'=4,'c'=2,'x'=4,'zl'=4] {'zh'}, use_global_device_ids=true, to_apply=%region_2.3 | all-reduce | flops 1024 | bytes 8192 | tf_op jit(solution)/shard_map/psum | solution.py:82
  87.4 0.2 fusion.10
  87.9 18.0 %psum.44 = f32[416]{0:T(512)S(1)} all-reduce(f32[416]{0:T(512)S(1)} %pad_maximum_fusion.8), channel_id=1, replica_groups=mesh['zh'=4,'y'=4,'c'=2,'x'=4,'zl'=4] {'x'}, use_global_device_ids=true, to_apply=%region_6.7 | all-reduce | flops 416 | bytes 3328 | tf_op jit(solution)/shard_map/psum | solution.py:89
  105.9 15.9 %psum.45 = f32[416]{0:T(512)S(1)} all-reduce(f32[416]{0:T(512)S(1)} %psum.44), channel_id=1, replica_groups=mesh['zh'=4,'y'=4,'c'=2,'x'=4,'zl'=4] {'zl'}, use_global_device_ids=true, to_apply=%region_7.8 | all-reduce | flops 416 | bytes 3328 | tf_op jit(solution)/shard_map/psum | solution.py:89
  121.9 0.1 split.14
  122.1 2.1 slice.65
  124.2 3.5 %convolution_convert_fusion = bf16[1280,768]{1,0:T(8,128)(2,1)S(1)} fusion(bf16[1280,1024]{1,0:T(8,128)(2,1)S(1)} %bitcast.39, bf16[192,1024]{1,0:T(8,128)(2,1)} %collective-permute-done.4, bf16[192,1024]{1,0:T(8,128)(2,1)} %collective-permute-done.3, bf16[192,1024]{1,0:T(8,128)(2,1)} %collective-permute-done.2, bf16[192,1024]{1,0:T(8,128)(2,1)S(1)} %copy-done.1), kind=kOutput, calls=%fused_computation.2 | convolution fusion | flops 2020540416 | bytes 6160384 | tf_op jit(solution)/shard_map/dot_general | solution.py:100
  127.7 0.1 dynamic-slice_bitcast_fusion.2
  127.8 1.2 pad_maximum_fusion.2
  129.0 1.9 collective-permute-start.7
  130.9 5.1 %collective-permute-start.5 = (bf16[336,768]{1,0:T(8,128)(2,1)}, bf16[336,768]{1,0:T(8,128)(2,1)}, u32[]{:S(2)}, u32[]{:S(2)}) collective-permute-start(bf16[336,768]{1,0:T(8,128)(2,1)} %get-tuple-element.26), channel_id=1, source_target_pairs={{0,12},{4,0},{8,4},{12,8},{1,13},{5,1},{9,5},{13,9},{2,14},{6,2},{... | collective-permute-start | bytes 1548296 | tf_op jit(solution)/shard_map/ppermute | solution.py:35
  136.1 0.2 tanh_reduce_fusion
  136.3 1.9 slice.72
  138.2 1.9 collective-permute-start.6
  140.2 12.3 %collective-permute-done.7 = bf16[336,768]{1,0:T(8,128)(2,1)S(1)} collective-permute-done((bf16[336,768]{1,0:T(8,128)(2,1)}, bf16[336,768]{1,0:T(8,128)(2,1)S(1)}, u32[]{:S(2)}, u32[]{:S(2)}) %collective-permute-start.7) | collective-permute-done | bytes 516128 | tf_op jit(solution)/shard_map/ppermute | solution.py:35
  152.5 1.2 collective-permute-done.5
  153.6 0.7 slice_bitcast_fusion.1
  154.4 0.7 slice_bitcast_fusion
  155.2 1.5 fusion.9
  156.6 0.3 copy.15
  157.0 1.9 collective-permute-start.12
  159.0 3.9 %collective-permute-start.8 = (bf16[192,320]{1,0:T(8,128)(2,1)S(1)}, bf16[192,320]{1,0:T(8,128)(2,1)S(1)}, u32[]{:S(2)}, u32[]{:S(2)}) collective-permute-start(bf16[192,320]{1,0:T(8,128)(2,1)S(1)} %get-tuple-element.19), channel_id=1, source_target_pairs={{0,1},{1,2},{2,3},{3,0},{4,5},{5,6},{6,7},{7,4},{8,9},{9,10},{10,1... | collective-permute-start | bytes 368648 | tf_op jit(solution)/shard_map/ppermute | solution.py:35
  162.9 3.7 %collective-permute-start.10 = (bf16[192,320]{1,0:T(8,128)(2,1)S(1)}, bf16[192,320]{1,0:T(8,128)(2,1)S(1)}, u32[]{:S(2)}, u32[]{:S(2)}) collective-permute-start(bf16[192,320]{1,0:T(8,128)(2,1)S(1)} %get-tuple-element.20), channel_id=1, source_target_pairs={{0,3},{1,0},{2,1},{3,2},{4,7},{5,4},{6,5},{7,6},{8,11},{9,8},{10,9... | collective-permute-start | bytes 368648 | tf_op jit(solution)/shard_map/ppermute | solution.py:35
  166.6 1.9 collective-permute-start.9
  168.6 0.2 dynamic_update_slice.6
  168.8 10.3 %psum.46 = f32[256]{0:T(256)S(1)} all-reduce(f32[256]{0:T(256)S(1)} %dynamic_update_slice.6), channel_id=1, replica_groups=mesh['zh'=4,'y'=4,'c'=2,'x'=4,'zl'=4] {'y','c'}, use_global_device_ids=true, to_apply=%region_9.10 | all-reduce | flops 256 | bytes 2048 | tf_op jit(solution)/shard_map/psum | solution.py:110
  179.2 4.3 %collective-permute-start.13 = (bf16[128,768]{1,0:T(8,128)(2,1)S(1)}, bf16[128,768]{1,0:T(8,128)(2,1)S(1)}, u32[]{:S(2)}, u32[]{:S(2)}) collective-permute-start(bf16[128,768]{1,0:T(8,128)(2,1)S(1)} %pad_maximum_fusion.5), channel_id=1, source_target_pairs={{0,3},{1,2},{2,1},{3,0},{4,7},{5,6},{6,5},{7,4},{8,11},{9,10},{10,... | collective-permute-start | bytes 589832 | tf_op jit(solution)/shard_map/ppermute | solution.py:44
  183.6 4.8 %collective-permute-start.11 = (bf16[192,320]{1,0:T(8,128)(2,1)S(1)}, bf16[192,320]{1,0:T(8,128)(2,1)S(1)}, u32[]{:S(2)}, u32[]{:S(2)}) collective-permute-start(bf16[192,320]{1,0:T(8,128)(2,1)S(1)} %fusion.16), channel_id=1, source_target_pairs={{0,0},{1,32},{2,64},{3,96},{32,1},{33,33},{34,65},{35,97},{64,2},{... | collective-permute-start | bytes 368648 | tf_op jit(solution)/shard_map/ppermute | solution.py:125
  188.4 0.3 dynamic_update_slice.7
  188.7 15.3 %psum.47 = f32[1024]{0:T(1024)S(1)} all-reduce(f32[1024]{0:T(1024)S(1)} %dynamic_update_slice.7), channel_id=1, replica_groups=mesh['zh'=4,'y'=4,'c'=2,'x'=4,'zl'=4] {'zh'}, use_global_device_ids=true, to_apply=%region_10.11 | all-reduce | flops 1024 | bytes 8192 | tf_op jit(solution)/shard_map/psum | solution.py:122
  203.9 0.7 select_reduce_fusion
  204.8 0.8 add_convert_fusion
  205.7 0.5 reshape.68
  206.2 3.3 %convolution_multiply_fusion = f32[160,1024]{1,0:T(8,128)} fusion(bf16[1024,1024]{1,0:T(8,128)(2,1)} %bitcast.48, bf16[1024,192]{1,0:T(8,128)(2,1)S(1)} %reshape.68, f32[1024]{0:T(1024)S(1)} %mul.137), kind=kOutput, calls=%fused_computation.10 | convolution fusion | flops 336199680 | bytes 3149824 | tf_op jit(solution)/shard_map/dot_general | solution.py:135
  (57 shorter events, 1.4 us)
Async XLA Ops:
  7.2 24.6 %copy-start.2 = (bf16[32,1024]{1,0:T(8,128)(2,1)S(1)}, bf16[32,1024]{1,0:T(8,128)(2,1)}, u32[]{:S(2)}) copy-start(bf16[32,1024]{1,0:T(8,128)(2,1)} %param.10) | copy-start | bytes 196612
  7.2 114.9 %all-gather.4.cloned.1.call-start = ((), (), s32[]{:S(2)}) async-start(), calls=%async_computation | async-start | bytes 3538944 | tf_op jit(solution)/shard_map/all_gather | solution.py:68
  9.0 28.2 %copy-start = (bf16[160,1024]{1,0:T(8,128)(2,1)S(1)}, bf16[160,1024]{1,0:T(8,128)(2,1)}, u32[]{:S(2)}) copy-start(bf16[160,1024]{1,0:T(8,128)(2,1)} %param.8) | copy-start | bytes 983044
  9.0 78.4 %copy-start.1 = (bf16[192,1024]{1,0:T(8,128)(2,1)S(1)}, bf16[192,1024]{1,0:T(8,128)(2,1)}, u32[]{:S(2)}) copy-start(bf16[192,1024]{1,0:T(8,128)(2,1)} %param.7) | copy-start | bytes 1179652
  9.0 197.2 %all-gather.6.cloned.1.call-start = ((), (), s32[]{:S(2)}) async-start(), calls=%async_computation.1 | async-start | bytes 2621440 | tf_op jit(solution)/shard_map/all_gather | solution.py:70
  9.1 115.1 %collective-permute-start.4 = (bf16[192,1024]{1,0:T(8,128)(2,1)}, bf16[192,1024]{1,0:T(8,128)(2,1)}, u32[]{:S(2)}, u32[]{:S(2)}) collective-permute-start(bf16[192,1024]{1,0:T(8,128)(2,1)} %param.7), channel_id=1, source_target_pairs={{0,32},{32,64},{64,96},{96,0},{1,33},{33,65},{65,97},{97,1},{2,34}... | collective-permute-start | bytes 1179656 | tf_op jit(solution)/shard_map/ppermute | solution.py:35
  16.7 107.5 %collective-permute-start.3 = (bf16[192,1024]{1,0:T(8,128)(2,1)}, bf16[192,1024]{1,0:T(8,128)(2,1)}, u32[]{:S(2)}, u32[]{:S(2)}) collective-permute-start(bf16[192,1024]{1,0:T(8,128)(2,1)} %param.7), channel_id=1, source_target_pairs={{0,64},{32,96},{64,0},{96,32},{1,65},{33,97},{65,1},{97,33},{2,66}... | collective-permute-start | bytes 1179656 | tf_op jit(solution)/shard_map/ppermute | solution.py:35
  18.7 105.6 %collective-permute-start.2 = (bf16[192,1024]{1,0:T(8,128)(2,1)}, bf16[192,1024]{1,0:T(8,128)(2,1)}, u32[]{:S(2)}, u32[]{:S(2)}) collective-permute-start(bf16[192,1024]{1,0:T(8,128)(2,1)} %param.7), channel_id=1, source_target_pairs={{0,96},{32,0},{64,32},{96,64},{1,97},{33,1},{65,33},{97,65},{2,98}... | collective-permute-start | bytes 1179656 | tf_op jit(solution)/shard_map/ppermute | solution.py:35
  22.4 65.3 %collective-permute-start.1 = (bf16[32,160]{1,0:T(8,128)(2,1)S(1)}, bf16[32,160]{1,0:T(8,128)(2,1)S(1)}, u32[]{:S(2)}, u32[]{:S(2)}) collective-permute-start(bf16[32,160]{1,0:T(8,128)(2,1)S(1)} %slice_select_fusion), channel_id=1, source_target_pairs={{0,16},{1,48},{2,80},{3,112},{4,144},{5,176},{6,208},{7,240},{8,27... | collective-permute-start | bytes 30728 | tf_op jit(solution)/shard_map/ppermute | solution.py:79
  27.3 10.0 %collective-permute-start = (f32[33,160]{1,0:T(8,128)S(1)}, f32[33,160]{1,0:T(8,128)S(1)}, u32[]{:S(2)}, u32[]{:S(2)}) collective-permute-start(f32[33,160]{1,0:T(8,128)S(1)} %fusion.20), channel_id=1, source_target_pairs={{0,0},{1,32},{2,64},{3,96},{4,128},{5,160},{6,192},{7,224},{8,256}... | collective-permute-start | bytes 63368 | tf_op jit(solution)/shard_map/ppermute | solution.py:78
  129.0 23.5 %collective-permute-start.7 = (bf16[336,768]{1,0:T(8,128)(2,1)}, bf16[336,768]{1,0:T(8,128)(2,1)S(1)}, u32[]{:S(2)}, u32[]{:S(2)}) collective-permute-start(bf16[336,768]{1,0:T(8,128)(2,1)} %get-tuple-element.28), channel_id=1, source_target_pairs={{0,4},{4,8},{8,12},{12,0},{1,5},{5,9},{9,13},{13,1},{2,6},{6,10},{... | collective-permute-start | bytes 1548296 | tf_op jit(solution)/shard_map/ppermute | solution.py:35
  130.9 22.7 %collective-permute-start.5 = (bf16[336,768]{1,0:T(8,128)(2,1)}, bf16[336,768]{1,0:T(8,128)(2,1)}, u32[]{:S(2)}, u32[]{:S(2)}) collective-permute-start(bf16[336,768]{1,0:T(8,128)(2,1)} %get-tuple-element.26), channel_id=1, source_target_pairs={{0,12},{4,0},{8,4},{12,8},{1,13},{5,1},{9,5},{13,9},{2,14},{6,2},{... | collective-permute-start | bytes 1548296 | tf_op jit(solution)/shard_map/ppermute | solution.py:35
  138.2 16.2 %collective-permute-start.6 = (bf16[336,768]{1,0:T(8,128)(2,1)}, bf16[336,768]{1,0:T(8,128)(2,1)}, u32[]{:S(2)}, u32[]{:S(2)}) collective-permute-start(bf16[336,768]{1,0:T(8,128)(2,1)} %get-tuple-element.27), channel_id=1, source_target_pairs={{0,8},{4,12},{8,0},{12,4},{1,9},{5,13},{9,1},{13,5},{2,10},{6,14},... | collective-permute-start | bytes 1548296 | tf_op jit(solution)/shard_map/ppermute | solution.py:35
  155.2 48.8 %copy-start.3 = (s32[1024]{0:T(1024)S(1)}, s32[1024]{0:T(1024)}, u32[]{:S(2)}) copy-start(s32[1024]{0:T(1024)} %param.13) | copy-start | bytes 12292
  155.2 49.4 %copy-start.4 = (f32[1024]{0:T(1024)S(1)}, f32[1024]{0:T(1024)}, u32[]{:S(2)}) copy-start(f32[1024]{0:T(1024)} %param.12) | copy-start | bytes 12292
  157.0 22.1 %collective-permute-start.12 = (bf16[64,768]{1,0:T(8,128)(2,1)S(1)}, bf16[64,768]{1,0:T(8,128)(2,1)S(1)}, u32[]{:S(2)}, u32[]{:S(2)}) collective-permute-start(bf16[64,768]{1,0:T(8,128)(2,1)S(1)} %bitcast.45), channel_id=1, source_target_pairs={{0,1},{1,0},{2,3},{3,2},{4,5},{5,4},{6,7},{7,6},{8,9},{9,8},{10,11... | collective-permute-start | bytes 294920 | tf_op jit(solution)/shard_map/ppermute | solution.py:44
  159.0 24.5 %collective-permute-start.8 = (bf16[192,320]{1,0:T(8,128)(2,1)S(1)}, bf16[192,320]{1,0:T(8,128)(2,1)S(1)}, u32[]{:S(2)}, u32[]{:S(2)}) collective-permute-start(bf16[192,320]{1,0:T(8,128)(2,1)S(1)} %get-tuple-element.19), channel_id=1, source_target_pairs={{0,1},{1,2},{2,3},{3,0},{4,5},{5,6},{6,7},{7,4},{8,9},{9,10},{10,1... | collective-permute-start | bytes 368648 | tf_op jit(solution)/shard_map/ppermute | solution.py:35
  162.9 20.6 %collective-permute-start.10 = (bf16[192,320]{1,0:T(8,128)(2,1)S(1)}, bf16[192,320]{1,0:T(8,128)(2,1)S(1)}, u32[]{:S(2)}, u32[]{:S(2)}) collective-permute-start(bf16[192,320]{1,0:T(8,128)(2,1)S(1)} %get-tuple-element.20), channel_id=1, source_target_pairs={{0,3},{1,0},{2,1},{3,2},{4,7},{5,4},{6,5},{7,6},{8,11},{9,8},{10,9... | collective-permute-start | bytes 368648 | tf_op jit(solution)/shard_map/ppermute | solution.py:35
  166.6 16.9 %collective-permute-start.9 = (bf16[192,320]{1,0:T(8,128)(2,1)S(1)}, bf16[192,320]{1,0:T(8,128)(2,1)S(1)}, u32[]{:S(2)}, u32[]{:S(2)}) collective-permute-start(bf16[192,320]{1,0:T(8,128)(2,1)S(1)} %get-tuple-element.21), channel_id=1, source_target_pairs={{0,2},{1,3},{2,0},{3,1},{4,6},{5,7},{6,4},{7,5},{8,10},{9,11},{10,... | collective-permute-start | bytes 368648 | tf_op jit(solution)/shard_map/ppermute | solution.py:35
  179.2 26.4 %collective-permute-start.13 = (bf16[128,768]{1,0:T(8,128)(2,1)S(1)}, bf16[128,768]{1,0:T(8,128)(2,1)S(1)}, u32[]{:S(2)}, u32[]{:S(2)}) collective-permute-start(bf16[128,768]{1,0:T(8,128)(2,1)S(1)} %pad_maximum_fusion.5), channel_id=1, source_target_pairs={{0,3},{1,2},{2,1},{3,0},{4,7},{5,6},{6,5},{7,4},{8,11},{9,10},{10,... | collective-permute-start | bytes 589832 | tf_op jit(solution)/shard_map/ppermute | solution.py:44
  183.6 21.2 %collective-permute-start.11 = (bf16[192,320]{1,0:T(8,128)(2,1)S(1)}, bf16[192,320]{1,0:T(8,128)(2,1)S(1)}, u32[]{:S(2)}, u32[]{:S(2)}) collective-permute-start(bf16[192,320]{1,0:T(8,128)(2,1)S(1)} %fusion.16), channel_id=1, source_target_pairs={{0,0},{1,32},{2,64},{3,96},{32,1},{33,33},{34,65},{35,97},{64,2},{... | collective-permute-start | bytes 368648 | tf_op jit(solution)/shard_map/ppermute | solution.py:125
Sparse Core Ops, SparseCore 0:
  10.7 86.3 all-gather.3
  138.3 29.1 all-gather.5

commit v7 on v6

--- a/solution.py
+++ b/solution.py
@@ -69,17 +69,22 @@
     weight = stack[:, :, :block].reshape(-1, width)
     rights = lax.all_gather(stack[:, :, block:], "y", axis=0, tiled=False)
 
+    level = jnp.where(first, probe[:block], probe[block:])
+    level = lax.ppermute(level, AXES, swapped(0))
+    direction = jnp.sum(down_weight.astype(f32) * level[:, None], axis=0)
+    direction = lax.psum(direction, ("y", "c"))
+
+    features, member_left, direction = lax.optimization_barrier((features, member_left, direction))
     around = [features] + [move(features, "y", -j) for j in (1, 2, 3)]
 
-    left_cols = lax.dynamic_slice(member_left, (0, (x * 4 + zl) * cols), (members, cols)).astype(f32)
-    payload = jnp.concatenate([left_cols, probe[None, :]], axis=0)
-    mine = jnp.where(first, payload[:, :block], payload[:, block:])
+    left_cols = lax.dynamic_slice(member_left, (0, (x * 4 + zl) * cols), (members, cols))
+    mine = jnp.where(first, left_cols[:, :block], left_cols[:, block:])
     other = jnp.where(first, left_cols[:, block:], left_cols[:, :block])
     mine = lax.ppermute(mine, AXES, swapped(0))
     other = lax.ppermute(other, AXES, swapped(1))
+    left_cols = left_cols.astype(f32)
 
-    direction = jnp.sum(down_weight.astype(f32) * mine[members][:, None], axis=0)
-    direction = lax.psum(lax.psum(direction, ("y", "c")), "zh")
+    direction = lax.psum(direction, "zh")
     wide = features.astype(f32)
     along = jnp.sum(wide * direction[None, :], axis=1)
     inner = jnp.sum(
@@ -91,12 +96,12 @@
     inner = spread * inner
     dots = along + inner * jnp.repeat(left_dot, tokens)
     scale = 0.5 / jnp.sqrt(f32(D))
-    own_score = jnp.mean(jnp.tanh(scale * dots).reshape(members, tokens), axis=1)
+    score = jnp.mean(jnp.tanh(scale * dots).reshape(members, tokens), axis=1)
+    score = lax.psum(placed(score, here, 8), ("y", "c"))
 
     many = 4 * rows
-    mine = mine[:members]
     lefts = jnp.where(first, jnp.concatenate([mine, other], 0), jnp.concatenate([other, mine], 0))
-    lefts = jnp.pad(lefts.astype(bf16), ((0, 0), (0, 192 - block))).reshape(-1, many)
+    lefts = jnp.pad(lefts, ((0, 0), (0, 192 - block))).reshape(-1, many)
     part = lax.dot_general(
         weight, jnp.concatenate(around, axis=0), (((1,), (1,)), ((), ())),
         preferred_element_type=f32,
@@ -106,8 +111,8 @@
         one = lax.dynamic_index_in_dim(part, lax.rem(x + k, 4), 0, keepdims=False)
         one = jnp.concatenate([one, lefts], axis=0)
         parts.append(one if k == 0 else move(one, "x", k))
-    own_score, parts[1] = lax.optimization_barrier((own_score, parts[1]))
-    score = lax.psum(placed(own_score, here, 8), ("y", "c"))
+    score, parts[1] = lax.optimization_barrier((score, parts[1]))
+    score = lax.psum(placed(score, zh, 4), "zh")
     total = sum(p[:cols].astype(f32) for p in parts).astype(bf16)
     lefts = jnp.stack([parts[k][cols:] for k in (0, 3, 2, 1)])
     lefts, total = lax.optimization_barrier((lefts, total))
@@ -118,8 +123,6 @@
     for k in range(4):
         one = lax.dynamic_index_in_dim(total, lax.rem(zl + k + 4 - y, 4), 0, keepdims=False)
         parts.append(one if k == 0 else move(one, "zl", k))
-    score, parts[1] = lax.optimization_barrier((score, parts[1]))
-    score = lax.psum(placed(score, zh, 4), "zh")
     total = sum(p.astype(f32) for p in parts).astype(bf16)
 
     total = lax.ppermute(total, ("y", "zl"), turned()).astype(f32)

time: 221 us -> 216 us (0.977)
  the two profiles are of different devices: /device:TPU:24 before, /device:TPU:36 now
where the time goes in v7:
time: 216 us; the launch traced here: 215 us
  blocking collectives  90.7 us (42%)
  starting transfers between devices  69.9 us (32%)
  between operations  14.6 us (7%)
  waiting for transfers between devices  14.1 us (7%)
  other arithmetic  10.5 us (5%)
  local copies, waits for them, and re-layouts  8.45 us (4%)
  matrix products  6.62 us (3%)
    ppermute x9, starting transfers between devices, move(): return lax.ppermute(value, axis, ring(step))  32.6 us
    psum x1, blocking collectives, per_device(): lax.psum(jnp.concatenate([along, inner, left_dot]), 'x')  21.3 us
    psum x1, blocking collectives, per_device(): score = lax.psum(placed(score, zh, 4), 'zh')  19.6 us
    psum x1, blocking collectives, per_device(): direction = lax.psum(direction, 'zh')  16.4 us
    ppermute x1, starting transfers between devices, per_device(): level = lax.ppermute(level, AXES, swapped(0))  15.3 us
    psum x1, blocking collectives, per_device(): direction = lax.psum(direction, ('y', 'c'))  14 us
    ppermute x1, starting transfers between devices, per_device(): mine = lax.ppermute(mine, AXES, swapped(0))  13.8 us
    psum x1, blocking collectives, per_device(): score = lax.psum(placed(score, here, 8), ('y', 'c'))  12.9 us
  transfers between devices with their start and end apart: 17, of which 4 were waited for; matrix products, arithmetic and copies ran while one was open for 7% of the time, Pallas kernels for 0%

profile of v7, /device:TPU:36, one launch (start us, length us, event | category | flops | bytes accessed | tf_op | source)
XLA Modules:
  0.0 214.9 jit_solution(259787562138253489)
XLA Ops:
  7.2 1.9 pad_maximum_fusion.3
  9.2 0.8 slice_select_fusion
  10.0 15.3 %collective-permute-start = (f32[160]{0:T(256)S(1)}, f32[160]{0:T(256)S(1)}, u32[]{:S(2)}, u32[]{:S(2)}) collective-permute-start(f32[160]{0:T(256)S(1)} %slice_select_fusion), channel_id=1, source_target_pairs={{0,0},{1,32},{2,64},{3,96},{4,128},{5,160},{6,192},{7,224},{8,256}... | collective-permute-start | bytes 1928 | tf_op jit(solution)/shard_map/ppermute | solution.py:73
  25.4 1.0 mul.113
  26.4 0.1 mul.114
  26.5 0.3 collective-permute-done
  26.9 0.1 multiply_reduce_fusion
  27.0 14.0 %psum.42 = f32[1024]{0:T(1024)S(1)} all-reduce(f32[1024]{0:T(1024)S(1)} %multiply_reduce_fusion), channel_id=1, replica_groups=mesh['zh'=4,'y'=4,'c'=2,'x'=4,'zl'=4] {'y','c'}, use_global_device_ids=true, to_apply=%region_1.2 | all-reduce | flops 1024 | bytes 8192 | tf_op jit(solution)/shard_map/psum | solution.py:75
  41.1 1.9 collective-permute-start.5
  43.0 2.7 %collective-permute-start.4 = (bf16[192,1024]{1,0:T(8,128)(2,1)S(1)}, bf16[192,1024]{1,0:T(8,128)(2,1)}, u32[]{:S(2)}, u32[]{:S(2)}) collective-permute-start(bf16[192,1024]{1,0:T(8,128)(2,1)S(1)} %copy-done.1), channel_id=1, source_target_pairs={{0,64},{32,96},{64,0},{96,32},{1,65},{33,97},{65,1},{97,33},{2,66}... | collective-permute-start | bytes 1179656 | tf_op jit(solution)/shard_map/ppermute | solution.py:35
  45.7 4.4 %collective-permute-start.3 = (bf16[192,1024]{1,0:T(8,128)(2,1)S(1)}, bf16[192,1024]{1,0:T(8,128)(2,1)}, u32[]{:S(2)}, u32[]{:S(2)}) collective-permute-start(bf16[192,1024]{1,0:T(8,128)(2,1)S(1)} %copy-done.1), channel_id=1, source_target_pairs={{0,96},{32,0},{64,32},{96,64},{1,97},{33,1},{65,33},{97,65},{2,98}... | collective-permute-start | bytes 1179656 | tf_op jit(solution)/shard_map/ppermute | solution.py:35
  50.1 0.9 broadcast_select_fusion.5
  51.0 13.8 %collective-permute-start.1 = (bf16[32,160]{1,0:T(8,128)(2,1)S(1)}, bf16[32,160]{1,0:T(8,128)(2,1)S(1)}, u32[]{:S(2)}, u32[]{:S(2)}) collective-permute-start(bf16[32,160]{1,0:T(8,128)(2,1)S(1)} %get-tuple-element.26), channel_id=1, source_target_pairs={{0,0},{1,32},{2,64},{3,96},{4,128},{5,160},{6,192},{7,224},{8,256}... | collective-permute-start | bytes 30728 | tf_op jit(solution)/shard_map/ppermute | solution.py:83
  64.8 1.9 collective-permute-start.2
  66.7 16.4 %psum.43 = f32[1024]{0:T(1024)S(1)} all-reduce(f32[1024]{0:T(1024)S(1)} %psum.42), channel_id=1, replica_groups=mesh['zh'=4,'y'=4,'c'=2,'x'=4,'zl'=4] {'zh'}, use_global_device_ids=true, to_apply=%region_2.3 | all-reduce | flops 1024 | bytes 8192 | tf_op jit(solution)/shard_map/psum | solution.py:87
  83.1 0.9 multiply_reduce_fusion.1
  84.0 0.2 fusion.10
  84.3 21.3 %psum.44 = f32[416]{0:T(512)S(1)} all-reduce(f32[416]{0:T(512)S(1)} %pad_maximum_fusion.7), channel_id=1, replica_groups=mesh['zh'=4,'y'=4,'c'=2,'x'=4,'zl'=4] {'x'}, use_global_device_ids=true, to_apply=%region_6.7 | all-reduce | flops 416 | bytes 3328 | tf_op jit(solution)/shard_map/psum | solution.py:94
  105.6 6.5 %psum.45 = f32[416]{0:T(512)S(1)} all-reduce(f32[416]{0:T(512)S(1)} %psum.44), channel_id=1, replica_groups=mesh['zh'=4,'y'=4,'c'=2,'x'=4,'zl'=4] {'zl'}, use_global_device_ids=true, to_apply=%region_7.8 | all-reduce | flops 416 | bytes 3328 | tf_op jit(solution)/shard_map/psum | solution.py:94
  112.4 2.1 slice.54
  114.6 3.4 %convolution_convert_fusion = bf16[1280,768]{1,0:T(8,128)(2,1)S(1)} fusion(bf16[1280,1024]{1,0:T(8,128)(2,1)S(1)} %bitcast.38, bf16[192,1024]{1,0:T(8,128)(2,1)S(1)} %collective-permute-done.5, bf16[192,1024]{1,0:T(8,128)(2,1)} %collective-permute-done.4, bf16[192,1024]{1,0:T(8,128)(2,1)} %collective-permute-done.3, bf16[192,1024]{1,0:T(8,128)(2,1)S(1)} %copy-done.1), kind=kOutput, calls=%fused_computation.2 | convolution fusion | flops 2020540416 | bytes 6160384 | tf_op jit(solution)/shard_map/dot_general | solution.py:105
  118.0 1.2 pad_maximum_fusion.2
  119.2 3.2 %collective-permute-start.8 = (bf16[336,768]{1,0:T(8,128)(2,1)}, bf16[336,768]{1,0:T(8,128)(2,1)S(1)}, u32[]{:S(2)}, u32[]{:S(2)}) collective-permute-start(bf16[336,768]{1,0:T(8,128)(2,1)} %get-tuple-element.32), channel_id=1, source_target_pairs={{0,4},{4,8},{8,12},{12,0},{1,5},{5,9},{9,13},{13,1},{2,6},{6,10},{... | collective-permute-start | bytes 1548296 | tf_op jit(solution)/shard_map/ppermute | solution.py:35
  122.7 0.2 tanh_reduce_fusion
  122.9 1.9 slice.60
  124.8 2.6 %collective-permute-start.6 = (bf16[336,768]{1,0:T(8,128)(2,1)}, bf16[336,768]{1,0:T(8,128)(2,1)}, u32[]{:S(2)}, u32[]{:S(2)}) collective-permute-start(bf16[336,768]{1,0:T(8,128)(2,1)} %get-tuple-element.30), channel_id=1, source_target_pairs={{0,12},{4,0},{8,4},{12,8},{1,13},{5,1},{9,5},{13,9},{2,14},{6,2},{... | collective-permute-start | bytes 1548296 | tf_op jit(solution)/shard_map/ppermute | solution.py:35
  127.5 5.8 %collective-permute-start.7 = (bf16[336,768]{1,0:T(8,128)(2,1)}, bf16[336,768]{1,0:T(8,128)(2,1)}, u32[]{:S(2)}, u32[]{:S(2)}) collective-permute-start(bf16[336,768]{1,0:T(8,128)(2,1)} %get-tuple-element.31), channel_id=1, source_target_pairs={{0,8},{4,12},{8,0},{12,4},{1,9},{5,13},{9,1},{13,5},{2,10},{6,14},... | collective-permute-start | bytes 1548296 | tf_op jit(solution)/shard_map/ppermute | solution.py:35
  133.3 0.8 dynamic-slice_convert_fusion
  134.2 12.9 %psum.46 = f32[256]{0:T(256)S(1)} all-reduce(f32[256]{0:T(256)S(1)} %multiply_dynamic-update-slice_fusion), channel_id=1, replica_groups=mesh['zh'=4,'y'=4,'c'=2,'x'=4,'zl'=4] {'y','c'}, use_global_device_ids=true, to_apply=%region_9.10 | all-reduce | flops 256 | bytes 2048 | tf_op jit(solution)/shard_map/psum | solution.py:100
  147.3 0.7 slice_bitcast_fusion.1
  148.0 0.7 slice_bitcast_fusion
  148.8 1.4 fusion.9
  150.2 0.3 copy.15
  150.6 3.9 %collective-permute-start.9 = (bf16[192,320]{1,0:T(8,128)(2,1)S(1)}, bf16[192,320]{1,0:T(8,128)(2,1)S(1)}, u32[]{:S(2)}, u32[]{:S(2)}) collective-permute-start(bf16[192,320]{1,0:T(8,128)(2,1)S(1)} %get-tuple-element.21), channel_id=1, source_target_pairs={{0,1},{1,2},{2,3},{3,0},{4,5},{5,6},{6,7},{7,4},{8,9},{9,10},{10,1... | collective-permute-start | bytes 368648 | tf_op jit(solution)/shard_map/ppermute | solution.py:35
  154.5 3.8 %collective-permute-start.11 = (bf16[192,320]{1,0:T(8,128)(2,1)S(1)}, bf16[192,320]{1,0:T(8,128)(2,1)S(1)}, u32[]{:S(2)}, u32[]{:S(2)}) collective-permute-start(bf16[192,320]{1,0:T(8,128)(2,1)S(1)} %get-tuple-element.22), channel_id=1, source_target_pairs={{0,3},{1,0},{2,1},{3,2},{4,7},{5,4},{6,5},{7,6},{8,11},{9,8},{10,9... | collective-permute-start | bytes 368648 | tf_op jit(solution)/shard_map/ppermute | solution.py:35
  158.3 4.3 %collective-permute-start.10 = (bf16[192,320]{1,0:T(8,128)(2,1)S(1)}, bf16[192,320]{1,0:T(8,128)(2,1)S(1)}, u32[]{:S(2)}, u32[]{:S(2)}) collective-permute-start(bf16[192,320]{1,0:T(8,128)(2,1)S(1)} %get-tuple-element.23), channel_id=1, source_target_pairs={{0,2},{1,3},{2,0},{3,1},{4,6},{5,7},{6,4},{7,5},{8,10},{9,11},{10,... | collective-permute-start | bytes 368648 | tf_op jit(solution)/shard_map/ppermute | solution.py:35
  162.6 0.3 dynamic_update_slice.7
  162.9 19.6 %psum.47 = f32[1024]{0:T(1024)S(1)} all-reduce(f32[1024]{0:T(1024)S(1)} %dynamic_update_slice.7), channel_id=1, replica_groups=mesh['zh'=4,'y'=4,'c'=2,'x'=4,'zl'=4] {'zh'}, use_global_device_ids=true, to_apply=%region_10.11 | all-reduce | flops 1024 | bytes 8192 | tf_op jit(solution)/shard_map/psum | solution.py:115
  182.4 0.7 select_reduce_fusion
  183.3 1.9 collective-permute-start.13
  185.4 1.9 collective-permute-start.12
  187.3 2.5 %collective-permute-done.13 = bf16[64,768]{1,0:T(8,128)(2,1)S(1)} collective-permute-done((bf16[64,768]{1,0:T(8,128)(2,1)S(1)}, bf16[64,768]{1,0:T(8,128)(2,1)S(1)}, u32[]{:S(2)}, u32[]{:S(2)}) %collective-permute-start.13) | collective-permute-done | bytes 98336 | tf_op jit(solution)/shard_map/ppermute | solution.py:44
  189.9 2.4 %collective-permute-start.14 = (bf16[128,768]{1,0:T(8,128)(2,1)S(1)}, bf16[128,768]{1,0:T(8,128)(2,1)S(1)}, u32[]{:S(2)}, u32[]{:S(2)}) collective-permute-start(bf16[128,768]{1,0:T(8,128)(2,1)S(1)} %pad_maximum_fusion.5), channel_id=1, source_target_pairs={{0,3},{1,2},{2,1},{3,0},{4,7},{5,6},{6,5},{7,4},{8,11},{9,10},{10,... | collective-permute-start | bytes 589832 | tf_op jit(solution)/shard_map/ppermute | solution.py:44
  192.3 8.8 %collective-permute-done.12 = bf16[192,320]{1,0:T(8,128)(2,1)S(1)} collective-permute-done((bf16[192,320]{1,0:T(8,128)(2,1)S(1)}, bf16[192,320]{1,0:T(8,128)(2,1)S(1)}, u32[]{:S(2)}, u32[]{:S(2)}) %collective-permute-start.12) | collective-permute-done | bytes 122912 | tf_op jit(solution)/shard_map/ppermute | solution.py:128
  201.0 0.8 add_convert_fusion
  201.8 2.4 %collective-permute-done.14 = bf16[128,768]{1,0:T(8,128)(2,1)S(1)} collective-permute-done((bf16[128,768]{1,0:T(8,128)(2,1)S(1)}, bf16[128,768]{1,0:T(8,128)(2,1)S(1)}, u32[]{:S(2)}, u32[]{:S(2)}) %collective-permute-start.14) | collective-permute-done | bytes 196640 | tf_op jit(solution)/shard_map/ppermute | solution.py:44
  204.3 0.5 reshape.68
  204.8 3.3 %convolution_multiply_fusion = f32[160,1024]{1,0:T(8,128)} fusion(bf16[1024,1024]{1,0:T(8,128)(2,1)} %bitcast.46, bf16[1024,192]{1,0:T(8,128)(2,1)S(1)} %reshape.68, f32[1024]{0:T(1024)S(1)} %mul.134), kind=kOutput, calls=%fused_computation.10 | convolution fusion | flops 336199680 | bytes 3149824 | tf_op jit(solution)/shard_map/dot_general | solution.py:138
  (55 shorter events, 1.6 us)
Async XLA Ops:
  7.2 19.7 %copy-start = (bf16[160,1024]{1,0:T(8,128)(2,1)S(1)}, bf16[160,1024]{1,0:T(8,128)(2,1)}, u32[]{:S(2)}) copy-start(bf16[160,1024]{1,0:T(8,128)(2,1)} %param.8) | copy-start | bytes 983044
  7.2 75.9 %copy-start.2 = (f32[320]{0:T(512)S(1)}, f32[320]{0:T(512)}, u32[]{:S(2)}) copy-start(f32[320]{0:T(512)} %param.11) | copy-start | bytes 3844
  7.2 33.9 %copy-start.1 = (bf16[192,1024]{1,0:T(8,128)(2,1)S(1)}, bf16[192,1024]{1,0:T(8,128)(2,1)}, u32[]{:S(2)}) copy-start(bf16[192,1024]{1,0:T(8,128)(2,1)} %param.7) | copy-start | bytes 1179652
  7.2 105.2 %all-gather.4.cloned.1.call-start = ((), (), s32[]{:S(2)}) async-start(), calls=%async_computation | async-start | bytes 3538944 | tf_op jit(solution)/shard_map/all_gather | solution.py:68
  9.1 195.7 %all-gather.6.cloned.1.call-start = ((), (), s32[]{:S(2)}) async-start(), calls=%async_computation.1 | async-start | bytes 2621440 | tf_op jit(solution)/shard_map/all_gather | solution.py:70
  10.0 16.9 %collective-permute-start = (f32[160]{0:T(256)S(1)}, f32[160]{0:T(256)S(1)}, u32[]{:S(2)}, u32[]{:S(2)}) collective-permute-start(f32[160]{0:T(256)S(1)} %slice_select_fusion), channel_id=1, source_target_pairs={{0,0},{1,32},{2,64},{3,96},{4,128},{5,160},{6,192},{7,224},{8,256}... | collective-permute-start | bytes 1928 | tf_op jit(solution)/shard_map/ppermute | solution.py:73
  41.1 73.5 %collective-permute-start.5 = (bf16[192,1024]{1,0:T(8,128)(2,1)S(1)}, bf16[192,1024]{1,0:T(8,128)(2,1)S(1)}, u32[]{:S(2)}, u32[]{:S(2)}) collective-permute-start(bf16[192,1024]{1,0:T(8,128)(2,1)S(1)} %copy-done.1), channel_id=1, source_target_pairs={{0,32},{32,64},{64,96},{96,0},{1,33},{33,65},{65,97},{97,1},{2,34}... | collective-permute-start | bytes 1179656 | tf_op jit(solution)/shard_map/ppermute | solution.py:35
  43.0 71.6 %collective-permute-start.4 = (bf16[192,1024]{1,0:T(8,128)(2,1)S(1)}, bf16[192,1024]{1,0:T(8,128)(2,1)}, u32[]{:S(2)}, u32[]{:S(2)}) collective-permute-start(bf16[192,1024]{1,0:T(8,128)(2,1)S(1)} %copy-done.1), channel_id=1, source_target_pairs={{0,64},{32,96},{64,0},{96,32},{1,65},{33,97},{65,1},{97,33},{2,66}... | collective-permute-start | bytes 1179656 | tf_op jit(solution)/shard_map/ppermute | solution.py:35
  45.7 68.9 %collective-permute-start.3 = (bf16[192,1024]{1,0:T(8,128)(2,1)S(1)}, bf16[192,1024]{1,0:T(8,128)(2,1)}, u32[]{:S(2)}, u32[]{:S(2)}) collective-permute-start(bf16[192,1024]{1,0:T(8,128)(2,1)S(1)} %copy-done.1), channel_id=1, source_target_pairs={{0,96},{32,0},{64,32},{96,64},{1,97},{33,1},{65,33},{97,65},{2,98}... | collective-permute-start | bytes 1179656 | tf_op jit(solution)/shard_map/ppermute | solution.py:35
  51.0 61.3 %collective-permute-start.1 = (bf16[32,160]{1,0:T(8,128)(2,1)S(1)}, bf16[32,160]{1,0:T(8,128)(2,1)S(1)}, u32[]{:S(2)}, u32[]{:S(2)}) collective-permute-start(bf16[32,160]{1,0:T(8,128)(2,1)S(1)} %get-tuple-element.26), channel_id=1, source_target_pairs={{0,0},{1,32},{2,64},{3,96},{4,128},{5,160},{6,192},{7,224},{8,256}... | collective-permute-start | bytes 30728 | tf_op jit(solution)/shard_map/ppermute | solution.py:83
  64.8 47.4 %collective-permute-start.2 = (bf16[32,160]{1,0:T(8,128)(2,1)S(1)}, bf16[32,160]{1,0:T(8,128)(2,1)S(1)}, u32[]{:S(2)}, u32[]{:S(2)}) collective-permute-start(bf16[32,160]{1,0:T(8,128)(2,1)S(1)} %get-tuple-element.27), channel_id=1, source_target_pairs={{0,16},{1,48},{2,80},{3,112},{4,144},{5,176},{6,208},{7,240},{8,27... | collective-permute-start | bytes 30728 | tf_op jit(solution)/shard_map/ppermute | solution.py:84
  119.2 28.0 %collective-permute-start.8 = (bf16[336,768]{1,0:T(8,128)(2,1)}, bf16[336,768]{1,0:T(8,128)(2,1)S(1)}, u32[]{:S(2)}, u32[]{:S(2)}) collective-permute-start(bf16[336,768]{1,0:T(8,128)(2,1)} %get-tuple-element.32), channel_id=1, source_target_pairs={{0,4},{4,8},{8,12},{12,0},{1,5},{5,9},{9,13},{13,1},{2,6},{6,10},{... | collective-permute-start | bytes 1548296 | tf_op jit(solution)/shard_map/ppermute | solution.py:35
  124.8 22.5 %collective-permute-start.6 = (bf16[336,768]{1,0:T(8,128)(2,1)}, bf16[336,768]{1,0:T(8,128)(2,1)}, u32[]{:S(2)}, u32[]{:S(2)}) collective-permute-start(bf16[336,768]{1,0:T(8,128)(2,1)} %get-tuple-element.30), channel_id=1, source_target_pairs={{0,12},{4,0},{8,4},{12,8},{1,13},{5,1},{9,5},{13,9},{2,14},{6,2},{... | collective-permute-start | bytes 1548296 | tf_op jit(solution)/shard_map/ppermute | solution.py:35
  127.5 20.5 %collective-permute-start.7 = (bf16[336,768]{1,0:T(8,128)(2,1)}, bf16[336,768]{1,0:T(8,128)(2,1)}, u32[]{:S(2)}, u32[]{:S(2)}) collective-permute-start(bf16[336,768]{1,0:T(8,128)(2,1)} %get-tuple-element.31), channel_id=1, source_target_pairs={{0,8},{4,12},{8,0},{12,4},{1,9},{5,13},{9,1},{13,5},{2,10},{6,14},... | collective-permute-start | bytes 1548296 | tf_op jit(solution)/shard_map/ppermute | solution.py:35
  134.2 48.2 %copy-start.3 = (s32[1024]{0:T(1024)S(1)}, s32[1024]{0:T(1024)}, u32[]{:S(2)}) copy-start(s32[1024]{0:T(1024)} %param.13) | copy-start | bytes 12292
  134.2 48.9 %copy-start.4 = (f32[1024]{0:T(1024)S(1)}, f32[1024]{0:T(1024)}, u32[]{:S(2)}) copy-start(f32[1024]{0:T(1024)} %param.12) | copy-start | bytes 12292
  150.6 34.6 %collective-permute-start.9 = (bf16[192,320]{1,0:T(8,128)(2,1)S(1)}, bf16[192,320]{1,0:T(8,128)(2,1)S(1)}, u32[]{:S(2)}, u32[]{:S(2)}) collective-permute-start(bf16[192,320]{1,0:T(8,128)(2,1)S(1)} %get-tuple-element.21), channel_id=1, source_target_pairs={{0,1},{1,2},{2,3},{3,0},{4,5},{5,6},{6,7},{7,4},{8,9},{9,10},{10,1... | collective-permute-start | bytes 368648 | tf_op jit(solution)/shard_map/ppermute | solution.py:35
  154.5 30.7 %collective-permute-start.11 = (bf16[192,320]{1,0:T(8,128)(2,1)S(1)}, bf16[192,320]{1,0:T(8,128)(2,1)S(1)}, u32[]{:S(2)}, u32[]{:S(2)}) collective-permute-start(bf16[192,320]{1,0:T(8,128)(2,1)S(1)} %get-tuple-element.22), channel_id=1, source_target_pairs={{0,3},{1,0},{2,1},{3,2},{4,7},{5,4},{6,5},{7,6},{8,11},{9,8},{10,9... | collective-permute-start | bytes 368648 | tf_op jit(solution)/shard_map/ppermute | solution.py:35
  158.3 26.9 %collective-permute-start.10 = (bf16[192,320]{1,0:T(8,128)(2,1)S(1)}, bf16[192,320]{1,0:T(8,128)(2,1)S(1)}, u32[]{:S(2)}, u32[]{:S(2)}) collective-permute-start(bf16[192,320]{1,0:T(8,128)(2,1)S(1)} %get-tuple-element.23), channel_id=1, source_target_pairs={{0,2},{1,3},{2,0},{3,1},{4,6},{5,7},{6,4},{7,5},{8,10},{9,11},{10,... | collective-permute-start | bytes 368648 | tf_op jit(solution)/shard_map/ppermute | solution.py:35
  183.3 6.5 %collective-permute-start.13 = (bf16[64,768]{1,0:T(8,128)(2,1)S(1)}, bf16[64,768]{1,0:T(8,128)(2,1)S(1)}, u32[]{:S(2)}, u32[]{:S(2)}) collective-permute-start(bf16[64,768]{1,0:T(8,128)(2,1)S(1)} %bitcast.44), channel_id=1, source_target_pairs={{0,1},{1,0},{2,3},{3,2},{4,5},{5,4},{6,7},{7,6},{8,9},{9,8},{10,11... | collective-permute-start | bytes 294920 | tf_op jit(solution)/shard_map/ppermute | solution.py:44
  185.4 15.7 %collective-permute-start.12 = (bf16[192,320]{1,0:T(8,128)(2,1)S(1)}, bf16[192,320]{1,0:T(8,128)(2,1)S(1)}, u32[]{:S(2)}, u32[]{:S(2)}) collective-permute-start(bf16[192,320]{1,0:T(8,128)(2,1)S(1)} %fusion.16), channel_id=1, source_target_pairs={{0,0},{1,32},{2,64},{3,96},{32,1},{33,33},{34,65},{35,97},{64,2},{... | collective-permute-start | bytes 368648 | tf_op jit(solution)/shard_map/ppermute | solution.py:128
  189.9 14.3 %collective-permute-start.14 = (bf16[128,768]{1,0:T(8,128)(2,1)S(1)}, bf16[128,768]{1,0:T(8,128)(2,1)S(1)}, u32[]{:S(2)}, u32[]{:S(2)}) collective-permute-start(bf16[128,768]{1,0:T(8,128)(2,1)S(1)} %pad_maximum_fusion.5), channel_id=1, source_target_pairs={{0,3},{1,2},{2,1},{3,0},{4,7},{5,6},{6,5},{7,4},{8,11},{9,10},{10,... | collective-permute-start | bytes 589832 | tf_op jit(solution)/shard_map/ppermute | solution.py:44
Sparse Core Ops, SparseCore 0:
  10.7 69.8 all-gather.3
  124.9 42.2 all-gather.5

commit v8 on v6

--- a/solution.py
+++ b/solution.py
@@ -69,17 +69,21 @@
     weight = stack[:, :, :block].reshape(-1, width)
     rights = lax.all_gather(stack[:, :, block:], "y", axis=0, tiled=False)
 
-    around = [features] + [move(features, "y", -j) for j in (1, 2, 3)]
-
     left_cols = lax.dynamic_slice(member_left, (0, (x * 4 + zl) * cols), (members, cols)).astype(f32)
     payload = jnp.concatenate([left_cols, probe[None, :]], axis=0)
     mine = jnp.where(first, payload[:, :block], payload[:, block:])
     other = jnp.where(first, left_cols[:, block:], left_cols[:, :block])
     mine = lax.ppermute(mine, AXES, swapped(0))
     other = lax.ppermute(other, AXES, swapped(1))
+    mine, other = lax.optimization_barrier((mine, other))
 
     direction = jnp.sum(down_weight.astype(f32) * mine[members][:, None], axis=0)
-    direction = lax.psum(lax.psum(direction, ("y", "c")), "zh")
+    direction = lax.psum(direction, ("y", "c"))
+
+    features, direction = lax.optimization_barrier((features, direction))
+    around = [features] + [move(features, "y", -j) for j in (1, 2, 3)]
+
+    direction = lax.psum(direction, "zh")
     wide = features.astype(f32)
     along = jnp.sum(wide * direction[None, :], axis=1)
     inner = jnp.sum(
@@ -91,7 +95,8 @@
     inner = spread * inner
     dots = along + inner * jnp.repeat(left_dot, tokens)
     scale = 0.5 / jnp.sqrt(f32(D))
-    own_score = jnp.mean(jnp.tanh(scale * dots).reshape(members, tokens), axis=1)
+    score = jnp.mean(jnp.tanh(scale * dots).reshape(members, tokens), axis=1)
+    score = lax.psum(placed(score, here, 8), ("y", "c"))
 
     many = 4 * rows
     mine = mine[:members]
@@ -106,11 +111,11 @@
         one = lax.dynamic_index_in_dim(part, lax.rem(x + k, 4), 0, keepdims=False)
         one = jnp.concatenate([one, lefts], axis=0)
         parts.append(one if k == 0 else move(one, "x", k))
-    own_score, parts[1] = lax.optimization_barrier((own_score, parts[1]))
-    score = lax.psum(placed(own_score, here, 8), ("y", "c"))
+    score, parts[1] = lax.optimization_barrier((score, parts[1]))
+    score = lax.psum(placed(score, zh, 4), "zh")
     total = sum(p[:cols].astype(f32) for p in parts).astype(bf16)
     lefts = jnp.stack([parts[k][cols:] for k in (0, 3, 2, 1)])
-    lefts, total = lax.optimization_barrier((lefts, total))
+    lefts, total, score = lax.optimization_barrier((lefts, total, score))
     lefts = joined(jnp.roll(lefts, x, axis=0).reshape(-1, many), "zl", zl)
 
     total = total.T.reshape(4, rows, cols)
@@ -118,8 +123,6 @@
     for k in range(4):
         one = lax.dynamic_index_in_dim(total, lax.rem(zl + k + 4 - y, 4), 0, keepdims=False)
         parts.append(one if k == 0 else move(one, "zl", k))
-    score, parts[1] = lax.optimization_barrier((score, parts[1]))
-    score = lax.psum(placed(score, zh, 4), "zh")
     total = sum(p.astype(f32) for p in parts).astype(bf16)
 
     total = lax.ppermute(total, ("y", "zl"), turned()).astype(f32)

time: 221 us -> 212 us (0.959)
  the two profiles are of different devices: /device:TPU:24 before, /device:TPU:32 now
where the time goes in v8:
time: 212 us; the launch traced here: 211 us
  blocking collectives  112 us (53%)
  starting transfers between devices  44.6 us (21%)
  waiting for transfers between devices  16 us (8%)
  between operations  14.6 us (7%)
  other arithmetic  8.95 us (4%)
  local copies, waits for them, and re-layouts  8.29 us (4%)
  matrix products  6.73 us (3%)
    psum x1, blocking collectives, per_device(): direction = lax.psum(direction, 'zh')  31.1 us
    ppermute x9, starting transfers between devices, move(): return lax.ppermute(value, axis, ring(step))  28 us
    psum x1, blocking collectives, per_device(): lax.psum(jnp.concatenate([along, inner, left_dot]), 'x')  25.3 us
    psum x1, blocking collectives, per_device(): direction = lax.psum(direction, ('y', 'c'))  20.1 us
    psum x1, blocking collectives, per_device(): score = lax.psum(placed(score, zh, 4), 'zh')  13.2 us
    psum x1, blocking collectives, per_device(): score = lax.psum(placed(score, here, 8), ('y', 'c'))  13.1 us
    psum x1, blocking collectives, per_device(): lax.psum(lax.psum(jnp.concatenate([along, inner, left_dot]), 'x'), 'zl')  9.15 us
    ppermute x2, starting transfers between devices, joined(): got = lax.ppermute(value, axis, pairs(step))  8.48 us
  transfers between devices with their start and end apart: 16, of which 4 were waited for; matrix products, arithmetic and copies ran while one was open for 7% of the time, Pallas kernels for 0%

profile of v8, /device:TPU:32, one launch (start us, length us, event | category | flops | bytes accessed | tf_op | source)
XLA Modules:
  0.0 211.2 jit_solution(4704899892928657949)
XLA Ops:
  7.2 1.8 pad_maximum_fusion.3
  9.1 0.9 dynamic-slice_convert_fusion
  10.1 2.5 %collective-permute-start.1 = (bf16[32,160]{1,0:T(8,128)(2,1)S(1)}, bf16[32,160]{1,0:T(8,128)(2,1)S(1)}, u32[]{:S(2)}, u32[]{:S(2)}) collective-permute-start(bf16[32,160]{1,0:T(8,128)(2,1)S(1)} %slice_select_fusion), channel_id=1, source_target_pairs={{0,16},{1,48},{2,80},{3,112},{4,144},{5,176},{6,208},{7,240},{8,27... | collective-permute-start | bytes 30728 | tf_op jit(solution)/shard_map/ppermute | solution.py:77
  12.5 0.7 broadcast_in_dim.14
  13.3 3.7 %collective-permute-start = (f32[33,160]{1,0:T(8,128)S(1)}, f32[33,160]{1,0:T(8,128)S(1)}, u32[]{:S(2)}, u32[]{:S(2)}) collective-permute-start(f32[33,160]{1,0:T(8,128)S(1)} %fusion.20), channel_id=1, source_target_pairs={{0,0},{1,32},{2,64},{3,96},{4,128},{5,160},{6,192},{7,224},{8,256}... | collective-permute-start | bytes 63368 | tf_op jit(solution)/shard_map/ppermute | solution.py:76
  17.0 1.0 multiply_reduce_fusion.1
  18.2 0.1 mul.116
  18.3 0.1 mul.117
  18.5 1.8 collective-permute-done
  20.2 0.1 multiply_reduce_fusion
  20.4 20.1 %psum.42 = f32[1024]{0:T(1024)S(1)} all-reduce(f32[1024]{0:T(1024)S(1)} %multiply_reduce_fusion), channel_id=1, replica_groups=mesh['zh'=4,'y'=4,'c'=2,'x'=4,'zl'=4] {'y','c'}, use_global_device_ids=true, to_apply=%region_1.2 | all-reduce | flops 1024 | bytes 8192 | tf_op jit(solution)/shard_map/psum | solution.py:81
  40.5 1.9 collective-permute-start.4
  42.4 1.9 collective-permute-start.3
  44.3 5.1 %collective-permute-start.2 = (bf16[192,1024]{1,0:T(8,128)(2,1)S(1)}, bf16[192,1024]{1,0:T(8,128)(2,1)}, u32[]{:S(2)}, u32[]{:S(2)}) collective-permute-start(bf16[192,1024]{1,0:T(8,128)(2,1)S(1)} %copy-done.1), channel_id=1, source_target_pairs={{0,96},{32,0},{64,32},{96,64},{1,97},{33,1},{65,33},{97,65},{2,98}... | collective-permute-start | bytes 1179656 | tf_op jit(solution)/shard_map/ppermute | solution.py:35
  49.5 31.1 %psum.43 = f32[1024]{0:T(1024)S(1)} all-reduce(f32[1024]{0:T(1024)S(1)} %psum.42), channel_id=1, replica_groups=mesh['zh'=4,'y'=4,'c'=2,'x'=4,'zl'=4] {'zh'}, use_global_device_ids=true, to_apply=%region_2.3 | all-reduce | flops 1024 | bytes 8192 | tf_op jit(solution)/shard_map/psum | solution.py:86
  80.5 0.2 fusion.10
  81.0 25.3 %psum.44 = f32[416]{0:T(512)S(1)} all-reduce(f32[416]{0:T(512)S(1)} %pad_maximum_fusion.8), channel_id=1, replica_groups=mesh['zh'=4,'y'=4,'c'=2,'x'=4,'zl'=4] {'x'}, use_global_device_ids=true, to_apply=%region_6.7 | all-reduce | flops 416 | bytes 3328 | tf_op jit(solution)/shard_map/psum | solution.py:93
  106.3 9.1 %psum.45 = f32[416]{0:T(512)S(1)} all-reduce(f32[416]{0:T(512)S(1)} %psum.44), channel_id=1, replica_groups=mesh['zh'=4,'y'=4,'c'=2,'x'=4,'zl'=4] {'zl'}, use_global_device_ids=true, to_apply=%region_7.8 | all-reduce | flops 416 | bytes 3328 | tf_op jit(solution)/shard_map/psum | solution.py:93
  115.8 2.1 %slice.64 = bf16[4,2,160,1024]{3,2,1,0:T(8,128)(2,1)S(1)} slice(bf16[4,2,192,1024]{3,2,1,0:T(8,128)(2,1)} %bitcast.37), slice={[0:4], [0:2], [0:160], [0:1024]} | slice | bytes 5242880 | tf_op jit(solution)/shard_map/slice | solution.py:69
  118.0 3.5 %convolution_convert_fusion = bf16[1280,768]{1,0:T(8,128)(2,1)S(1)} fusion(bf16[1280,1024]{1,0:T(8,128)(2,1)S(1)} %bitcast.39, bf16[192,1024]{1,0:T(8,128)(2,1)} %collective-permute-done.4, bf16[192,1024]{1,0:T(8,128)(2,1)} %collective-permute-done.3, bf16[192,1024]{1,0:T(8,128)(2,1)} %collective-permute-done.2, bf16[192,1024]{1,0:T(8,128)(2,1)S(1)} %copy-done.1), kind=kOutput, calls=%fused_computation.2 | convolution fusion | flops 2020540416 | bytes 6160384 | tf_op jit(solution)/shard_map/dot_general | solution.py:105
  121.5 0.1 dynamic-slice_bitcast_fusion.2
  121.6 1.2 pad_maximum_fusion.2
  122.8 1.9 collective-permute-start.7
  124.7 5.1 %collective-permute-start.5 = (bf16[336,768]{1,0:T(8,128)(2,1)}, bf16[336,768]{1,0:T(8,128)(2,1)}, u32[]{:S(2)}, u32[]{:S(2)}) collective-permute-start(bf16[336,768]{1,0:T(8,128)(2,1)} %get-tuple-element.32), channel_id=1, source_target_pairs={{0,12},{4,0},{8,4},{12,8},{1,13},{5,1},{9,5},{13,9},{2,14},{6,2},{... | collective-permute-start | bytes 1548296 | tf_op jit(solution)/shard_map/ppermute | solution.py:35
  129.8 0.2 tanh_reduce_fusion
  130.0 1.9 slice.70
  131.9 1.9 collective-permute-start.6
  133.9 0.1 multiply_dynamic-update-slice_fusion
  134.1 13.1 %psum.46 = f32[256]{0:T(256)S(1)} all-reduce(f32[256]{0:T(256)S(1)} %multiply_dynamic-update-slice_fusion), channel_id=1, replica_groups=mesh['zh'=4,'y'=4,'c'=2,'x'=4,'zl'=4] {'y','c'}, use_global_device_ids=true, to_apply=%region_9.10 | all-reduce | flops 256 | bytes 2048 | tf_op jit(solution)/shard_map/psum | solution.py:99
  147.2 0.2 dynamic_update_slice.7
  147.4 13.2 %psum.47 = f32[1024]{0:T(1024)S(1)} all-reduce(f32[1024]{0:T(1024)S(1)} %dynamic_update_slice.7), channel_id=1, replica_groups=mesh['zh'=4,'y'=4,'c'=2,'x'=4,'zl'=4] {'zh'}, use_global_device_ids=true, to_apply=%region_10.11 | all-reduce | flops 1024 | bytes 8192 | tf_op jit(solution)/shard_map/psum | solution.py:115
  160.7 0.7 slice_bitcast_fusion.1
  161.4 0.7 slice_bitcast_fusion
  162.2 1.4 fusion.9
  163.6 0.3 copy.15
  164.0 2.0 collective-permute-start.8
  166.0 3.9 %collective-permute-start.10 = (bf16[192,320]{1,0:T(8,128)(2,1)S(1)}, bf16[192,320]{1,0:T(8,128)(2,1)S(1)}, u32[]{:S(2)}, u32[]{:S(2)}) collective-permute-start(bf16[192,320]{1,0:T(8,128)(2,1)S(1)} %get-tuple-element.26), channel_id=1, source_target_pairs={{0,3},{1,0},{2,1},{3,2},{4,7},{5,4},{6,5},{7,6},{8,11},{9,8},{10,9... | collective-permute-start | bytes 368648 | tf_op jit(solution)/shard_map/ppermute | solution.py:35
  169.9 4.2 %collective-permute-start.9 = (bf16[192,320]{1,0:T(8,128)(2,1)S(1)}, bf16[192,320]{1,0:T(8,128)(2,1)S(1)}, u32[]{:S(2)}, u32[]{:S(2)}) collective-permute-start(bf16[192,320]{1,0:T(8,128)(2,1)S(1)} %get-tuple-element.27), channel_id=1, source_target_pairs={{0,2},{1,3},{2,0},{3,1},{4,6},{5,7},{6,4},{7,5},{8,10},{9,11},{10,... | collective-permute-start | bytes 368648 | tf_op jit(solution)/shard_map/ppermute | solution.py:35
  174.0 0.7 select_reduce_fusion
  174.9 3.4 %collective-permute-start.12 = (bf16[64,768]{1,0:T(8,128)(2,1)S(1)}, bf16[64,768]{1,0:T(8,128)(2,1)S(1)}, u32[]{:S(2)}, u32[]{:S(2)}) collective-permute-start(bf16[64,768]{1,0:T(8,128)(2,1)S(1)} %bitcast.45), channel_id=1, source_target_pairs={{0,1},{1,0},{2,3},{3,2},{4,5},{5,4},{6,7},{7,6},{8,9},{9,8},{10,11... | collective-permute-start | bytes 294920 | tf_op jit(solution)/shard_map/ppermute | solution.py:44
  178.3 2.3 %collective-permute-done.9 = bf16[192,320]{1,0:T(8,128)(2,1)S(1)} collective-permute-done((bf16[192,320]{1,0:T(8,128)(2,1)S(1)}, bf16[192,320]{1,0:T(8,128)(2,1)S(1)}, u32[]{:S(2)}, u32[]{:S(2)}) %collective-permute-start.9) | collective-permute-done | bytes 122912 | tf_op jit(solution)/shard_map/ppermute | solution.py:35
  180.7 1.9 collective-permute-start.11
  182.7 5.1 %collective-permute-start.13 = (bf16[128,768]{1,0:T(8,128)(2,1)S(1)}, bf16[128,768]{1,0:T(8,128)(2,1)S(1)}, u32[]{:S(2)}, u32[]{:S(2)}) collective-permute-start(bf16[128,768]{1,0:T(8,128)(2,1)S(1)} %pad_maximum_fusion.5), channel_id=1, source_target_pairs={{0,3},{1,2},{2,1},{3,0},{4,7},{5,6},{6,5},{7,4},{8,11},{9,10},{10,... | collective-permute-start | bytes 589832 | tf_op jit(solution)/shard_map/ppermute | solution.py:44
  187.8 8.1 %collective-permute-done.11 = bf16[192,320]{1,0:T(8,128)(2,1)S(1)} collective-permute-done((bf16[192,320]{1,0:T(8,128)(2,1)S(1)}, bf16[192,320]{1,0:T(8,128)(2,1)S(1)}, u32[]{:S(2)}, u32[]{:S(2)}) %collective-permute-start.11) | collective-permute-done | bytes 122912 | tf_op jit(solution)/shard_map/ppermute | solution.py:128
  196.0 0.8 add_convert_fusion
  196.7 3.7 %collective-permute-done.13 = bf16[128,768]{1,0:T(8,128)(2,1)S(1)} collective-permute-done((bf16[128,768]{1,0:T(8,128)(2,1)S(1)}, bf16[128,768]{1,0:T(8,128)(2,1)S(1)}, u32[]{:S(2)}, u32[]{:S(2)}) %collective-permute-start.13) | collective-permute-done | bytes 196640 | tf_op jit(solution)/shard_map/ppermute | solution.py:44
  200.5 0.5 reshape.68
  201.1 3.3 %convolution_multiply_fusion = f32[160,1024]{1,0:T(8,128)} fusion(bf16[1024,1024]{1,0:T(8,128)(2,1)} %bitcast.48, bf16[1024,192]{1,0:T(8,128)(2,1)S(1)} %reshape.68, f32[1024]{0:T(1024)S(1)} %mul.137), kind=kOutput, calls=%fused_computation.10 | convolution fusion | flops 336199680 | bytes 3149824 | tf_op jit(solution)/shard_map/dot_general | solution.py:138
  (56 shorter events, 1.5 us)
Async XLA Ops:
  7.2 11.0 %copy-start.2 = (bf16[32,1024]{1,0:T(8,128)(2,1)S(1)}, bf16[32,1024]{1,0:T(8,128)(2,1)}, u32[]{:S(2)}) copy-start(bf16[32,1024]{1,0:T(8,128)(2,1)} %param.10) | copy-start | bytes 196612
  7.2 108.6 %all-gather.4.cloned.1.call-start = ((), (), s32[]{:S(2)}) async-start(), calls=%async_computation | async-start | bytes 3538944 | tf_op jit(solution)/shard_map/all_gather | solution.py:68
  9.0 11.2 %copy-start = (bf16[160,1024]{1,0:T(8,128)(2,1)S(1)}, bf16[160,1024]{1,0:T(8,128)(2,1)}, u32[]{:S(2)}) copy-start(bf16[160,1024]{1,0:T(8,128)(2,1)} %param.8) | copy-start | bytes 983044
  9.0 31.5 %copy-start.1 = (bf16[192,1024]{1,0:T(8,128)(2,1)S(1)}, bf16[192,1024]{1,0:T(8,128)(2,1)}, u32[]{:S(2)}) copy-start(bf16[192,1024]{1,0:T(8,128)(2,1)} %param.7) | copy-start | bytes 1179652
  9.0 192.0 %all-gather.6.cloned.1.call-start = ((), (), s32[]{:S(2)}) async-start(), calls=%async_computation.1 | async-start | bytes 2621440 | tf_op jit(solution)/shard_map/all_gather | solution.py:70
  10.1 8.4 %collective-permute-start.1 = (bf16[32,160]{1,0:T(8,128)(2,1)S(1)}, bf16[32,160]{1,0:T(8,128)(2,1)S(1)}, u32[]{:S(2)}, u32[]{:S(2)}) collective-permute-start(bf16[32,160]{1,0:T(8,128)(2,1)S(1)} %slice_select_fusion), channel_id=1, source_target_pairs={{0,16},{1,48},{2,80},{3,112},{4,144},{5,176},{6,208},{7,240},{8,27... | collective-permute-start | bytes 30728 | tf_op jit(solution)/shard_map/ppermute | solution.py:77
  13.3 6.9 %collective-permute-start = (f32[33,160]{1,0:T(8,128)S(1)}, f32[33,160]{1,0:T(8,128)S(1)}, u32[]{:S(2)}, u32[]{:S(2)}) collective-permute-start(f32[33,160]{1,0:T(8,128)S(1)} %fusion.20), channel_id=1, source_target_pairs={{0,0},{1,32},{2,64},{3,96},{4,128},{5,160},{6,192},{7,224},{8,256}... | collective-permute-start | bytes 63368 | tf_op jit(solution)/shard_map/ppermute | solution.py:76
  40.5 77.5 %collective-permute-start.4 = (bf16[192,1024]{1,0:T(8,128)(2,1)S(1)}, bf16[192,1024]{1,0:T(8,128)(2,1)}, u32[]{:S(2)}, u32[]{:S(2)}) collective-permute-start(bf16[192,1024]{1,0:T(8,128)(2,1)S(1)} %copy-done.1), channel_id=1, source_target_pairs={{0,32},{32,64},{64,96},{96,0},{1,33},{33,65},{65,97},{97,1},{2,34}... | collective-permute-start | bytes 1179656 | tf_op jit(solution)/shard_map/ppermute | solution.py:35
  42.4 75.6 %collective-permute-start.3 = (bf16[192,1024]{1,0:T(8,128)(2,1)S(1)}, bf16[192,1024]{1,0:T(8,128)(2,1)}, u32[]{:S(2)}, u32[]{:S(2)}) collective-permute-start(bf16[192,1024]{1,0:T(8,128)(2,1)S(1)} %copy-done.1), channel_id=1, source_target_pairs={{0,64},{32,96},{64,0},{96,32},{1,65},{33,97},{65,1},{97,33},{2,66}... | collective-permute-start | bytes 1179656 | tf_op jit(solution)/shard_map/ppermute | solution.py:35
  44.3 73.6 %collective-permute-start.2 = (bf16[192,1024]{1,0:T(8,128)(2,1)S(1)}, bf16[192,1024]{1,0:T(8,128)(2,1)}, u32[]{:S(2)}, u32[]{:S(2)}) collective-permute-start(bf16[192,1024]{1,0:T(8,128)(2,1)S(1)} %copy-done.1), channel_id=1, source_target_pairs={{0,96},{32,0},{64,32},{96,64},{1,97},{33,1},{65,33},{97,65},{2,98}... | collective-permute-start | bytes 1179656 | tf_op jit(solution)/shard_map/ppermute | solution.py:35
  122.8 24.4 %collective-permute-start.7 = (bf16[336,768]{1,0:T(8,128)(2,1)}, bf16[336,768]{1,0:T(8,128)(2,1)S(1)}, u32[]{:S(2)}, u32[]{:S(2)}) collective-permute-start(bf16[336,768]{1,0:T(8,128)(2,1)} %get-tuple-element.34), channel_id=1, source_target_pairs={{0,4},{4,8},{8,12},{12,0},{1,5},{5,9},{9,13},{13,1},{2,6},{6,10},{... | collective-permute-start | bytes 1548296 | tf_op jit(solution)/shard_map/ppermute | solution.py:35
  124.7 36.0 %collective-permute-start.5 = (bf16[336,768]{1,0:T(8,128)(2,1)}, bf16[336,768]{1,0:T(8,128)(2,1)}, u32[]{:S(2)}, u32[]{:S(2)}) collective-permute-start(bf16[336,768]{1,0:T(8,128)(2,1)} %get-tuple-element.32), channel_id=1, source_target_pairs={{0,12},{4,0},{8,4},{12,8},{1,13},{5,1},{9,5},{13,9},{2,14},{6,2},{... | collective-permute-start | bytes 1548296 | tf_op jit(solution)/shard_map/ppermute | solution.py:35
  131.9 42.1 %copy-start.3 = (s32[1024]{0:T(1024)S(1)}, s32[1024]{0:T(1024)}, u32[]{:S(2)}) copy-start(s32[1024]{0:T(1024)} %param.13) | copy-start | bytes 12292
  131.9 42.8 %copy-start.4 = (f32[1024]{0:T(1024)S(1)}, f32[1024]{0:T(1024)}, u32[]{:S(2)}) copy-start(f32[1024]{0:T(1024)} %param.12) | copy-start | bytes 12292
  131.9 29.5 %collective-permute-start.6 = (bf16[336,768]{1,0:T(8,128)(2,1)}, bf16[336,768]{1,0:T(8,128)(2,1)}, u32[]{:S(2)}, u32[]{:S(2)}) collective-permute-start(bf16[336,768]{1,0:T(8,128)(2,1)} %get-tuple-element.33), channel_id=1, source_target_pairs={{0,8},{4,12},{8,0},{12,4},{1,9},{5,13},{9,1},{13,5},{2,10},{6,14},... | collective-permute-start | bytes 1548296 | tf_op jit(solution)/shard_map/ppermute | solution.py:35
  164.0 14.3 %collective-permute-start.8 = (bf16[192,320]{1,0:T(8,128)(2,1)S(1)}, bf16[192,320]{1,0:T(8,128)(2,1)S(1)}, u32[]{:S(2)}, u32[]{:S(2)}) collective-permute-start(bf16[192,320]{1,0:T(8,128)(2,1)S(1)} %get-tuple-element.25), channel_id=1, source_target_pairs={{0,1},{1,2},{2,3},{3,0},{4,5},{5,6},{6,7},{7,4},{8,9},{9,10},{10,1... | collective-permute-start | bytes 368648 | tf_op jit(solution)/shard_map/ppermute | solution.py:35
  166.0 12.3 %collective-permute-start.10 = (bf16[192,320]{1,0:T(8,128)(2,1)S(1)}, bf16[192,320]{1,0:T(8,128)(2,1)S(1)}, u32[]{:S(2)}, u32[]{:S(2)}) collective-permute-start(bf16[192,320]{1,0:T(8,128)(2,1)S(1)} %get-tuple-element.26), channel_id=1, source_target_pairs={{0,3},{1,0},{2,1},{3,2},{4,7},{5,4},{6,5},{7,6},{8,11},{9,8},{10,9... | collective-permute-start | bytes 368648 | tf_op jit(solution)/shard_map/ppermute | solution.py:35
  169.9 10.8 %collective-permute-start.9 = (bf16[192,320]{1,0:T(8,128)(2,1)S(1)}, bf16[192,320]{1,0:T(8,128)(2,1)S(1)}, u32[]{:S(2)}, u32[]{:S(2)}) collective-permute-start(bf16[192,320]{1,0:T(8,128)(2,1)S(1)} %get-tuple-element.27), channel_id=1, source_target_pairs={{0,2},{1,3},{2,0},{3,1},{4,6},{5,7},{6,4},{7,5},{8,10},{9,11},{10,... | collective-permute-start | bytes 368648 | tf_op jit(solution)/shard_map/ppermute | solution.py:35
  174.9 7.7 %collective-permute-start.12 = (bf16[64,768]{1,0:T(8,128)(2,1)S(1)}, bf16[64,768]{1,0:T(8,128)(2,1)S(1)}, u32[]{:S(2)}, u32[]{:S(2)}) collective-permute-start(bf16[64,768]{1,0:T(8,128)(2,1)S(1)} %bitcast.45), channel_id=1, source_target_pairs={{0,1},{1,0},{2,3},{3,2},{4,5},{5,4},{6,7},{7,6},{8,9},{9,8},{10,11... | collective-permute-start | bytes 294920 | tf_op jit(solution)/shard_map/ppermute | solution.py:44
  180.7 15.3 %collective-permute-start.11 = (bf16[192,320]{1,0:T(8,128)(2,1)S(1)}, bf16[192,320]{1,0:T(8,128)(2,1)S(1)}, u32[]{:S(2)}, u32[]{:S(2)}) collective-permute-start(bf16[192,320]{1,0:T(8,128)(2,1)S(1)} %fusion.16), channel_id=1, source_target_pairs={{0,0},{1,32},{2,64},{3,96},{32,1},{33,33},{34,65},{35,97},{64,2},{... | collective-permute-start | bytes 368648 | tf_op jit(solution)/shard_map/ppermute | solution.py:128
  182.7 17.7 %collective-permute-start.13 = (bf16[128,768]{1,0:T(8,128)(2,1)S(1)}, bf16[128,768]{1,0:T(8,128)(2,1)S(1)}, u32[]{:S(2)}, u32[]{:S(2)}) collective-permute-start(bf16[128,768]{1,0:T(8,128)(2,1)S(1)} %pad_maximum_fusion.5), channel_id=1, source_target_pairs={{0,3},{1,2},{2,1},{3,0},{4,7},{5,6},{6,5},{7,4},{8,11},{9,10},{10,... | collective-permute-start | bytes 589832 | tf_op jit(solution)/shard_map/ppermute | solution.py:44
Sparse Core Ops, SparseCore 0:
  10.7 72.8 all-gather.3
  132.1 31.5 all-gather.5

commit v9 on v6

v9 whole, which is shorter than its diff:
```python
import jax
import jax.numpy as jnp
from jax import lax
from jax.sharding import Mesh, PartitionSpec as P

D = 5120
FF = 16384
AXES = ("zh", "y", "c", "x", "zl")
SIZES = (4, 4, 2, 4, 4)


def place(*index):
    at = 0
    for i, size in zip(index, SIZES):
        at = at * size + i
    return at


def ring(step):
    return [(i, (i + step) % 4) for i in range(4)]


def swapped():
    return [
        (place(zh, y, c, x, zl), place(x, zl, c, zh, y))
        for zh in range(4) for y in range(4) for c in range(2) for x in range(4) for zl in range(4)
    ]


def turned():
    return [(y * 4 + zl, zl * 4 + y) for y in range(4) for zl in range(4)]


def move(value, axis, step):
    return lax.ppermute(value, axis, ring(step))


def pairs(step):
    return [(i, i ^ step) for i in range(4)]


def joined(value, axis, index):
    for step, later in ((1, index % 2 == 1), (3, index >= 2)):
        got = lax.ppermute(value, axis, pairs(step))
        value = jnp.concatenate([jnp.where(later, got, value), jnp.where(later, value, got)], axis=0)
    return value


def in_three(value):
    terms = []
    for _ in range(3):
        term = lax.reduce_precision(value, 8, 7)
        terms.append(term.astype(jnp.bfloat16))
        value = value - term
    return jnp.stack(terms)


def placed(value, index, count):
    size = value.shape[0]
    return lax.dynamic_update_slice(jnp.zeros((size * count,), value.dtype), value, (index * size,))


def per_device(features, down_weight, member_left, member_right, probe, payoff, opponent):
    f32, bf16 = jnp.float32, jnp.bfloat16
    rows, width = features.shape
    members = member_right.shape[0]
    tokens = rows // members
    population = payoff.shape[0]
    block = down_weight.shape[0]
    cols = probe.shape[0]
    spread = 1.0 / jnp.sqrt(f32(FF))
    zh, y, c, x, zl = (lax.axis_index(a) for a in AXES)
    first = c == 0
    many = 4 * rows

    weight = lax.all_gather(down_weight, ("zh", "c"), axis=0, tiled=True)

    around = [features] + [move(features, "y", -j) for j in (1, 2, 3)]
    around = jnp.concatenate(around, axis=0)

    cut = members // 2
    before = move(member_right, "zh", 1)
    after = move(member_right, "zh", -1)
    far = [move(before[:cut], "zh", 1), move(after[cut:], "zh", -1)]
    rights = jnp.concatenate([member_right, after] + far + [before], axis=0)
    rights = jnp.roll(rights.reshape(4, members, width), zh, axis=0)
    rights = lax.all_gather(rights, ("y", "c"), axis=0, tiled=False)

    probes = lax.psum(placed(probe, x, 4), "x")
    probes = lax.ppermute(probes, ("y", "zl"), turned())

    left_cols = lax.dynamic_slice(member_left, (0, (x * 4 + zl) * cols), (members, cols))
    lefts = lax.ppermute(left_cols, AXES, swapped())
    mine = jnp.where(first, lefts[:, :block], lefts[:, block:])
    other = jnp.where(first, lefts[:, block:], lefts[:, :block])
    other = lax.ppermute(other, "c", [(0, 1), (1, 0)])
    lefts = jnp.where(first, jnp.concatenate([mine, other], 0), jnp.concatenate([other, mine], 0))
    lefts = jnp.pad(lefts, ((0, 0), (0, 192 - block))).reshape(-1, many)
    left_cols = left_cols.astype(f32)

    part = lax.dot_general(
        weight, around, (((1,), (1,)), ((), ())), preferred_element_type=f32
    ).astype(bf16).reshape(4, cols, many)
    parts = []
    for k in range(4):
        one = lax.dynamic_index_in_dim(part, lax.rem(x + k, 4), 0, keepdims=False)
        one = jnp.concatenate([one, lefts], axis=0)
        parts.append(one if k == 0 else move(one, "x", k))

    direction = lax.dot_general(
        in_three(probes), weight, (((1,), (0,)), ((), ())), preferred_element_type=f32
    ).sum(0)
    along = lax.dot_general(
        in_three(direction), around, (((1,), (1,)), ((), ())), preferred_element_type=f32
    ).sum(0)
    along = jnp.roll(along.reshape(4, rows), y, axis=0).reshape(many)
    inner = jnp.sum(
        features.astype(f32).reshape(members, tokens, width) * member_right.astype(f32)[:, None, :],
        axis=2,
    ).reshape(rows)
    left_dot = jnp.sum(left_cols * probe[None, :], axis=1)
    sums = jnp.concatenate([along, placed(inner, y, 4), placed(left_dot, y, 4)])
    sums, parts[1] = lax.optimization_barrier((sums, parts[1]))
    sums = lax.psum(lax.psum(lax.psum(sums, "y"), "x"), "zl")
    along, inner, left_dot = jnp.split(sums, [many, 2 * many])
    inner = spread * inner
    dots = along + inner * jnp.repeat(left_dot, tokens)
    scale = 0.5 / jnp.sqrt(f32(D))
    score = jnp.mean(jnp.tanh(scale * dots).reshape(4, members, tokens), axis=2)
    score = jnp.stack([jnp.where(first, score, 0.0), jnp.where(first, 0.0, score)], axis=1)

    total = sum(p[:cols].astype(f32) for p in parts).astype(bf16)
    lefts = jnp.stack([parts[k][cols:] for k in (0, 3, 2, 1)])
    lefts, total = lax.optimization_barrier((lefts, total))
    lefts = joined(jnp.roll(lefts, x, axis=0).reshape(-1, many), "zl", zl)

    total = total.T.reshape(4, rows, cols)
    parts = []
    for k in range(4):
        one = lax.dynamic_index_in_dim(total, lax.rem(zl + k + 4 - y, 4), 0, keepdims=False)
        parts.append(one if k == 0 else move(one, "zl", k))
    score, parts[1] = lax.optimization_barrier((score, parts[1]))
    score = lax.psum(score.reshape(-1), "c")
    score = lax.psum(placed(score, zh, 4), "zh")
    total = sum(p.astype(f32) for p in parts).astype(bf16)

    total = lax.ppermute(total, ("y", "zl"), turned()).astype(f32)
    inner = lax.dynamic_slice(inner, (y * rows,), (rows,))
    lowrank = inner.reshape(members, tokens)[:, :, None] * left_cols[:, None, :]
    mixed = (total + lowrank.reshape(rows, cols)).astype(bf16)

    labels = jnp.arange(population, dtype=jnp.int32)
    rival = jnp.sum(jnp.where(opponent[:, None] == labels[None, :], score[None, :], 0.0), axis=1)
    fitness = payoff * (score - rival)
    fitness = fitness.reshape(4, 4, 2, members).transpose(1, 2, 0, 3)
    scaled = lefts.reshape(4, 4, 2, members, 192)[..., :block].transpose(0, 2, 1, 3, 4).astype(f32)
    scaled = (fitness[..., None] * scaled).astype(bf16).reshape(population, block)
    term = lax.dot_general(
        scaled, rights.reshape(population, width), (((0,), (0,)), ((), ())),
        preferred_element_type=f32,
    )
    return mixed, term / jnp.sqrt(f32(population))


def solution(mesh):
    fine = Mesh(mesh.devices.reshape(SIZES), AXES)
    member, tensor = ("zh", "y", "c"), ("x", "zl")
    in_specs = (
        P(member, tensor), P(member, tensor), P(member, None), P(member, tensor), P(tensor), P(), P(),
    )
    out_specs = (P(member, tensor), P(member, tensor))
    return jax.shard_map(
        per_device, mesh=fine, in_specs=in_specs, out_specs=out_specs, check_vma=False
    )
```

time: 221 us -> 236 us (1.068); the launches traced: 216 us -> 234 us
  blocking collectives: 109 us -> 56.5 us
  starting transfers between devices: 49.4 us -> 84.4 us
  waiting for transfers between devices: 18.7 us -> 43.9 us
  local copies, waits for them, and re-layouts: 8.54 us -> 15.4 us
  matrix products: 6.73 us -> 9.26 us
    psum x5, blocking collectives: 94.1 us -> 42.8 us  [the longest x3 27.8 us: per_device(): sums = lax.psum(lax.psum(lax.psum(sums, 'y'), 'x'), 'zl')]
    ppermute x9 -> x13, starting transfers between devices: 30.9 us -> 61.3 us  [move(): return lax.ppermute(value, axis, ring(step))]
    ppermute x9 -> x13, waiting for transfers between devices: 13.4 us -> 28.4 us  [move(): return lax.ppermute(value, axis, ring(step))]
    ppermute x2, waiting for transfers between devices: 0.01 us -> 5.91 us  [joined(): got = lax.ppermute(value, axis, pairs(step))]
    ppermute x2 -> x3, waiting for transfers between devices: 5.21 us -> 8.78 us  [the longest x1 8.28 us: per_device(): probes = lax.ppermute(probes, ('y', 'zl'), turned())]
    ppermute x2 -> x3, starting transfers between devices: 7.46 us -> 10.9 us  [the longest x1 5.29 us: per_device(): probes = lax.ppermute(probes, ('y', 'zl'), turned())]
    slice x4 -> x2, local copies, waits for them, and re-layouts: 4.02 us -> 0.77 us  [per_device(): far = [move(before[:cut], 'zh', 1), move(after[cut:], 'zh', -1)]]
    unnamed x10 -> x29, local copies, waits for them, and re-layouts: 0.02 us -> 3.2 us
  transfers between devices with their start and end apart: 16 -> 21, of which waited for: 3 -> 7; matrix products, arithmetic and copies ran while one was open for 7% -> 13% of each run, Pallas kernels for 0% -> 0%
where the time goes in v9:
time: 236 us; the launch traced here: 234 us
  starting transfers between devices  84.4 us (36%)
  blocking collectives  56.5 us (24%)
  waiting for transfers between devices  43.9 us (19%)
  local copies, waits for them, and re-layouts  15.4 us (7%)
  between operations  14.8 us (6%)
  other arithmetic  9.58 us (4%)
  matrix products  9.26 us (4%)
    ppermute x13, starting transfers between devices, move(): return lax.ppermute(value, axis, ring(step))  61.3 us
    ppermute x13, waiting for transfers between devices, move(): return lax.ppermute(value, axis, ring(step))  28.4 us
    psum x3, blocking collectives, per_device(): sums = lax.psum(lax.psum(lax.psum(sums, 'y'), 'x'), 'zl')  27.8 us
    psum x1, blocking collectives, per_device(): score = lax.psum(placed(score, zh, 4), 'zh')  13.7 us
    psum x1, blocking collectives, per_device(): probes = lax.psum(placed(probe, x, 4), 'x')  12.6 us
    ppermute x1, waiting for transfers between devices, per_device(): probes = lax.ppermute(probes, ('y', 'zl'), turned())  8.28 us
    ppermute x1, starting transfers between devices, per_device(): total = lax.ppermute(total, ('y', 'zl'), turned()).astype(f32)  6.87 us
    ppermute x2, waiting for transfers between devices, joined(): got = lax.ppermute(value, axis, pairs(step))  5.91 us
  transfers between devices with their start and end apart: 21, of which 7 were waited for; matrix products, arithmetic and copies ran while one was open for 13% of the time, Pallas kernels for 0%

profile of v9, /device:TPU:24, one launch (start us, length us, event | category | flops | bytes accessed | tf_op | source)
XLA Modules:
  0.0 233.7 jit_solution(17966746768986014120)
XLA Ops:
  8.0 2.7 %collective-permute-start.2 = (bf16[192,1024]{1,0:T(8,128)(2,1)}, bf16[192,1024]{1,0:T(8,128)(2,1)}, u32[]{:S(2)}, u32[]{:S(2)}) collective-permute-start(bf16[192,1024]{1,0:T(8,128)(2,1)} %param.7), channel_id=1, source_target_pairs={{0,96},{32,0},{64,32},{96,64},{1,97},{33,1},{65,33},{97,65},{2,98}... | collective-permute-start | bytes 1179656 | tf_op jit(solution)/shard_map/ppermute | solution.py:35
  10.6 8.2 %collective-permute-start.3 = (bf16[192,1024]{1,0:T(8,128)(2,1)}, bf16[192,1024]{1,0:T(8,128)(2,1)S(1)}, u32[]{:S(2)}, u32[]{:S(2)}) collective-permute-start(bf16[192,1024]{1,0:T(8,128)(2,1)} %param.7), channel_id=1, source_target_pairs={{0,64},{32,96},{64,0},{96,32},{1,65},{33,97},{65,1},{97,33},{2,66}... | collective-permute-start | bytes 1179656 | tf_op jit(solution)/shard_map/ppermute | solution.py:35
  18.8 1.9 collective-permute-start.4
  20.8 1.6 multiply_reduce_fusion.1
  22.4 3.7 %collective-permute-start = (bf16[32,320]{1,0:T(8,128)(2,1)}, bf16[32,320]{1,0:T(8,128)(2,1)}, u32[]{:S(2)}, u32[]{:S(2)}) collective-permute-start(bf16[32,320]{1,0:T(8,128)(2,1)} %get-tuple-element.15), channel_id=1, source_target_pairs={{0,0},{1,32},{2,64},{3,96},{4,128},{5,160},{6,192},{7,224},{8,256}... | collective-permute-start | bytes 61448 | tf_op jit(solution)/shard_map/ppermute | solution.py:93
  26.1 9.5 %collective-permute-start.15 = (bf16[32,1024]{1,0:T(8,128)(2,1)}, bf16[32,1024]{1,0:T(8,128)(2,1)}, u32[]{:S(2)}, u32[]{:S(2)}) collective-permute-start(bf16[32,1024]{1,0:T(8,128)(2,1)} %param.10), channel_id=1, source_target_pairs={{0,384},{128,0},{256,128},{384,256},{1,385},{129,1},{257,129},{385... | collective-permute-start | bytes 196616 | tf_op jit(solution)/shard_map/ppermute | solution.py:35
  35.6 1.0 mul.94
  37.5 0.8 mul.111
  38.3 0.8 mul.112
  39.8 12.6 %psum.42 = f32[1280]{0:T(1024)S(1)} all-reduce(f32[1280]{0:T(1024)S(1)} %dynamic_update_slice.12), channel_id=1, replica_groups=mesh['zh'=4,'y'=4,'c'=2,'x'=4,'zl'=4] {'x'}, use_global_device_ids=true, to_apply=%region_0.1 | all-reduce | flops 1280 | bytes 10240 | tf_op jit(solution)/shard_map/psum | solution.py:89
  52.4 5.3 %collective-permute-start.7 = (f32[1280]{0:T(1024)S(1)}, f32[1280]{0:T(1024)S(1)}, u32[]{:S(2)}, u32[]{:S(2)}) collective-permute-start(f32[1280]{0:T(1024)S(1)} %psum.42), channel_id=1, source_target_pairs={{0,0},{1,32},{2,64},{3,96},{32,1},{33,33},{34,65},{35,97},{64,2},{... | collective-permute-start | bytes 15368 | tf_op jit(solution)/shard_map/ppermute | solution.py:90
  57.7 0.9 broadcast_select_fusion.5
  58.5 8.3 %collective-permute-done.7 = f32[1280]{0:T(1024)S(1)} collective-permute-done((f32[1280]{0:T(1024)S(1)}, f32[1280]{0:T(1024)S(1)}, u32[]{:S(2)}, u32[]{:S(2)}) %collective-permute-start.7) | collective-permute-done | bytes 5152 | tf_op jit(solution)/shard_map/ppermute | solution.py:90
  66.8 1.9 collective-permute-start.1
  69.9 6.1 %collective-permute-start.16 = (bf16[32,1024]{1,0:T(8,128)(2,1)}, bf16[32,1024]{1,0:T(8,128)(2,1)S(1)}, u32[]{:S(2)}, u32[]{:S(2)}) collective-permute-start(bf16[32,1024]{1,0:T(8,128)(2,1)} %param.10), channel_id=1, source_target_pairs={{0,128},{128,256},{256,384},{384,0},{1,129},{129,257},{257,385},{3... | collective-permute-start | bytes 196616 | tf_op jit(solution)/shard_map/ppermute | solution.py:35
  77.5 6.6 %collective-permute-done.16 = bf16[32,1024]{1,0:T(8,128)(2,1)S(1)} collective-permute-done((bf16[32,1024]{1,0:T(8,128)(2,1)}, bf16[32,1024]{1,0:T(8,128)(2,1)S(1)}, u32[]{:S(2)}, u32[]{:S(2)}) %collective-permute-start.16) | collective-permute-done | bytes 65568 | tf_op jit(solution)/shard_map/ppermute | solution.py:35
  84.1 5.9 %collective-permute-start.17 = (bf16[16,1024]{1,0:T(8,128)(2,1)S(1)}, bf16[16,1024]{1,0:T(8,128)(2,1)S(1)}, u32[]{:S(2)}, u32[]{:S(2)}) collective-permute-start(bf16[16,1024]{1,0:T(8,128)(2,1)S(1)} %slice.59), channel_id=1, source_target_pairs={{0,128},{128,256},{256,384},{384,0},{1,129},{129,257},{257,385},{3... | collective-permute-start | bytes 98312 | tf_op jit(solution)/shard_map/ppermute | solution.py:35
  90.0 0.8 slice.60
  90.7 3.8 %collective-permute-start.18 = (bf16[16,1024]{1,0:T(8,128)(2,1)S(1)}, bf16[16,1024]{1,0:T(8,128)(2,1)S(1)}, u32[]{:S(2)}, u32[]{:S(2)}) collective-permute-start(bf16[16,1024]{1,0:T(8,128)(2,1)S(1)} %slice.60), channel_id=1, source_target_pairs={{0,384},{128,0},{256,128},{384,256},{1,385},{129,1},{257,129},{385... | collective-permute-start | bytes 98312 | tf_op jit(solution)/shard_map/ppermute | solution.py:35
  94.6 0.8 constant_dynamic-update-slice_fusion.7
  95.4 5.1 %collective-permute-done.18 = bf16[16,1024]{1,0:T(8,128)(2,1)S(1)} collective-permute-done((bf16[16,1024]{1,0:T(8,128)(2,1)S(1)}, bf16[16,1024]{1,0:T(8,128)(2,1)S(1)}, u32[]{:S(2)}, u32[]{:S(2)}) %collective-permute-start.18) | collective-permute-done | bytes 32800 | tf_op jit(solution)/shard_map/ppermute | solution.py:35
  100.5 0.8 fusion.8
  101.4 1.0 constant_dynamic-update-slice_fusion.2
  102.5 5.3 %fusion = bf16[1280,768]{0,1:T(8,128)(2,1)} fusion(bf16[768,1024]{1,0:T(8,128)(2,1)S(1)} %constant_dynamic-update-slice_fusion, bf16[1280,1024]{1,0:T(8,128)(2,1)} %all-gather.4.cloned.1.call-done), kind=kOutput, calls=%fused_computation.3 | convolution fusion | flops 2014248960 | bytes 6160384 | tf_op jit(solution)/shard_map/dot_general | solution.py:101
  107.9 2.7 %copy.30 = bf16[1280,768]{1,0:T(8,128)(2,1)S(1)} copy(bf16[1280,768]{0,1:T(8,128)(2,1)} %fusion) | data formatting | bytes 3932160 | tf_op jit(solution)/shard_map/convert_element_type | solution.py:103
  111.3 1.2 pad_maximum_fusion.2
  112.4 1.9 collective-permute-start.8
  114.9 3.0 %collective-permute-start.6 = (bf16[336,768]{1,0:T(8,128)(2,1)}, bf16[336,768]{1,0:T(8,128)(2,1)}, u32[]{:S(2)}, u32[]{:S(2)}) collective-permute-start(bf16[336,768]{1,0:T(8,128)(2,1)} %get-tuple-element.27), channel_id=1, source_target_pairs={{0,8},{4,12},{8,0},{12,4},{1,9},{5,13},{9,1},{13,5},{2,10},{6,14},... | collective-permute-start | bytes 1548296 | tf_op jit(solution)/shard_map/ppermute | solution.py:35
  118.6 4.5 %collective-permute-start.5 = (bf16[336,768]{1,0:T(8,128)(2,1)}, bf16[336,768]{1,0:T(8,128)(2,1)S(1)}, u32[]{:S(2)}, u32[]{:S(2)}) collective-permute-start(bf16[336,768]{1,0:T(8,128)(2,1)} %get-tuple-element.26), channel_id=1, source_target_pairs={{0,12},{4,0},{8,4},{12,8},{1,13},{5,1},{9,5},{13,9},{2,14},{6,2},{... | collective-permute-start | bytes 1548296 | tf_op jit(solution)/shard_map/ppermute | solution.py:35
  123.8 15.3 %collective-permute-done.8 = bf16[336,768]{1,0:T(8,128)(2,1)} collective-permute-done((bf16[336,768]{1,0:T(8,128)(2,1)}, bf16[336,768]{1,0:T(8,128)(2,1)}, u32[]{:S(2)}, u32[]{:S(2)}) %collective-permute-start.8) | collective-permute-done | bytes 516128 | tf_op jit(solution)/shard_map/ppermute | solution.py:35
  139.8 0.7 slice_bitcast_fusion
  140.5 1.5 collective-permute-done.5
  142.0 0.8 pad_maximum_fusion.5
  142.7 1.4 fusion.4
  144.6 1.9 collective-permute-start.11
  146.5 8.1 %collective-permute-start.10 = (bf16[192,320]{1,0:T(8,128)(2,1)S(1)}, bf16[192,320]{1,0:T(8,128)(2,1)S(1)}, u32[]{:S(2)}, u32[]{:S(2)}) collective-permute-start(bf16[192,320]{1,0:T(8,128)(2,1)S(1)} %get-tuple-element.21), channel_id=1, source_target_pairs={{0,2},{1,3},{2,0},{3,1},{4,6},{5,7},{6,4},{7,5},{8,10},{9,11},{10,... | collective-permute-start | bytes 368648 | tf_op jit(solution)/shard_map/ppermute | solution.py:35
  154.6 8.2 %psum.43 = f32[1664]{0:T(1024)S(1)} all-reduce(f32[1664]{0:T(1024)S(1)} %pad_maximum_fusion.6), channel_id=1, replica_groups=mesh['zh'=4,'y'=4,'c'=2,'x'=4,'zl'=4] {'y'}, use_global_device_ids=true, to_apply=%region_5.6 | all-reduce | flops 1664 | bytes 13312 | tf_op jit(solution)/shard_map/psum | solution.py:124
  162.8 10.5 %psum.44 = f32[1664]{0:T(1024)S(1)} all-reduce(f32[1664]{0:T(1024)S(1)} %psum.43), channel_id=1, replica_groups=mesh['zh'=4,'y'=4,'c'=2,'x'=4,'zl'=4] {'x'}, use_global_device_ids=true, to_apply=%region_6.7 | all-reduce | flops 1664 | bytes 13312 | tf_op jit(solution)/shard_map/psum | solution.py:124
  173.3 9.1 %psum.45 = f32[1664]{0:T(1024)S(1)} all-reduce(f32[1664]{0:T(1024)S(1)} %psum.44), channel_id=1, replica_groups=mesh['zh'=4,'y'=4,'c'=2,'x'=4,'zl'=4] {'zl'}, use_global_device_ids=true, to_apply=%region_7.8 | all-reduce | flops 1664 | bytes 13312 | tf_op jit(solution)/shard_map/psum | solution.py:124
  182.7 3.8 %collective-permute-start.9 = (bf16[192,320]{1,0:T(8,128)(2,1)S(1)}, bf16[192,320]{1,0:T(8,128)(2,1)S(1)}, u32[]{:S(2)}, u32[]{:S(2)}) collective-permute-start(bf16[192,320]{1,0:T(8,128)(2,1)S(1)} %get-tuple-element.19), channel_id=1, source_target_pairs={{0,1},{1,2},{2,3},{3,0},{4,5},{5,6},{6,7},{7,4},{8,9},{9,10},{10,1... | collective-permute-start | bytes 368648 | tf_op jit(solution)/shard_map/ppermute | solution.py:35
  186.7 1.9 collective-permute-start.13
  188.8 5.9 %collective-permute-done.13 = bf16[64,768]{1,0:T(8,128)(2,1)S(1)} collective-permute-done((bf16[64,768]{1,0:T(8,128)(2,1)S(1)}, bf16[64,768]{1,0:T(8,128)(2,1)S(1)}, u32[]{:S(2)}, u32[]{:S(2)}) %collective-permute-start.13) | collective-permute-done | bytes 98336 | tf_op jit(solution)/shard_map/ppermute | solution.py:44
  194.8 3.3 %collective-permute-start.14 = (bf16[128,768]{1,0:T(8,128)(2,1)S(1)}, bf16[128,768]{1,0:T(8,128)(2,1)S(1)}, u32[]{:S(2)}, u32[]{:S(2)}) collective-permute-start(bf16[128,768]{1,0:T(8,128)(2,1)S(1)} %pad_maximum_fusion.4), channel_id=1, source_target_pairs={{0,3},{1,2},{2,1},{3,0},{4,7},{5,6},{6,5},{7,4},{8,11},{9,10},{10,... | collective-permute-start | bytes 589832 | tf_op jit(solution)/shard_map/ppermute | solution.py:44
  198.2 6.9 %collective-permute-start.12 = (bf16[192,320]{1,0:T(8,128)(2,1)S(1)}, bf16[192,320]{1,0:T(8,128)(2,1)S(1)}, u32[]{:S(2)}, u32[]{:S(2)}) collective-permute-start(bf16[192,320]{1,0:T(8,128)(2,1)S(1)} %fusion.7), channel_id=1, source_target_pairs={{0,0},{1,32},{2,64},{3,96},{32,1},{33,33},{34,65},{35,97},{64,2},{... | collective-permute-start | bytes 368648 | tf_op jit(solution)/shard_map/ppermute | solution.py:147
  205.2 2.4 %psum.46 = f32[256]{0:T(256)S(1)} all-reduce(f32[256]{0:T(256)S(1)} %reshape.143), channel_id=1, replica_groups=mesh['zh'=4,'y'=4,'c'=2,'x'=4,'zl'=4] {'c'}, use_global_device_ids=true, to_apply=%region_9.10 | all-reduce | flops 256 | bytes 2048 | tf_op jit(solution)/shard_map/psum | solution.py:143
  207.8 13.7 %psum.47 = f32[1024]{0:T(1024)S(1)} all-reduce(f32[1024]{0:T(1024)S(1)} %dynamic_update_slice.15), channel_id=1, replica_groups=mesh['zh'=4,'y'=4,'c'=2,'x'=4,'zl'=4] {'zh'}, use_global_device_ids=true, to_apply=%region_10.11 | all-reduce | flops 1024 | bytes 8192 | tf_op jit(solution)/shard_map/psum | solution.py:144
  222.2 0.8 add_convert_fusion
  223.9 3.0 %convolution_multiply_fusion = f32[160,1024]{1,0:T(8,128)} fusion(bf16[1024,160]{1,0:T(8,128)(2,1)S(1)} %bitcast.59, bf16[1024,1024]{1,0:T(8,128)(2,1)} %bitcast.58), kind=kOutput, calls=%fused_computation.4 | convolution fusion | flops 335708160 | bytes 3080192 | tf_op jit(solution)/shard_map/dot_general | solution.py:158
  (102 shorter events, 11.4 us)
Async XLA Ops:
  7.2 29.5 %copy-start.1 = (bf16[192,1024]{1,0:T(8,128)(2,1)S(1)}, bf16[192,1024]{1,0:T(8,128)(2,1)}, u32[]{:S(2)}) copy-start(bf16[192,1024]{1,0:T(8,128)(2,1)} %param.7) | copy-start | bytes 1179652
  7.2 95.4 %all-gather.4.cloned.1.call-start = ((), (), s32[]{:S(2)}) async-start(), calls=%async_computation | async-start | bytes 2949120 | tf_op jit(solution)/shard_map/all_gather | solution.py:76
  7.9 216.0 %all-gather.6.cloned.1.call-start = ((), (), s32[]{:S(2)}) async-start(), calls=%async_computation.1 | async-start | bytes 2359296 | tf_op jit(solution)/shard_map/all_gather | solution.py:87
  8.0 93.4 %collective-permute-start.2 = (bf16[192,1024]{1,0:T(8,128)(2,1)}, bf16[192,1024]{1,0:T(8,128)(2,1)}, u32[]{:S(2)}, u32[]{:S(2)}) collective-permute-start(bf16[192,1024]{1,0:T(8,128)(2,1)} %param.7), channel_id=1, source_target_pairs={{0,96},{32,0},{64,32},{96,64},{1,97},{33,1},{65,33},{97,65},{2,98}... | collective-permute-start | bytes 1179656 | tf_op jit(solution)/shard_map/ppermute | solution.py:35
  10.6 91.8 %collective-permute-start.3 = (bf16[192,1024]{1,0:T(8,128)(2,1)}, bf16[192,1024]{1,0:T(8,128)(2,1)S(1)}, u32[]{:S(2)}, u32[]{:S(2)}) collective-permute-start(bf16[192,1024]{1,0:T(8,128)(2,1)} %param.7), channel_id=1, source_target_pairs={{0,64},{32,96},{64,0},{96,32},{1,65},{33,97},{65,1},{97,33},{2,66}... | collective-permute-start | bytes 1179656 | tf_op jit(solution)/shard_map/ppermute | solution.py:35
  18.8 83.6 %collective-permute-start.4 = (bf16[192,1024]{1,0:T(8,128)(2,1)}, bf16[192,1024]{1,0:T(8,128)(2,1)S(1)}, u32[]{:S(2)}, u32[]{:S(2)}) collective-permute-start(bf16[192,1024]{1,0:T(8,128)(2,1)} %param.7), channel_id=1, source_target_pairs={{0,32},{32,64},{64,96},{96,0},{1,33},{33,65},{65,97},{97,1},{2,34}... | collective-permute-start | bytes 1179656 | tf_op jit(solution)/shard_map/ppermute | solution.py:35
  22.4 30.0 %collective-permute-start = (bf16[32,320]{1,0:T(8,128)(2,1)}, bf16[32,320]{1,0:T(8,128)(2,1)}, u32[]{:S(2)}, u32[]{:S(2)}) collective-permute-start(bf16[32,320]{1,0:T(8,128)(2,1)} %get-tuple-element.15), channel_id=1, source_target_pairs={{0,0},{1,32},{2,64},{3,96},{4,128},{5,160},{6,192},{7,224},{8,256}... | collective-permute-start | bytes 61448 | tf_op jit(solution)/shard_map/ppermute | solution.py:93
  26.1 63.9 %collective-permute-start.15 = (bf16[32,1024]{1,0:T(8,128)(2,1)}, bf16[32,1024]{1,0:T(8,128)(2,1)}, u32[]{:S(2)}, u32[]{:S(2)}) collective-permute-start(bf16[32,1024]{1,0:T(8,128)(2,1)} %param.10), channel_id=1, source_target_pairs={{0,384},{128,0},{256,128},{384,256},{1,385},{129,1},{257,129},{385... | collective-permute-start | bytes 196616 | tf_op jit(solution)/shard_map/ppermute | solution.py:35
  36.7 0.8 copy-start.3
  36.7 2.4 %copy-start.7 = (f32[320]{0:T(512)S(1)}, f32[320]{0:T(512)}, u32[]{:S(2)}) copy-start(f32[320]{0:T(512)} %param.11) | copy-start | bytes 3844
  39.5 29.2 %copy-start.10 = (f32[128]{0:T(128)}, f32[128]{0:T(128)S(1)}, u32[]{:S(2)}) copy-start(f32[128]{0:T(128)S(1)} %dynamic_update_slice.14) | copy-start | bytes 1540
  39.7 36.3 %copy-start.6 = (f32[768]{0:T(1024)}, f32[768]{0:T(1024)S(1)}, u32[]{:S(2)}) copy-start(f32[768]{0:T(1024)S(1)} %dynamic_update_slice.13) | copy-start | bytes 9220
  52.4 14.4 %collective-permute-start.7 = (f32[1280]{0:T(1024)S(1)}, f32[1280]{0:T(1024)S(1)}, u32[]{:S(2)}, u32[]{:S(2)}) collective-permute-start(f32[1280]{0:T(1024)S(1)} %psum.42), channel_id=1, source_target_pairs={{0,0},{1,32},{2,64},{3,96},{32,1},{33,33},{34,65},{35,97},{64,2},{... | collective-permute-start | bytes 15368 | tf_op jit(solution)/shard_map/ppermute | solution.py:90
  66.8 3.1 %collective-permute-start.1 = (bf16[32,160]{1,0:T(8,128)(2,1)S(1)}, bf16[32,160]{1,0:T(8,128)(2,1)S(1)}, u32[]{:S(2)}, u32[]{:S(2)}) collective-permute-start(bf16[32,160]{1,0:T(8,128)(2,1)S(1)} %get-tuple-element.30), channel_id=1, source_target_pairs={{0,16},{16,0},{1,17},{17,1},{2,18},{18,2},{3,19},{19,3},{4,20},{20... | collective-permute-start | bytes 30728 | tf_op jit(solution)/shard_map/ppermute | solution.py:96
  69.9 14.2 %collective-permute-start.16 = (bf16[32,1024]{1,0:T(8,128)(2,1)}, bf16[32,1024]{1,0:T(8,128)(2,1)S(1)}, u32[]{:S(2)}, u32[]{:S(2)}) collective-permute-start(bf16[32,1024]{1,0:T(8,128)(2,1)} %param.10), channel_id=1, source_target_pairs={{0,128},{128,256},{256,384},{384,0},{1,129},{129,257},{257,385},{3... | collective-permute-start | bytes 196616 | tf_op jit(solution)/shard_map/ppermute | solution.py:35
  84.1 11.4 %collective-permute-start.17 = (bf16[16,1024]{1,0:T(8,128)(2,1)S(1)}, bf16[16,1024]{1,0:T(8,128)(2,1)S(1)}, u32[]{:S(2)}, u32[]{:S(2)}) collective-permute-start(bf16[16,1024]{1,0:T(8,128)(2,1)S(1)} %slice.59), channel_id=1, source_target_pairs={{0,128},{128,256},{256,384},{384,0},{1,129},{129,257},{257,385},{3... | collective-permute-start | bytes 98312 | tf_op jit(solution)/shard_map/ppermute | solution.py:35
  90.7 9.8 %collective-permute-start.18 = (bf16[16,1024]{1,0:T(8,128)(2,1)S(1)}, bf16[16,1024]{1,0:T(8,128)(2,1)S(1)}, u32[]{:S(2)}, u32[]{:S(2)}) collective-permute-start(bf16[16,1024]{1,0:T(8,128)(2,1)S(1)} %slice.60), channel_id=1, source_target_pairs={{0,384},{128,0},{256,128},{384,256},{1,385},{129,1},{257,129},{385... | collective-permute-start | bytes 98312 | tf_op jit(solution)/shard_map/ppermute | solution.py:35
  110.5 0.7 copy-start.4
  110.7 3.7 %copy-start = (bf16[1280,1024]{1,0:T(8,128)(2,1)S(1)}, bf16[1280,1024]{1,0:T(8,128)(2,1)}, u32[]{:S(2)}) copy-start(bf16[1280,1024]{1,0:T(8,128)(2,1)} %all-gather.4.cloned.1.call-done) | copy-start | bytes 7864324
  110.7 3.7 %copy-start.5 = (bf16[1,1280]{1,0:T(2,128)(2,1)S(1)}, bf16[1,1280]{1,0:T(2,128)(2,1)}, u32[]{:S(2)}) copy-start(bf16[1,1280]{1,0:T(2,128)(2,1)} %stack.37) | copy-start | bytes 7684
  112.4 26.6 %collective-permute-start.8 = (bf16[336,768]{1,0:T(8,128)(2,1)}, bf16[336,768]{1,0:T(8,128)(2,1)}, u32[]{:S(2)}, u32[]{:S(2)}) collective-permute-start(bf16[336,768]{1,0:T(8,128)(2,1)} %get-tuple-element.28), channel_id=1, source_target_pairs={{0,4},{4,8},{8,12},{12,0},{1,5},{5,9},{9,13},{13,1},{2,6},{6,10},{... | collective-permute-start | bytes 1548296 | tf_op jit(solution)/shard_map/ppermute | solution.py:35
  114.9 24.9 %collective-permute-start.6 = (bf16[336,768]{1,0:T(8,128)(2,1)}, bf16[336,768]{1,0:T(8,128)(2,1)}, u32[]{:S(2)}, u32[]{:S(2)}) collective-permute-start(bf16[336,768]{1,0:T(8,128)(2,1)} %get-tuple-element.27), channel_id=1, source_target_pairs={{0,8},{4,12},{8,0},{12,4},{1,9},{5,13},{9,1},{13,5},{2,10},{6,14},... | collective-permute-start | bytes 1548296 | tf_op jit(solution)/shard_map/ppermute | solution.py:35
  118.6 23.4 %collective-permute-start.5 = (bf16[336,768]{1,0:T(8,128)(2,1)}, bf16[336,768]{1,0:T(8,128)(2,1)S(1)}, u32[]{:S(2)}, u32[]{:S(2)}) collective-permute-start(bf16[336,768]{1,0:T(8,128)(2,1)} %get-tuple-element.26), channel_id=1, source_target_pairs={{0,12},{4,0},{8,4},{12,8},{1,13},{5,1},{9,5},{13,9},{2,14},{6,2},{... | collective-permute-start | bytes 1548296 | tf_op jit(solution)/shard_map/ppermute | solution.py:35
  144.2 77.3 %copy-start.8 = (s32[1024]{0:T(1024)S(1)}, s32[1024]{0:T(1024)}, u32[]{:S(2)}) copy-start(s32[1024]{0:T(1024)} %param.13) | copy-start | bytes 12292
  144.2 77.9 %copy-start.9 = (f32[1024]{0:T(1024)S(1)}, f32[1024]{0:T(1024)}, u32[]{:S(2)}) copy-start(f32[1024]{0:T(1024)} %param.12) | copy-start | bytes 12292
  144.2 78.0 %copy-start.2 = (f32[192,320]{1,0:T(8,128)S(1)}, f32[192,320]{1,0:T(8,128)}, u32[]{:S(2)}) copy-start(f32[192,320]{1,0:T(8,128)} %mul.112) | copy-start | bytes 737284
  144.6 53.5 %collective-permute-start.11 = (bf16[192,320]{1,0:T(8,128)(2,1)S(1)}, bf16[192,320]{1,0:T(8,128)(2,1)S(1)}, u32[]{:S(2)}, u32[]{:S(2)}) collective-permute-start(bf16[192,320]{1,0:T(8,128)(2,1)S(1)} %get-tuple-element.20), channel_id=1, source_target_pairs={{0,3},{1,0},{2,1},{3,2},{4,7},{5,4},{6,5},{7,6},{8,11},{9,8},{10,9... | collective-permute-start | bytes 368648 | tf_op jit(solution)/shard_map/ppermute | solution.py:35
  146.5 51.6 %collective-permute-start.10 = (bf16[192,320]{1,0:T(8,128)(2,1)S(1)}, bf16[192,320]{1,0:T(8,128)(2,1)S(1)}, u32[]{:S(2)}, u32[]{:S(2)}) collective-permute-start(bf16[192,320]{1,0:T(8,128)(2,1)S(1)} %get-tuple-element.21), channel_id=1, source_target_pairs={{0,2},{1,3},{2,0},{3,1},{4,6},{5,7},{6,4},{7,5},{8,10},{9,11},{10,... | collective-permute-start | bytes 368648 | tf_op jit(solution)/shard_map/ppermute | solution.py:35
  182.7 15.3 %collective-permute-start.9 = (bf16[192,320]{1,0:T(8,128)(2,1)S(1)}, bf16[192,320]{1,0:T(8,128)(2,1)S(1)}, u32[]{:S(2)}, u32[]{:S(2)}) collective-permute-start(bf16[192,320]{1,0:T(8,128)(2,1)S(1)} %get-tuple-element.19), channel_id=1, source_target_pairs={{0,1},{1,2},{2,3},{3,0},{4,5},{5,6},{6,7},{7,4},{8,9},{9,10},{10,1... | collective-permute-start | bytes 368648 | tf_op jit(solution)/shard_map/ppermute | solution.py:35
  186.7 8.0 %collective-permute-start.13 = (bf16[64,768]{1,0:T(8,128)(2,1)S(1)}, bf16[64,768]{1,0:T(8,128)(2,1)S(1)}, u32[]{:S(2)}, u32[]{:S(2)}) collective-permute-start(bf16[64,768]{1,0:T(8,128)(2,1)S(1)} %bitcast.62), channel_id=1, source_target_pairs={{0,1},{1,0},{2,3},{3,2},{4,5},{5,4},{6,7},{7,6},{8,9},{9,8},{10,11... | collective-permute-start | bytes 294920 | tf_op jit(solution)/shard_map/ppermute | solution.py:44
  194.8 28.2 %collective-permute-start.14 = (bf16[128,768]{1,0:T(8,128)(2,1)S(1)}, bf16[128,768]{1,0:T(8,128)(2,1)S(1)}, u32[]{:S(2)}, u32[]{:S(2)}) collective-permute-start(bf16[128,768]{1,0:T(8,128)(2,1)S(1)} %pad_maximum_fusion.4), channel_id=1, source_target_pairs={{0,3},{1,2},{2,1},{3,0},{4,7},{5,6},{6,5},{7,4},{8,11},{9,10},{10,... | collective-permute-start | bytes 589832 | tf_op jit(solution)/shard_map/ppermute | solution.py:44
  198.2 24.0 %collective-permute-start.12 = (bf16[192,320]{1,0:T(8,128)(2,1)S(1)}, bf16[192,320]{1,0:T(8,128)(2,1)S(1)}, u32[]{:S(2)}, u32[]{:S(2)}) collective-permute-start(bf16[192,320]{1,0:T(8,128)(2,1)S(1)} %fusion.7), channel_id=1, source_target_pairs={{0,0},{1,32},{2,64},{3,96},{32,1},{33,33},{34,65},{35,97},{64,2},{... | collective-permute-start | bytes 368648 | tf_op jit(solution)/shard_map/ppermute | solution.py:147
Sparse Core Ops, SparseCore 0:
  10.1 81.1 all-gather.3
  101.5 31.4 all-gather.5

commit v10 on v9

--- a/solution.py
+++ b/solution.py
@@ -73,18 +73,12 @@
     first = c == 0
     many = 4 * rows
 
-    weight = lax.all_gather(down_weight, ("zh", "c"), axis=0, tiled=True)
+    own = jnp.concatenate([down_weight, member_right], axis=0)
+    stack = lax.all_gather(own, ("zh", "c"), axis=0, tiled=True).reshape(4, 2, -1, width)
+    weight = stack[:, :, :block].reshape(-1, width)
+    rights = lax.all_gather(stack[:, :, block:], "y", axis=0, tiled=False)
 
     around = [features] + [move(features, "y", -j) for j in (1, 2, 3)]
-    around = jnp.concatenate(around, axis=0)
-
-    cut = members // 2
-    before = move(member_right, "zh", 1)
-    after = move(member_right, "zh", -1)
-    far = [move(before[:cut], "zh", 1), move(after[cut:], "zh", -1)]
-    rights = jnp.concatenate([member_right, after] + far + [before], axis=0)
-    rights = jnp.roll(rights.reshape(4, members, width), zh, axis=0)
-    rights = lax.all_gather(rights, ("y", "c"), axis=0, tiled=False)
 
     probes = lax.psum(placed(probe, x, 4), "x")
     probes = lax.ppermute(probes, ("y", "zl"), turned())
@@ -96,32 +90,47 @@
     other = lax.ppermute(other, "c", [(0, 1), (1, 0)])
     lefts = jnp.where(first, jnp.concatenate([mine, other], 0), jnp.concatenate([other, mine], 0))
     lefts = jnp.pad(lefts, ((0, 0), (0, 192 - block))).reshape(-1, many)
+    lefts = joined(lefts, "x", x)
     left_cols = left_cols.astype(f32)
 
     part = lax.dot_general(
-        weight, around, (((1,), (1,)), ((), ())), preferred_element_type=f32
+        weight, jnp.concatenate(around, axis=0), (((1,), (1,)), ((), ())), preferred_element_type=f32
     ).astype(bf16).reshape(4, cols, many)
     parts = []
     for k in range(4):
         one = lax.dynamic_index_in_dim(part, lax.rem(x + k, 4), 0, keepdims=False)
-        one = jnp.concatenate([one, lefts], axis=0)
         parts.append(one if k == 0 else move(one, "x", k))
 
     direction = lax.dot_general(
         in_three(probes), weight, (((1,), (0,)), ((), ())), preferred_element_type=f32
     ).sum(0)
-    along = lax.dot_general(
-        in_three(direction), around, (((1,), (1,)), ((), ())), preferred_element_type=f32
-    ).sum(0)
-    along = jnp.roll(along.reshape(4, rows), y, axis=0).reshape(many)
+    along = jnp.stack([
+        lax.dot_general(
+            in_three(direction), f, (((1,), (1,)), ((), ())), preferred_element_type=f32
+        ).sum(0)
+        for f in around
+    ])
+    along = jnp.roll(along, y, axis=0).reshape(many)
     inner = jnp.sum(
         features.astype(f32).reshape(members, tokens, width) * member_right.astype(f32)[:, None, :],
         axis=2,
     ).reshape(rows)
     left_dot = jnp.sum(left_cols * probe[None, :], axis=1)
     sums = jnp.concatenate([along, placed(inner, y, 4), placed(left_dot, y, 4)])
-    sums, parts[1] = lax.optimization_barrier((sums, parts[1]))
-    sums = lax.psum(lax.psum(lax.psum(sums, "y"), "x"), "zl")
+    sums, lefts, parts[1] = lax.optimization_barrier((sums, lefts, parts[1]))
+    sums = lax.psum(lax.psum(sums, "y"), "x")
+    lefts = joined(lefts, "zl", zl)
+    total = sum(p.astype(f32) for p in parts).astype(bf16)
+    sums, lefts, total = lax.optimization_barrier((sums, lefts, total))
+
+    sums = lax.psum(sums, "zl")
+    total = total.T.reshape(4, rows, cols)
+    parts = []
+    for k in range(4):
+        one = lax.dynamic_index_in_dim(total, lax.rem(zl + k + 4 - y, 4), 0, keepdims=False)
+        parts.append(one if k == 0 else move(one, "zl", k))
+    total = sum(p.astype(f32) for p in parts).astype(bf16)
+    sums, total = lax.optimization_barrier((sums, total))
     along, inner, left_dot = jnp.split(sums, [many, 2 * many])
     inner = spread * inner
     dots = along + inner * jnp.repeat(left_dot, tokens)
@@ -129,20 +138,8 @@
     score = jnp.mean(jnp.tanh(scale * dots).reshape(4, members, tokens), axis=2)
     score = jnp.stack([jnp.where(first, score, 0.0), jnp.where(first, 0.0, score)], axis=1)
 
-    total = sum(p[:cols].astype(f32) for p in parts).astype(bf16)
-    lefts = jnp.stack([parts[k][cols:] for k in (0, 3, 2, 1)])
-    lefts, total = lax.optimization_barrier((lefts, total))
-    lefts = joined(jnp.roll(lefts, x, axis=0).reshape(-1, many), "zl", zl)
-
-    total = total.T.reshape(4, rows, cols)
-    parts = []
-    for k in range(4):
-        one = lax.dynamic_index_in_dim(total, lax.rem(zl + k + 4 - y, 4), 0, keepdims=False)
-        parts.append(one if k == 0 else move(one, "zl", k))
-    score, parts[1] = lax.optimization_barrier((score, parts[1]))
     score = lax.psum(score.reshape(-1), "c")
     score = lax.psum(placed(score, zh, 4), "zh")
-    total = sum(p.astype(f32) for p in parts).astype(bf16)
 
     total = lax.ppermute(total, ("y", "zl"), turned()).astype(f32)
     inner = lax.dynamic_slice(inner, (y * rows,), (rows,))
@@ -152,9 +149,9 @@
     labels = jnp.arange(population, dtype=jnp.int32)
     rival = jnp.sum(jnp.where(opponent[:, None] == labels[None, :], score[None, :], 0.0), axis=1)
     fitness = payoff * (score - rival)
-    fitness = fitness.reshape(4, 4, 2, members).transpose(1, 2, 0, 3)
-    scaled = lefts.reshape(4, 4, 2, members, 192)[..., :block].transpose(0, 2, 1, 3, 4).astype(f32)
-    scaled = (fitness[..., None] * scaled).astype(bf16).reshape(population, block)
+    fitness = fitness.reshape(4, 4, -1).transpose(1, 0, 2).reshape(population, 1)
+    scaled = lefts.reshape(population, 192)[:, :block].astype(f32)
+    scaled = (fitness * scaled).astype(bf16)
     term = lax.dot_general(
         scaled, rights.reshape(population, width), (((0,), (0,)), ((), ())),
         preferred_element_type=f32,

time: 236 us -> 217 us (0.919)
  starting transfers between devices: 84.4 us -> 64.2 us
  blocking collectives: 56.5 us -> 68.6 us
  local copies, waits for them, and re-layouts: 15.4 us -> 9.59 us
  other arithmetic: 9.58 us -> 7.01 us
  matrix products: 9.26 us -> 6.83 us
    ppermute x13 -> x9, starting transfers between devices: 61.3 us -> 31.1 us  [move(): return lax.ppermute(value, axis, ring(step))]
    ppermute x13 -> x9, waiting for transfers between devices: 28.4 us -> 4.11 us  [move(): return lax.ppermute(value, axis, ring(step))]
    all_gather x2, waiting for transfers between devices: 0.04 us -> 23.8 us  [the longest x1 23.8 us: per_device(): lax.all_gather(own, ('zh', 'c'), axis=0, tiled=True)]
    psum x3, blocking collectives: 27.8 us -> 37 us  [the longest x2 25.5 us: per_device(): sums = lax.psum(lax.psum(sums, 'y'), 'x')]
    ppermute x1, waiting for transfers between devices: 8.28 us -> 0.01 us  [per_device(): probes = lax.ppermute(probes, ('y', 'zl'), turned())]
    ppermute x2 -> x4, starting transfers between devices: 5.2 us -> 11.5 us  [joined(): got = lax.ppermute(value, axis, pairs(step))]
    ppermute x2 -> x4, waiting for transfers between devices: 5.91 us -> 10.5 us  [joined(): got = lax.ppermute(value, axis, pairs(step))]
    psum x1, blocking collectives: 12.6 us -> 16.6 us  [per_device(): probes = lax.psum(placed(probe, x, 4), 'x')]
  transfers between devices with their start and end apart: 21 -> 19, of which waited for: 7 -> 6; matrix products, arithmetic and copies ran while one was open for 13% -> 7% of each run, Pallas kernels for 0% -> 0%
where the time goes in v10:
time: 217 us; the launch traced here: 213 us
  blocking collectives  68.6 us (32%)
  starting transfers between devices  64.2 us (30%)
  waiting for transfers between devices  42.2 us (19%)
  between operations  14.9 us (7%)
  local copies, waits for them, and re-layouts  9.59 us (4%)
  other arithmetic  7.01 us (3%)
  matrix products  6.83 us (3%)
    ppermute x9, starting transfers between devices, move(): return lax.ppermute(value, axis, ring(step))  31.1 us
    psum x2, blocking collectives, per_device(): sums = lax.psum(lax.psum(sums, 'y'), 'x')  25.5 us
    all_gather x1, waiting for transfers between devices, per_device(): lax.all_gather(own, ('zh', 'c'), axis=0, tiled=True)  23.8 us
    psum x1, blocking collectives, per_device(): probes = lax.psum(placed(probe, x, 4), 'x')  16.6 us
    psum x1, blocking collectives, per_device(): score = lax.psum(placed(score, zh, 4), 'zh')  12.5 us
    ppermute x4, starting transfers between devices, joined(): got = lax.ppermute(value, axis, pairs(step))  11.5 us
    psum x1, blocking collectives, per_device(): sums = lax.psum(sums, 'zl')  11.5 us
    ppermute x4, waiting for transfers between devices, joined(): got = lax.ppermute(value, axis, pairs(step))  10.5 us
  transfers between devices with their start and end apart: 19, of which 6 were waited for; matrix products, arithmetic and copies ran while one was open for 7% of the time, Pallas kernels for 0%

profile of v10, /device:TPU:24, one launch (start us, length us, event | category | flops | bytes accessed | tf_op | source)
XLA Modules:
  0.0 213.2 jit_solution(5132164832947701111)
XLA Ops:
  7.2 1.8 pad_maximum_fusion
  9.1 1.0 multiply_reduce_fusion.1
  10.1 6.2 %collective-permute-start.4 = (bf16[32,320]{1,0:T(8,128)(2,1)S(1)}, bf16[32,320]{1,0:T(8,128)(2,1)S(1)}, u32[]{:S(2)}, u32[]{:S(2)}) collective-permute-start(bf16[32,320]{1,0:T(8,128)(2,1)S(1)} %get-tuple-element.19), channel_id=1, source_target_pairs={{0,0},{1,32},{2,64},{3,96},{4,128},{5,160},{6,192},{7,224},{8,256}... | collective-permute-start | bytes 61448 | tf_op jit(solution)/shard_map/ppermute | solution.py:87
  16.3 3.7 %collective-permute-done.4 = bf16[32,320]{1,0:T(8,128)(2,1)S(1)} collective-permute-done((bf16[32,320]{1,0:T(8,128)(2,1)S(1)}, bf16[32,320]{1,0:T(8,128)(2,1)S(1)}, u32[]{:S(2)}, u32[]{:S(2)}) %collective-permute-start.4) | collective-permute-done | bytes 20512 | tf_op jit(solution)/shard_map/ppermute | solution.py:87
  20.1 1.9 collective-permute-start.5
  22.0 1.9 collective-permute-start.3
  23.9 3.8 %collective-permute-start.2 = (bf16[192,1024]{1,0:T(8,128)(2,1)}, bf16[192,1024]{1,0:T(8,128)(2,1)S(1)}, u32[]{:S(2)}, u32[]{:S(2)}) collective-permute-start(bf16[192,1024]{1,0:T(8,128)(2,1)} %param.7), channel_id=1, source_target_pairs={{0,64},{32,96},{64,0},{96,32},{1,65},{33,97},{65,1},{97,33},{2,66}... | collective-permute-start | bytes 1179656 | tf_op jit(solution)/shard_map/ppermute | solution.py:35
  27.8 2.0 collective-permute-start.1
  29.8 0.9 dynamic_update_slice.12
  30.7 16.6 %psum.42 = f32[1280]{0:T(1024)S(1)} all-reduce(f32[1280]{0:T(1024)S(1)} %dynamic_update_slice.12), channel_id=1, replica_groups=mesh['zh'=4,'y'=4,'c'=2,'x'=4,'zl'=4] {'x'}, use_global_device_ids=true, to_apply=%region_0.0 | all-reduce | flops 1280 | bytes 10240 | tf_op jit(solution)/shard_map/psum | solution.py:83
  47.3 8.6 %collective-permute-start = (f32[1280]{0:T(1024)S(1)}, f32[1280]{0:T(1024)S(1)}, u32[]{:S(2)}, u32[]{:S(2)}) collective-permute-start(f32[1280]{0:T(1024)S(1)} %psum.42), channel_id=1, source_target_pairs={{0,0},{1,32},{2,64},{3,96},{32,1},{33,33},{34,65},{35,97},{64,2},{... | collective-permute-start | bytes 15368 | tf_op jit(solution)/shard_map/ppermute | solution.py:84
  55.9 1.0 mul.94
  57.1 3.9 %collective-permute-start.6 = (bf16[16,768]{1,0:T(8,128)(2,1)S(1)}, bf16[16,768]{1,0:T(8,128)(2,1)S(1)}, u32[]{:S(2)}, u32[]{:S(2)}) collective-permute-start(bf16[16,768]{1,0:T(8,128)(2,1)S(1)} %reshape.136), channel_id=1, source_target_pairs={{0,4},{4,0},{8,12},{12,8},{1,5},{5,1},{9,13},{13,9},{2,6},{6,2},{1... | collective-permute-start | bytes 73736 | tf_op jit(solution)/shard_map/ppermute | solution.py:44
  61.2 0.2 dynamic_update_slice.14
  61.7 1.2 collective-permute-done.6
  62.9 3.9 %collective-permute-start.7 = (bf16[32,768]{1,0:T(8,128)(2,1)S(1)}, bf16[32,768]{1,0:T(8,128)(2,1)S(1)}, u32[]{:S(2)}, u32[]{:S(2)}) collective-permute-start(bf16[32,768]{1,0:T(8,128)(2,1)S(1)} %pad_maximum_fusion.4), channel_id=1, source_target_pairs={{0,12},{4,8},{8,4},{12,0},{1,13},{5,9},{9,5},{13,1},{2,14},{6,10},... | collective-permute-start | bytes 147464 | tf_op jit(solution)/shard_map/ppermute | solution.py:44
  66.8 3.3 %collective-permute-done.7 = bf16[32,768]{1,0:T(8,128)(2,1)S(1)} collective-permute-done((bf16[32,768]{1,0:T(8,128)(2,1)S(1)}, bf16[32,768]{1,0:T(8,128)(2,1)S(1)}, u32[]{:S(2)}, u32[]{:S(2)}) %collective-permute-start.7) | collective-permute-done | bytes 49184 | tf_op jit(solution)/shard_map/ppermute | solution.py:44
  70.1 0.6 pad_maximum_fusion.3
  70.7 23.8 %all-gather.4.cloned.1.call-done = bf16[1536,1024]{1,0:T(8,128)(2,1)} async-done(((bf16[192,1024]{1,0:T(8,128)(2,1)}), bf16[1536,1024]{1,0:T(8,128)(2,1)}) %all-gather.4.cloned.1.call-update) | async-done | bytes 3145744 | tf_op jit(solution)/shard_map/all_gather | solution.py:77
  94.5 2.1 slice.28
  96.7 0.5 convolution_reduce_fusion
  97.2 2.2 %convolution_convert_fusion = bf16[1280,768]{1,0:T(8,128)(2,1)S(1)} fusion(bf16[1280,1024]{1,0:T(8,128)(2,1)S(1)} %bitcast.42, bf16[192,1024]{1,0:T(8,128)(2,1)S(1)} %collective-permute-done.3, bf16[192,1024]{1,0:T(8,128)(2,1)S(1)} %collective-permute-done.2, bf16[192,1024]{1,0:T(8,128)(2,1)S(1)} %collective-permute-done.1, bf16[192,1024]{1,0:T(8,128)(2,1)S(1)} %copy-done), kind=kOutput, calls=%fused_computation.2 | convolution fusion | flops 2020540416 | bytes 6160384 | tf_op jit(solution)/shard_map/dot_general | solution.py:96
  99.6 1.0 dynamic-slice_bitcast_fusion.1
  100.6 3.0 %collective-permute-start.8 = (bf16[320,768]{1,0:T(8,128)(2,1)}, bf16[320,768]{1,0:T(8,128)(2,1)S(1)}, u32[]{:S(2)}, u32[]{:S(2)}) collective-permute-start(bf16[320,768]{1,0:T(8,128)(2,1)} %get-tuple-element.22), channel_id=1, source_target_pairs={{0,4},{4,8},{8,12},{12,0},{1,5},{5,9},{9,13},{13,1},{2,6},{6,10},{... | collective-permute-start | bytes 1474568 | tf_op jit(solution)/shard_map/ppermute | solution.py:35
  103.8 0.2 convolution_reduce_fusion.3
  104.3 0.2 convolution_reduce_fusion.1
  104.7 4.8 %collective-permute-start.11 = (bf16[320,768]{1,0:T(8,128)(2,1)}, bf16[320,768]{1,0:T(8,128)(2,1)}, u32[]{:S(2)}, u32[]{:S(2)}) collective-permute-start(bf16[320,768]{1,0:T(8,128)(2,1)} %get-tuple-element.20), channel_id=1, source_target_pairs={{0,8},{4,12},{8,0},{12,4},{1,9},{5,13},{9,1},{13,5},{2,10},{6,14},... | collective-permute-start | bytes 1474568 | tf_op jit(solution)/shard_map/ppermute | solution.py:35
  109.5 3.7 %collective-permute-start.12 = (bf16[320,768]{1,0:T(8,128)(2,1)S(1)}, bf16[320,768]{1,0:T(8,128)(2,1)}, u32[]{:S(2)}, u32[]{:S(2)}) collective-permute-start(bf16[320,768]{1,0:T(8,128)(2,1)S(1)} %get-tuple-element.21), channel_id=1, source_target_pairs={{0,12},{4,0},{8,4},{12,8},{1,13},{5,1},{9,5},{13,9},{2,14},{6,2},{... | collective-permute-start | bytes 1474568 | tf_op jit(solution)/shard_map/ppermute | solution.py:35
  113.2 4.1 %collective-permute-done.8 = bf16[320,768]{1,0:T(8,128)(2,1)S(1)} collective-permute-done((bf16[320,768]{1,0:T(8,128)(2,1)}, bf16[320,768]{1,0:T(8,128)(2,1)S(1)}, u32[]{:S(2)}, u32[]{:S(2)}) %collective-permute-start.8) | collective-permute-done | bytes 491552 | tf_op jit(solution)/shard_map/ppermute | solution.py:35
  117.3 1.9 collective-permute-start.9
  119.2 1.9 slice.32
  121.1 7.6 %psum.43 = f32[1664]{0:T(1024)S(1)} all-reduce(f32[1664]{0:T(1024)S(1)} %pad_maximum_fusion.6), channel_id=1, replica_groups=mesh['zh'=4,'y'=4,'c'=2,'x'=4,'zl'=4] {'y'}, use_global_device_ids=true, to_apply=%region_8.9 | all-reduce | flops 1664 | bytes 13312 | tf_op jit(solution)/shard_map/psum | solution.py:121
  128.7 17.9 %psum.44 = f32[1664]{0:T(1024)S(1)} all-reduce(f32[1664]{0:T(1024)S(1)} %psum.43), channel_id=1, replica_groups=mesh['zh'=4,'y'=4,'c'=2,'x'=4,'zl'=4] {'x'}, use_global_device_ids=true, to_apply=%region_9.10 | all-reduce | flops 1664 | bytes 13312 | tf_op jit(solution)/shard_map/psum | solution.py:121
  146.7 1.9 collective-permute-start.10
  148.7 1.4 fusion.9
  150.1 6.1 %collective-permute-done.10 = bf16[128,768]{1,0:T(8,128)(2,1)S(1)} collective-permute-done((bf16[128,768]{1,0:T(8,128)(2,1)S(1)}, bf16[128,768]{1,0:T(8,128)(2,1)S(1)}, u32[]{:S(2)}, u32[]{:S(2)}) %collective-permute-start.10) | collective-permute-done | bytes 196640 | tf_op jit(solution)/shard_map/ppermute | solution.py:44
  156.3 0.3 copy.18
  156.7 6.5 %collective-permute-start.13 = (bf16[192,320]{1,0:T(8,128)(2,1)S(1)}, bf16[192,320]{1,0:T(8,128)(2,1)S(1)}, u32[]{:S(2)}, u32[]{:S(2)}) collective-permute-start(bf16[192,320]{1,0:T(8,128)(2,1)S(1)} %get-tuple-element.23), channel_id=1, source_target_pairs={{0,1},{1,2},{2,3},{3,0},{4,5},{5,6},{6,7},{7,4},{8,9},{9,10},{10,1... | collective-permute-start | bytes 368648 | tf_op jit(solution)/shard_map/ppermute | solution.py:35
  163.3 1.9 collective-permute-start.15
  165.2 3.4 %collective-permute-start.14 = (bf16[192,320]{1,0:T(8,128)(2,1)S(1)}, bf16[192,320]{1,0:T(8,128)(2,1)S(1)}, u32[]{:S(2)}, u32[]{:S(2)}) collective-permute-start(bf16[192,320]{1,0:T(8,128)(2,1)S(1)} %get-tuple-element.25), channel_id=1, source_target_pairs={{0,2},{1,3},{2,0},{3,1},{4,6},{5,7},{6,4},{7,5},{8,10},{9,11},{10,... | collective-permute-start | bytes 368648 | tf_op jit(solution)/shard_map/ppermute | solution.py:35
  168.7 0.5 reshape.141
  169.2 11.5 %psum.45 = f32[1664]{0:T(1024)S(1)} all-reduce(f32[1664]{0:T(1024)S(1)} %psum.44), channel_id=1, replica_groups=mesh['zh'=4,'y'=4,'c'=2,'x'=4,'zl'=4] {'zl'}, use_global_device_ids=true, to_apply=%region_10.11 | all-reduce | flops 1664 | bytes 13312 | tf_op jit(solution)/shard_map/psum | solution.py:126
  181.6 4.8 %collective-permute-start.16 = (bf16[192,320]{1,0:T(8,128)(2,1)S(1)}, bf16[192,320]{1,0:T(8,128)(2,1)S(1)}, u32[]{:S(2)}, u32[]{:S(2)}) collective-permute-start(bf16[192,320]{1,0:T(8,128)(2,1)S(1)} %fusion.14), channel_id=1, source_target_pairs={{0,0},{1,32},{2,64},{3,96},{32,1},{33,33},{34,65},{35,97},{64,2},{... | collective-permute-start | bytes 368648 | tf_op jit(solution)/shard_map/ppermute | solution.py:144
  186.4 2.5 %psum.46 = f32[256]{0:T(256)S(1)} all-reduce(f32[256]{0:T(256)S(1)} %reshape.139), channel_id=1, replica_groups=mesh['zh'=4,'y'=4,'c'=2,'x'=4,'zl'=4] {'c'}, use_global_device_ids=true, to_apply=%region_12.13 | all-reduce | flops 256 | bytes 2048 | tf_op jit(solution)/shard_map/psum | solution.py:141
  189.0 12.5 %psum.47 = f32[1024]{0:T(1024)S(1)} all-reduce(f32[1024]{0:T(1024)S(1)} %dynamic_update_slice.15), channel_id=1, replica_groups=mesh['zh'=4,'y'=4,'c'=2,'x'=4,'zl'=4] {'zh'}, use_global_device_ids=true, to_apply=%region_13.14 | all-reduce | flops 1024 | bytes 8192 | tf_op jit(solution)/shard_map/psum | solution.py:142
  201.5 0.7 select_reduce_fusion
  202.4 0.8 add_convert_fusion
  203.1 3.3 %convolution_multiply_fusion = f32[160,1024]{1,0:T(8,128)} fusion(bf16[1024,1024]{1,0:T(8,128)(2,1)} %bitcast.60, bf16[1024,192]{1,0:T(8,128)(2,1)S(1)} %reshape.141, f32[1024]{0:T(1024)S(1)} %mul.118), kind=kOutput, calls=%fused_computation.10 | convolution fusion | flops 336199680 | bytes 3149824 | tf_op jit(solution)/shard_map/dot_general | solution.py:155
  (90 shorter events, 3.0 us)
Async XLA Ops:
  7.2 53.8 %copy-start = (bf16[192,1024]{1,0:T(8,128)(2,1)S(1)}, bf16[192,1024]{1,0:T(8,128)(2,1)}, u32[]{:S(2)}) copy-start(bf16[192,1024]{1,0:T(8,128)(2,1)} %param.7) | copy-start | bytes 1179652
  7.2 87.4 %all-gather.4.cloned.1.call-start = ((), (), s32[]{:S(2)}) async-start(), calls=%async_computation | async-start | bytes 3538944 | tf_op jit(solution)/shard_map/all_gather | solution.py:77
  9.1 194.1 %all-gather.6.cloned.1.call-start = ((), (), s32[]{:S(2)}) async-start(), calls=%async_computation.1 | async-start | bytes 2621440 | tf_op jit(solution)/shard_map/all_gather | solution.py:79
  10.1 45.8 %copy-start.8 = (bf16[32,320]{1,0:T(8,128)(2,1)}, bf16[32,320]{1,0:T(8,128)(2,1)S(1)}, u32[]{:S(2)}) copy-start(bf16[32,320]{1,0:T(8,128)(2,1)S(1)} %get-tuple-element.19) | copy-start | bytes 61444
  10.1 9.9 %collective-permute-start.4 = (bf16[32,320]{1,0:T(8,128)(2,1)S(1)}, bf16[32,320]{1,0:T(8,128)(2,1)S(1)}, u32[]{:S(2)}, u32[]{:S(2)}) collective-permute-start(bf16[32,320]{1,0:T(8,128)(2,1)S(1)} %get-tuple-element.19), channel_id=1, source_target_pairs={{0,0},{1,32},{2,64},{3,96},{4,128},{5,160},{6,192},{7,224},{8,256}... | collective-permute-start | bytes 61448 | tf_op jit(solution)/shard_map/ppermute | solution.py:87
  20.1 36.9 %collective-permute-start.5 = (bf16[32,160]{1,0:T(8,128)(2,1)S(1)}, bf16[32,160]{1,0:T(8,128)(2,1)S(1)}, u32[]{:S(2)}, u32[]{:S(2)}) collective-permute-start(bf16[32,160]{1,0:T(8,128)(2,1)S(1)} %get-tuple-element.35), channel_id=1, source_target_pairs={{0,16},{16,0},{1,17},{17,1},{2,18},{18,2},{3,19},{19,3},{4,20},{20... | collective-permute-start | bytes 30728 | tf_op jit(solution)/shard_map/ppermute | solution.py:90
  22.0 75.2 %collective-permute-start.3 = (bf16[192,1024]{1,0:T(8,128)(2,1)}, bf16[192,1024]{1,0:T(8,128)(2,1)S(1)}, u32[]{:S(2)}, u32[]{:S(2)}) collective-permute-start(bf16[192,1024]{1,0:T(8,128)(2,1)} %param.7), channel_id=1, source_target_pairs={{0,32},{32,64},{64,96},{96,0},{1,33},{33,65},{65,97},{97,1},{2,34}... | collective-permute-start | bytes 1179656 | tf_op jit(solution)/shard_map/ppermute | solution.py:35
  23.9 73.3 %collective-permute-start.2 = (bf16[192,1024]{1,0:T(8,128)(2,1)}, bf16[192,1024]{1,0:T(8,128)(2,1)S(1)}, u32[]{:S(2)}, u32[]{:S(2)}) collective-permute-start(bf16[192,1024]{1,0:T(8,128)(2,1)} %param.7), channel_id=1, source_target_pairs={{0,64},{32,96},{64,0},{96,32},{1,65},{33,97},{65,1},{97,33},{2,66}... | collective-permute-start | bytes 1179656 | tf_op jit(solution)/shard_map/ppermute | solution.py:35
  27.8 69.4 %collective-permute-start.1 = (bf16[192,1024]{1,0:T(8,128)(2,1)}, bf16[192,1024]{1,0:T(8,128)(2,1)S(1)}, u32[]{:S(2)}, u32[]{:S(2)}) collective-permute-start(bf16[192,1024]{1,0:T(8,128)(2,1)} %param.7), channel_id=1, source_target_pairs={{0,96},{32,0},{64,32},{96,64},{1,97},{33,1},{65,33},{97,65},{2,98}... | collective-permute-start | bytes 1179656 | tf_op jit(solution)/shard_map/ppermute | solution.py:35
  47.3 19.5 %collective-permute-start = (f32[1280]{0:T(1024)S(1)}, f32[1280]{0:T(1024)S(1)}, u32[]{:S(2)}, u32[]{:S(2)}) collective-permute-start(f32[1280]{0:T(1024)S(1)} %psum.42), channel_id=1, source_target_pairs={{0,0},{1,32},{2,64},{3,96},{32,1},{33,33},{34,65},{35,97},{64,2},{... | collective-permute-start | bytes 15368 | tf_op jit(solution)/shard_map/ppermute | solution.py:84
  57.1 5.7 %collective-permute-start.6 = (bf16[16,768]{1,0:T(8,128)(2,1)S(1)}, bf16[16,768]{1,0:T(8,128)(2,1)S(1)}, u32[]{:S(2)}, u32[]{:S(2)}) collective-permute-start(bf16[16,768]{1,0:T(8,128)(2,1)S(1)} %reshape.136), channel_id=1, source_target_pairs={{0,4},{4,0},{8,12},{12,8},{1,5},{5,1},{9,13},{13,9},{2,6},{6,2},{1... | collective-permute-start | bytes 73736 | tf_op jit(solution)/shard_map/ppermute | solution.py:44
  62.9 7.2 %collective-permute-start.7 = (bf16[32,768]{1,0:T(8,128)(2,1)S(1)}, bf16[32,768]{1,0:T(8,128)(2,1)S(1)}, u32[]{:S(2)}, u32[]{:S(2)}) collective-permute-start(bf16[32,768]{1,0:T(8,128)(2,1)S(1)} %pad_maximum_fusion.4), channel_id=1, source_target_pairs={{0,12},{4,8},{8,4},{12,0},{1,13},{5,9},{9,5},{13,1},{2,14},{6,10},... | collective-permute-start | bytes 147464 | tf_op jit(solution)/shard_map/ppermute | solution.py:44
  97.2 2.3 %copy-start.1 = (bf16[192,1024]{1,0:T(8,128)(2,1)}, bf16[192,1024]{1,0:T(8,128)(2,1)S(1)}, u32[]{:S(2)}) copy-start(bf16[192,1024]{1,0:T(8,128)(2,1)S(1)} %collective-permute-done.3) | copy-start | bytes 1179652
  97.2 2.3 %copy-start.3 = (bf16[192,1024]{1,0:T(8,128)(2,1)}, bf16[192,1024]{1,0:T(8,128)(2,1)S(1)}, u32[]{:S(2)}) copy-start(bf16[192,1024]{1,0:T(8,128)(2,1)S(1)} %collective-permute-done.2) | copy-start | bytes 1179652
  97.2 2.3 %copy-start.5 = (bf16[192,1024]{1,0:T(8,128)(2,1)}, bf16[192,1024]{1,0:T(8,128)(2,1)S(1)}, u32[]{:S(2)}) copy-start(bf16[192,1024]{1,0:T(8,128)(2,1)S(1)} %collective-permute-done.1) | copy-start | bytes 1179652
  99.5 4.3 %copy-start.6 = (bf16[192,1024]{1,0:T(8,128)(2,1)S(1)}, bf16[192,1024]{1,0:T(8,128)(2,1)}, u32[]{:S(2)}) copy-start(bf16[192,1024]{1,0:T(8,128)(2,1)} %copy-done.5) | copy-start | bytes 1179652
  99.5 4.5 %copy-start.4 = (bf16[192,1024]{1,0:T(8,128)(2,1)S(1)}, bf16[192,1024]{1,0:T(8,128)(2,1)}, u32[]{:S(2)}) copy-start(bf16[192,1024]{1,0:T(8,128)(2,1)} %copy-done.3) | copy-start | bytes 1179652
  99.5 4.8 %copy-start.2 = (bf16[192,1024]{1,0:T(8,128)(2,1)S(1)}, bf16[192,1024]{1,0:T(8,128)(2,1)}, u32[]{:S(2)}) copy-start(bf16[192,1024]{1,0:T(8,128)(2,1)} %copy-done.1) | copy-start | bytes 1179652
  99.5 17.7 %copy-start.7 = (bf16[64,768]{1,0:T(8,128)(2,1)S(1)}, bf16[64,768]{1,0:T(8,128)(2,1)}, u32[]{:S(2)}) copy-start(bf16[64,768]{1,0:T(8,128)(2,1)} %pad_maximum_fusion.3) | copy-start | bytes 294916
  100.6 16.7 %collective-permute-start.8 = (bf16[320,768]{1,0:T(8,128)(2,1)}, bf16[320,768]{1,0:T(8,128)(2,1)S(1)}, u32[]{:S(2)}, u32[]{:S(2)}) collective-permute-start(bf16[320,768]{1,0:T(8,128)(2,1)} %get-tuple-element.22), channel_id=1, source_target_pairs={{0,4},{4,8},{8,12},{12,0},{1,5},{5,9},{9,13},{13,1},{2,6},{6,10},{... | collective-permute-start | bytes 1474568 | tf_op jit(solution)/shard_map/ppermute | solution.py:35
  104.7 44.0 %collective-permute-start.11 = (bf16[320,768]{1,0:T(8,128)(2,1)}, bf16[320,768]{1,0:T(8,128)(2,1)}, u32[]{:S(2)}, u32[]{:S(2)}) collective-permute-start(bf16[320,768]{1,0:T(8,128)(2,1)} %get-tuple-element.20), channel_id=1, source_target_pairs={{0,8},{4,12},{8,0},{12,4},{1,9},{5,13},{9,1},{13,5},{2,10},{6,14},... | collective-permute-start | bytes 1474568 | tf_op jit(solution)/shard_map/ppermute | solution.py:35
  109.5 39.2 %collective-permute-start.12 = (bf16[320,768]{1,0:T(8,128)(2,1)S(1)}, bf16[320,768]{1,0:T(8,128)(2,1)}, u32[]{:S(2)}, u32[]{:S(2)}) collective-permute-start(bf16[320,768]{1,0:T(8,128)(2,1)S(1)} %get-tuple-element.21), channel_id=1, source_target_pairs={{0,12},{4,0},{8,4},{12,8},{1,13},{5,1},{9,5},{13,9},{2,14},{6,2},{... | collective-permute-start | bytes 1474568 | tf_op jit(solution)/shard_map/ppermute | solution.py:35
  117.3 29.4 %collective-permute-start.9 = (bf16[64,768]{1,0:T(8,128)(2,1)S(1)}, bf16[64,768]{1,0:T(8,128)(2,1)S(1)}, u32[]{:S(2)}, u32[]{:S(2)}) collective-permute-start(bf16[64,768]{1,0:T(8,128)(2,1)S(1)} %copy-done.7), channel_id=1, source_target_pairs={{0,1},{1,0},{2,3},{3,2},{4,5},{5,4},{6,7},{7,6},{8,9},{9,8},{10,11... | collective-permute-start | bytes 294920 | tf_op jit(solution)/shard_map/ppermute | solution.py:44
  146.7 21.9 %copy-start.9 = (bf16[32,320]{1,0:T(8,128)(2,1)S(1)}, bf16[32,320]{1,0:T(8,128)(2,1)}, u32[]{:S(2)}) copy-start(bf16[32,320]{1,0:T(8,128)(2,1)} %copy-done.8) | copy-start | bytes 61444
  146.7 9.5 %collective-permute-start.10 = (bf16[128,768]{1,0:T(8,128)(2,1)S(1)}, bf16[128,768]{1,0:T(8,128)(2,1)S(1)}, u32[]{:S(2)}, u32[]{:S(2)}) collective-permute-start(bf16[128,768]{1,0:T(8,128)(2,1)S(1)} %pad_maximum_fusion.2), channel_id=1, source_target_pairs={{0,3},{1,2},{2,1},{3,0},{4,7},{5,6},{6,5},{7,4},{8,11},{9,10},{10,... | collective-permute-start | bytes 589832 | tf_op jit(solution)/shard_map/ppermute | solution.py:44
  156.3 45.2 %copy-start.10 = (s32[1024]{0:T(1024)S(1)}, s32[1024]{0:T(1024)}, u32[]{:S(2)}) copy-start(s32[1024]{0:T(1024)} %param.13) | copy-start | bytes 12292
  156.3 45.9 %copy-start.11 = (f32[1024]{0:T(1024)S(1)}, f32[1024]{0:T(1024)}, u32[]{:S(2)}) copy-start(f32[1024]{0:T(1024)} %param.12) | copy-start | bytes 12292
  156.7 24.0 %collective-permute-start.13 = (bf16[192,320]{1,0:T(8,128)(2,1)S(1)}, bf16[192,320]{1,0:T(8,128)(2,1)S(1)}, u32[]{:S(2)}, u32[]{:S(2)}) collective-permute-start(bf16[192,320]{1,0:T(8,128)(2,1)S(1)} %get-tuple-element.23), channel_id=1, source_target_pairs={{0,1},{1,2},{2,3},{3,0},{4,5},{5,6},{6,7},{7,4},{8,9},{9,10},{10,1... | collective-permute-start | bytes 368648 | tf_op jit(solution)/shard_map/ppermute | solution.py:35
  163.3 17.5 %collective-permute-start.15 = (bf16[192,320]{1,0:T(8,128)(2,1)S(1)}, bf16[192,320]{1,0:T(8,128)(2,1)S(1)}, u32[]{:S(2)}, u32[]{:S(2)}) collective-permute-start(bf16[192,320]{1,0:T(8,128)(2,1)S(1)} %get-tuple-element.24), channel_id=1, source_target_pairs={{0,3},{1,0},{2,1},{3,2},{4,7},{5,4},{6,5},{7,6},{8,11},{9,8},{10,9... | collective-permute-start | bytes 368648 | tf_op jit(solution)/shard_map/ppermute | solution.py:35
  165.2 15.5 %collective-permute-start.14 = (bf16[192,320]{1,0:T(8,128)(2,1)S(1)}, bf16[192,320]{1,0:T(8,128)(2,1)S(1)}, u32[]{:S(2)}, u32[]{:S(2)}) collective-permute-start(bf16[192,320]{1,0:T(8,128)(2,1)S(1)} %get-tuple-element.25), channel_id=1, source_target_pairs={{0,2},{1,3},{2,0},{3,1},{4,6},{5,7},{6,4},{7,5},{8,10},{9,11},{10,... | collective-permute-start | bytes 368648 | tf_op jit(solution)/shard_map/ppermute | solution.py:35
  181.6 20.8 %collective-permute-start.16 = (bf16[192,320]{1,0:T(8,128)(2,1)S(1)}, bf16[192,320]{1,0:T(8,128)(2,1)S(1)}, u32[]{:S(2)}, u32[]{:S(2)}) collective-permute-start(bf16[192,320]{1,0:T(8,128)(2,1)S(1)} %fusion.14), channel_id=1, source_target_pairs={{0,0},{1,32},{2,64},{3,96},{32,1},{33,33},{34,65},{35,97},{64,2},{... | collective-permute-start | bytes 368648 | tf_op jit(solution)/shard_map/ppermute | solution.py:144
Sparse Core Ops, SparseCore 0:
  10.7 83.7 all-gather.3
  121.2 42.1 all-gather.5

commit v11 on v10

--- a/solution.py
+++ b/solution.py
@@ -20,9 +20,9 @@
     return [(i, (i + step) % 4) for i in range(4)]
 
 
-def swapped():
+def swapped(flip):
     return [
-        (place(zh, y, c, x, zl), place(x, zl, c, zh, y))
+        (place(zh, y, c, x, zl), place(x, zl, c ^ flip, zh, y))
         for zh in range(4) for y in range(4) for c in range(2) for x in range(4) for zl in range(4)
     ]
 
@@ -55,6 +55,15 @@
     return jnp.stack(terms)
 
 
+def pack(value, width):
+    terms = in_three(value).reshape(-1)
+    return jnp.pad(terms, (0, -terms.shape[0] % (8 * width))).reshape(-1, width)
+
+
+def unpack(rows, size):
+    return rows.reshape(-1)[: 3 * size].reshape(3, size).sum(0)
+
+
 def placed(value, index, count):
     size = value.shape[0]
     return lax.dynamic_update_slice(jnp.zeros((size * count,), value.dtype), value, (index * size,))
@@ -78,32 +87,34 @@
     weight = stack[:, :, :block].reshape(-1, width)
     rights = lax.all_gather(stack[:, :, block:], "y", axis=0, tiled=False)
 
+    left_cols = lax.dynamic_slice(member_left, (0, (x * 4 + zl) * cols), (members, cols)).astype(f32)
+    payload = jnp.concatenate([left_cols, probe[None, :]], axis=0)
+    mine = jnp.where(first, payload[:, :block], payload[:, block:])
+    other = jnp.where(first, left_cols[:, block:], left_cols[:, :block])
+    mine = lax.ppermute(mine, AXES, swapped(0))
+    other = lax.ppermute(other, AXES, swapped(1))
+    mine, other = lax.optimization_barrier((mine, other))
+
+    direction = jnp.sum(down_weight.astype(f32) * mine[members][:, None], axis=0)
+    inner = jnp.sum(
+        features.astype(f32).reshape(members, tokens, width) * member_right.astype(f32)[:, None, :],
+        axis=2,
+    ).reshape(rows)
+    left_dot = jnp.sum(left_cols * probe[None, :], axis=1)
+    here = y * 2 + c
+    early = jnp.concatenate([direction, placed(inner, here, 8), placed(left_dot, here, 8)])
+    early = lax.psum(early, ("y", "c"))
+
+    features, early = lax.optimization_barrier((features, early))
     around = [features] + [move(features, "y", -j) for j in (1, 2, 3)]
+    direction, inner, left_dot = jnp.split(early, [width, width + 2 * many])
+    direction = lax.psum(direction, "zh")
 
-    probes = lax.psum(placed(probe, x, 4), "x")
-    probes = lax.ppermute(probes, ("y", "zl"), turned())
+    mine = mine[:members]
+    lefts = jnp.where(first, jnp.concatenate([mine, other], 0), jnp.concatenate([other, mine], 0))
+    lefts = jnp.pad(lefts.astype(bf16), ((0, 0), (0, 192 - block))).reshape(-1, many)
+    lefts = joined(lefts, "x", x)
 
-    left_cols = lax.dynamic_slice(member_left, (0, (x * 4 + zl) * cols), (members, cols))
-    lefts = lax.ppermute(left_cols, AXES, swapped())
-    mine = jnp.where(first, lefts[:, :block], lefts[:, block:])
-    other = jnp.where(first, lefts[:, block:], lefts[:, :block])
-    other = lax.ppermute(other, "c", [(0, 1), (1, 0)])
-    lefts = jnp.where(first, jnp.concatenate([mine, other], 0), jnp.concatenate([other, mine], 0))
-    lefts = jnp.pad(lefts, ((0, 0), (0, 192 - block))).reshape(-1, many)
-    lefts = joined(lefts, "x", x)
-    left_cols = left_cols.astype(f32)
-
-    part = lax.dot_general(
-        weight, jnp.concatenate(around, axis=0), (((1,), (1,)), ((), ())), preferred_element_type=f32
-    ).astype(bf16).reshape(4, cols, many)
-    parts = []
-    for k in range(4):
-        one = lax.dynamic_index_in_dim(part, lax.rem(x + k, 4), 0, keepdims=False)
-        parts.append(one if k == 0 else move(one, "x", k))
-
-    direction = lax.dot_general(
-        in_three(probes), weight, (((1,), (0,)), ((), ())), preferred_element_type=f32
-    ).sum(0)
     along = jnp.stack([
         lax.dot_general(
             in_three(direction), f, (((1,), (1,)), ((), ())), preferred_element_type=f32
@@ -111,26 +122,37 @@
         for f in around
     ])
     along = jnp.roll(along, y, axis=0).reshape(many)
-    inner = jnp.sum(
-        features.astype(f32).reshape(members, tokens, width) * member_right.astype(f32)[:, None, :],
-        axis=2,
-    ).reshape(rows)
-    left_dot = jnp.sum(left_cols * probe[None, :], axis=1)
-    sums = jnp.concatenate([along, placed(inner, y, 4), placed(left_dot, y, 4)])
-    sums, lefts, parts[1] = lax.optimization_barrier((sums, lefts, parts[1]))
-    sums = lax.psum(lax.psum(sums, "y"), "x")
+    inner, left_dot = inner.reshape(4, 2, -1), left_dot.reshape(4, 2, -1)
+    inner = jnp.where(first, inner[:, 0], inner[:, 1]).reshape(-1)
+    left_dot = jnp.where(first, left_dot[:, 0], left_dot[:, 1]).reshape(-1)
+    sums = jnp.concatenate([along, inner, left_dot])
+    size = sums.shape[0]
+
+    part = lax.dot_general(
+        weight, jnp.concatenate(around, axis=0), (((1,), (1,)), ((), ())), preferred_element_type=f32
+    ).astype(bf16).reshape(4, cols, many)
+    ride = pack(sums, many)
+    parts = []
+    for k in range(4):
+        one = lax.dynamic_index_in_dim(part, lax.rem(x + k, 4), 0, keepdims=False)
+        one = jnp.concatenate([one, ride], axis=0)
+        parts.append(one if k == 0 else move(one, "x", k))
+    lefts, parts[1] = lax.optimization_barrier((lefts, parts[1]))
     lefts = joined(lefts, "zl", zl)
-    total = sum(p.astype(f32) for p in parts).astype(bf16)
-    sums, lefts, total = lax.optimization_barrier((sums, lefts, total))
+    total = sum(p.astype(f32) for p in parts)
+    ride = pack(unpack(total[cols:], size), cols)
 
-    sums = lax.psum(sums, "zl")
-    total = total.T.reshape(4, rows, cols)
+    total = total[:cols].astype(bf16).T.reshape(4, rows, cols)
     parts = []
     for k in range(4):
         one = lax.dynamic_index_in_dim(total, lax.rem(zl + k + 4 - y, 4), 0, keepdims=False)
+        one = jnp.concatenate([one, ride], axis=0)
         parts.append(one if k == 0 else move(one, "zl", k))
-    total = sum(p.astype(f32) for p in parts).astype(bf16)
-    sums, total = lax.optimization_barrier((sums, total))
+    total = sum(p.astype(f32) for p in parts)
+    sums = unpack(total[rows:], size)
+    total = total[:rows].astype(bf16)
+
+
     along, inner, left_dot = jnp.split(sums, [many, 2 * many])
     inner = spread * inner
     dots = along + inner * jnp.repeat(left_dot, tokens)

time: 217 us -> 208 us (0.959)
  starting transfers between devices: 64.2 us -> 87.1 us
  waiting for transfers between devices: 42.2 us -> 23.7 us
  blocking collectives: 68.6 us -> 54.8 us
    all_gather x1, waiting for transfers between devices: 23.8 us -> 0.02 us  [per_device(): lax.all_gather(own, ('zh', 'c'), axis=0, tiled=True)]
    ppermute x4, starting transfers between devices: 11.5 us -> 28 us  [joined(): got = lax.ppermute(value, axis, pairs(step))]
    psum x4 -> x2, blocking collectives: 53.6 us -> 40 us  [the longest x1 22.2 us: per_device(): early = lax.psum(early, ('y', 'c'))]
    ppermute x9, starting transfers between devices: 31.1 us -> 43.2 us  [move(): return lax.ppermute(value, axis, ring(step))]
    ppermute x3 -> x2, starting transfers between devices: 16.7 us -> 9.17 us  [the longest x1 5.62 us: per_device(): other = lax.ppermute(other, AXES, swapped(1))]
    ppermute x9, waiting for transfers between devices: 4.11 us -> 9.34 us  [move(): return lax.ppermute(value, axis, ring(step))]
  transfers between devices with their start and end apart: 19 -> 18, of which waited for: 6 -> 4; matrix products, arithmetic and copies ran while one was open for 7% -> 7% of each run, Pallas kernels for 0% -> 0%
where the time goes in v11:
time: 208 us; the launch traced here: 205 us
  starting transfers between devices  87.1 us (42%)
  blocking collectives  54.8 us (26%)
  waiting for transfers between devices  23.7 us (11%)
  between operations  14.8 us (7%)
  local copies, waits for them, and re-layouts  9.18 us (4%)
  other arithmetic  8.62 us (4%)
  matrix products  6.36 us (3%)
    ppermute x9, starting transfers between devices, move(): return lax.ppermute(value, axis, ring(step))  43.2 us
    ppermute x4, starting transfers between devices, joined(): got = lax.ppermute(value, axis, pairs(step))  28 us
    psum x1, blocking collectives, per_device(): early = lax.psum(early, ('y', 'c'))  22.2 us
    psum x1, blocking collectives, per_device(): direction = lax.psum(direction, 'zh')  17.8 us
    psum x1, blocking collectives, per_device(): score = lax.psum(placed(score, zh, 4), 'zh')  12.4 us
    ppermute x4, waiting for transfers between devices, joined(): got = lax.ppermute(value, axis, pairs(step))  10.6 us
    ppermute x9, waiting for transfers between devices, move(): return lax.ppermute(value, axis, ring(step))  9.34 us
    ppermute x1, starting transfers between devices, per_device(): total = lax.ppermute(total, ('y', 'zl'), turned()).astype(f32)  6.65 us
  transfers between devices with their start and end apart: 18, of which 4 were waited for; matrix products, arithmetic and copies ran while one was open for 7% of the time, Pallas kernels for 0%

profile of v11, /device:TPU:24, one launch (start us, length us, event | category | flops | bytes accessed | tf_op | source)
XLA Modules:
  0.0 204.6 jit_solution(6422357222195445130)
XLA Ops:
  7.2 1.8 pad_maximum_fusion.4
  9.1 0.8 dynamic-slice_convert_fusion
  10.1 5.6 %collective-permute-start.1 = (bf16[32,160]{1,0:T(8,128)(2,1)S(1)}, bf16[32,160]{1,0:T(8,128)(2,1)S(1)}, u32[]{:S(2)}, u32[]{:S(2)}) collective-permute-start(bf16[32,160]{1,0:T(8,128)(2,1)S(1)} %slice_select_fusion), channel_id=1, source_target_pairs={{0,16},{1,48},{2,80},{3,112},{4,144},{5,176},{6,208},{7,240},{8,27... | collective-permute-start | bytes 30728 | tf_op jit(solution)/shard_map/ppermute | solution.py:95
  15.7 0.7 broadcast_in_dim.37
  16.5 3.6 %collective-permute-start = (f32[33,160]{1,0:T(8,128)S(1)}, f32[33,160]{1,0:T(8,128)S(1)}, u32[]{:S(2)}, u32[]{:S(2)}) collective-permute-start(f32[33,160]{1,0:T(8,128)S(1)} %fusion.12), channel_id=1, source_target_pairs={{0,0},{1,32},{2,64},{3,96},{4,128},{5,160},{6,192},{7,224},{8,256}... | collective-permute-start | bytes 63368 | tf_op jit(solution)/shard_map/ppermute | solution.py:94
  20.0 1.0 mul.110
  21.1 0.2 multiply_reduce_fusion
  21.3 1.0 multiply_reduce_fusion.2
  22.3 0.2 dynamic_update_slice.10
  22.5 0.2 dynamic_update_slice.9
  22.8 3.6 %collective-permute-done = f32[33,160]{1,0:T(8,128)S(1)} collective-permute-done((f32[33,160]{1,0:T(8,128)S(1)}, f32[33,160]{1,0:T(8,128)S(1)}, u32[]{:S(2)}, u32[]{:S(2)}) %collective-permute-start) | collective-permute-done | bytes 21152 | tf_op jit(solution)/shard_map/ppermute | solution.py:94
  26.6 22.2 %psum.28 = f32[2816]{0:T(1024)S(1)} all-reduce(f32[2816]{0:T(1024)S(1)} %pad_maximum_fusion.16), channel_id=1, replica_groups=mesh['zh'=4,'y'=4,'c'=2,'x'=4,'zl'=4] {'y','c'}, use_global_device_ids=true, to_apply=%region_3.4 | all-reduce | flops 2816 | bytes 22528 | tf_op jit(solution)/shard_map/psum | solution.py:106
  48.8 6.6 %collective-permute-start.4 = (bf16[192,1024]{1,0:T(8,128)(2,1)S(1)}, bf16[192,1024]{1,0:T(8,128)(2,1)S(1)}, u32[]{:S(2)}, u32[]{:S(2)}) collective-permute-start(bf16[192,1024]{1,0:T(8,128)(2,1)S(1)} %copy-done), channel_id=1, source_target_pairs={{0,32},{32,64},{64,96},{96,0},{1,33},{33,65},{65,97},{97,1},{2,34}... | collective-permute-start | bytes 1179656 | tf_op jit(solution)/shard_map/ppermute | solution.py:35
  55.4 1.9 collective-permute-start.3
  57.3 2.8 %collective-permute-start.2 = (bf16[192,1024]{1,0:T(8,128)(2,1)S(1)}, bf16[192,1024]{1,0:T(8,128)(2,1)S(1)}, u32[]{:S(2)}, u32[]{:S(2)}) collective-permute-start(bf16[192,1024]{1,0:T(8,128)(2,1)S(1)} %copy-done), channel_id=1, source_target_pairs={{0,96},{32,0},{64,32},{96,64},{1,97},{33,1},{65,33},{97,65},{2,98}... | collective-permute-start | bytes 1179656 | tf_op jit(solution)/shard_map/ppermute | solution.py:35
  60.2 16.5 %collective-permute-start.5 = (bf16[16,768]{1,0:T(8,128)(2,1)S(1)}, bf16[16,768]{1,0:T(8,128)(2,1)S(1)}, u32[]{:S(2)}, u32[]{:S(2)}) collective-permute-start(bf16[16,768]{1,0:T(8,128)(2,1)S(1)} %reshape.341), channel_id=1, source_target_pairs={{0,4},{4,0},{8,12},{12,8},{1,5},{5,1},{9,13},{13,9},{2,6},{6,2},{1... | collective-permute-start | bytes 73736 | tf_op jit(solution)/shard_map/ppermute | solution.py:44
  76.8 17.8 %psum.29 = f32[1024]{0:T(1024)S(1)} all-reduce(f32[1024]{0:T(1024)S(1)} %split.22), channel_id=1, replica_groups=mesh['zh'=4,'y'=4,'c'=2,'x'=4,'zl'=4] {'zh'}, use_global_device_ids=true, to_apply=%region_4.5 | all-reduce | flops 1024 | bytes 8192 | tf_op jit(solution)/shard_map/psum | solution.py:111
  94.6 0.2 convolution_reduce_fusion.3
  95.2 0.2 convolution_reduce_fusion
  95.4 0.2 convolution_reduce_fusion.1
  95.7 0.2 convolution_reduce_fusion.2
  96.2 2.1 %slice.92 = bf16[4,2,160,1024]{3,2,1,0:T(8,128)(2,1)S(1)} slice(bf16[4,2,192,1024]{3,2,1,0:T(8,128)(2,1)} %bitcast.40), slice={[0:4], [0:2], [0:160], [0:1024]} | slice | bytes 5242880 | tf_op jit(solution)/shard_map/slice | solution.py:87
  98.4 2.2 %convolution_convert_fusion = bf16[1280,768]{1,0:T(8,128)(2,1)S(1)} fusion(bf16[1280,1024]{1,0:T(8,128)(2,1)S(1)} %bitcast.42, bf16[192,1024]{1,0:T(8,128)(2,1)S(1)} %collective-permute-done.4, bf16[192,1024]{1,0:T(8,128)(2,1)S(1)} %collective-permute-done.3, bf16[192,1024]{1,0:T(8,128)(2,1)S(1)} %collective-permute-done.2, bf16[192,1024]{1,0:T(8,128)(2,1)S(1)} %copy-done), kind=kOutput, calls=%fused_computation.2 | convolution fusion | flops 2020540416 | bytes 6160384 | tf_op jit(solution)/shard_map/dot_general | solution.py:131
  100.7 1.1 pad_maximum_fusion.2
  101.8 1.9 collective-permute-start.7
  103.8 15.9 %collective-permute-start.8 = (bf16[328,768]{1,0:T(8,128)(2,1)}, bf16[328,768]{1,0:T(8,128)(2,1)S(1)}, u32[]{:S(2)}, u32[]{:S(2)}) collective-permute-start(bf16[328,768]{1,0:T(8,128)(2,1)} %get-tuple-element.34), channel_id=1, source_target_pairs={{0,8},{4,12},{8,0},{12,4},{1,9},{5,13},{9,1},{13,5},{2,10},{6,14},... | collective-permute-start | bytes 1511432 | tf_op jit(solution)/shard_map/ppermute | solution.py:35
  119.7 4.5 %collective-permute-start.9 = (bf16[328,768]{1,0:T(8,128)(2,1)S(1)}, bf16[328,768]{1,0:T(8,128)(2,1)}, u32[]{:S(2)}, u32[]{:S(2)}) collective-permute-start(bf16[328,768]{1,0:T(8,128)(2,1)S(1)} %get-tuple-element.35), channel_id=1, source_target_pairs={{0,12},{4,0},{8,4},{12,8},{1,13},{5,1},{9,5},{13,9},{2,14},{6,2},{... | collective-permute-start | bytes 1511432 | tf_op jit(solution)/shard_map/ppermute | solution.py:35
  124.2 1.9 collective-permute-start.6
  126.3 10.6 %collective-permute-done.6 = bf16[32,768]{1,0:T(8,128)(2,1)S(1)} collective-permute-done((bf16[32,768]{1,0:T(8,128)(2,1)S(1)}, bf16[32,768]{1,0:T(8,128)(2,1)S(1)}, u32[]{:S(2)}, u32[]{:S(2)}) %collective-permute-start.6) | collective-permute-done | bytes 49184 | tf_op jit(solution)/shard_map/ppermute | solution.py:44
  137.0 1.9 slice.108
  138.9 7.2 %collective-permute-start.14 = (bf16[64,768]{1,0:T(8,128)(2,1)S(1)}, bf16[64,768]{1,0:T(8,128)(2,1)S(1)}, u32[]{:S(2)}, u32[]{:S(2)}) collective-permute-start(bf16[64,768]{1,0:T(8,128)(2,1)S(1)} %pad_maximum_fusion.11), channel_id=1, source_target_pairs={{0,1},{1,0},{2,3},{3,2},{4,5},{5,4},{6,7},{7,6},{8,9},{9,8},{10,11... | collective-permute-start | bytes 294920 | tf_op jit(solution)/shard_map/ppermute | solution.py:44
  146.1 1.3 convert_add_fusion
  147.7 0.3 copy.23
  148.2 1.9 collective-permute-start.10
  150.1 4.1 %collective-permute-start.11 = (bf16[208,320]{1,0:T(8,128)(2,1)S(1)}, bf16[208,320]{1,0:T(8,128)(2,1)S(1)}, u32[]{:S(2)}, u32[]{:S(2)}) collective-permute-start(bf16[208,320]{1,0:T(8,128)(2,1)S(1)} %get-tuple-element.31), channel_id=1, source_target_pairs={{0,2},{1,3},{2,0},{3,1},{4,6},{5,7},{6,4},{7,5},{8,10},{9,11},{10,... | collective-permute-start | bytes 399368 | tf_op jit(solution)/shard_map/ppermute | solution.py:35
  154.2 3.6 %collective-permute-start.12 = (bf16[208,320]{1,0:T(8,128)(2,1)S(1)}, bf16[208,320]{1,0:T(8,128)(2,1)S(1)}, u32[]{:S(2)}, u32[]{:S(2)}) collective-permute-start(bf16[208,320]{1,0:T(8,128)(2,1)S(1)} %get-tuple-element.32), channel_id=1, source_target_pairs={{0,3},{1,0},{2,1},{3,2},{4,7},{5,4},{6,5},{7,6},{8,11},{9,8},{10,9... | collective-permute-start | bytes 399368 | tf_op jit(solution)/shard_map/ppermute | solution.py:35
  157.8 2.5 %collective-permute-start.15 = (bf16[128,768]{1,0:T(8,128)(2,1)S(1)}, bf16[128,768]{1,0:T(8,128)(2,1)S(1)}, u32[]{:S(2)}, u32[]{:S(2)}) collective-permute-start(bf16[128,768]{1,0:T(8,128)(2,1)S(1)} %pad_maximum_fusion.10), channel_id=1, source_target_pairs={{0,3},{1,2},{2,1},{3,0},{4,7},{5,6},{6,5},{7,4},{8,11},{9,10},{10,... | collective-permute-start | bytes 589832 | tf_op jit(solution)/shard_map/ppermute | solution.py:44
  160.3 8.5 %collective-permute-done.11 = bf16[208,320]{1,0:T(8,128)(2,1)S(1)} collective-permute-done((bf16[208,320]{1,0:T(8,128)(2,1)S(1)}, bf16[208,320]{1,0:T(8,128)(2,1)S(1)}, u32[]{:S(2)}, u32[]{:S(2)}) %collective-permute-start.11) | collective-permute-done | bytes 133152 | tf_op jit(solution)/shard_map/ppermute | solution.py:35
  168.8 0.8 collective-permute-done.12
  170.2 0.2 tanh_reduce_fusion
  170.5 6.7 %collective-permute-start.13 = (bf16[192,320]{1,0:T(8,128)(2,1)S(1)}, bf16[192,320]{1,0:T(8,128)(2,1)S(1)}, u32[]{:S(2)}, u32[]{:S(2)}) collective-permute-start(bf16[192,320]{1,0:T(8,128)(2,1)S(1)} %slice.131), channel_id=1, source_target_pairs={{0,0},{1,32},{2,64},{3,96},{32,1},{33,33},{34,65},{35,97},{64,2},{... | collective-permute-start | bytes 368648 | tf_op jit(solution)/shard_map/ppermute | solution.py:166
  177.2 2.5 %psum.30 = f32[256]{0:T(256)S(1)} all-reduce(f32[256]{0:T(256)S(1)} %reshape.349), channel_id=1, replica_groups=mesh['zh'=4,'y'=4,'c'=2,'x'=4,'zl'=4] {'c'}, use_global_device_ids=true, to_apply=%region_12.13 | all-reduce | flops 256 | bytes 2048 | tf_op jit(solution)/shard_map/psum | solution.py:163
  179.7 0.2 dynamic_update_slice.11
  179.8 12.4 %psum.31 = f32[1024]{0:T(1024)S(1)} all-reduce(f32[1024]{0:T(1024)S(1)} %dynamic_update_slice.11), channel_id=1, replica_groups=mesh['zh'=4,'y'=4,'c'=2,'x'=4,'zl'=4] {'zh'}, use_global_device_ids=true, to_apply=%region_13.14 | all-reduce | flops 1024 | bytes 8192 | tf_op jit(solution)/shard_map/psum | solution.py:164
  192.2 0.7 select_reduce_fusion
  193.2 0.8 add_convert_fusion
  194.0 0.5 reshape.351
  194.6 3.3 %convolution_multiply_fusion = f32[160,1024]{1,0:T(8,128)} fusion(bf16[1024,1024]{1,0:T(8,128)(2,1)} %bitcast.56, bf16[1024,192]{1,0:T(8,128)(2,1)S(1)} %reshape.351, f32[1024]{0:T(1024)S(1)} %mul.134), kind=kOutput, calls=%fused_computation.10 | convolution fusion | flops 336199680 | bytes 3149824 | tf_op jit(solution)/shard_map/dot_general | solution.py:177
  (109 shorter events, 3.2 us)
Async XLA Ops:
  7.2 14.1 %copy-start.2 = (f32[320]{0:T(512)S(1)}, f32[320]{0:T(512)}, u32[]{:S(2)}) copy-start(f32[320]{0:T(512)} %param.11) | copy-start | bytes 3844
  7.2 13.9 %copy-start = (bf16[192,1024]{1,0:T(8,128)(2,1)S(1)}, bf16[192,1024]{1,0:T(8,128)(2,1)}, u32[]{:S(2)}) copy-start(bf16[192,1024]{1,0:T(8,128)(2,1)} %param.7) | copy-start | bytes 1179652
  7.2 89.0 %all-gather.4.cloned.1.call-start = ((), (), s32[]{:S(2)}) async-start(), calls=%async_computation | async-start | bytes 3538944 | tf_op jit(solution)/shard_map/all_gather | solution.py:86
  9.1 17.4 %copy-start.1 = (bf16[160,1024]{1,0:T(8,128)(2,1)S(1)}, bf16[160,1024]{1,0:T(8,128)(2,1)}, u32[]{:S(2)}) copy-start(bf16[160,1024]{1,0:T(8,128)(2,1)} %param.8) | copy-start | bytes 983044
  9.1 185.5 %all-gather.6.cloned.1.call-start = ((), (), s32[]{:S(2)}) async-start(), calls=%async_computation.1 | async-start | bytes 2621440 | tf_op jit(solution)/shard_map/all_gather | solution.py:88
  10.1 12.7 %collective-permute-start.1 = (bf16[32,160]{1,0:T(8,128)(2,1)S(1)}, bf16[32,160]{1,0:T(8,128)(2,1)S(1)}, u32[]{:S(2)}, u32[]{:S(2)}) collective-permute-start(bf16[32,160]{1,0:T(8,128)(2,1)S(1)} %slice_select_fusion), channel_id=1, source_target_pairs={{0,16},{1,48},{2,80},{3,112},{4,144},{5,176},{6,208},{7,240},{8,27... | collective-permute-start | bytes 30728 | tf_op jit(solution)/shard_map/ppermute | solution.py:95
  16.5 9.9 %collective-permute-start = (f32[33,160]{1,0:T(8,128)S(1)}, f32[33,160]{1,0:T(8,128)S(1)}, u32[]{:S(2)}, u32[]{:S(2)}) collective-permute-start(f32[33,160]{1,0:T(8,128)S(1)} %fusion.12), channel_id=1, source_target_pairs={{0,0},{1,32},{2,64},{3,96},{4,128},{5,160},{6,192},{7,224},{8,256}... | collective-permute-start | bytes 63368 | tf_op jit(solution)/shard_map/ppermute | solution.py:94
  48.8 46.4 %collective-permute-start.4 = (bf16[192,1024]{1,0:T(8,128)(2,1)S(1)}, bf16[192,1024]{1,0:T(8,128)(2,1)S(1)}, u32[]{:S(2)}, u32[]{:S(2)}) collective-permute-start(bf16[192,1024]{1,0:T(8,128)(2,1)S(1)} %copy-done), channel_id=1, source_target_pairs={{0,32},{32,64},{64,96},{96,0},{1,33},{33,65},{65,97},{97,1},{2,34}... | collective-permute-start | bytes 1179656 | tf_op jit(solution)/shard_map/ppermute | solution.py:35
  55.4 40.0 %collective-permute-start.3 = (bf16[192,1024]{1,0:T(8,128)(2,1)S(1)}, bf16[192,1024]{1,0:T(8,128)(2,1)S(1)}, u32[]{:S(2)}, u32[]{:S(2)}) collective-permute-start(bf16[192,1024]{1,0:T(8,128)(2,1)S(1)} %copy-done), channel_id=1, source_target_pairs={{0,64},{32,96},{64,0},{96,32},{1,65},{33,97},{65,1},{97,33},{2,66}... | collective-permute-start | bytes 1179656 | tf_op jit(solution)/shard_map/ppermute | solution.py:35
  57.3 38.4 %collective-permute-start.2 = (bf16[192,1024]{1,0:T(8,128)(2,1)S(1)}, bf16[192,1024]{1,0:T(8,128)(2,1)S(1)}, u32[]{:S(2)}, u32[]{:S(2)}) collective-permute-start(bf16[192,1024]{1,0:T(8,128)(2,1)S(1)} %copy-done), channel_id=1, source_target_pairs={{0,96},{32,0},{64,32},{96,64},{1,97},{33,1},{65,33},{97,65},{2,98}... | collective-permute-start | bytes 1179656 | tf_op jit(solution)/shard_map/ppermute | solution.py:35
  60.2 35.0 %collective-permute-start.5 = (bf16[16,768]{1,0:T(8,128)(2,1)S(1)}, bf16[16,768]{1,0:T(8,128)(2,1)S(1)}, u32[]{:S(2)}, u32[]{:S(2)}) collective-permute-start(bf16[16,768]{1,0:T(8,128)(2,1)S(1)} %reshape.341), channel_id=1, source_target_pairs={{0,4},{4,0},{8,12},{12,8},{1,5},{5,1},{9,13},{13,9},{2,6},{6,2},{1... | collective-permute-start | bytes 73736 | tf_op jit(solution)/shard_map/ppermute | solution.py:44
  101.8 37.1 %collective-permute-start.7 = (bf16[328,768]{1,0:T(8,128)(2,1)}, bf16[328,768]{1,0:T(8,128)(2,1)S(1)}, u32[]{:S(2)}, u32[]{:S(2)}) collective-permute-start(bf16[328,768]{1,0:T(8,128)(2,1)} %get-tuple-element.33), channel_id=1, source_target_pairs={{0,4},{4,8},{8,12},{12,0},{1,5},{5,9},{9,13},{13,1},{2,6},{6,10},{... | collective-permute-start | bytes 1511432 | tf_op jit(solution)/shard_map/ppermute | solution.py:35
  103.8 42.3 %collective-permute-start.8 = (bf16[328,768]{1,0:T(8,128)(2,1)}, bf16[328,768]{1,0:T(8,128)(2,1)S(1)}, u32[]{:S(2)}, u32[]{:S(2)}) collective-permute-start(bf16[328,768]{1,0:T(8,128)(2,1)} %get-tuple-element.34), channel_id=1, source_target_pairs={{0,8},{4,12},{8,0},{12,4},{1,9},{5,13},{9,1},{13,5},{2,10},{6,14},... | collective-permute-start | bytes 1511432 | tf_op jit(solution)/shard_map/ppermute | solution.py:35
  119.7 26.4 %collective-permute-start.9 = (bf16[328,768]{1,0:T(8,128)(2,1)S(1)}, bf16[328,768]{1,0:T(8,128)(2,1)}, u32[]{:S(2)}, u32[]{:S(2)}) collective-permute-start(bf16[328,768]{1,0:T(8,128)(2,1)S(1)} %get-tuple-element.35), channel_id=1, source_target_pairs={{0,12},{4,0},{8,4},{12,8},{1,13},{5,1},{9,5},{13,9},{2,14},{6,2},{... | collective-permute-start | bytes 1511432 | tf_op jit(solution)/shard_map/ppermute | solution.py:35
  124.2 12.7 %collective-permute-start.6 = (bf16[32,768]{1,0:T(8,128)(2,1)S(1)}, bf16[32,768]{1,0:T(8,128)(2,1)S(1)}, u32[]{:S(2)}, u32[]{:S(2)}) collective-permute-start(bf16[32,768]{1,0:T(8,128)(2,1)S(1)} %pad_maximum_fusion.12), channel_id=1, source_target_pairs={{0,12},{4,8},{8,4},{12,0},{1,13},{5,9},{9,5},{13,1},{2,14},{6,10},... | collective-permute-start | bytes 147464 | tf_op jit(solution)/shard_map/ppermute | solution.py:44
  138.9 18.9 %collective-permute-start.14 = (bf16[64,768]{1,0:T(8,128)(2,1)S(1)}, bf16[64,768]{1,0:T(8,128)(2,1)S(1)}, u32[]{:S(2)}, u32[]{:S(2)}) collective-permute-start(bf16[64,768]{1,0:T(8,128)(2,1)S(1)} %pad_maximum_fusion.11), channel_id=1, source_target_pairs={{0,1},{1,0},{2,3},{3,2},{4,5},{5,4},{6,7},{7,6},{8,9},{9,8},{10,11... | collective-permute-start | bytes 294920 | tf_op jit(solution)/shard_map/ppermute | solution.py:44
  148.0 44.2 %copy-start.3 = (s32[1024]{0:T(1024)S(1)}, s32[1024]{0:T(1024)}, u32[]{:S(2)}) copy-start(s32[1024]{0:T(1024)} %param.13) | copy-start | bytes 12292
  148.0 44.9 %copy-start.4 = (f32[1024]{0:T(1024)S(1)}, f32[1024]{0:T(1024)}, u32[]{:S(2)}) copy-start(f32[1024]{0:T(1024)} %param.12) | copy-start | bytes 12292
  148.2 12.1 %collective-permute-start.10 = (bf16[208,320]{1,0:T(8,128)(2,1)S(1)}, bf16[208,320]{1,0:T(8,128)(2,1)S(1)}, u32[]{:S(2)}, u32[]{:S(2)}) collective-permute-start(bf16[208,320]{1,0:T(8,128)(2,1)S(1)} %get-tuple-element.30), channel_id=1, source_target_pairs={{0,1},{1,2},{2,3},{3,0},{4,5},{5,6},{6,7},{7,4},{8,9},{9,10},{10,1... | collective-permute-start | bytes 399368 | tf_op jit(solution)/shard_map/ppermute | solution.py:35
  150.1 18.7 %collective-permute-start.11 = (bf16[208,320]{1,0:T(8,128)(2,1)S(1)}, bf16[208,320]{1,0:T(8,128)(2,1)S(1)}, u32[]{:S(2)}, u32[]{:S(2)}) collective-permute-start(bf16[208,320]{1,0:T(8,128)(2,1)S(1)} %get-tuple-element.31), channel_id=1, source_target_pairs={{0,2},{1,3},{2,0},{3,1},{4,6},{5,7},{6,4},{7,5},{8,10},{9,11},{10,... | collective-permute-start | bytes 399368 | tf_op jit(solution)/shard_map/ppermute | solution.py:35
  154.2 15.5 %collective-permute-start.12 = (bf16[208,320]{1,0:T(8,128)(2,1)S(1)}, bf16[208,320]{1,0:T(8,128)(2,1)S(1)}, u32[]{:S(2)}, u32[]{:S(2)}) collective-permute-start(bf16[208,320]{1,0:T(8,128)(2,1)S(1)} %get-tuple-element.32), channel_id=1, source_target_pairs={{0,3},{1,0},{2,1},{3,2},{4,7},{5,4},{6,5},{7,6},{8,11},{9,8},{10,9... | collective-permute-start | bytes 399368 | tf_op jit(solution)/shard_map/ppermute | solution.py:35
  157.8 36.1 %collective-permute-start.15 = (bf16[128,768]{1,0:T(8,128)(2,1)S(1)}, bf16[128,768]{1,0:T(8,128)(2,1)S(1)}, u32[]{:S(2)}, u32[]{:S(2)}) collective-permute-start(bf16[128,768]{1,0:T(8,128)(2,1)S(1)} %pad_maximum_fusion.10), channel_id=1, source_target_pairs={{0,3},{1,2},{2,1},{3,0},{4,7},{5,6},{6,5},{7,4},{8,11},{9,10},{10,... | collective-permute-start | bytes 589832 | tf_op jit(solution)/shard_map/ppermute | solution.py:44
  170.5 22.6 %collective-permute-start.13 = (bf16[192,320]{1,0:T(8,128)(2,1)S(1)}, bf16[192,320]{1,0:T(8,128)(2,1)S(1)}, u32[]{:S(2)}, u32[]{:S(2)}) collective-permute-start(bf16[192,320]{1,0:T(8,128)(2,1)S(1)} %slice.131), channel_id=1, source_target_pairs={{0,0},{1,32},{2,64},{3,96},{32,1},{33,33},{34,65},{35,97},{64,2},{... | collective-permute-start | bytes 368648 | tf_op jit(solution)/shard_map/ppermute | solution.py:166
Sparse Core Ops, SparseCore 0:
  10.7 84.7 all-gather.3
  139.0 38.8 all-gather.5

commit v12 on v11

--- a/solution.py
+++ b/solution.py
@@ -101,19 +101,18 @@
         axis=2,
     ).reshape(rows)
     left_dot = jnp.sum(left_cols * probe[None, :], axis=1)
-    here = y * 2 + c
-    early = jnp.concatenate([direction, placed(inner, here, 8), placed(left_dot, here, 8)])
-    early = lax.psum(early, ("y", "c"))
+    direction = lax.psum(direction, "c")
+    early = jnp.concatenate([direction, placed(inner, y, 4), placed(left_dot, y, 4)])
+    early = lax.psum(early, "y")
 
     features, early = lax.optimization_barrier((features, early))
     around = [features] + [move(features, "y", -j) for j in (1, 2, 3)]
-    direction, inner, left_dot = jnp.split(early, [width, width + 2 * many])
+    direction, inner, left_dot = jnp.split(early, [width, width + many])
     direction = lax.psum(direction, "zh")
 
     mine = mine[:members]
     lefts = jnp.where(first, jnp.concatenate([mine, other], 0), jnp.concatenate([other, mine], 0))
     lefts = jnp.pad(lefts.astype(bf16), ((0, 0), (0, 192 - block))).reshape(-1, many)
-    lefts = joined(lefts, "x", x)
 
     along = jnp.stack([
         lax.dot_general(
@@ -122,24 +121,23 @@
         for f in around
     ])
     along = jnp.roll(along, y, axis=0).reshape(many)
-    inner, left_dot = inner.reshape(4, 2, -1), left_dot.reshape(4, 2, -1)
-    inner = jnp.where(first, inner[:, 0], inner[:, 1]).reshape(-1)
-    left_dot = jnp.where(first, left_dot[:, 0], left_dot[:, 1]).reshape(-1)
     sums = jnp.concatenate([along, inner, left_dot])
     size = sums.shape[0]
 
     part = lax.dot_general(
         weight, jnp.concatenate(around, axis=0), (((1,), (1,)), ((), ())), preferred_element_type=f32
     ).astype(bf16).reshape(4, cols, many)
-    ride = pack(sums, many)
+    ride = jnp.concatenate([pack(sums, many), lefts], axis=0)
+    end = part.shape[1] + ride.shape[0] - lefts.shape[0]
     parts = []
     for k in range(4):
         one = lax.dynamic_index_in_dim(part, lax.rem(x + k, 4), 0, keepdims=False)
         one = jnp.concatenate([one, ride], axis=0)
         parts.append(one if k == 0 else move(one, "x", k))
-    lefts, parts[1] = lax.optimization_barrier((lefts, parts[1]))
-    lefts = joined(lefts, "zl", zl)
-    total = sum(p.astype(f32) for p in parts)
+    total = sum(p[:end].astype(f32) for p in parts)
+    lefts = jnp.stack([parts[k][end:] for k in (0, 3, 2, 1)])
+    lefts, total = lax.optimization_barrier((lefts, total))
+    lefts = joined(jnp.roll(lefts, x, axis=0).reshape(-1, many), "zl", zl)
     ride = pack(unpack(total[cols:], size), cols)
 
     total = total[:cols].astype(bf16).T.reshape(4, rows, cols)
@@ -152,14 +150,12 @@
     sums = unpack(total[rows:], size)
     total = total[:rows].astype(bf16)
 
-
     along, inner, left_dot = jnp.split(sums, [many, 2 * many])
     inner = spread * inner
     dots = along + inner * jnp.repeat(left_dot, tokens)
     scale = 0.5 / jnp.sqrt(f32(D))
     score = jnp.mean(jnp.tanh(scale * dots).reshape(4, members, tokens), axis=2)
     score = jnp.stack([jnp.where(first, score, 0.0), jnp.where(first, 0.0, score)], axis=1)
-
     score = lax.psum(score.reshape(-1), "c")
     score = lax.psum(placed(score, zh, 4), "zh")
 

time: 208 us -> 197 us (0.947)
  starting transfers between devices: 87.1 us -> 51.4 us
  waiting for transfers between devices: 23.7 us -> 40.5 us
  blocking collectives: 54.8 us -> 65.6 us
    psum x1, blocking collectives: 17.8 us -> 40.6 us  [per_device(): direction = lax.psum(direction, 'zh')]
    ppermute x4 -> x2, starting transfers between devices: 28 us -> 5.36 us  [joined(): got = lax.ppermute(value, axis, pairs(step))]
    ppermute x9, waiting for transfers between devices: 9.34 us -> 29.7 us  [move(): return lax.ppermute(value, axis, ring(step))]
    ppermute x9, starting transfers between devices: 43.2 us -> 29.8 us  [move(): return lax.ppermute(value, axis, ring(step))]
    psum x1 -> x2, blocking collectives: 22.2 us -> 10 us  [the longest x1 7.57 us: per_device(): early = lax.psum(early, 'y')]
    ppermute x4 -> x2, waiting for transfers between devices: 10.6 us -> 0.01 us  [joined(): got = lax.ppermute(value, axis, pairs(step))]
    all_gather x1, waiting for transfers between devices: 0.02 us -> 7.07 us  [per_device(): lax.all_gather(own, ('zh', 'c'), axis=0, tiled=True)]
  transfers between devices with their start and end apart: 18 -> 16, of which waited for: 4 -> 7; matrix products, arithmetic and copies ran while one was open for 7% -> 6% of each run, Pallas kernels for 0% -> 0%
where the time goes in v12:
time: 197 us; the launch traced here: 195 us
  blocking collectives  65.6 us (33%)
  starting transfers between devices  51.4 us (26%)
  waiting for transfers between devices  40.5 us (21%)
  between operations  14.8 us (8%)
  local copies, waits for them, and re-layouts  8.95 us (5%)
  other arithmetic  7.54 us (4%)
  matrix products  6.36 us (3%)
    psum x1, blocking collectives, per_device(): direction = lax.psum(direction, 'zh')  40.6 us
    ppermute x9, starting transfers between devices, move(): return lax.ppermute(value, axis, ring(step))  29.8 us
    ppermute x9, waiting for transfers between devices, move(): return lax.ppermute(value, axis, ring(step))  29.7 us
    psum x1, blocking collectives, per_device(): score = lax.psum(placed(score, zh, 4), 'zh')  12.4 us
    psum x1, blocking collectives, per_device(): early = lax.psum(early, 'y')  7.57 us
    all_gather x1, waiting for transfers between devices, per_device(): lax.all_gather(own, ('zh', 'c'), axis=0, tiled=True)  7.07 us
    ppermute x1, starting transfers between devices, per_device(): total = lax.ppermute(total, ('y', 'zl'), turned()).astype(f32)  6.79 us
    ppermute x1, starting transfers between devices, per_device(): other = lax.ppermute(other, AXES, swapped(1))  5.62 us
  transfers between devices with their start and end apart: 16, of which 7 were waited for; matrix products, arithmetic and copies ran while one was open for 6% of the time, Pallas kernels for 0%

profile of v12, /device:TPU:24, one launch (start us, length us, event | category | flops | bytes accessed | tf_op | source)
XLA Modules:
  0.0 195.0 jit_solution(1385083558743714070)
XLA Ops:
  7.2 1.8 pad_maximum_fusion.6
  9.1 0.8 dynamic-slice_convert_fusion
  10.1 5.6 %collective-permute-start.1 = (bf16[32,160]{1,0:T(8,128)(2,1)S(1)}, bf16[32,160]{1,0:T(8,128)(2,1)S(1)}, u32[]{:S(2)}, u32[]{:S(2)}) collective-permute-start(bf16[32,160]{1,0:T(8,128)(2,1)S(1)} %slice_select_fusion), channel_id=1, source_target_pairs={{0,16},{1,48},{2,80},{3,112},{4,144},{5,176},{6,208},{7,240},{8,27... | collective-permute-start | bytes 30728 | tf_op jit(solution)/shard_map/ppermute | solution.py:95
  15.7 0.7 broadcast_in_dim.37
  16.5 3.7 %collective-permute-start = (f32[33,160]{1,0:T(8,128)S(1)}, f32[33,160]{1,0:T(8,128)S(1)}, u32[]{:S(2)}, u32[]{:S(2)}) collective-permute-start(f32[33,160]{1,0:T(8,128)S(1)} %fusion.13), channel_id=1, source_target_pairs={{0,0},{1,32},{2,64},{3,96},{4,128},{5,160},{6,192},{7,224},{8,256}... | collective-permute-start | bytes 63368 | tf_op jit(solution)/shard_map/ppermute | solution.py:94
  20.2 1.0 mul.105
  21.4 1.0 multiply_reduce_fusion.2
  22.4 0.2 dynamic_update_slice.10
  22.7 0.2 dynamic_update_slice.9
  22.9 3.7 %collective-permute-done = f32[33,160]{1,0:T(8,128)S(1)} collective-permute-done((f32[33,160]{1,0:T(8,128)S(1)}, f32[33,160]{1,0:T(8,128)S(1)}, u32[]{:S(2)}, u32[]{:S(2)}) %collective-permute-start) | collective-permute-done | bytes 21152 | tf_op jit(solution)/shard_map/ppermute | solution.py:94
  26.7 2.5 %psum.35 = f32[1024]{0:T(1024)S(1)} all-reduce(f32[1024]{0:T(1024)S(1)} %multiply_reduce_fusion.1), channel_id=1, replica_groups=mesh['zh'=4,'y'=4,'c'=2,'x'=4,'zl'=4] {'c'}, use_global_device_ids=true, to_apply=%region_1.2 | all-reduce | flops 1024 | bytes 8192 | tf_op jit(solution)/shard_map/psum | solution.py:104
  29.2 7.6 %psum.36 = f32[1920]{0:T(1024)S(1)} all-reduce(f32[1920]{0:T(1024)S(1)} %pad_maximum_fusion.17), channel_id=1, replica_groups=mesh['zh'=4,'y'=4,'c'=2,'x'=4,'zl'=4] {'y'}, use_global_device_ids=true, to_apply=%region_4.5 | all-reduce | flops 1920 | bytes 15360 | tf_op jit(solution)/shard_map/psum | solution.py:106
  36.8 5.4 %collective-permute-start.4 = (bf16[192,1024]{1,0:T(8,128)(2,1)S(1)}, bf16[192,1024]{1,0:T(8,128)(2,1)S(1)}, u32[]{:S(2)}, u32[]{:S(2)}) collective-permute-start(bf16[192,1024]{1,0:T(8,128)(2,1)S(1)} %copy-done), channel_id=1, source_target_pairs={{0,32},{32,64},{64,96},{96,0},{1,33},{33,65},{65,97},{97,1},{2,34}... | collective-permute-start | bytes 1179656 | tf_op jit(solution)/shard_map/ppermute | solution.py:35
  42.2 2.2 %collective-permute-start.3 = (bf16[192,1024]{1,0:T(8,128)(2,1)S(1)}, bf16[192,1024]{1,0:T(8,128)(2,1)S(1)}, u32[]{:S(2)}, u32[]{:S(2)}) collective-permute-start(bf16[192,1024]{1,0:T(8,128)(2,1)S(1)} %copy-done), channel_id=1, source_target_pairs={{0,64},{32,96},{64,0},{96,32},{1,65},{33,97},{65,1},{97,33},{2,66}... | collective-permute-start | bytes 1179656 | tf_op jit(solution)/shard_map/ppermute | solution.py:35
  44.4 2.5 %collective-permute-start.2 = (bf16[192,1024]{1,0:T(8,128)(2,1)S(1)}, bf16[192,1024]{1,0:T(8,128)(2,1)S(1)}, u32[]{:S(2)}, u32[]{:S(2)}) collective-permute-start(bf16[192,1024]{1,0:T(8,128)(2,1)S(1)} %copy-done), channel_id=1, source_target_pairs={{0,96},{32,0},{64,32},{96,64},{1,97},{33,1},{65,33},{97,65},{2,98}... | collective-permute-start | bytes 1179656 | tf_op jit(solution)/shard_map/ppermute | solution.py:35
  47.0 40.6 %psum.37 = f32[1024]{0:T(1024)S(1)} all-reduce(f32[1024]{0:T(1024)S(1)} %split.20), channel_id=1, replica_groups=mesh['zh'=4,'y'=4,'c'=2,'x'=4,'zl'=4] {'zh'}, use_global_device_ids=true, to_apply=%region_5.6 | all-reduce | flops 1024 | bytes 8192 | tf_op jit(solution)/shard_map/psum | solution.py:111
  87.7 0.2 convolution_reduce_fusion.3
  87.9 0.2 convolution_reduce_fusion
  88.2 0.2 convolution_reduce_fusion.1
  88.4 0.2 convolution_reduce_fusion.2
  88.9 7.1 %all-gather.4.cloned.1.call-done = bf16[1536,1024]{1,0:T(8,128)(2,1)} async-done(((bf16[192,1024]{1,0:T(8,128)(2,1)}), bf16[1536,1024]{1,0:T(8,128)(2,1)}) %all-gather.4.cloned.1.call-update) | async-done | bytes 3145744 | tf_op jit(solution)/shard_map/all_gather | solution.py:86
  96.0 2.1 %slice.99 = bf16[4,2,160,1024]{3,2,1,0:T(8,128)(2,1)S(1)} slice(bf16[4,2,192,1024]{3,2,1,0:T(8,128)(2,1)} %bitcast.49), slice={[0:4], [0:2], [0:160], [0:1024]} | slice | bytes 5242880 | tf_op jit(solution)/shard_map/slice | solution.py:87
  98.1 2.2 %convolution_convert_fusion = bf16[1280,768]{1,0:T(8,128)(2,1)S(1)} fusion(bf16[1280,1024]{1,0:T(8,128)(2,1)S(1)} %bitcast.51, bf16[192,1024]{1,0:T(8,128)(2,1)S(1)} %collective-permute-done.4, bf16[192,1024]{1,0:T(8,128)(2,1)S(1)} %collective-permute-done.3, bf16[192,1024]{1,0:T(8,128)(2,1)S(1)} %collective-permute-done.2, bf16[192,1024]{1,0:T(8,128)(2,1)S(1)} %copy-done), kind=kOutput, calls=%fused_computation.2 | convolution fusion | flops 2020540416 | bytes 6160384 | tf_op jit(solution)/shard_map/dot_general | solution.py:127
  100.5 1.1 pad_maximum_fusion.5
  101.6 3.5 %collective-permute-start.5 = (bf16[344,768]{1,0:T(8,128)(2,1)}, bf16[344,768]{1,0:T(8,128)(2,1)S(1)}, u32[]{:S(2)}, u32[]{:S(2)}) collective-permute-start(bf16[344,768]{1,0:T(8,128)(2,1)} %get-tuple-element.26), channel_id=1, source_target_pairs={{0,12},{4,0},{8,4},{12,8},{1,13},{5,1},{9,5},{13,9},{2,14},{6,2},{... | collective-permute-start | bytes 1585160 | tf_op jit(solution)/shard_map/ppermute | solution.py:35
  105.2 2.4 %collective-permute-start.6 = (bf16[344,768]{1,0:T(8,128)(2,1)}, bf16[344,768]{1,0:T(8,128)(2,1)S(1)}, u32[]{:S(2)}, u32[]{:S(2)}) collective-permute-start(bf16[344,768]{1,0:T(8,128)(2,1)} %get-tuple-element.27), channel_id=1, source_target_pairs={{0,8},{4,12},{8,0},{12,4},{1,9},{5,13},{9,1},{13,5},{2,10},{6,14},... | collective-permute-start | bytes 1585160 | tf_op jit(solution)/shard_map/ppermute | solution.py:35
  107.6 3.1 %collective-permute-start.7 = (bf16[344,768]{1,0:T(8,128)(2,1)S(1)}, bf16[344,768]{1,0:T(8,128)(2,1)S(1)}, u32[]{:S(2)}, u32[]{:S(2)}) collective-permute-start(bf16[344,768]{1,0:T(8,128)(2,1)S(1)} %get-tuple-element.28), channel_id=1, source_target_pairs={{0,4},{4,8},{8,12},{12,0},{1,5},{5,9},{9,13},{13,1},{2,6},{6,10},{... | collective-permute-start | bytes 1585160 | tf_op jit(solution)/shard_map/ppermute | solution.py:35
  111.0 1.9 slice.112
  113.0 5.6 %collective-permute-done.5 = bf16[344,768]{1,0:T(8,128)(2,1)S(1)} collective-permute-done((bf16[344,768]{1,0:T(8,128)(2,1)}, bf16[344,768]{1,0:T(8,128)(2,1)S(1)}, u32[]{:S(2)}, u32[]{:S(2)}) %collective-permute-start.5) | collective-permute-done | bytes 528416 | tf_op jit(solution)/shard_map/ppermute | solution.py:35
  118.6 5.1 %collective-permute-done.6 = bf16[344,768]{1,0:T(8,128)(2,1)S(1)} collective-permute-done((bf16[344,768]{1,0:T(8,128)(2,1)}, bf16[344,768]{1,0:T(8,128)(2,1)S(1)}, u32[]{:S(2)}, u32[]{:S(2)}) %collective-permute-start.6) | collective-permute-done | bytes 528416 | tf_op jit(solution)/shard_map/ppermute | solution.py:35
  123.7 10.3 %collective-permute-done.7 = bf16[344,768]{1,0:T(8,128)(2,1)S(1)} collective-permute-done((bf16[344,768]{1,0:T(8,128)(2,1)S(1)}, bf16[344,768]{1,0:T(8,128)(2,1)S(1)}, u32[]{:S(2)}, u32[]{:S(2)}) %collective-permute-start.7) | collective-permute-done | bytes 528416 | tf_op jit(solution)/shard_map/ppermute | solution.py:35
  134.0 0.3 convert_add_fusion
  134.6 0.3 copy.18
  134.9 3.4 %collective-permute-start.12 = (bf16[64,768]{1,0:T(8,128)(2,1)S(1)}, bf16[64,768]{1,0:T(8,128)(2,1)S(1)}, u32[]{:S(2)}, u32[]{:S(2)}) collective-permute-start(bf16[64,768]{1,0:T(8,128)(2,1)S(1)} %bitcast.54), channel_id=1, source_target_pairs={{0,1},{1,0},{2,3},{3,2},{4,5},{5,4},{6,7},{7,6},{8,9},{9,8},{10,11... | collective-permute-start | bytes 294920 | tf_op jit(solution)/shard_map/ppermute | solution.py:44
  138.6 2.4 %collective-permute-start.8 = (bf16[208,320]{1,0:T(8,128)(2,1)S(1)}, bf16[208,320]{1,0:T(8,128)(2,1)S(1)}, u32[]{:S(2)}, u32[]{:S(2)}) collective-permute-start(bf16[208,320]{1,0:T(8,128)(2,1)S(1)} %get-tuple-element.29), channel_id=1, source_target_pairs={{0,1},{1,2},{2,3},{3,0},{4,5},{5,6},{6,7},{7,4},{8,9},{9,10},{10,1... | collective-permute-start | bytes 399368 | tf_op jit(solution)/shard_map/ppermute | solution.py:35
  141.0 3.4 %collective-permute-start.9 = (bf16[208,320]{1,0:T(8,128)(2,1)S(1)}, bf16[208,320]{1,0:T(8,128)(2,1)S(1)}, u32[]{:S(2)}, u32[]{:S(2)}) collective-permute-start(bf16[208,320]{1,0:T(8,128)(2,1)S(1)} %get-tuple-element.30), channel_id=1, source_target_pairs={{0,2},{1,3},{2,0},{3,1},{4,6},{5,7},{6,4},{7,5},{8,10},{9,11},{10,... | collective-permute-start | bytes 399368 | tf_op jit(solution)/shard_map/ppermute | solution.py:35
  144.4 4.8 %collective-permute-start.10 = (bf16[208,320]{1,0:T(8,128)(2,1)S(1)}, bf16[208,320]{1,0:T(8,128)(2,1)S(1)}, u32[]{:S(2)}, u32[]{:S(2)}) collective-permute-start(bf16[208,320]{1,0:T(8,128)(2,1)S(1)} %get-tuple-element.31), channel_id=1, source_target_pairs={{0,3},{1,0},{2,1},{3,2},{4,7},{5,4},{6,5},{7,6},{8,11},{9,8},{10,9... | collective-permute-start | bytes 399368 | tf_op jit(solution)/shard_map/ppermute | solution.py:35
  149.2 1.9 collective-permute-start.13
  151.2 4.3 %collective-permute-done.9 = bf16[208,320]{1,0:T(8,128)(2,1)S(1)} collective-permute-done((bf16[208,320]{1,0:T(8,128)(2,1)S(1)}, bf16[208,320]{1,0:T(8,128)(2,1)S(1)}, u32[]{:S(2)}, u32[]{:S(2)}) %collective-permute-start.9) | collective-permute-done | bytes 133152 | tf_op jit(solution)/shard_map/ppermute | solution.py:35
  155.5 4.3 %collective-permute-done.10 = bf16[208,320]{1,0:T(8,128)(2,1)S(1)} collective-permute-done((bf16[208,320]{1,0:T(8,128)(2,1)S(1)}, bf16[208,320]{1,0:T(8,128)(2,1)S(1)}, u32[]{:S(2)}, u32[]{:S(2)}) %collective-permute-start.10) | collective-permute-done | bytes 133152 | tf_op jit(solution)/shard_map/ppermute | solution.py:35
  160.8 6.8 %collective-permute-start.11 = (bf16[192,320]{1,0:T(8,128)(2,1)S(1)}, bf16[192,320]{1,0:T(8,128)(2,1)S(1)}, u32[]{:S(2)}, u32[]{:S(2)}) collective-permute-start(bf16[192,320]{1,0:T(8,128)(2,1)S(1)} %slice.137), channel_id=1, source_target_pairs={{0,0},{1,32},{2,64},{3,96},{32,1},{33,33},{34,65},{35,97},{64,2},{... | collective-permute-start | bytes 368648 | tf_op jit(solution)/shard_map/ppermute | solution.py:162
  167.6 2.5 %psum.38 = f32[256]{0:T(256)S(1)} all-reduce(f32[256]{0:T(256)S(1)} %reshape.276), channel_id=1, replica_groups=mesh['zh'=4,'y'=4,'c'=2,'x'=4,'zl'=4] {'c'}, use_global_device_ids=true, to_apply=%region_13.14 | all-reduce | flops 256 | bytes 2048 | tf_op jit(solution)/shard_map/psum | solution.py:159
  170.1 0.2 dynamic_update_slice.11
  170.3 12.4 %psum.39 = f32[1024]{0:T(1024)S(1)} all-reduce(f32[1024]{0:T(1024)S(1)} %dynamic_update_slice.11), channel_id=1, replica_groups=mesh['zh'=4,'y'=4,'c'=2,'x'=4,'zl'=4] {'zh'}, use_global_device_ids=true, to_apply=%region_14.15 | all-reduce | flops 1024 | bytes 8192 | tf_op jit(solution)/shard_map/psum | solution.py:160
  182.7 0.7 select_reduce_fusion
  183.5 0.8 add_convert_fusion
  184.4 0.5 reshape.279
  184.9 3.3 %convolution_multiply_fusion = f32[160,1024]{1,0:T(8,128)} fusion(bf16[1024,1024]{1,0:T(8,128)(2,1)} %bitcast.66, bf16[1024,192]{1,0:T(8,128)(2,1)S(1)} %reshape.279, f32[1024]{0:T(1024)S(1)} %mul.127), kind=kOutput, calls=%fused_computation.10 | convolution fusion | flops 336199680 | bytes 3149824 | tf_op jit(solution)/shard_map/dot_general | solution.py:173
  (100 shorter events, 3.2 us)
Async XLA Ops:
  7.2 14.1 %copy-start = (bf16[192,1024]{1,0:T(8,128)(2,1)S(1)}, bf16[192,1024]{1,0:T(8,128)(2,1)}, u32[]{:S(2)}) copy-start(bf16[192,1024]{1,0:T(8,128)(2,1)} %param.7) | copy-start | bytes 1179652
  7.2 88.8 %all-gather.4.cloned.1.call-start = ((), (), s32[]{:S(2)}) async-start(), calls=%async_computation | async-start | bytes 3538944 | tf_op jit(solution)/shard_map/all_gather | solution.py:86
  9.1 175.8 %all-gather.6.cloned.1.call-start = ((), (), s32[]{:S(2)}) async-start(), calls=%async_computation.1 | async-start | bytes 2621440 | tf_op jit(solution)/shard_map/all_gather | solution.py:88
  10.1 12.8 %collective-permute-start.1 = (bf16[32,160]{1,0:T(8,128)(2,1)S(1)}, bf16[32,160]{1,0:T(8,128)(2,1)S(1)}, u32[]{:S(2)}, u32[]{:S(2)}) collective-permute-start(bf16[32,160]{1,0:T(8,128)(2,1)S(1)} %slice_select_fusion), channel_id=1, source_target_pairs={{0,16},{1,48},{2,80},{3,112},{4,144},{5,176},{6,208},{7,240},{8,27... | collective-permute-start | bytes 30728 | tf_op jit(solution)/shard_map/ppermute | solution.py:95
  16.4 5.0 %copy-start.2 = (f32[320]{0:T(512)S(1)}, f32[320]{0:T(512)}, u32[]{:S(2)}) copy-start(f32[320]{0:T(512)} %param.11) | copy-start | bytes 3844
  16.4 10.1 %copy-start.1 = (bf16[160,1024]{1,0:T(8,128)(2,1)S(1)}, bf16[160,1024]{1,0:T(8,128)(2,1)}, u32[]{:S(2)}) copy-start(bf16[160,1024]{1,0:T(8,128)(2,1)} %param.8) | copy-start | bytes 983044
  16.5 10.1 %collective-permute-start = (f32[33,160]{1,0:T(8,128)S(1)}, f32[33,160]{1,0:T(8,128)S(1)}, u32[]{:S(2)}, u32[]{:S(2)}) collective-permute-start(f32[33,160]{1,0:T(8,128)S(1)} %fusion.13), channel_id=1, source_target_pairs={{0,0},{1,32},{2,64},{3,96},{4,128},{5,160},{6,192},{7,224},{8,256}... | collective-permute-start | bytes 63368 | tf_op jit(solution)/shard_map/ppermute | solution.py:94
  36.8 51.2 %collective-permute-start.4 = (bf16[192,1024]{1,0:T(8,128)(2,1)S(1)}, bf16[192,1024]{1,0:T(8,128)(2,1)S(1)}, u32[]{:S(2)}, u32[]{:S(2)}) collective-permute-start(bf16[192,1024]{1,0:T(8,128)(2,1)S(1)} %copy-done), channel_id=1, source_target_pairs={{0,32},{32,64},{64,96},{96,0},{1,33},{33,65},{65,97},{97,1},{2,34}... | collective-permute-start | bytes 1179656 | tf_op jit(solution)/shard_map/ppermute | solution.py:35
  42.2 46.0 %collective-permute-start.3 = (bf16[192,1024]{1,0:T(8,128)(2,1)S(1)}, bf16[192,1024]{1,0:T(8,128)(2,1)S(1)}, u32[]{:S(2)}, u32[]{:S(2)}) collective-permute-start(bf16[192,1024]{1,0:T(8,128)(2,1)S(1)} %copy-done), channel_id=1, source_target_pairs={{0,64},{32,96},{64,0},{96,32},{1,65},{33,97},{65,1},{97,33},{2,66}... | collective-permute-start | bytes 1179656 | tf_op jit(solution)/shard_map/ppermute | solution.py:35
  44.4 44.0 %collective-permute-start.2 = (bf16[192,1024]{1,0:T(8,128)(2,1)S(1)}, bf16[192,1024]{1,0:T(8,128)(2,1)S(1)}, u32[]{:S(2)}, u32[]{:S(2)}) collective-permute-start(bf16[192,1024]{1,0:T(8,128)(2,1)S(1)} %copy-done), channel_id=1, source_target_pairs={{0,96},{32,0},{64,32},{96,64},{1,97},{33,1},{65,33},{97,65},{2,98}... | collective-permute-start | bytes 1179656 | tf_op jit(solution)/shard_map/ppermute | solution.py:35
  101.6 16.9 %collective-permute-start.5 = (bf16[344,768]{1,0:T(8,128)(2,1)}, bf16[344,768]{1,0:T(8,128)(2,1)S(1)}, u32[]{:S(2)}, u32[]{:S(2)}) collective-permute-start(bf16[344,768]{1,0:T(8,128)(2,1)} %get-tuple-element.26), channel_id=1, source_target_pairs={{0,12},{4,0},{8,4},{12,8},{1,13},{5,1},{9,5},{13,9},{2,14},{6,2},{... | collective-permute-start | bytes 1585160 | tf_op jit(solution)/shard_map/ppermute | solution.py:35
  105.2 18.5 %collective-permute-start.6 = (bf16[344,768]{1,0:T(8,128)(2,1)}, bf16[344,768]{1,0:T(8,128)(2,1)S(1)}, u32[]{:S(2)}, u32[]{:S(2)}) collective-permute-start(bf16[344,768]{1,0:T(8,128)(2,1)} %get-tuple-element.27), channel_id=1, source_target_pairs={{0,8},{4,12},{8,0},{12,4},{1,9},{5,13},{9,1},{13,5},{2,10},{6,14},... | collective-permute-start | bytes 1585160 | tf_op jit(solution)/shard_map/ppermute | solution.py:35
  107.6 26.3 %collective-permute-start.7 = (bf16[344,768]{1,0:T(8,128)(2,1)S(1)}, bf16[344,768]{1,0:T(8,128)(2,1)S(1)}, u32[]{:S(2)}, u32[]{:S(2)}) collective-permute-start(bf16[344,768]{1,0:T(8,128)(2,1)S(1)} %get-tuple-element.28), channel_id=1, source_target_pairs={{0,4},{4,8},{8,12},{12,0},{1,5},{5,9},{9,13},{13,1},{2,6},{6,10},{... | collective-permute-start | bytes 1585160 | tf_op jit(solution)/shard_map/ppermute | solution.py:35
  134.9 14.2 %collective-permute-start.12 = (bf16[64,768]{1,0:T(8,128)(2,1)S(1)}, bf16[64,768]{1,0:T(8,128)(2,1)S(1)}, u32[]{:S(2)}, u32[]{:S(2)}) collective-permute-start(bf16[64,768]{1,0:T(8,128)(2,1)S(1)} %bitcast.54), channel_id=1, source_target_pairs={{0,1},{1,0},{2,3},{3,2},{4,5},{5,4},{6,7},{7,6},{8,9},{9,8},{10,11... | collective-permute-start | bytes 294920 | tf_op jit(solution)/shard_map/ppermute | solution.py:44
  138.4 44.3 %copy-start.3 = (s32[1024]{0:T(1024)S(1)}, s32[1024]{0:T(1024)}, u32[]{:S(2)}) copy-start(s32[1024]{0:T(1024)} %param.13) | copy-start | bytes 12292
  138.4 44.9 %copy-start.4 = (f32[1024]{0:T(1024)S(1)}, f32[1024]{0:T(1024)}, u32[]{:S(2)}) copy-start(f32[1024]{0:T(1024)} %param.12) | copy-start | bytes 12292
  138.6 12.6 %collective-permute-start.8 = (bf16[208,320]{1,0:T(8,128)(2,1)S(1)}, bf16[208,320]{1,0:T(8,128)(2,1)S(1)}, u32[]{:S(2)}, u32[]{:S(2)}) collective-permute-start(bf16[208,320]{1,0:T(8,128)(2,1)S(1)} %get-tuple-element.29), channel_id=1, source_target_pairs={{0,1},{1,2},{2,3},{3,0},{4,5},{5,6},{6,7},{7,4},{8,9},{9,10},{10,1... | collective-permute-start | bytes 399368 | tf_op jit(solution)/shard_map/ppermute | solution.py:35
  141.0 14.5 %collective-permute-start.9 = (bf16[208,320]{1,0:T(8,128)(2,1)S(1)}, bf16[208,320]{1,0:T(8,128)(2,1)S(1)}, u32[]{:S(2)}, u32[]{:S(2)}) collective-permute-start(bf16[208,320]{1,0:T(8,128)(2,1)S(1)} %get-tuple-element.30), channel_id=1, source_target_pairs={{0,2},{1,3},{2,0},{3,1},{4,6},{5,7},{6,4},{7,5},{8,10},{9,11},{10,... | collective-permute-start | bytes 399368 | tf_op jit(solution)/shard_map/ppermute | solution.py:35
  144.4 15.5 %collective-permute-start.10 = (bf16[208,320]{1,0:T(8,128)(2,1)S(1)}, bf16[208,320]{1,0:T(8,128)(2,1)S(1)}, u32[]{:S(2)}, u32[]{:S(2)}) collective-permute-start(bf16[208,320]{1,0:T(8,128)(2,1)S(1)} %get-tuple-element.31), channel_id=1, source_target_pairs={{0,3},{1,0},{2,1},{3,2},{4,7},{5,4},{6,5},{7,6},{8,11},{9,8},{10,9... | collective-permute-start | bytes 399368 | tf_op jit(solution)/shard_map/ppermute | solution.py:35
  149.2 35.0 %collective-permute-start.13 = (bf16[128,768]{1,0:T(8,128)(2,1)S(1)}, bf16[128,768]{1,0:T(8,128)(2,1)S(1)}, u32[]{:S(2)}, u32[]{:S(2)}) collective-permute-start(bf16[128,768]{1,0:T(8,128)(2,1)S(1)} %pad_maximum_fusion.12), channel_id=1, source_target_pairs={{0,3},{1,2},{2,1},{3,0},{4,7},{5,6},{6,5},{7,4},{8,11},{9,10},{10,... | collective-permute-start | bytes 589832 | tf_op jit(solution)/shard_map/ppermute | solution.py:44
  160.8 22.7 %collective-permute-start.11 = (bf16[192,320]{1,0:T(8,128)(2,1)S(1)}, bf16[192,320]{1,0:T(8,128)(2,1)S(1)}, u32[]{:S(2)}, u32[]{:S(2)}) collective-permute-start(bf16[192,320]{1,0:T(8,128)(2,1)S(1)} %slice.137), channel_id=1, source_target_pairs={{0,0},{1,32},{2,64},{3,96},{32,1},{33,33},{34,65},{35,97},{64,2},{... | collective-permute-start | bytes 368648 | tf_op jit(solution)/shard_map/ppermute | solution.py:162
Sparse Core Ops, SparseCore 0:
  10.7 85.2 all-gather.3
  113.1 32.6 all-gather.5

commit v13 on v10

--- a/solution.py
+++ b/solution.py
@@ -53,6 +53,15 @@
         terms.append(term.astype(jnp.bfloat16))
         value = value - term
     return jnp.stack(terms)
+
+
+def pack(value, width):
+    terms = in_three(value).reshape(-1)
+    return jnp.pad(terms, (0, -terms.shape[0] % (8 * width))).reshape(-1, width)
+
+
+def unpack(rows, size):
+    return rows.reshape(-1)[: 3 * size].reshape(3, size).sum(0)
 
 
 def placed(value, index, count):
@@ -73,10 +82,9 @@
     first = c == 0
     many = 4 * rows
 
-    own = jnp.concatenate([down_weight, member_right], axis=0)
-    stack = lax.all_gather(own, ("zh", "c"), axis=0, tiled=True).reshape(4, 2, -1, width)
-    weight = stack[:, :, :block].reshape(-1, width)
-    rights = lax.all_gather(stack[:, :, block:], "y", axis=0, tiled=False)
+    lead = 128
+    rest = block - lead
+    weight_one = lax.all_gather(down_weight[:lead], ("zh", "c"), axis=0, tiled=True)
 
     around = [features] + [move(features, "y", -j) for j in (1, 2, 3)]
 
@@ -85,6 +93,9 @@
 
     left_cols = lax.dynamic_slice(member_left, (0, (x * 4 + zl) * cols), (members, cols))
     lefts = lax.ppermute(left_cols, AXES, swapped())
+    own = jnp.concatenate([down_weight[lead:], member_right], axis=0)
+    own, lefts = lax.optimization_barrier((own, lefts))
+    stack = lax.all_gather(own, ("zh", "c"), axis=0, tiled=True).reshape(4, 2, -1, width)
     mine = jnp.where(first, lefts[:, :block], lefts[:, block:])
     other = jnp.where(first, lefts[:, block:], lefts[:, :block])
     other = lax.ppermute(other, "c", [(0, 1), (1, 0)])
@@ -93,17 +104,29 @@
     lefts = joined(lefts, "x", x)
     left_cols = left_cols.astype(f32)
 
-    part = lax.dot_general(
-        weight, jnp.concatenate(around, axis=0), (((1,), (1,)), ((), ())), preferred_element_type=f32
-    ).astype(bf16).reshape(4, cols, many)
-    parts = []
-    for k in range(4):
-        one = lax.dynamic_index_in_dim(part, lax.rem(x + k, 4), 0, keepdims=False)
-        parts.append(one if k == 0 else move(one, "x", k))
-
-    direction = lax.dot_general(
-        in_three(probes), weight, (((1,), (0,)), ((), ())), preferred_element_type=f32
-    ).sum(0)
+    def products(weight):
+        part = lax.dot_general(
+            weight, jnp.concatenate(around, axis=0), (((1,), (1,)), ((), ())),
+            preferred_element_type=f32,
+        ).astype(bf16).reshape(4, -1, many)
+        return [
+            lax.dynamic_index_in_dim(part, lax.rem(x + k, 4), 0, keepdims=False) for k in range(4)
+        ]
+
+    ones = products(weight_one)
+    ones = [ones[0]] + [move(ones[k], "x", k) for k in (1, 2, 3)]
+    lefts, stack, ones = lax.optimization_barrier((lefts, stack, ones))
+    weight_two = stack[:, :, :rest].reshape(-1, width)
+    rights = lax.all_gather(stack[:, :, rest:], "y", axis=0, tiled=False)
+    lefts = joined(lefts, "zl", zl)
+
+    probes = probes.reshape(4, 2, block)
+    direction = sum(
+        lax.dot_general(
+            in_three(p.reshape(-1)), w, (((1,), (0,)), ((), ())), preferred_element_type=f32
+        ).sum(0)
+        for p, w in ((probes[:, :, :lead], weight_one), (probes[:, :, lead:], weight_two))
+    )
     along = jnp.stack([
         lax.dot_general(
             in_three(direction), f, (((1,), (1,)), ((), ())), preferred_element_type=f32
@@ -117,20 +140,28 @@
     ).reshape(rows)
     left_dot = jnp.sum(left_cols * probe[None, :], axis=1)
     sums = jnp.concatenate([along, placed(inner, y, 4), placed(left_dot, y, 4)])
-    sums, lefts, parts[1] = lax.optimization_barrier((sums, lefts, parts[1]))
-    sums = lax.psum(lax.psum(sums, "y"), "x")
-    lefts = joined(lefts, "zl", zl)
-    total = sum(p.astype(f32) for p in parts).astype(bf16)
-    sums, lefts, total = lax.optimization_barrier((sums, lefts, total))
-
-    sums = lax.psum(sums, "zl")
+    size = sums.shape[0]
+    ride = pack(sums, many)
+    twos = [jnp.concatenate([p, ride], axis=0) for p in products(weight_two)]
+    twos = [twos[0]] + [move(twos[k], "x", k) for k in (1, 2, 3)]
+    total_one = sum(p.astype(f32) for p in ones).astype(bf16)
+    total_two = sum(p.astype(f32) for p in twos)
+    ride = pack(unpack(total_two[2 * rest :], size), cols)
+    total_two = total_two[: 2 * rest].astype(bf16)
+    total = jnp.concatenate(
+        [total_one.reshape(2, lead, many), total_two.reshape(2, rest, many)], axis=1
+    ).reshape(cols, many)
+
     total = total.T.reshape(4, rows, cols)
     parts = []
     for k in range(4):
         one = lax.dynamic_index_in_dim(total, lax.rem(zl + k + 4 - y, 4), 0, keepdims=False)
+        one = jnp.concatenate([one, ride], axis=0)
         parts.append(one if k == 0 else move(one, "zl", k))
-    total = sum(p.astype(f32) for p in parts).astype(bf16)
-    sums, total = lax.optimization_barrier((sums, total))
+    total = sum(p.astype(f32) for p in parts)
+    sums = lax.psum(unpack(total[rows:], size), "y")
+    total = total[:rows].astype(bf16)
+
     along, inner, left_dot = jnp.split(sums, [many, 2 * many])
     inner = spread * inner
     dots = along + inner * jnp.repeat(left_dot, tokens)

time: 217 us -> 216 us (level)
  the two profiles are of different devices: /device:TPU:24 before, /device:TPU:64 now
where the time goes in v13:
time: 216 us; the launch traced here: 215 us
  starting transfers between devices  90.5 us (42%)
  waiting for transfers between devices  39.1 us (18%)
  blocking collectives  37.2 us (17%)
  local copies, waits for them, and re-layouts  16.4 us (8%)
  between operations  14.7 us (7%)
  matrix products  9.22 us (4%)
  other arithmetic  7.76 us (4%)
    ppermute x12, starting transfers between devices, move(): return lax.ppermute(value, axis, ring(step))  40.9 us
    ppermute x4, starting transfers between devices, joined(): got = lax.ppermute(value, axis, pairs(step))  32 us
    all_gather x1, waiting for transfers between devices, per_device(): lax.all_gather(own, ('zh', 'c'), axis=0, tiled=True)  25.9 us
    psum x1, blocking collectives, per_device(): score = lax.psum(placed(score, zh, 4), 'zh')  14.4 us
    ppermute x12, waiting for transfers between devices, move(): return lax.ppermute(value, axis, ring(step))  10.7 us
    psum x1, blocking collectives, per_device(): probes = lax.psum(placed(probe, x, 4), 'x')  10.6 us
    psum x1, blocking collectives, per_device(): sums = lax.psum(unpack(total[rows:], size), 'y')  9.84 us
    ppermute x1, starting transfers between devices, per_device(): total = lax.ppermute(total, ('y', 'zl'), turned()).astype(f32)  6.45 us
  transfers between devices with their start and end apart: 23, of which 7 were waited for; matrix products, arithmetic and copies ran while one was open for 11% of the time, Pallas kernels for 0%

profile of v13, /device:TPU:64, one launch (start us, length us, event | category | flops | bytes accessed | tf_op | source)
XLA Modules:
  0.0 214.9 jit_solution(7312346504764865149)
XLA Ops:
  7.2 1.7 slice.58
  9.0 4.9 %collective-permute-start.4 = (bf16[192,1024]{1,0:T(8,128)(2,1)}, bf16[192,1024]{1,0:T(8,128)(2,1)S(1)}, u32[]{:S(2)}, u32[]{:S(2)}) collective-permute-start(bf16[192,1024]{1,0:T(8,128)(2,1)} %param.7), channel_id=1, source_target_pairs={{0,96},{32,0},{64,32},{96,64},{1,97},{33,1},{65,33},{97,65},{2,98}... | collective-permute-start | bytes 1179656 | tf_op jit(solution)/shard_map/ppermute | solution.py:35
  13.9 2.5 %collective-permute-start.5 = (bf16[192,1024]{1,0:T(8,128)(2,1)}, bf16[192,1024]{1,0:T(8,128)(2,1)S(1)}, u32[]{:S(2)}, u32[]{:S(2)}) collective-permute-start(bf16[192,1024]{1,0:T(8,128)(2,1)} %param.7), channel_id=1, source_target_pairs={{0,64},{32,96},{64,0},{96,32},{1,65},{33,97},{65,1},{97,33},{2,66}... | collective-permute-start | bytes 1179656 | tf_op jit(solution)/shard_map/ppermute | solution.py:35
  16.4 2.9 %collective-permute-start.6 = (bf16[192,1024]{1,0:T(8,128)(2,1)}, bf16[192,1024]{1,0:T(8,128)(2,1)S(1)}, u32[]{:S(2)}, u32[]{:S(2)}) collective-permute-start(bf16[192,1024]{1,0:T(8,128)(2,1)} %param.7), channel_id=1, source_target_pairs={{0,32},{32,64},{64,96},{96,0},{1,33},{33,65},{65,97},{97,1},{2,34}... | collective-permute-start | bytes 1179656 | tf_op jit(solution)/shard_map/ppermute | solution.py:35
  19.3 0.9 dynamic_update_slice.14
  20.2 10.6 %psum.28 = f32[1280]{0:T(1024)S(1)} all-reduce(f32[1280]{0:T(1024)S(1)} %dynamic_update_slice.14), channel_id=1, replica_groups=mesh['zh'=4,'y'=4,'c'=2,'x'=4,'zl'=4] {'x'}, use_global_device_ids=true, to_apply=%region_0.0 | all-reduce | flops 1280 | bytes 10240 | tf_op jit(solution)/shard_map/psum | solution.py:91
  30.8 5.2 %collective-permute-start.10 = (f32[1280]{0:T(1024)S(1)}, f32[1280]{0:T(1024)}, u32[]{:S(2)}, u32[]{:S(2)}) collective-permute-start(f32[1280]{0:T(1024)S(1)} %psum.28), channel_id=1, source_target_pairs={{0,0},{1,32},{2,64},{3,96},{32,1},{33,33},{34,65},{35,97},{64,2},{... | collective-permute-start | bytes 15368 | tf_op jit(solution)/shard_map/ppermute | solution.py:92
  36.0 1.6 multiply_reduce_fusion.1
  37.6 4.0 %collective-permute-start = (bf16[32,320]{1,0:T(8,128)(2,1)}, bf16[32,320]{1,0:T(8,128)(2,1)}, u32[]{:S(2)}, u32[]{:S(2)}) collective-permute-start(bf16[32,320]{1,0:T(8,128)(2,1)} %get-tuple-element.21), channel_id=1, source_target_pairs={{0,0},{1,32},{2,64},{3,96},{4,128},{5,160},{6,192},{7,224},{8,256}... | collective-permute-start | bytes 61448 | tf_op jit(solution)/shard_map/ppermute | solution.py:95
  41.6 1.0 mul.96
  42.7 0.8 constant_dynamic-update-slice_fusion.3
  44.4 0.8 mul.106
  45.1 0.8 mul.107
  46.5 0.8 reshape.480
  47.5 0.9 broadcast_select_fusion.9
  48.4 1.9 collective-permute-start.1
  50.4 1.0 collective-permute-done.1
  51.6 11.2 %collective-permute-start.2 = (bf16[16,768]{1,0:T(8,128)(2,1)S(1)}, bf16[16,768]{1,0:T(8,128)(2,1)S(1)}, u32[]{:S(2)}, u32[]{:S(2)}) collective-permute-start(bf16[16,768]{1,0:T(8,128)(2,1)S(1)} %reshape.474), channel_id=1, source_target_pairs={{0,4},{4,0},{8,12},{12,8},{1,5},{5,1},{9,13},{13,9},{2,6},{6,2},{1... | collective-permute-start | bytes 73736 | tf_op jit(solution)/shard_map/ppermute | solution.py:44
  63.4 1.1 collective-permute-done.2
  65.2 14.0 %collective-permute-start.3 = (bf16[32,768]{1,0:T(8,128)(2,1)}, bf16[32,768]{1,0:T(8,128)(2,1)}, u32[]{:S(2)}, u32[]{:S(2)}) collective-permute-start(bf16[32,768]{1,0:T(8,128)(2,1)} %pad_maximum_fusion.13), channel_id=1, source_target_pairs={{0,12},{4,8},{8,4},{12,0},{1,13},{5,9},{9,5},{13,1},{2,14},{6,10},... | collective-permute-start | bytes 147464 | tf_op jit(solution)/shard_map/ppermute | solution.py:44
  79.2 0.8 constant_dynamic-update-slice_fusion.2
  80.1 0.9 constant_dynamic-update-slice_fusion.1
  80.9 0.8 constant_dynamic-update-slice_fusion
  81.8 3.9 %fusion = bf16[1024,768]{0,1:T(8,128)(2,1)S(1)} fusion(bf16[768,1024]{1,0:T(8,128)(2,1)} %constant_dynamic-update-slice_fusion, bf16[1024,1024]{1,0:T(8,128)(2,1)} %all-gather.7.cloned.1.call-done), kind=kOutput, calls=%fused_computation.3 | convolution fusion | flops 1611399168 | bytes 5242880 | tf_op jit(solution)/shard_map/dot_general | solution.py:108
  85.7 0.7 copy.40
  86.5 1.0 dynamic-slice_bitcast_fusion
  87.5 1.9 collective-permute-start.7
  89.4 3.4 %collective-permute-start.8 = (bf16[256,768]{1,0:T(8,128)(2,1)}, bf16[256,768]{1,0:T(8,128)(2,1)S(1)}, u32[]{:S(2)}, u32[]{:S(2)}) collective-permute-start(bf16[256,768]{1,0:T(8,128)(2,1)} %get-tuple-element.23), channel_id=1, source_target_pairs={{0,8},{4,12},{8,0},{12,4},{1,9},{5,13},{9,1},{13,5},{2,10},{6,14},... | collective-permute-start | bytes 1179656 | tf_op jit(solution)/shard_map/ppermute | solution.py:35
  92.8 3.7 %collective-permute-start.9 = (bf16[256,768]{1,0:T(8,128)(2,1)S(1)}, bf16[256,768]{1,0:T(8,128)(2,1)S(1)}, u32[]{:S(2)}, u32[]{:S(2)}) collective-permute-start(bf16[256,768]{1,0:T(8,128)(2,1)S(1)} %get-tuple-element.22), channel_id=1, source_target_pairs={{0,12},{4,0},{8,4},{12,8},{1,13},{5,1},{9,5},{13,9},{2,14},{6,2},{... | collective-permute-start | bytes 1179656 | tf_op jit(solution)/shard_map/ppermute | solution.py:35
  96.5 0.8 broadcast_select_fusion.5
  97.7 25.9 %all-gather.5.cloned.1.call-done = bf16[512,1024]{1,0:T(8,128)(2,1)} async-done(((bf16[64,1024]{1,0:T(8,128)(2,1)}), bf16[512,1024]{1,0:T(8,128)(2,1)}) %all-gather.5.cloned.1.call-update) | async-done | bytes 1048592 | tf_op jit(solution)/shard_map/all_gather | solution.py:98
  123.7 2.2 %fusion.25 = (bf16[4,2,32,1024]{3,2,1,0:T(8,128)(2,1)}, bf16[4,2,32,1024]{3,2,1,0:T(8,128)(2,1)S(1)}) fusion(bf16[4,2,64,1024]{3,2,1,0:T(8,128)(2,1)} %bitcast.68), kind=kLoop, calls=%fused_computation.119 | loop fusion | bytes 2097152 | tf_op jit(solution)/shard_map/slice | solution.py:120
  128.1 4.2 %collective-permute-start.13 = (bf16[72,768]{1,0:T(8,128)(2,1)S(1)}, bf16[72,768]{1,0:T(8,128)(2,1)S(1)}, u32[]{:S(2)}, u32[]{:S(2)}) collective-permute-start(bf16[72,768]{1,0:T(8,128)(2,1)S(1)} %get-tuple-element.51), channel_id=1, source_target_pairs={{0,12},{4,0},{8,4},{12,8},{1,13},{5,1},{9,5},{13,9},{2,14},{6,2},{... | collective-permute-start | bytes 331784 | tf_op jit(solution)/shard_map/ppermute | solution.py:35
  132.3 2.9 %collective-permute-start.12 = (bf16[72,768]{1,0:T(8,128)(2,1)S(1)}, bf16[72,768]{1,0:T(8,128)(2,1)S(1)}, u32[]{:S(2)}, u32[]{:S(2)}) collective-permute-start(bf16[72,768]{1,0:T(8,128)(2,1)S(1)} %get-tuple-element.50), channel_id=1, source_target_pairs={{0,8},{4,12},{8,0},{12,4},{1,9},{5,13},{9,1},{13,5},{2,10},{6,14},... | collective-permute-start | bytes 331784 | tf_op jit(solution)/shard_map/ppermute | solution.py:35
  135.2 2.8 %collective-permute-start.11 = (bf16[72,768]{1,0:T(8,128)(2,1)S(1)}, bf16[72,768]{1,0:T(8,128)(2,1)S(1)}, u32[]{:S(2)}, u32[]{:S(2)}) collective-permute-start(bf16[72,768]{1,0:T(8,128)(2,1)S(1)} %get-tuple-element.49), channel_id=1, source_target_pairs={{0,4},{4,8},{8,12},{12,0},{1,5},{5,9},{9,13},{13,1},{2,6},{6,10},{... | collective-permute-start | bytes 331784 | tf_op jit(solution)/shard_map/ppermute | solution.py:35
  138.0 4.3 %collective-permute-start.18 = (bf16[64,768]{1,0:T(8,128)(2,1)S(1)}, bf16[64,768]{1,0:T(8,128)(2,1)S(1)}, u32[]{:S(2)}, u32[]{:S(2)}) collective-permute-start(bf16[64,768]{1,0:T(8,128)(2,1)S(1)} %pad_maximum_fusion.12), channel_id=1, source_target_pairs={{0,1},{1,0},{2,3},{3,2},{4,5},{5,4},{6,7},{7,6},{8,9},{9,8},{10,11... | collective-permute-start | bytes 294920 | tf_op jit(solution)/shard_map/ppermute | solution.py:44
  144.0 3.4 %collective-permute-start.16 = (bf16[208,320]{1,0:T(8,128)(2,1)S(1)}, bf16[208,320]{1,0:T(8,128)(2,1)S(1)}, u32[]{:S(2)}, u32[]{:S(2)}) collective-permute-start(bf16[208,320]{1,0:T(8,128)(2,1)S(1)} %get-tuple-element.48), channel_id=1, source_target_pairs={{0,3},{1,0},{2,1},{3,2},{4,7},{5,4},{6,5},{7,6},{8,11},{9,8},{10,9... | collective-permute-start | bytes 399368 | tf_op jit(solution)/shard_map/ppermute | solution.py:35
  147.4 5.1 %collective-permute-start.15 = (bf16[208,320]{1,0:T(8,128)(2,1)S(1)}, bf16[208,320]{1,0:T(8,128)(2,1)S(1)}, u32[]{:S(2)}, u32[]{:S(2)}) collective-permute-start(bf16[208,320]{1,0:T(8,128)(2,1)S(1)} %get-tuple-element.47), channel_id=1, source_target_pairs={{0,2},{1,3},{2,0},{3,1},{4,6},{5,7},{6,4},{7,5},{8,10},{9,11},{10,... | collective-permute-start | bytes 399368 | tf_op jit(solution)/shard_map/ppermute | solution.py:35
  152.6 3.3 %collective-permute-start.14 = (bf16[208,320]{1,0:T(8,128)(2,1)S(1)}, bf16[208,320]{1,0:T(8,128)(2,1)S(1)}, u32[]{:S(2)}, u32[]{:S(2)}) collective-permute-start(bf16[208,320]{1,0:T(8,128)(2,1)S(1)} %get-tuple-element.46), channel_id=1, source_target_pairs={{0,1},{1,2},{2,3},{3,0},{4,5},{5,6},{6,7},{7,4},{8,9},{9,10},{10,1... | collective-permute-start | bytes 399368 | tf_op jit(solution)/shard_map/ppermute | solution.py:35
  155.9 2.6 %collective-permute-start.19 = (bf16[128,768]{1,0:T(8,128)(2,1)S(1)}, bf16[128,768]{1,0:T(8,128)(2,1)S(1)}, u32[]{:S(2)}, u32[]{:S(2)}) collective-permute-start(bf16[128,768]{1,0:T(8,128)(2,1)S(1)} %pad_maximum_fusion.10), channel_id=1, source_target_pairs={{0,3},{1,2},{2,1},{3,0},{4,7},{5,6},{6,5},{7,4},{8,11},{9,10},{10,... | collective-permute-start | bytes 589832 | tf_op jit(solution)/shard_map/ppermute | solution.py:44
  158.5 8.4 %collective-permute-done.15 = bf16[208,320]{1,0:T(8,128)(2,1)S(1)} collective-permute-done((bf16[208,320]{1,0:T(8,128)(2,1)S(1)}, bf16[208,320]{1,0:T(8,128)(2,1)S(1)}, u32[]{:S(2)}, u32[]{:S(2)}) %collective-permute-start.15) | collective-permute-done | bytes 133152 | tf_op jit(solution)/shard_map/ppermute | solution.py:35
  167.0 1.6 collective-permute-done.14
  168.7 6.5 %collective-permute-start.17 = (bf16[192,320]{1,0:T(8,128)(2,1)S(1)}, bf16[192,320]{1,0:T(8,128)(2,1)S(1)}, u32[]{:S(2)}, u32[]{:S(2)}) collective-permute-start(bf16[192,320]{1,0:T(8,128)(2,1)S(1)} %slice.89), channel_id=1, source_target_pairs={{0,0},{1,32},{2,64},{3,96},{32,1},{33,33},{34,65},{35,97},{64,2},{... | collective-permute-start | bytes 368648 | tf_op jit(solution)/shard_map/ppermute | solution.py:175
  175.2 9.8 %psum.29 = f32[1664]{0:T(1024)S(1)} all-reduce(f32[1664]{0:T(1024)S(1)} %reduce_sum.120), channel_id=1, replica_groups=mesh['zh'=4,'y'=4,'c'=2,'x'=4,'zl'=4] {'y'}, use_global_device_ids=true, to_apply=%region_11.12 | all-reduce | flops 1664 | bytes 13312 | tf_op jit(solution)/shard_map/psum | solution.py:162
  185.9 2.4 %psum.30 = f32[256]{0:T(256)S(1)} all-reduce(f32[256]{0:T(256)S(1)} %reshape.494), channel_id=1, replica_groups=mesh['zh'=4,'y'=4,'c'=2,'x'=4,'zl'=4] {'c'}, use_global_device_ids=true, to_apply=%region_13.14 | all-reduce | flops 256 | bytes 2048 | tf_op jit(solution)/shard_map/psum | solution.py:172
  188.5 14.4 %psum.31 = f32[1024]{0:T(1024)S(1)} all-reduce(f32[1024]{0:T(1024)S(1)} %dynamic_update_slice.17), channel_id=1, replica_groups=mesh['zh'=4,'y'=4,'c'=2,'x'=4,'zl'=4] {'zh'}, use_global_device_ids=true, to_apply=%region_14.15 | all-reduce | flops 1024 | bytes 8192 | tf_op jit(solution)/shard_map/psum | solution.py:173
  204.3 0.8 add_convert_fusion.1
  205.1 3.3 %convolution_multiply_fusion = f32[160,1024]{1,0:T(8,128)} fusion(bf16[1024,1024]{1,0:T(8,128)(2,1)} %bitcast.85, bf16[1024,192]{1,0:T(8,128)(2,1)S(1)} %reshape.496, f32[1024]{0:T(1024)S(1)} %mul.118), kind=kOutput, calls=%fused_computation.4 | convolution fusion | flops 336199680 | bytes 3149824 | tf_op jit(solution)/shard_map/dot_general | solution.py:186
  (155 shorter events, 10.2 us)
Async XLA Ops:
  7.2 74.7 %all-gather.7.cloned.1.call-start = ((), (), s32[]{:S(2)}) async-start(), calls=%async_computation.1 | async-start | bytes 2359296 | tf_op jit(solution)/shard_map/all_gather | solution.py:87
  8.9 114.7 %all-gather.5.cloned.1.call-start = ((), (), s32[]{:S(2)}) async-start(), calls=%async_computation | async-start | bytes 1179648 | tf_op jit(solution)/shard_map/all_gather | solution.py:98
  9.0 70.3 %collective-permute-start.4 = (bf16[192,1024]{1,0:T(8,128)(2,1)}, bf16[192,1024]{1,0:T(8,128)(2,1)S(1)}, u32[]{:S(2)}, u32[]{:S(2)}) collective-permute-start(bf16[192,1024]{1,0:T(8,128)(2,1)} %param.7), channel_id=1, source_target_pairs={{0,96},{32,0},{64,32},{96,64},{1,97},{33,1},{65,33},{97,65},{2,98}... | collective-permute-start | bytes 1179656 | tf_op jit(solution)/shard_map/ppermute | solution.py:35
  13.9 66.2 %collective-permute-start.5 = (bf16[192,1024]{1,0:T(8,128)(2,1)}, bf16[192,1024]{1,0:T(8,128)(2,1)S(1)}, u32[]{:S(2)}, u32[]{:S(2)}) collective-permute-start(bf16[192,1024]{1,0:T(8,128)(2,1)} %param.7), channel_id=1, source_target_pairs={{0,64},{32,96},{64,0},{96,32},{1,65},{33,97},{65,1},{97,33},{2,66}... | collective-permute-start | bytes 1179656 | tf_op jit(solution)/shard_map/ppermute | solution.py:35
  16.4 64.5 %collective-permute-start.6 = (bf16[192,1024]{1,0:T(8,128)(2,1)}, bf16[192,1024]{1,0:T(8,128)(2,1)S(1)}, u32[]{:S(2)}, u32[]{:S(2)}) collective-permute-start(bf16[192,1024]{1,0:T(8,128)(2,1)} %param.7), channel_id=1, source_target_pairs={{0,32},{32,64},{64,96},{96,0},{1,33},{33,65},{65,97},{97,1},{2,34}... | collective-permute-start | bytes 1179656 | tf_op jit(solution)/shard_map/ppermute | solution.py:35
  30.8 15.3 %collective-permute-start.10 = (f32[1280]{0:T(1024)S(1)}, f32[1280]{0:T(1024)}, u32[]{:S(2)}, u32[]{:S(2)}) collective-permute-start(f32[1280]{0:T(1024)S(1)} %psum.28), channel_id=1, source_target_pairs={{0,0},{1,32},{2,64},{3,96},{32,1},{33,33},{34,65},{35,97},{64,2},{... | collective-permute-start | bytes 15368 | tf_op jit(solution)/shard_map/ppermute | solution.py:92
  36.0 6.7 %copy-start = (bf16[192,1024]{1,0:T(8,128)(2,1)S(1)}, bf16[192,1024]{1,0:T(8,128)(2,1)}, u32[]{:S(2)}) copy-start(bf16[192,1024]{1,0:T(8,128)(2,1)} %param.7) | copy-start | bytes 1179652
  37.6 9.9 %collective-permute-start = (bf16[32,320]{1,0:T(8,128)(2,1)}, bf16[32,320]{1,0:T(8,128)(2,1)}, u32[]{:S(2)}, u32[]{:S(2)}) collective-permute-start(bf16[32,320]{1,0:T(8,128)(2,1)} %get-tuple-element.21), channel_id=1, source_target_pairs={{0,0},{1,32},{2,64},{3,96},{4,128},{5,160},{6,192},{7,224},{8,256}... | collective-permute-start | bytes 61448 | tf_op jit(solution)/shard_map/ppermute | solution.py:95
  42.6 1.1 slice-start
  42.6 1.1 copy-start.9
  46.0 0.6 copy-start.20
  48.4 3.1 %collective-permute-start.1 = (bf16[32,160]{1,0:T(8,128)(2,1)S(1)}, bf16[32,160]{1,0:T(8,128)(2,1)S(1)}, u32[]{:S(2)}, u32[]{:S(2)}) collective-permute-start(bf16[32,160]{1,0:T(8,128)(2,1)S(1)} %get-tuple-element.45), channel_id=1, source_target_pairs={{0,16},{16,0},{1,17},{17,1},{2,18},{18,2},{3,19},{19,3},{4,20},{20... | collective-permute-start | bytes 30728 | tf_op jit(solution)/shard_map/ppermute | solution.py:101
  51.6 13.0 %collective-permute-start.2 = (bf16[16,768]{1,0:T(8,128)(2,1)S(1)}, bf16[16,768]{1,0:T(8,128)(2,1)S(1)}, u32[]{:S(2)}, u32[]{:S(2)}) collective-permute-start(bf16[16,768]{1,0:T(8,128)(2,1)S(1)} %reshape.474), channel_id=1, source_target_pairs={{0,4},{4,0},{8,12},{12,8},{1,5},{5,1},{9,13},{13,9},{2,6},{6,2},{1... | collective-permute-start | bytes 73736 | tf_op jit(solution)/shard_map/ppermute | solution.py:44
  63.4 141.7 %all-gather.9.cloned.1.call-start = ((), (), s32[]{:S(2)}) async-start(), calls=%async_computation.2 | async-start | bytes 2621440 | tf_op jit(solution)/shard_map/all_gather | solution.py:120
  64.6 0.6 copy-start.10
  64.6 14.6 %copy-start.12 = (bf16[16,768]{1,0:T(8,128)(2,1)}, bf16[16,768]{1,0:T(8,128)(2,1)S(1)}, u32[]{:S(2)}) copy-start(bf16[16,768]{1,0:T(8,128)(2,1)S(1)} %get-tuple-element.43) | copy-start | bytes 73732
  65.2 31.2 %collective-permute-start.3 = (bf16[32,768]{1,0:T(8,128)(2,1)}, bf16[32,768]{1,0:T(8,128)(2,1)}, u32[]{:S(2)}, u32[]{:S(2)}) collective-permute-start(bf16[32,768]{1,0:T(8,128)(2,1)} %pad_maximum_fusion.13), channel_id=1, source_target_pairs={{0,12},{4,8},{8,4},{12,0},{1,13},{5,9},{9,5},{13,1},{2,14},{6,10},... | collective-permute-start | bytes 147464 | tf_op jit(solution)/shard_map/ppermute | solution.py:44
  79.2 2.5 %copy-start.2 = (bf16[192,1024]{1,0:T(8,128)(2,1)}, bf16[192,1024]{1,0:T(8,128)(2,1)S(1)}, u32[]{:S(2)}) copy-start(bf16[192,1024]{1,0:T(8,128)(2,1)S(1)} %collective-permute-done.4) | copy-start | bytes 1179652
  80.1 1.7 copy-start.4
  80.9 0.9 copy-start.6
  86.4 10.0 %copy-start.11 = (bf16[16,768]{1,0:T(8,128)(2,1)S(1)}, bf16[16,768]{1,0:T(8,128)(2,1)}, u32[]{:S(2)}) copy-start(bf16[16,768]{1,0:T(8,128)(2,1)} %copy-done.10) | copy-start | bytes 73732
  86.5 10.0 %copy-start.13 = (bf16[16,768]{1,0:T(8,128)(2,1)S(1)}, bf16[16,768]{1,0:T(8,128)(2,1)}, u32[]{:S(2)}) copy-start(bf16[16,768]{1,0:T(8,128)(2,1)} %copy-done.12) | copy-start | bytes 73732
  86.5 10.9 %copy-start.1 = (bf16[1024,1024]{1,0:T(8,128)(2,1)S(1)}, bf16[1024,1024]{1,0:T(8,128)(2,1)}, u32[]{:S(2)}) copy-start(bf16[1024,1024]{1,0:T(8,128)(2,1)} %all-gather.7.cloned.1.call-done) | copy-start | bytes 6291460
  87.5 36.2 %collective-permute-start.7 = (bf16[256,768]{1,0:T(8,128)(2,1)}, bf16[256,768]{1,0:T(8,128)(2,1)S(1)}, u32[]{:S(2)}, u32[]{:S(2)}) collective-permute-start(bf16[256,768]{1,0:T(8,128)(2,1)} %get-tuple-element.24), channel_id=1, source_target_pairs={{0,4},{4,8},{8,12},{12,0},{1,5},{5,9},{9,13},{13,1},{2,6},{6,10},{... | collective-permute-start | bytes 1179656 | tf_op jit(solution)/shard_map/ppermute | solution.py:35
  89.4 34.3 %collective-permute-start.8 = (bf16[256,768]{1,0:T(8,128)(2,1)}, bf16[256,768]{1,0:T(8,128)(2,1)S(1)}, u32[]{:S(2)}, u32[]{:S(2)}) collective-permute-start(bf16[256,768]{1,0:T(8,128)(2,1)} %get-tuple-element.23), channel_id=1, source_target_pairs={{0,8},{4,12},{8,0},{12,4},{1,9},{5,13},{9,1},{13,5},{2,10},{6,14},... | collective-permute-start | bytes 1179656 | tf_op jit(solution)/shard_map/ppermute | solution.py:35
  92.8 30.9 %collective-permute-start.9 = (bf16[256,768]{1,0:T(8,128)(2,1)S(1)}, bf16[256,768]{1,0:T(8,128)(2,1)S(1)}, u32[]{:S(2)}, u32[]{:S(2)}) collective-permute-start(bf16[256,768]{1,0:T(8,128)(2,1)S(1)} %get-tuple-element.22), channel_id=1, source_target_pairs={{0,12},{4,0},{8,4},{12,8},{1,13},{5,1},{9,5},{13,9},{2,14},{6,2},{... | collective-permute-start | bytes 1179656 | tf_op jit(solution)/shard_map/ppermute | solution.py:35
  123.7 2.2 %copy-start.14 = (bf16[768,1024]{1,0:T(8,128)(2,1)S(1)}, bf16[768,1024]{1,0:T(8,128)(2,1)}, u32[]{:S(2)}) copy-start(bf16[768,1024]{1,0:T(8,128)(2,1)} %constant_dynamic-update-slice_fusion) | copy-start | bytes 4718596
  125.9 0.7 copy-start.15
  125.9 0.7 copy-start.16
  125.9 0.7 copy-start.17
  125.9 1.2 copy-start.3
  125.9 1.4 copy-start.5
  125.9 1.6 copy-start.7
  126.5 1.4 copy-start.21
  128.1 14.3 %collective-permute-start.13 = (bf16[72,768]{1,0:T(8,128)(2,1)S(1)}, bf16[72,768]{1,0:T(8,128)(2,1)S(1)}, u32[]{:S(2)}, u32[]{:S(2)}) collective-permute-start(bf16[72,768]{1,0:T(8,128)(2,1)S(1)} %get-tuple-element.51), channel_id=1, source_target_pairs={{0,12},{4,0},{8,4},{12,8},{1,13},{5,1},{9,5},{13,9},{2,14},{6,2},{... | collective-permute-start | bytes 331784 | tf_op jit(solution)/shard_map/ppermute | solution.py:35
  132.3 10.2 %collective-permute-start.12 = (bf16[72,768]{1,0:T(8,128)(2,1)S(1)}, bf16[72,768]{1,0:T(8,128)(2,1)S(1)}, u32[]{:S(2)}, u32[]{:S(2)}) collective-permute-start(bf16[72,768]{1,0:T(8,128)(2,1)S(1)} %get-tuple-element.50), channel_id=1, source_target_pairs={{0,8},{4,12},{8,0},{12,4},{1,9},{5,13},{9,1},{13,5},{2,10},{6,14},... | collective-permute-start | bytes 331784 | tf_op jit(solution)/shard_map/ppermute | solution.py:35
  135.2 8.0 %collective-permute-start.11 = (bf16[72,768]{1,0:T(8,128)(2,1)S(1)}, bf16[72,768]{1,0:T(8,128)(2,1)S(1)}, u32[]{:S(2)}, u32[]{:S(2)}) collective-permute-start(bf16[72,768]{1,0:T(8,128)(2,1)S(1)} %get-tuple-element.49), channel_id=1, source_target_pairs={{0,4},{4,8},{8,12},{12,0},{1,5},{5,9},{9,13},{13,1},{2,6},{6,10},{... | collective-permute-start | bytes 331784 | tf_op jit(solution)/shard_map/ppermute | solution.py:35
  138.0 17.9 %collective-permute-start.18 = (bf16[64,768]{1,0:T(8,128)(2,1)S(1)}, bf16[64,768]{1,0:T(8,128)(2,1)S(1)}, u32[]{:S(2)}, u32[]{:S(2)}) collective-permute-start(bf16[64,768]{1,0:T(8,128)(2,1)S(1)} %pad_maximum_fusion.12), channel_id=1, source_target_pairs={{0,1},{1,0},{2,3},{3,2},{4,5},{5,4},{6,7},{7,6},{8,9},{9,8},{10,11... | collective-permute-start | bytes 294920 | tf_op jit(solution)/shard_map/ppermute | solution.py:44
  143.9 58.9 %copy-start.18 = (s32[1024]{0:T(1024)S(1)}, s32[1024]{0:T(1024)}, u32[]{:S(2)}) copy-start(s32[1024]{0:T(1024)} %param.13) | copy-start | bytes 12292
  144.0 59.5 %copy-start.19 = (f32[1024]{0:T(1024)S(1)}, f32[1024]{0:T(1024)}, u32[]{:S(2)}) copy-start(f32[1024]{0:T(1024)} %param.12) | copy-start | bytes 12292
  144.0 14.5 %collective-permute-start.16 = (bf16[208,320]{1,0:T(8,128)(2,1)S(1)}, bf16[208,320]{1,0:T(8,128)(2,1)S(1)}, u32[]{:S(2)}, u32[]{:S(2)}) collective-permute-start(bf16[208,320]{1,0:T(8,128)(2,1)S(1)} %get-tuple-element.48), channel_id=1, source_target_pairs={{0,3},{1,0},{2,1},{3,2},{4,7},{5,4},{6,5},{7,6},{8,11},{9,8},{10,9... | collective-permute-start | bytes 399368 | tf_op jit(solution)/shard_map/ppermute | solution.py:35
  147.4 19.5 %collective-permute-start.15 = (bf16[208,320]{1,0:T(8,128)(2,1)S(1)}, bf16[208,320]{1,0:T(8,128)(2,1)S(1)}, u32[]{:S(2)}, u32[]{:S(2)}) collective-permute-start(bf16[208,320]{1,0:T(8,128)(2,1)S(1)} %get-tuple-element.47), channel_id=1, source_target_pairs={{0,2},{1,3},{2,0},{3,1},{4,6},{5,7},{6,4},{7,5},{8,10},{9,11},{10,... | collective-permute-start | bytes 399368 | tf_op jit(solution)/shard_map/ppermute | solution.py:35
  152.6 15.9 %collective-permute-start.14 = (bf16[208,320]{1,0:T(8,128)(2,1)S(1)}, bf16[208,320]{1,0:T(8,128)(2,1)S(1)}, u32[]{:S(2)}, u32[]{:S(2)}) collective-permute-start(bf16[208,320]{1,0:T(8,128)(2,1)S(1)} %get-tuple-element.46), channel_id=1, source_target_pairs={{0,1},{1,2},{2,3},{3,0},{4,5},{5,6},{6,7},{7,4},{8,9},{9,10},{10,1... | collective-permute-start | bytes 399368 | tf_op jit(solution)/shard_map/ppermute | solution.py:35
  155.9 47.8 %collective-permute-start.19 = (bf16[128,768]{1,0:T(8,128)(2,1)S(1)}, bf16[128,768]{1,0:T(8,128)(2,1)S(1)}, u32[]{:S(2)}, u32[]{:S(2)}) collective-permute-start(bf16[128,768]{1,0:T(8,128)(2,1)S(1)} %pad_maximum_fusion.10), channel_id=1, source_target_pairs={{0,3},{1,2},{2,1},{3,0},{4,7},{5,6},{6,5},{7,4},{8,11},{9,10},{10,... | collective-permute-start | bytes 589832 | tf_op jit(solution)/shard_map/ppermute | solution.py:44
  168.6 35.7 %copy-start.8 = (f32[192,320]{1,0:T(8,128)S(1)}, f32[192,320]{1,0:T(8,128)}, u32[]{:S(2)}) copy-start(f32[192,320]{1,0:T(8,128)} %mul.107) | copy-start | bytes 737284
  168.7 35.6 %collective-permute-start.17 = (bf16[192,320]{1,0:T(8,128)(2,1)S(1)}, bf16[192,320]{1,0:T(8,128)(2,1)S(1)}, u32[]{:S(2)}, u32[]{:S(2)}) collective-permute-start(bf16[192,320]{1,0:T(8,128)(2,1)S(1)} %slice.89), channel_id=1, source_target_pairs={{0,0},{1,32},{2,64},{3,96},{32,1},{33,33},{34,65},{35,97},{64,2},{... | collective-permute-start | bytes 368648 | tf_op jit(solution)/shard_map/ppermute | solution.py:175
Sparse Core Ops, SparseCore 0:
  10.7 61.9 all-gather.6
  75.4 48.1 all-gather.4
  138.1 35.5 all-gather.8

commit v14 on v12

--- a/solution.py
+++ b/solution.py
@@ -129,13 +129,24 @@
     ).astype(bf16).reshape(4, cols, many)
     ride = jnp.concatenate([pack(sums, many), lefts], axis=0)
     end = part.shape[1] + ride.shape[0] - lefts.shape[0]
-    parts = []
-    for k in range(4):
-        one = lax.dynamic_index_in_dim(part, lax.rem(x + k, 4), 0, keepdims=False)
-        one = jnp.concatenate([one, ride], axis=0)
-        parts.append(one if k == 0 else move(one, "x", k))
-    total = sum(p[:end].astype(f32) for p in parts)
-    lefts = jnp.stack([parts[k][end:] for k in (0, 3, 2, 1)])
+    parts = [
+        jnp.concatenate([
+            lax.dynamic_index_in_dim(part, lax.rem(x + k, 4), 0, keepdims=False), ride
+        ], axis=0)
+        for k in range(4)
+    ]
+    cut = 168
+    near = parts[3]
+    passing = move(parts[2][:cut], "x", -1)
+    two = move(parts[2][cut:], "x", 2)
+    passing, two = lax.optimization_barrier((passing, two))
+    one = move(parts[1], "x", 1)
+    added = (near[:cut].astype(f32) + passing.astype(f32)).astype(bf16)
+    near = jnp.concatenate([added, near[cut:]], axis=0)
+    three = move(near, "x", -1)
+    total = parts[0][:end].astype(f32) + one[:end].astype(f32) + three[:end].astype(f32)
+    total = jnp.concatenate([total[:cut], total[cut:] + two[: end - cut].astype(f32)], axis=0)
+    lefts = jnp.stack([parts[0][end:], three[end:], two[end - cut :], one[end:]])
     lefts, total = lax.optimization_barrier((lefts, total))
     lefts = joined(jnp.roll(lefts, x, axis=0).reshape(-1, many), "zl", zl)
     ride = pack(unpack(total[cols:], size), cols)

time: 197 us -> 201 us (1.020)
  starting transfers between devices: 51.4 us -> 60.3 us
  waiting for transfers between devices: 40.5 us -> 36.9 us
    ppermute x9 -> x10, starting transfers between devices: 29.8 us -> 35.8 us  [move(): return lax.ppermute(value, axis, ring(step))]
    ppermute x1, starting transfers between devices: 6.79 us -> 11.1 us  [per_device(): total = lax.ppermute(total, ('y', 'zl'), turned()).astype(f32)]
    ppermute x9 -> x10, waiting for transfers between devices: 29.7 us -> 26.5 us  [move(): return lax.ppermute(value, axis, ring(step))]
  transfers between devices with their start and end apart: 16 -> 17, of which waited for: 7 -> 7; matrix products, arithmetic and copies ran while one was open for 6% -> 6% of each run, Pallas kernels for 0% -> 0%
where the time goes in v14:
time: 201 us
  blocking collectives  65.7 us (33%)
  starting transfers between devices  60.3 us (30%)
  waiting for transfers between devices  36.9 us (18%)
  between operations  14.8 us (7%)
  local copies, waits for them, and re-layouts  9 us (4%)
  other arithmetic  7.47 us (4%)
  matrix products  6.36 us (3%)
    psum x1, blocking collectives, per_device(): direction = lax.psum(direction, 'zh')  41.1 us
    ppermute x10, starting transfers between devices, move(): return lax.ppermute(value, axis, ring(step))  35.8 us
    ppermute x10, waiting for transfers between devices, move(): return lax.ppermute(value, axis, ring(step))  26.5 us
    psum x1, blocking collectives, per_device(): score = lax.psum(placed(score, zh, 4), 'zh')  12.1 us
    ppermute x1, starting transfers between devices, per_device(): total = lax.ppermute(total, ('y', 'zl'), turned()).astype(f32)  11.1 us
    psum x1, blocking collectives, per_device(): early = lax.psum(early, 'y')  7.57 us
    all_gather x1, waiting for transfers between devices, per_device(): lax.all_gather(own, ('zh', 'c'), axis=0, tiled=True)  6.59 us
    ppermute x1, starting transfers between devices, per_device(): other = lax.ppermute(other, AXES, swapped(1))  5.62 us
  transfers between devices with their start and end apart: 17, of which 7 were waited for; matrix products, arithmetic and copies ran while one was open for 6% of the time, Pallas kernels for 0%

profile of v14, /device:TPU:24, one launch (start us, length us, event | category | flops | bytes accessed | tf_op | source)
XLA Modules:
  0.0 200.6 jit_solution(4831977492448627240)
XLA Ops:
  7.2 1.8 pad_maximum_fusion.5
  9.1 0.9 dynamic-slice_convert_fusion
  10.0 5.6 %collective-permute-start.1 = (bf16[32,160]{1,0:T(8,128)(2,1)S(1)}, bf16[32,160]{1,0:T(8,128)(2,1)S(1)}, u32[]{:S(2)}, u32[]{:S(2)}) collective-permute-start(bf16[32,160]{1,0:T(8,128)(2,1)S(1)} %slice_select_fusion), channel_id=1, source_target_pairs={{0,16},{1,48},{2,80},{3,112},{4,144},{5,176},{6,208},{7,240},{8,27... | collective-permute-start | bytes 30728 | tf_op jit(solution)/shard_map/ppermute | solution.py:95
  15.7 0.7 broadcast_in_dim.37
  16.5 3.7 %collective-permute-start = (f32[33,160]{1,0:T(8,128)S(1)}, f32[33,160]{1,0:T(8,128)S(1)}, u32[]{:S(2)}, u32[]{:S(2)}) collective-permute-start(f32[33,160]{1,0:T(8,128)S(1)} %fusion.16), channel_id=1, source_target_pairs={{0,0},{1,32},{2,64},{3,96},{4,128},{5,160},{6,192},{7,224},{8,256}... | collective-permute-start | bytes 63368 | tf_op jit(solution)/shard_map/ppermute | solution.py:94
  20.2 1.0 mul.105
  21.4 1.0 multiply_reduce_fusion.2
  22.4 0.2 dynamic_update_slice.10
  22.7 0.2 dynamic_update_slice.9
  22.9 3.7 %collective-permute-done = f32[33,160]{1,0:T(8,128)S(1)} collective-permute-done((f32[33,160]{1,0:T(8,128)S(1)}, f32[33,160]{1,0:T(8,128)S(1)}, u32[]{:S(2)}, u32[]{:S(2)}) %collective-permute-start) | collective-permute-done | bytes 21152 | tf_op jit(solution)/shard_map/ppermute | solution.py:94
  26.7 2.5 %psum.35 = f32[1024]{0:T(1024)S(1)} all-reduce(f32[1024]{0:T(1024)S(1)} %multiply_reduce_fusion.1), channel_id=1, replica_groups=mesh['zh'=4,'y'=4,'c'=2,'x'=4,'zl'=4] {'c'}, use_global_device_ids=true, to_apply=%region_1.2 | all-reduce | flops 1024 | bytes 8192 | tf_op jit(solution)/shard_map/psum | solution.py:104
  29.2 7.6 %psum.36 = f32[1920]{0:T(1024)S(1)} all-reduce(f32[1920]{0:T(1024)S(1)} %pad_maximum_fusion.18), channel_id=1, replica_groups=mesh['zh'=4,'y'=4,'c'=2,'x'=4,'zl'=4] {'y'}, use_global_device_ids=true, to_apply=%region_4.5 | all-reduce | flops 1920 | bytes 15360 | tf_op jit(solution)/shard_map/psum | solution.py:106
  36.8 5.4 %collective-permute-start.4 = (bf16[192,1024]{1,0:T(8,128)(2,1)S(1)}, bf16[192,1024]{1,0:T(8,128)(2,1)S(1)}, u32[]{:S(2)}, u32[]{:S(2)}) collective-permute-start(bf16[192,1024]{1,0:T(8,128)(2,1)S(1)} %copy-done), channel_id=1, source_target_pairs={{0,32},{32,64},{64,96},{96,0},{1,33},{33,65},{65,97},{97,1},{2,34}... | collective-permute-start | bytes 1179656 | tf_op jit(solution)/shard_map/ppermute | solution.py:35
  42.2 2.2 %collective-permute-start.3 = (bf16[192,1024]{1,0:T(8,128)(2,1)S(1)}, bf16[192,1024]{1,0:T(8,128)(2,1)S(1)}, u32[]{:S(2)}, u32[]{:S(2)}) collective-permute-start(bf16[192,1024]{1,0:T(8,128)(2,1)S(1)} %copy-done), channel_id=1, source_target_pairs={{0,64},{32,96},{64,0},{96,32},{1,65},{33,97},{65,1},{97,33},{2,66}... | collective-permute-start | bytes 1179656 | tf_op jit(solution)/shard_map/ppermute | solution.py:35
  44.4 2.5 %collective-permute-start.2 = (bf16[192,1024]{1,0:T(8,128)(2,1)S(1)}, bf16[192,1024]{1,0:T(8,128)(2,1)S(1)}, u32[]{:S(2)}, u32[]{:S(2)}) collective-permute-start(bf16[192,1024]{1,0:T(8,128)(2,1)S(1)} %copy-done), channel_id=1, source_target_pairs={{0,96},{32,0},{64,32},{96,64},{1,97},{33,1},{65,33},{97,65},{2,98}... | collective-permute-start | bytes 1179656 | tf_op jit(solution)/shard_map/ppermute | solution.py:35
  47.0 41.1 %psum.37 = f32[1024]{0:T(1024)S(1)} all-reduce(f32[1024]{0:T(1024)S(1)} %split.20), channel_id=1, replica_groups=mesh['zh'=4,'y'=4,'c'=2,'x'=4,'zl'=4] {'zh'}, use_global_device_ids=true, to_apply=%region_5.6 | all-reduce | flops 1024 | bytes 8192 | tf_op jit(solution)/shard_map/psum | solution.py:111
  88.2 0.2 convolution_reduce_fusion.3
  88.4 0.2 convolution_reduce_fusion
  88.7 0.2 convolution_reduce_fusion.1
  88.9 0.2 convolution_reduce_fusion.2
  89.4 6.6 %all-gather.4.cloned.1.call-done = bf16[1536,1024]{1,0:T(8,128)(2,1)} async-done(((bf16[192,1024]{1,0:T(8,128)(2,1)}), bf16[1536,1024]{1,0:T(8,128)(2,1)}) %all-gather.4.cloned.1.call-update) | async-done | bytes 3145744 | tf_op jit(solution)/shard_map/all_gather | solution.py:86
  96.0 2.1 %slice.128 = bf16[4,2,160,1024]{3,2,1,0:T(8,128)(2,1)S(1)} slice(bf16[4,2,192,1024]{3,2,1,0:T(8,128)(2,1)} %bitcast.56), slice={[0:4], [0:2], [0:160], [0:1024]} | slice | bytes 5242880 | tf_op jit(solution)/shard_map/slice | solution.py:87
  98.2 2.2 %convolution_convert_fusion = bf16[1280,768]{1,0:T(8,128)(2,1)S(1)} fusion(bf16[1280,1024]{1,0:T(8,128)(2,1)S(1)} %bitcast.61, bf16[192,1024]{1,0:T(8,128)(2,1)S(1)} %collective-permute-done.4, bf16[192,1024]{1,0:T(8,128)(2,1)S(1)} %collective-permute-done.3, bf16[192,1024]{1,0:T(8,128)(2,1)S(1)} %collective-permute-done.2, bf16[192,1024]{1,0:T(8,128)(2,1)S(1)} %copy-done), kind=kOutput, calls=%fused_computation.2 | convolution fusion | flops 2020540416 | bytes 6160384 | tf_op jit(solution)/shard_map/dot_general | solution.py:127
  100.6 3.8 %collective-permute-start.6 = (bf16[176,768]{1,0:T(8,128)(2,1)S(1)}, bf16[176,768]{1,0:T(8,128)(2,1)S(1)}, u32[]{:S(2)}, u32[]{:S(2)}) collective-permute-start(bf16[176,768]{1,0:T(8,128)(2,1)S(1)} %pad_maximum_fusion.11), channel_id=1, source_target_pairs={{0,8},{4,12},{8,0},{12,4},{1,9},{5,13},{9,1},{13,5},{2,10},{6,14},... | collective-permute-start | bytes 811016 | tf_op jit(solution)/shard_map/ppermute | solution.py:35
  104.4 2.7 %collective-permute-start.5 = (bf16[168,768]{1,0:T(8,128)(2,1)S(1)}, bf16[168,768]{1,0:T(8,128)(2,1)S(1)}, u32[]{:S(2)}, u32[]{:S(2)}) collective-permute-start(bf16[168,768]{1,0:T(8,128)(2,1)S(1)} %dynamic-slice_bitcast_fusion.4), channel_id=1, source_target_pairs={{0,12},{4,0},{8,4},{12,8},{1,13},{5,1},{9,5},{13,9},{2,14},{6,2},{... | collective-permute-start | bytes 774152 | tf_op jit(solution)/shard_map/ppermute | solution.py:35
  107.2 9.3 %collective-permute-done.5 = bf16[168,768]{1,0:T(8,128)(2,1)S(1)} collective-permute-done((bf16[168,768]{1,0:T(8,128)(2,1)S(1)}, bf16[168,768]{1,0:T(8,128)(2,1)S(1)}, u32[]{:S(2)}, u32[]{:S(2)}) %collective-permute-start.5) | collective-permute-done | bytes 258080 | tf_op jit(solution)/shard_map/ppermute | solution.py:35
  116.5 0.9 fusion.8
  117.4 4.5 %collective-permute-start.7 = (bf16[344,768]{1,0:T(8,128)(2,1)}, bf16[344,768]{1,0:T(8,128)(2,1)S(1)}, u32[]{:S(2)}, u32[]{:S(2)}) collective-permute-start(bf16[344,768]{1,0:T(8,128)(2,1)} %get-tuple-element.30), channel_id=1, source_target_pairs={{0,12},{4,0},{8,4},{12,8},{1,13},{5,1},{9,5},{13,9},{2,14},{6,2},{... | collective-permute-start | bytes 1585160 | tf_op jit(solution)/shard_map/ppermute | solution.py:35
  121.9 1.9 collective-permute-start.8
  124.1 1.9 slice.141
  126.0 7.6 %collective-permute-done.7 = bf16[344,768]{1,0:T(8,128)(2,1)S(1)} collective-permute-done((bf16[344,768]{1,0:T(8,128)(2,1)}, bf16[344,768]{1,0:T(8,128)(2,1)S(1)}, u32[]{:S(2)}, u32[]{:S(2)}) %collective-permute-start.7) | collective-permute-done | bytes 528416 | tf_op jit(solution)/shard_map/ppermute | solution.py:35
  133.7 5.0 %collective-permute-done.8 = bf16[344,768]{1,0:T(8,128)(2,1)S(1)} collective-permute-done((bf16[344,768]{1,0:T(8,128)(2,1)S(1)}, bf16[344,768]{1,0:T(8,128)(2,1)S(1)}, u32[]{:S(2)}, u32[]{:S(2)}) %collective-permute-start.8) | collective-permute-done | bytes 528416 | tf_op jit(solution)/shard_map/ppermute | solution.py:35
  138.7 0.2 convert_add_fusion
  139.4 0.3 copy.18
  139.8 2.1 %collective-permute-start.13 = (bf16[64,768]{1,0:T(8,128)(2,1)S(1)}, bf16[64,768]{1,0:T(8,128)(2,1)S(1)}, u32[]{:S(2)}, u32[]{:S(2)}) collective-permute-start(bf16[64,768]{1,0:T(8,128)(2,1)S(1)} %bitcast.63), channel_id=1, source_target_pairs={{0,1},{1,0},{2,3},{3,2},{4,5},{5,4},{6,7},{7,6},{8,9},{9,8},{10,11... | collective-permute-start | bytes 294920 | tf_op jit(solution)/shard_map/ppermute | solution.py:44
  142.0 3.8 %collective-permute-start.9 = (bf16[208,320]{1,0:T(8,128)(2,1)S(1)}, bf16[208,320]{1,0:T(8,128)(2,1)S(1)}, u32[]{:S(2)}, u32[]{:S(2)}) collective-permute-start(bf16[208,320]{1,0:T(8,128)(2,1)S(1)} %get-tuple-element.32), channel_id=1, source_target_pairs={{0,1},{1,2},{2,3},{3,0},{4,5},{5,6},{6,7},{7,4},{8,9},{9,10},{10,1... | collective-permute-start | bytes 399368 | tf_op jit(solution)/shard_map/ppermute | solution.py:35
  145.8 4.1 %collective-permute-start.10 = (bf16[208,320]{1,0:T(8,128)(2,1)S(1)}, bf16[208,320]{1,0:T(8,128)(2,1)S(1)}, u32[]{:S(2)}, u32[]{:S(2)}) collective-permute-start(bf16[208,320]{1,0:T(8,128)(2,1)S(1)} %get-tuple-element.33), channel_id=1, source_target_pairs={{0,2},{1,3},{2,0},{3,1},{4,6},{5,7},{6,4},{7,5},{8,10},{9,11},{10,... | collective-permute-start | bytes 399368 | tf_op jit(solution)/shard_map/ppermute | solution.py:35
  150.0 4.8 %collective-permute-start.11 = (bf16[208,320]{1,0:T(8,128)(2,1)S(1)}, bf16[208,320]{1,0:T(8,128)(2,1)S(1)}, u32[]{:S(2)}, u32[]{:S(2)}) collective-permute-start(bf16[208,320]{1,0:T(8,128)(2,1)S(1)} %get-tuple-element.34), channel_id=1, source_target_pairs={{0,3},{1,0},{2,1},{3,2},{4,7},{5,4},{6,5},{7,6},{8,11},{9,8},{10,9... | collective-permute-start | bytes 399368 | tf_op jit(solution)/shard_map/ppermute | solution.py:35
  154.9 1.9 collective-permute-start.14
  156.8 1.9 collective-permute-done.10
  158.6 2.7 %collective-permute-done.11 = bf16[208,320]{1,0:T(8,128)(2,1)S(1)} collective-permute-done((bf16[208,320]{1,0:T(8,128)(2,1)S(1)}, bf16[208,320]{1,0:T(8,128)(2,1)S(1)}, u32[]{:S(2)}, u32[]{:S(2)}) %collective-permute-start.11) | collective-permute-done | bytes 133152 | tf_op jit(solution)/shard_map/ppermute | solution.py:35
  162.4 11.1 %collective-permute-start.12 = (bf16[192,320]{1,0:T(8,128)(2,1)S(1)}, bf16[192,320]{1,0:T(8,128)(2,1)S(1)}, u32[]{:S(2)}, u32[]{:S(2)}) collective-permute-start(bf16[192,320]{1,0:T(8,128)(2,1)S(1)} %slice.167), channel_id=1, source_target_pairs={{0,0},{1,32},{2,64},{3,96},{32,1},{33,33},{34,65},{35,97},{64,2},{... | collective-permute-start | bytes 368648 | tf_op jit(solution)/shard_map/ppermute | solution.py:173
  173.5 2.5 %psum.38 = f32[256]{0:T(256)S(1)} all-reduce(f32[256]{0:T(256)S(1)} %reshape.280), channel_id=1, replica_groups=mesh['zh'=4,'y'=4,'c'=2,'x'=4,'zl'=4] {'c'}, use_global_device_ids=true, to_apply=%region_13.14 | all-reduce | flops 256 | bytes 2048 | tf_op jit(solution)/shard_map/psum | solution.py:170
  176.1 12.1 %psum.39 = f32[1024]{0:T(1024)S(1)} all-reduce(f32[1024]{0:T(1024)S(1)} %dynamic_update_slice.11), channel_id=1, replica_groups=mesh['zh'=4,'y'=4,'c'=2,'x'=4,'zl'=4] {'zh'}, use_global_device_ids=true, to_apply=%region_14.15 | all-reduce | flops 1024 | bytes 8192 | tf_op jit(solution)/shard_map/psum | solution.py:171
  188.2 0.7 select_reduce_fusion
  189.1 0.8 add_convert_fusion
  189.9 0.5 reshape.283
  190.5 3.3 %convolution_multiply_fusion = f32[160,1024]{1,0:T(8,128)} fusion(bf16[1024,1024]{1,0:T(8,128)(2,1)} %bitcast.75, bf16[1024,192]{1,0:T(8,128)(2,1)S(1)} %reshape.283, f32[1024]{0:T(1024)S(1)} %mul.127), kind=kOutput, calls=%fused_computation.10 | convolution fusion | flops 336199680 | bytes 3149824 | tf_op jit(solution)/shard_map/dot_general | solution.py:184
  (108 shorter events, 3.7 us)
Async XLA Ops:
  7.2 88.9 %all-gather.4.cloned.1.call-start = ((), (), s32[]{:S(2)}) async-start(), calls=%async_computation | async-start | bytes 3538944 | tf_op jit(solution)/shard_map/all_gather | solution.py:86
  9.0 12.2 %copy-start = (bf16[192,1024]{1,0:T(8,128)(2,1)S(1)}, bf16[192,1024]{1,0:T(8,128)(2,1)}, u32[]{:S(2)}) copy-start(bf16[192,1024]{1,0:T(8,128)(2,1)} %param.7) | copy-start | bytes 1179652
  9.0 181.4 %all-gather.6.cloned.1.call-start = ((), (), s32[]{:S(2)}) async-start(), calls=%async_computation.1 | async-start | bytes 2621440 | tf_op jit(solution)/shard_map/all_gather | solution.py:88
  10.0 12.8 %collective-permute-start.1 = (bf16[32,160]{1,0:T(8,128)(2,1)S(1)}, bf16[32,160]{1,0:T(8,128)(2,1)S(1)}, u32[]{:S(2)}, u32[]{:S(2)}) collective-permute-start(bf16[32,160]{1,0:T(8,128)(2,1)S(1)} %slice_select_fusion), channel_id=1, source_target_pairs={{0,16},{1,48},{2,80},{3,112},{4,144},{5,176},{6,208},{7,240},{8,27... | collective-permute-start | bytes 30728 | tf_op jit(solution)/shard_map/ppermute | solution.py:95
  16.4 5.0 %copy-start.2 = (f32[320]{0:T(512)S(1)}, f32[320]{0:T(512)}, u32[]{:S(2)}) copy-start(f32[320]{0:T(512)} %param.11) | copy-start | bytes 3844
  16.4 10.1 %copy-start.1 = (bf16[160,1024]{1,0:T(8,128)(2,1)S(1)}, bf16[160,1024]{1,0:T(8,128)(2,1)}, u32[]{:S(2)}) copy-start(bf16[160,1024]{1,0:T(8,128)(2,1)} %param.8) | copy-start | bytes 983044
  16.5 10.1 %collective-permute-start = (f32[33,160]{1,0:T(8,128)S(1)}, f32[33,160]{1,0:T(8,128)S(1)}, u32[]{:S(2)}, u32[]{:S(2)}) collective-permute-start(f32[33,160]{1,0:T(8,128)S(1)} %fusion.16), channel_id=1, source_target_pairs={{0,0},{1,32},{2,64},{3,96},{4,128},{5,160},{6,192},{7,224},{8,256}... | collective-permute-start | bytes 63368 | tf_op jit(solution)/shard_map/ppermute | solution.py:94
  36.8 51.6 %collective-permute-start.4 = (bf16[192,1024]{1,0:T(8,128)(2,1)S(1)}, bf16[192,1024]{1,0:T(8,128)(2,1)S(1)}, u32[]{:S(2)}, u32[]{:S(2)}) collective-permute-start(bf16[192,1024]{1,0:T(8,128)(2,1)S(1)} %copy-done), channel_id=1, source_target_pairs={{0,32},{32,64},{64,96},{96,0},{1,33},{33,65},{65,97},{97,1},{2,34}... | collective-permute-start | bytes 1179656 | tf_op jit(solution)/shard_map/ppermute | solution.py:35
  42.2 46.5 %collective-permute-start.3 = (bf16[192,1024]{1,0:T(8,128)(2,1)S(1)}, bf16[192,1024]{1,0:T(8,128)(2,1)S(1)}, u32[]{:S(2)}, u32[]{:S(2)}) collective-permute-start(bf16[192,1024]{1,0:T(8,128)(2,1)S(1)} %copy-done), channel_id=1, source_target_pairs={{0,64},{32,96},{64,0},{96,32},{1,65},{33,97},{65,1},{97,33},{2,66}... | collective-permute-start | bytes 1179656 | tf_op jit(solution)/shard_map/ppermute | solution.py:35
  44.4 44.5 %collective-permute-start.2 = (bf16[192,1024]{1,0:T(8,128)(2,1)S(1)}, bf16[192,1024]{1,0:T(8,128)(2,1)S(1)}, u32[]{:S(2)}, u32[]{:S(2)}) collective-permute-start(bf16[192,1024]{1,0:T(8,128)(2,1)S(1)} %copy-done), channel_id=1, source_target_pairs={{0,96},{32,0},{64,32},{96,64},{1,97},{33,1},{65,33},{97,65},{2,98}... | collective-permute-start | bytes 1179656 | tf_op jit(solution)/shard_map/ppermute | solution.py:35
  100.6 15.9 %collective-permute-start.6 = (bf16[176,768]{1,0:T(8,128)(2,1)S(1)}, bf16[176,768]{1,0:T(8,128)(2,1)S(1)}, u32[]{:S(2)}, u32[]{:S(2)}) collective-permute-start(bf16[176,768]{1,0:T(8,128)(2,1)S(1)} %pad_maximum_fusion.11), channel_id=1, source_target_pairs={{0,8},{4,12},{8,0},{12,4},{1,9},{5,13},{9,1},{13,5},{2,10},{6,14},... | collective-permute-start | bytes 811016 | tf_op jit(solution)/shard_map/ppermute | solution.py:35
  104.4 12.0 %collective-permute-start.5 = (bf16[168,768]{1,0:T(8,128)(2,1)S(1)}, bf16[168,768]{1,0:T(8,128)(2,1)S(1)}, u32[]{:S(2)}, u32[]{:S(2)}) collective-permute-start(bf16[168,768]{1,0:T(8,128)(2,1)S(1)} %dynamic-slice_bitcast_fusion.4), channel_id=1, source_target_pairs={{0,12},{4,0},{8,4},{12,8},{1,13},{5,1},{9,5},{13,9},{2,14},{6,2},{... | collective-permute-start | bytes 774152 | tf_op jit(solution)/shard_map/ppermute | solution.py:35
  117.4 16.3 %collective-permute-start.7 = (bf16[344,768]{1,0:T(8,128)(2,1)}, bf16[344,768]{1,0:T(8,128)(2,1)S(1)}, u32[]{:S(2)}, u32[]{:S(2)}) collective-permute-start(bf16[344,768]{1,0:T(8,128)(2,1)} %get-tuple-element.30), channel_id=1, source_target_pairs={{0,12},{4,0},{8,4},{12,8},{1,13},{5,1},{9,5},{13,9},{2,14},{6,2},{... | collective-permute-start | bytes 1585160 | tf_op jit(solution)/shard_map/ppermute | solution.py:35
  121.9 16.8 %collective-permute-start.8 = (bf16[344,768]{1,0:T(8,128)(2,1)S(1)}, bf16[344,768]{1,0:T(8,128)(2,1)S(1)}, u32[]{:S(2)}, u32[]{:S(2)}) collective-permute-start(bf16[344,768]{1,0:T(8,128)(2,1)S(1)} %get-tuple-element.31), channel_id=1, source_target_pairs={{0,4},{4,8},{8,12},{12,0},{1,5},{5,9},{9,13},{13,1},{2,6},{6,10},{... | collective-permute-start | bytes 1585160 | tf_op jit(solution)/shard_map/ppermute | solution.py:35
  139.8 15.0 %collective-permute-start.13 = (bf16[64,768]{1,0:T(8,128)(2,1)S(1)}, bf16[64,768]{1,0:T(8,128)(2,1)S(1)}, u32[]{:S(2)}, u32[]{:S(2)}) collective-permute-start(bf16[64,768]{1,0:T(8,128)(2,1)S(1)} %bitcast.63), channel_id=1, source_target_pairs={{0,1},{1,0},{2,3},{3,2},{4,5},{5,4},{6,7},{7,6},{8,9},{9,8},{10,11... | collective-permute-start | bytes 294920 | tf_op jit(solution)/shard_map/ppermute | solution.py:44
  142.0 46.2 %copy-start.3 = (s32[1024]{0:T(1024)S(1)}, s32[1024]{0:T(1024)}, u32[]{:S(2)}) copy-start(s32[1024]{0:T(1024)} %param.13) | copy-start | bytes 12292
  142.0 46.9 %copy-start.4 = (f32[1024]{0:T(1024)S(1)}, f32[1024]{0:T(1024)}, u32[]{:S(2)}) copy-start(f32[1024]{0:T(1024)} %param.12) | copy-start | bytes 12292
  142.0 14.7 %collective-permute-start.9 = (bf16[208,320]{1,0:T(8,128)(2,1)S(1)}, bf16[208,320]{1,0:T(8,128)(2,1)S(1)}, u32[]{:S(2)}, u32[]{:S(2)}) collective-permute-start(bf16[208,320]{1,0:T(8,128)(2,1)S(1)} %get-tuple-element.32), channel_id=1, source_target_pairs={{0,1},{1,2},{2,3},{3,0},{4,5},{5,6},{6,7},{7,4},{8,9},{9,10},{10,1... | collective-permute-start | bytes 399368 | tf_op jit(solution)/shard_map/ppermute | solution.py:35
  145.8 12.8 %collective-permute-start.10 = (bf16[208,320]{1,0:T(8,128)(2,1)S(1)}, bf16[208,320]{1,0:T(8,128)(2,1)S(1)}, u32[]{:S(2)}, u32[]{:S(2)}) collective-permute-start(bf16[208,320]{1,0:T(8,128)(2,1)S(1)} %get-tuple-element.33), channel_id=1, source_target_pairs={{0,2},{1,3},{2,0},{3,1},{4,6},{5,7},{6,4},{7,5},{8,10},{9,11},{10,... | collective-permute-start | bytes 399368 | tf_op jit(solution)/shard_map/ppermute | solution.py:35
  150.0 11.4 %collective-permute-start.11 = (bf16[208,320]{1,0:T(8,128)(2,1)S(1)}, bf16[208,320]{1,0:T(8,128)(2,1)S(1)}, u32[]{:S(2)}, u32[]{:S(2)}) collective-permute-start(bf16[208,320]{1,0:T(8,128)(2,1)S(1)} %get-tuple-element.34), channel_id=1, source_target_pairs={{0,3},{1,0},{2,1},{3,2},{4,7},{5,4},{6,5},{7,6},{8,11},{9,8},{10,9... | collective-permute-start | bytes 399368 | tf_op jit(solution)/shard_map/ppermute | solution.py:35
  154.9 35.0 %collective-permute-start.14 = (bf16[128,768]{1,0:T(8,128)(2,1)S(1)}, bf16[128,768]{1,0:T(8,128)(2,1)S(1)}, u32[]{:S(2)}, u32[]{:S(2)}) collective-permute-start(bf16[128,768]{1,0:T(8,128)(2,1)S(1)} %pad_maximum_fusion.13), channel_id=1, source_target_pairs={{0,3},{1,2},{2,1},{3,0},{4,7},{5,6},{6,5},{7,4},{8,11},{9,10},{10,... | collective-permute-start | bytes 589832 | tf_op jit(solution)/shard_map/ppermute | solution.py:44
  162.4 26.7 %collective-permute-start.12 = (bf16[192,320]{1,0:T(8,128)(2,1)S(1)}, bf16[192,320]{1,0:T(8,128)(2,1)S(1)}, u32[]{:S(2)}, u32[]{:S(2)}) collective-permute-start(bf16[192,320]{1,0:T(8,128)(2,1)S(1)} %slice.167), channel_id=1, source_target_pairs={{0,0},{1,32},{2,64},{3,96},{32,1},{33,33},{34,65},{35,97},{64,2},{... | collective-permute-start | bytes 368648 | tf_op jit(solution)/shard_map/ppermute | solution.py:173
Sparse Core Ops, SparseCore 0:
  10.7 85.2 all-gather.3
  126.2 33.3 all-gather.5

commit v15 on v12

--- a/solution.py
+++ b/solution.py
@@ -27,8 +27,8 @@
     ]
 
 
-def turned():
-    return [(y * 4 + zl, zl * 4 + y) for y in range(4) for zl in range(4)]
+def turned(step):
+    return [(y * 4 + zl, (zl + step) % 4 * 4 + y) for y in range(4) for zl in range(4)]
 
 
 def move(value, axis, step):
@@ -145,10 +145,10 @@
     for k in range(4):
         one = lax.dynamic_index_in_dim(total, lax.rem(zl + k + 4 - y, 4), 0, keepdims=False)
         one = jnp.concatenate([one, ride], axis=0)
-        parts.append(one if k == 0 else move(one, "zl", k))
+        parts.append(lax.ppermute(one, ("y", "zl"), turned(k)))
     total = sum(p.astype(f32) for p in parts)
     sums = unpack(total[rows:], size)
-    total = total[:rows].astype(bf16)
+    total = total[:rows]
 
     along, inner, left_dot = jnp.split(sums, [many, 2 * many])
     inner = spread * inner
@@ -159,7 +159,6 @@
     score = lax.psum(score.reshape(-1), "c")
     score = lax.psum(placed(score, zh, 4), "zh")
 
-    total = lax.ppermute(total, ("y", "zl"), turned()).astype(f32)
     inner = lax.dynamic_slice(inner, (y * rows,), (rows,))
     lowrank = inner.reshape(members, tokens)[:, :, None] * left_cols[:, None, :]
     mixed = (total + lowrank.reshape(rows, cols)).astype(bf16)

time: 197 us -> 218 us (1.11)
  waiting for transfers between devices: 40.5 us -> 59.8 us
    ppermute x1 -> x4, waiting for transfers between devices: 0.01 us -> 28 us  [per_device(): parts.append(lax.ppermute(one, ('y', 'zl'), turned(k)))]
    ppermute x9 -> x6, starting transfers between devices: 29.8 us -> 19.2 us  [move(): return lax.ppermute(value, axis, ring(step))]
    ppermute x9 -> x6, waiting for transfers between devices: 29.7 us -> 21 us  [move(): return lax.ppermute(value, axis, ring(step))]
    ppermute x1 -> x4, starting transfers between devices: 6.79 us -> 14.1 us  [per_device(): parts.append(lax.ppermute(one, ('y', 'zl'), turned(k)))]
    ppermute x2, starting transfers between devices: 5.36 us -> 7.85 us  [joined(): got = lax.ppermute(value, axis, pairs(step))]
where the time goes in v15:
time: 218 us; the launch traced here: 214 us
  blocking collectives  66.2 us (30%)
  waiting for transfers between devices  59.8 us (27%)
  starting transfers between devices  50.6 us (23%)
  between operations  14.8 us (7%)
  local copies, waits for them, and re-layouts  8.93 us (4%)
  other arithmetic  7.56 us (3%)
  matrix products  6.37 us (3%)
    psum x1, blocking collectives, per_device(): direction = lax.psum(direction, 'zh')  40.6 us
    ppermute x4, waiting for transfers between devices, per_device(): parts.append(lax.ppermute(one, ('y', 'zl'), turned(k)))  28 us
    ppermute x6, waiting for transfers between devices, move(): return lax.ppermute(value, axis, ring(step))  21 us
    ppermute x6, starting transfers between devices, move(): return lax.ppermute(value, axis, ring(step))  19.2 us
    ppermute x4, starting transfers between devices, per_device(): parts.append(lax.ppermute(one, ('y', 'zl'), turned(k)))  14.1 us
    psum x1, blocking collectives, per_device(): score = lax.psum(placed(score, zh, 4), 'zh')  13.1 us
    ppermute x2, starting transfers between devices, joined(): got = lax.ppermute(value, axis, pairs(step))  7.85 us
    psum x1, blocking collectives, per_device(): early = lax.psum(early, 'y')  7.57 us
  transfers between devices with their start and end apart: 16, of which 7 were waited for; matrix products, arithmetic and copies ran while one was open for 6% of the time, Pallas kernels for 0%

profile of v15, /device:TPU:24, one launch (start us, length us, event | category | flops | bytes accessed | tf_op | source)
XLA Modules:
  0.0 214.2 jit_solution(2471748971104142056)
XLA Ops:
  7.2 1.8 pad_maximum_fusion.6
  9.1 0.8 dynamic-slice_convert_fusion
  10.1 5.6 %collective-permute-start.1 = (bf16[32,160]{1,0:T(8,128)(2,1)S(1)}, bf16[32,160]{1,0:T(8,128)(2,1)S(1)}, u32[]{:S(2)}, u32[]{:S(2)}) collective-permute-start(bf16[32,160]{1,0:T(8,128)(2,1)S(1)} %slice_select_fusion), channel_id=1, source_target_pairs={{0,16},{1,48},{2,80},{3,112},{4,144},{5,176},{6,208},{7,240},{8,27... | collective-permute-start | bytes 30728 | tf_op jit(solution)/shard_map/ppermute | solution.py:95
  15.7 0.7 broadcast_in_dim.37
  16.5 3.7 %collective-permute-start = (f32[33,160]{1,0:T(8,128)S(1)}, f32[33,160]{1,0:T(8,128)S(1)}, u32[]{:S(2)}, u32[]{:S(2)}) collective-permute-start(f32[33,160]{1,0:T(8,128)S(1)} %fusion.14), channel_id=1, source_target_pairs={{0,0},{1,32},{2,64},{3,96},{4,128},{5,160},{6,192},{7,224},{8,256}... | collective-permute-start | bytes 63368 | tf_op jit(solution)/shard_map/ppermute | solution.py:94
  20.2 1.0 mul.105
  21.4 1.0 multiply_reduce_fusion.2
  22.4 0.2 dynamic_update_slice.10
  22.7 0.2 dynamic_update_slice.9
  22.9 3.7 %collective-permute-done = f32[33,160]{1,0:T(8,128)S(1)} collective-permute-done((f32[33,160]{1,0:T(8,128)S(1)}, f32[33,160]{1,0:T(8,128)S(1)}, u32[]{:S(2)}, u32[]{:S(2)}) %collective-permute-start) | collective-permute-done | bytes 21152 | tf_op jit(solution)/shard_map/ppermute | solution.py:94
  26.7 2.5 %psum.35 = f32[1024]{0:T(1024)S(1)} all-reduce(f32[1024]{0:T(1024)S(1)} %multiply_reduce_fusion.1), channel_id=1, replica_groups=mesh['zh'=4,'y'=4,'c'=2,'x'=4,'zl'=4] {'c'}, use_global_device_ids=true, to_apply=%region_1.2 | all-reduce | flops 1024 | bytes 8192 | tf_op jit(solution)/shard_map/psum | solution.py:104
  29.2 7.6 %psum.36 = f32[1920]{0:T(1024)S(1)} all-reduce(f32[1920]{0:T(1024)S(1)} %pad_maximum_fusion.17), channel_id=1, replica_groups=mesh['zh'=4,'y'=4,'c'=2,'x'=4,'zl'=4] {'y'}, use_global_device_ids=true, to_apply=%region_4.5 | all-reduce | flops 1920 | bytes 15360 | tf_op jit(solution)/shard_map/psum | solution.py:106
  36.8 5.4 %collective-permute-start.4 = (bf16[192,1024]{1,0:T(8,128)(2,1)S(1)}, bf16[192,1024]{1,0:T(8,128)(2,1)S(1)}, u32[]{:S(2)}, u32[]{:S(2)}) collective-permute-start(bf16[192,1024]{1,0:T(8,128)(2,1)S(1)} %copy-done), channel_id=1, source_target_pairs={{0,32},{32,64},{64,96},{96,0},{1,33},{33,65},{65,97},{97,1},{2,34}... | collective-permute-start | bytes 1179656 | tf_op jit(solution)/shard_map/ppermute | solution.py:35
  42.2 2.2 %collective-permute-start.3 = (bf16[192,1024]{1,0:T(8,128)(2,1)S(1)}, bf16[192,1024]{1,0:T(8,128)(2,1)S(1)}, u32[]{:S(2)}, u32[]{:S(2)}) collective-permute-start(bf16[192,1024]{1,0:T(8,128)(2,1)S(1)} %copy-done), channel_id=1, source_target_pairs={{0,64},{32,96},{64,0},{96,32},{1,65},{33,97},{65,1},{97,33},{2,66}... | collective-permute-start | bytes 1179656 | tf_op jit(solution)/shard_map/ppermute | solution.py:35
  44.4 2.5 %collective-permute-start.2 = (bf16[192,1024]{1,0:T(8,128)(2,1)S(1)}, bf16[192,1024]{1,0:T(8,128)(2,1)S(1)}, u32[]{:S(2)}, u32[]{:S(2)}) collective-permute-start(bf16[192,1024]{1,0:T(8,128)(2,1)S(1)} %copy-done), channel_id=1, source_target_pairs={{0,96},{32,0},{64,32},{96,64},{1,97},{33,1},{65,33},{97,65},{2,98}... | collective-permute-start | bytes 1179656 | tf_op jit(solution)/shard_map/ppermute | solution.py:35
  47.0 40.6 %psum.37 = f32[1024]{0:T(1024)S(1)} all-reduce(f32[1024]{0:T(1024)S(1)} %split.20), channel_id=1, replica_groups=mesh['zh'=4,'y'=4,'c'=2,'x'=4,'zl'=4] {'zh'}, use_global_device_ids=true, to_apply=%region_5.6 | all-reduce | flops 1024 | bytes 8192 | tf_op jit(solution)/shard_map/psum | solution.py:111
  87.7 0.2 convolution_reduce_fusion.3
  87.9 0.2 convolution_reduce_fusion
  88.2 0.2 convolution_reduce_fusion.1
  88.4 0.2 convolution_reduce_fusion.2
  88.9 7.1 %all-gather.4.cloned.1.call-done = bf16[1536,1024]{1,0:T(8,128)(2,1)} async-done(((bf16[192,1024]{1,0:T(8,128)(2,1)}), bf16[1536,1024]{1,0:T(8,128)(2,1)}) %all-gather.4.cloned.1.call-update) | async-done | bytes 3145744 | tf_op jit(solution)/shard_map/all_gather | solution.py:86
  96.0 2.1 slice.98
  98.1 2.2 %convolution_convert_fusion = bf16[1280,768]{1,0:T(8,128)(2,1)S(1)} fusion(bf16[1280,1024]{1,0:T(8,128)(2,1)S(1)} %bitcast.51, bf16[192,1024]{1,0:T(8,128)(2,1)S(1)} %collective-permute-done.4, bf16[192,1024]{1,0:T(8,128)(2,1)S(1)} %collective-permute-done.3, bf16[192,1024]{1,0:T(8,128)(2,1)S(1)} %collective-permute-done.2, bf16[192,1024]{1,0:T(8,128)(2,1)S(1)} %copy-done), kind=kOutput, calls=%fused_computation.2 | convolution fusion | flops 2020540416 | bytes 6160384 | tf_op jit(solution)/shard_map/dot_general | solution.py:127
  100.5 1.1 pad_maximum_fusion.5
  101.6 3.5 %collective-permute-start.5 = (bf16[344,768]{1,0:T(8,128)(2,1)}, bf16[344,768]{1,0:T(8,128)(2,1)S(1)}, u32[]{:S(2)}, u32[]{:S(2)}) collective-permute-start(bf16[344,768]{1,0:T(8,128)(2,1)} %get-tuple-element.26), channel_id=1, source_target_pairs={{0,12},{4,0},{8,4},{12,8},{1,13},{5,1},{9,5},{13,9},{2,14},{6,2},{... | collective-permute-start | bytes 1585160 | tf_op jit(solution)/shard_map/ppermute | solution.py:35
  105.2 2.4 %collective-permute-start.6 = (bf16[344,768]{1,0:T(8,128)(2,1)}, bf16[344,768]{1,0:T(8,128)(2,1)S(1)}, u32[]{:S(2)}, u32[]{:S(2)}) collective-permute-start(bf16[344,768]{1,0:T(8,128)(2,1)} %get-tuple-element.27), channel_id=1, source_target_pairs={{0,8},{4,12},{8,0},{12,4},{1,9},{5,13},{9,1},{13,5},{2,10},{6,14},... | collective-permute-start | bytes 1585160 | tf_op jit(solution)/shard_map/ppermute | solution.py:35
  107.6 3.1 %collective-permute-start.7 = (bf16[344,768]{1,0:T(8,128)(2,1)S(1)}, bf16[344,768]{1,0:T(8,128)(2,1)S(1)}, u32[]{:S(2)}, u32[]{:S(2)}) collective-permute-start(bf16[344,768]{1,0:T(8,128)(2,1)S(1)} %get-tuple-element.28), channel_id=1, source_target_pairs={{0,4},{4,8},{8,12},{12,0},{1,5},{5,9},{9,13},{13,1},{2,6},{6,10},{... | collective-permute-start | bytes 1585160 | tf_op jit(solution)/shard_map/ppermute | solution.py:35
  111.0 1.9 slice.111
  113.0 5.6 %collective-permute-done.5 = bf16[344,768]{1,0:T(8,128)(2,1)S(1)} collective-permute-done((bf16[344,768]{1,0:T(8,128)(2,1)}, bf16[344,768]{1,0:T(8,128)(2,1)S(1)}, u32[]{:S(2)}, u32[]{:S(2)}) %collective-permute-start.5) | collective-permute-done | bytes 528416 | tf_op jit(solution)/shard_map/ppermute | solution.py:35
  118.6 5.1 %collective-permute-done.6 = bf16[344,768]{1,0:T(8,128)(2,1)S(1)} collective-permute-done((bf16[344,768]{1,0:T(8,128)(2,1)}, bf16[344,768]{1,0:T(8,128)(2,1)S(1)}, u32[]{:S(2)}, u32[]{:S(2)}) %collective-permute-start.6) | collective-permute-done | bytes 528416 | tf_op jit(solution)/shard_map/ppermute | solution.py:35
  123.7 10.3 %collective-permute-done.7 = bf16[344,768]{1,0:T(8,128)(2,1)S(1)} collective-permute-done((bf16[344,768]{1,0:T(8,128)(2,1)S(1)}, bf16[344,768]{1,0:T(8,128)(2,1)S(1)}, u32[]{:S(2)}, u32[]{:S(2)}) %collective-permute-start.7) | collective-permute-done | bytes 528416 | tf_op jit(solution)/shard_map/ppermute | solution.py:35
  134.0 0.3 convert_add_fusion
  134.6 0.3 copy.18
  134.9 3.4 %collective-permute-start.12 = (bf16[64,768]{1,0:T(8,128)(2,1)S(1)}, bf16[64,768]{1,0:T(8,128)(2,1)S(1)}, u32[]{:S(2)}, u32[]{:S(2)}) collective-permute-start(bf16[64,768]{1,0:T(8,128)(2,1)S(1)} %bitcast.54), channel_id=1, source_target_pairs={{0,1},{1,0},{2,3},{3,2},{4,5},{5,4},{6,7},{7,6},{8,9},{9,8},{10,11... | collective-permute-start | bytes 294920 | tf_op jit(solution)/shard_map/ppermute | solution.py:44
  138.6 5.1 %collective-permute-start.8 = (bf16[208,320]{1,0:T(8,128)(2,1)S(1)}, bf16[208,320]{1,0:T(8,128)(2,1)S(1)}, u32[]{:S(2)}, u32[]{:S(2)}) collective-permute-start(bf16[208,320]{1,0:T(8,128)(2,1)S(1)} %get-tuple-element.29), channel_id=1, source_target_pairs={{0,0},{1,32},{2,64},{3,96},{32,1},{33,33},{34,65},{35,97},{64,2},{... | collective-permute-start | bytes 399368 | tf_op jit(solution)/shard_map/ppermute | solution.py:148
  143.7 3.9 %collective-permute-start.9 = (bf16[208,320]{1,0:T(8,128)(2,1)S(1)}, bf16[208,320]{1,0:T(8,128)(2,1)S(1)}, u32[]{:S(2)}, u32[]{:S(2)}) collective-permute-start(bf16[208,320]{1,0:T(8,128)(2,1)S(1)} %get-tuple-element.30), channel_id=1, source_target_pairs={{0,32},{1,64},{2,96},{3,0},{32,33},{33,65},{34,97},{35,1},{64,34},... | collective-permute-start | bytes 399368 | tf_op jit(solution)/shard_map/ppermute | solution.py:148
  147.7 2.5 %collective-permute-start.10 = (bf16[208,320]{1,0:T(8,128)(2,1)S(1)}, bf16[208,320]{1,0:T(8,128)(2,1)S(1)}, u32[]{:S(2)}, u32[]{:S(2)}) collective-permute-start(bf16[208,320]{1,0:T(8,128)(2,1)S(1)} %get-tuple-element.31), channel_id=1, source_target_pairs={{0,64},{1,96},{2,0},{3,32},{32,65},{33,97},{34,1},{35,33},{64,66},... | collective-permute-start | bytes 399368 | tf_op jit(solution)/shard_map/ppermute | solution.py:148
  150.2 2.6 %collective-permute-start.11 = (bf16[208,320]{1,0:T(8,128)(2,1)S(1)}, bf16[208,320]{1,0:T(8,128)(2,1)S(1)}, u32[]{:S(2)}, u32[]{:S(2)}) collective-permute-start(bf16[208,320]{1,0:T(8,128)(2,1)S(1)} %get-tuple-element.32), channel_id=1, source_target_pairs={{0,96},{1,0},{2,32},{3,64},{32,97},{33,1},{34,33},{35,65},{64,98},... | collective-permute-start | bytes 399368 | tf_op jit(solution)/shard_map/ppermute | solution.py:148
  152.8 4.4 %collective-permute-start.13 = (bf16[128,768]{1,0:T(8,128)(2,1)S(1)}, bf16[128,768]{1,0:T(8,128)(2,1)S(1)}, u32[]{:S(2)}, u32[]{:S(2)}) collective-permute-start(bf16[128,768]{1,0:T(8,128)(2,1)S(1)} %pad_maximum_fusion.12), channel_id=1, source_target_pairs={{0,3},{1,2},{2,1},{3,0},{4,7},{5,6},{6,5},{7,4},{8,11},{9,10},{10,... | collective-permute-start | bytes 589832 | tf_op jit(solution)/shard_map/ppermute | solution.py:44
  157.2 13.7 %collective-permute-done.9 = bf16[208,320]{1,0:T(8,128)(2,1)S(1)} collective-permute-done((bf16[208,320]{1,0:T(8,128)(2,1)S(1)}, bf16[208,320]{1,0:T(8,128)(2,1)S(1)}, u32[]{:S(2)}, u32[]{:S(2)}) %collective-permute-start.9) | collective-permute-done | bytes 133152 | tf_op jit(solution)/shard_map/ppermute | solution.py:148
  171.0 14.2 %collective-permute-done.10 = bf16[208,320]{1,0:T(8,128)(2,1)S(1)} collective-permute-done((bf16[208,320]{1,0:T(8,128)(2,1)S(1)}, bf16[208,320]{1,0:T(8,128)(2,1)S(1)}, u32[]{:S(2)}, u32[]{:S(2)}) %collective-permute-start.10) | collective-permute-done | bytes 133152 | tf_op jit(solution)/shard_map/ppermute | solution.py:148
  186.2 2.4 %psum.38 = f32[256]{0:T(256)S(1)} all-reduce(f32[256]{0:T(256)S(1)} %reshape.276), channel_id=1, replica_groups=mesh['zh'=4,'y'=4,'c'=2,'x'=4,'zl'=4] {'c'}, use_global_device_ids=true, to_apply=%region_13.14 | all-reduce | flops 256 | bytes 2048 | tf_op jit(solution)/shard_map/psum | solution.py:159
  188.6 0.2 dynamic_update_slice.11
  188.8 13.1 %psum.39 = f32[1024]{0:T(1024)S(1)} all-reduce(f32[1024]{0:T(1024)S(1)} %dynamic_update_slice.11), channel_id=1, replica_groups=mesh['zh'=4,'y'=4,'c'=2,'x'=4,'zl'=4] {'zh'}, use_global_device_ids=true, to_apply=%region_14.15 | all-reduce | flops 1024 | bytes 8192 | tf_op jit(solution)/shard_map/psum | solution.py:160
  201.9 0.7 select_reduce_fusion
  202.7 0.8 fusion.10
  203.6 0.5 reshape.279
  204.1 3.3 %convolution_multiply_fusion = f32[160,1024]{1,0:T(8,128)} fusion(bf16[1024,1024]{1,0:T(8,128)(2,1)} %bitcast.66, bf16[1024,192]{1,0:T(8,128)(2,1)S(1)} %reshape.279, f32[1024]{0:T(1024)S(1)} %mul.127), kind=kOutput, calls=%fused_computation.10 | convolution fusion | flops 336199680 | bytes 3149824 | tf_op jit(solution)/shard_map/dot_general | solution.py:172
  (99 shorter events, 3.2 us)
Async XLA Ops:
  7.2 14.1 %copy-start = (bf16[192,1024]{1,0:T(8,128)(2,1)S(1)}, bf16[192,1024]{1,0:T(8,128)(2,1)}, u32[]{:S(2)}) copy-start(bf16[192,1024]{1,0:T(8,128)(2,1)} %param.7) | copy-start | bytes 1179652
  7.2 88.8 %all-gather.4.cloned.1.call-start = ((), (), s32[]{:S(2)}) async-start(), calls=%async_computation | async-start | bytes 3538944 | tf_op jit(solution)/shard_map/all_gather | solution.py:86
  9.1 195.0 %all-gather.6.cloned.1.call-start = ((), (), s32[]{:S(2)}) async-start(), calls=%async_computation.1 | async-start | bytes 2621440 | tf_op jit(solution)/shard_map/all_gather | solution.py:88
  10.1 12.8 %collective-permute-start.1 = (bf16[32,160]{1,0:T(8,128)(2,1)S(1)}, bf16[32,160]{1,0:T(8,128)(2,1)S(1)}, u32[]{:S(2)}, u32[]{:S(2)}) collective-permute-start(bf16[32,160]{1,0:T(8,128)(2,1)S(1)} %slice_select_fusion), channel_id=1, source_target_pairs={{0,16},{1,48},{2,80},{3,112},{4,144},{5,176},{6,208},{7,240},{8,27... | collective-permute-start | bytes 30728 | tf_op jit(solution)/shard_map/ppermute | solution.py:95
  16.4 5.0 %copy-start.2 = (f32[320]{0:T(512)S(1)}, f32[320]{0:T(512)}, u32[]{:S(2)}) copy-start(f32[320]{0:T(512)} %param.11) | copy-start | bytes 3844
  16.4 10.1 %copy-start.1 = (bf16[160,1024]{1,0:T(8,128)(2,1)S(1)}, bf16[160,1024]{1,0:T(8,128)(2,1)}, u32[]{:S(2)}) copy-start(bf16[160,1024]{1,0:T(8,128)(2,1)} %param.8) | copy-start | bytes 983044
  16.5 10.1 %collective-permute-start = (f32[33,160]{1,0:T(8,128)S(1)}, f32[33,160]{1,0:T(8,128)S(1)}, u32[]{:S(2)}, u32[]{:S(2)}) collective-permute-start(f32[33,160]{1,0:T(8,128)S(1)} %fusion.14), channel_id=1, source_target_pairs={{0,0},{1,32},{2,64},{3,96},{4,128},{5,160},{6,192},{7,224},{8,256}... | collective-permute-start | bytes 63368 | tf_op jit(solution)/shard_map/ppermute | solution.py:94
  36.8 51.2 %collective-permute-start.4 = (bf16[192,1024]{1,0:T(8,128)(2,1)S(1)}, bf16[192,1024]{1,0:T(8,128)(2,1)S(1)}, u32[]{:S(2)}, u32[]{:S(2)}) collective-permute-start(bf16[192,1024]{1,0:T(8,128)(2,1)S(1)} %copy-done), channel_id=1, source_target_pairs={{0,32},{32,64},{64,96},{96,0},{1,33},{33,65},{65,97},{97,1},{2,34}... | collective-permute-start | bytes 1179656 | tf_op jit(solution)/shard_map/ppermute | solution.py:35
  42.2 46.0 %collective-permute-start.3 = (bf16[192,1024]{1,0:T(8,128)(2,1)S(1)}, bf16[192,1024]{1,0:T(8,128)(2,1)S(1)}, u32[]{:S(2)}, u32[]{:S(2)}) collective-permute-start(bf16[192,1024]{1,0:T(8,128)(2,1)S(1)} %copy-done), channel_id=1, source_target_pairs={{0,64},{32,96},{64,0},{96,32},{1,65},{33,97},{65,1},{97,33},{2,66}... | collective-permute-start | bytes 1179656 | tf_op jit(solution)/shard_map/ppermute | solution.py:35
  44.4 44.0 %collective-permute-start.2 = (bf16[192,1024]{1,0:T(8,128)(2,1)S(1)}, bf16[192,1024]{1,0:T(8,128)(2,1)S(1)}, u32[]{:S(2)}, u32[]{:S(2)}) collective-permute-start(bf16[192,1024]{1,0:T(8,128)(2,1)S(1)} %copy-done), channel_id=1, source_target_pairs={{0,96},{32,0},{64,32},{96,64},{1,97},{33,1},{65,33},{97,65},{2,98}... | collective-permute-start | bytes 1179656 | tf_op jit(solution)/shard_map/ppermute | solution.py:35
  101.6 16.9 %collective-permute-start.5 = (bf16[344,768]{1,0:T(8,128)(2,1)}, bf16[344,768]{1,0:T(8,128)(2,1)S(1)}, u32[]{:S(2)}, u32[]{:S(2)}) collective-permute-start(bf16[344,768]{1,0:T(8,128)(2,1)} %get-tuple-element.26), channel_id=1, source_target_pairs={{0,12},{4,0},{8,4},{12,8},{1,13},{5,1},{9,5},{13,9},{2,14},{6,2},{... | collective-permute-start | bytes 1585160 | tf_op jit(solution)/shard_map/ppermute | solution.py:35
  105.2 18.5 %collective-permute-start.6 = (bf16[344,768]{1,0:T(8,128)(2,1)}, bf16[344,768]{1,0:T(8,128)(2,1)S(1)}, u32[]{:S(2)}, u32[]{:S(2)}) collective-permute-start(bf16[344,768]{1,0:T(8,128)(2,1)} %get-tuple-element.27), channel_id=1, source_target_pairs={{0,8},{4,12},{8,0},{12,4},{1,9},{5,13},{9,1},{13,5},{2,10},{6,14},... | collective-permute-start | bytes 1585160 | tf_op jit(solution)/shard_map/ppermute | solution.py:35
  107.6 26.3 %collective-permute-start.7 = (bf16[344,768]{1,0:T(8,128)(2,1)S(1)}, bf16[344,768]{1,0:T(8,128)(2,1)S(1)}, u32[]{:S(2)}, u32[]{:S(2)}) collective-permute-start(bf16[344,768]{1,0:T(8,128)(2,1)S(1)} %get-tuple-element.28), channel_id=1, source_target_pairs={{0,4},{4,8},{8,12},{12,0},{1,5},{5,9},{9,13},{13,1},{2,6},{6,10},{... | collective-permute-start | bytes 1585160 | tf_op jit(solution)/shard_map/ppermute | solution.py:35
  134.9 17.8 %collective-permute-start.12 = (bf16[64,768]{1,0:T(8,128)(2,1)S(1)}, bf16[64,768]{1,0:T(8,128)(2,1)S(1)}, u32[]{:S(2)}, u32[]{:S(2)}) collective-permute-start(bf16[64,768]{1,0:T(8,128)(2,1)S(1)} %bitcast.54), channel_id=1, source_target_pairs={{0,1},{1,0},{2,3},{3,2},{4,5},{5,4},{6,7},{7,6},{8,9},{9,8},{10,11... | collective-permute-start | bytes 294920 | tf_op jit(solution)/shard_map/ppermute | solution.py:44
  138.4 63.5 %copy-start.3 = (s32[1024]{0:T(1024)S(1)}, s32[1024]{0:T(1024)}, u32[]{:S(2)}) copy-start(s32[1024]{0:T(1024)} %param.13) | copy-start | bytes 12292
  138.4 64.1 %copy-start.4 = (f32[1024]{0:T(1024)S(1)}, f32[1024]{0:T(1024)}, u32[]{:S(2)}) copy-start(f32[1024]{0:T(1024)} %param.12) | copy-start | bytes 12292
  138.6 18.7 %collective-permute-start.8 = (bf16[208,320]{1,0:T(8,128)(2,1)S(1)}, bf16[208,320]{1,0:T(8,128)(2,1)S(1)}, u32[]{:S(2)}, u32[]{:S(2)}) collective-permute-start(bf16[208,320]{1,0:T(8,128)(2,1)S(1)} %get-tuple-element.29), channel_id=1, source_target_pairs={{0,0},{1,32},{2,64},{3,96},{32,1},{33,33},{34,65},{35,97},{64,2},{... | collective-permute-start | bytes 399368 | tf_op jit(solution)/shard_map/ppermute | solution.py:148
  143.7 27.2 %collective-permute-start.9 = (bf16[208,320]{1,0:T(8,128)(2,1)S(1)}, bf16[208,320]{1,0:T(8,128)(2,1)S(1)}, u32[]{:S(2)}, u32[]{:S(2)}) collective-permute-start(bf16[208,320]{1,0:T(8,128)(2,1)S(1)} %get-tuple-element.30), channel_id=1, source_target_pairs={{0,32},{1,64},{2,96},{3,0},{32,33},{33,65},{34,97},{35,1},{64,34},... | collective-permute-start | bytes 399368 | tf_op jit(solution)/shard_map/ppermute | solution.py:148
  147.7 37.5 %collective-permute-start.10 = (bf16[208,320]{1,0:T(8,128)(2,1)S(1)}, bf16[208,320]{1,0:T(8,128)(2,1)S(1)}, u32[]{:S(2)}, u32[]{:S(2)}) collective-permute-start(bf16[208,320]{1,0:T(8,128)(2,1)S(1)} %get-tuple-element.31), channel_id=1, source_target_pairs={{0,64},{1,96},{2,0},{3,32},{32,65},{33,97},{34,1},{35,33},{64,66},... | collective-permute-start | bytes 399368 | tf_op jit(solution)/shard_map/ppermute | solution.py:148
  150.2 35.0 %collective-permute-start.11 = (bf16[208,320]{1,0:T(8,128)(2,1)S(1)}, bf16[208,320]{1,0:T(8,128)(2,1)S(1)}, u32[]{:S(2)}, u32[]{:S(2)}) collective-permute-start(bf16[208,320]{1,0:T(8,128)(2,1)S(1)} %get-tuple-element.32), channel_id=1, source_target_pairs={{0,96},{1,0},{2,32},{3,64},{32,97},{33,1},{34,33},{35,65},{64,98},... | collective-permute-start | bytes 399368 | tf_op jit(solution)/shard_map/ppermute | solution.py:148
  152.8 50.7 %collective-permute-start.13 = (bf16[128,768]{1,0:T(8,128)(2,1)S(1)}, bf16[128,768]{1,0:T(8,128)(2,1)S(1)}, u32[]{:S(2)}, u32[]{:S(2)}) collective-permute-start(bf16[128,768]{1,0:T(8,128)(2,1)S(1)} %pad_maximum_fusion.12), channel_id=1, source_target_pairs={{0,3},{1,2},{2,1},{3,0},{4,7},{5,6},{6,5},{7,4},{8,11},{9,10},{10,... | collective-permute-start | bytes 589832 | tf_op jit(solution)/shard_map/ppermute | solution.py:44
Sparse Core Ops, SparseCore 0:
  10.7 85.2 all-gather.3
  113.1 32.6 all-gather.5

commit v16 on v12

--- a/solution.py
+++ b/solution.py
@@ -82,10 +82,9 @@
     first = c == 0
     many = 4 * rows
 
-    own = jnp.concatenate([down_weight, member_right], axis=0)
-    stack = lax.all_gather(own, ("zh", "c"), axis=0, tiled=True).reshape(4, 2, -1, width)
-    weight = stack[:, :, :block].reshape(-1, width)
-    rights = lax.all_gather(stack[:, :, block:], "y", axis=0, tiled=False)
+    weight = lax.all_gather(down_weight, ("zh", "c"), axis=0, tiled=True)
+    rights, weight = lax.optimization_barrier((member_right, weight))
+    rights = lax.all_gather(rights, ("zh", "y", "c"), axis=0, tiled=True)
 
     left_cols = lax.dynamic_slice(member_left, (0, (x * 4 + zl) * cols), (members, cols)).astype(f32)
     payload = jnp.concatenate([left_cols, probe[None, :]], axis=0)
@@ -167,11 +166,10 @@
     labels = jnp.arange(population, dtype=jnp.int32)
     rival = jnp.sum(jnp.where(opponent[:, None] == labels[None, :], score[None, :], 0.0), axis=1)
     fitness = payoff * (score - rival)
-    fitness = fitness.reshape(4, 4, -1).transpose(1, 0, 2).reshape(population, 1)
-    scaled = lefts.reshape(population, 192)[:, :block].astype(f32)
-    scaled = (fitness * scaled).astype(bf16)
+    scaled = lefts.reshape(4, 4, -1, 192)[..., :block].transpose(1, 0, 2, 3)
+    scaled = (fitness[:, None] * scaled.reshape(population, block).astype(f32)).astype(bf16)
     term = lax.dot_general(
-        scaled, rights.reshape(population, width), (((0,), (0,)), ((), ())),
+        scaled, rights, (((0,), (0,)), ((), ())),
         preferred_element_type=f32,
     )
     return mixed, term / jnp.sqrt(f32(population))

time: 197 us -> 203 us (1.030)
  the two profiles are of different devices: /device:TPU:24 before, /device:TPU:67 now
where the time goes in v16:
time: 203 us
  waiting for transfers between devices  58.4 us (29%)
  blocking collectives  55.4 us (27%)
  starting transfers between devices  55.1 us (27%)
  between operations  14.8 us (7%)
  matrix products  7.81 us (4%)
  other arithmetic  6.18 us (3%)
  local copies, waits for them, and re-layouts  4.86 us (2%)
    ppermute x9, waiting for transfers between devices, move(): return lax.ppermute(value, axis, ring(step))  32 us
    ppermute x9, starting transfers between devices, move(): return lax.ppermute(value, axis, ring(step))  27.4 us
    psum x1, blocking collectives, per_device(): direction = lax.psum(direction, 'zh')  21.4 us
    psum x1, blocking collectives, per_device(): score = lax.psum(placed(score, zh, 4), 'zh')  14.6 us
    all_gather x1, waiting for transfers between devices, per_device(): rights = lax.all_gather(rights, ('zh', 'y', 'c'), axis=0, tiled=True)  14.5 us
    psum x1, blocking collectives, per_device(): early = lax.psum(early, 'y')  11.9 us
    ppermute x1, starting transfers between devices, per_device(): mine = lax.ppermute(mine, AXES, swapped(0))  8.84 us
    ppermute x2, starting transfers between devices, joined(): got = lax.ppermute(value, axis, pairs(step))  8.31 us
  transfers between devices with their start and end apart: 16, of which 8 were waited for; matrix products, arithmetic and copies ran while one was open for 5% of the time, Pallas kernels for 0%

profile of v16, /device:TPU:67, one launch (start us, length us, event | category | flops | bytes accessed | tf_op | source)
XLA Modules:
  0.0 202.5 jit_solution(4749493609729833769)
XLA Ops:
  7.2 0.7 all-gather.3.cloned.1.call-update
  8.0 0.7 broadcast_in_dim.38
  8.7 0.8 dynamic-slice_convert_fusion
  9.6 8.8 %collective-permute-start = (f32[33,160]{1,0:T(8,128)S(1)}, f32[33,160]{1,0:T(8,128)S(1)}, u32[]{:S(2)}, u32[]{:S(2)}) collective-permute-start(f32[33,160]{1,0:T(8,128)S(1)} %fusion.12), channel_id=1, source_target_pairs={{0,0},{1,32},{2,64},{3,96},{4,128},{5,160},{6,192},{7,224},{8,256}... | collective-permute-start | bytes 63368 | tf_op jit(solution)/shard_map/ppermute | solution.py:93
  18.5 2.9 %collective-permute-start.1 = (bf16[32,160]{1,0:T(8,128)(2,1)S(1)}, bf16[32,160]{1,0:T(8,128)(2,1)S(1)}, u32[]{:S(2)}, u32[]{:S(2)}) collective-permute-start(bf16[32,160]{1,0:T(8,128)(2,1)S(1)} %slice_select_fusion), channel_id=1, source_target_pairs={{0,16},{1,48},{2,80},{3,112},{4,144},{5,176},{6,208},{7,240},{8,27... | collective-permute-start | bytes 30728 | tf_op jit(solution)/shard_map/ppermute | solution.py:94
  21.5 1.0 mul.103
  22.7 1.0 multiply_reduce_fusion.2
  23.7 0.2 dynamic_update_slice.10
  24.0 0.2 dynamic_update_slice.9
  24.2 5.3 %collective-permute-done.1 = bf16[32,160]{1,0:T(8,128)(2,1)S(1)} collective-permute-done((bf16[32,160]{1,0:T(8,128)(2,1)S(1)}, bf16[32,160]{1,0:T(8,128)(2,1)S(1)}, u32[]{:S(2)}, u32[]{:S(2)}) %collective-permute-start.1) | collective-permute-done | bytes 10272 | tf_op jit(solution)/shard_map/ppermute | solution.py:94
  29.7 3.3 %psum.35 = f32[1024]{0:T(1024)S(1)} all-reduce(f32[1024]{0:T(1024)S(1)} %multiply_reduce_fusion.1), channel_id=1, replica_groups=mesh['zh'=4,'y'=4,'c'=2,'x'=4,'zl'=4] {'c'}, use_global_device_ids=true, to_apply=%region_1.2 | all-reduce | flops 1024 | bytes 8192 | tf_op jit(solution)/shard_map/psum | solution.py:103
  32.9 11.9 %psum.36 = f32[1920]{0:T(1024)S(1)} all-reduce(f32[1920]{0:T(1024)S(1)} %pad_maximum_fusion.16), channel_id=1, replica_groups=mesh['zh'=4,'y'=4,'c'=2,'x'=4,'zl'=4] {'y'}, use_global_device_ids=true, to_apply=%region_4.5 | all-reduce | flops 1920 | bytes 15360 | tf_op jit(solution)/shard_map/psum | solution.py:105
  44.8 1.9 collective-permute-start.2
  46.7 2.5 %collective-permute-start.3 = (bf16[192,1024]{1,0:T(8,128)(2,1)S(1)}, bf16[192,1024]{1,0:T(8,128)(2,1)S(1)}, u32[]{:S(2)}, u32[]{:S(2)}) collective-permute-start(bf16[192,1024]{1,0:T(8,128)(2,1)S(1)} %copy-done), channel_id=1, source_target_pairs={{0,64},{32,96},{64,0},{96,32},{1,65},{33,97},{65,1},{97,33},{2,66}... | collective-permute-start | bytes 1179656 | tf_op jit(solution)/shard_map/ppermute | solution.py:35
  49.2 2.8 %collective-permute-start.4 = (bf16[192,1024]{1,0:T(8,128)(2,1)S(1)}, bf16[192,1024]{1,0:T(8,128)(2,1)S(1)}, u32[]{:S(2)}, u32[]{:S(2)}) collective-permute-start(bf16[192,1024]{1,0:T(8,128)(2,1)S(1)} %copy-done), channel_id=1, source_target_pairs={{0,32},{32,64},{64,96},{96,0},{1,33},{33,65},{65,97},{97,1},{2,34}... | collective-permute-start | bytes 1179656 | tf_op jit(solution)/shard_map/ppermute | solution.py:35
  52.0 21.4 %psum.37 = f32[1024]{0:T(1024)S(1)} all-reduce(f32[1024]{0:T(1024)S(1)} %split.20), channel_id=1, replica_groups=mesh['zh'=4,'y'=4,'c'=2,'x'=4,'zl'=4] {'zh'}, use_global_device_ids=true, to_apply=%region_5.6 | all-reduce | flops 1024 | bytes 8192 | tf_op jit(solution)/shard_map/psum | solution.py:110
  73.6 0.2 convolution_reduce_fusion.3
  73.9 0.2 convolution_reduce_fusion
  74.1 0.2 convolution_reduce_fusion.1
  74.3 0.2 convolution_reduce_fusion.2
  74.9 5.9 %all-gather.3.cloned.1.call-done = bf16[1280,1024]{1,0:T(8,128)(2,1)} async-done(((bf16[160,1024]{1,0:T(8,128)(2,1)}), bf16[1280,1024]{1,0:T(8,128)(2,1)}) %all-gather.3.cloned.1.call-update) | async-done | bytes 2621456 | tf_op jit(solution)/shard_map/all_gather | solution.py:85
  80.8 4.0 %convolution_convert_fusion = bf16[1280,768]{1,0:T(8,128)(2,1)S(1)} fusion(bf16[1280,1024]{1,0:T(8,128)(2,1)} %all-gather.3.cloned.1.call-done, bf16[192,1024]{1,0:T(8,128)(2,1)S(1)} %collective-permute-done.4, bf16[192,1024]{1,0:T(8,128)(2,1)S(1)} %collective-permute-done.3, bf16[192,1024]{1,0:T(8,128)(2,1)S(1)} %collective-permute-done.2, ...), kind=kOutput, calls=%fused_computation.2 | convolution fusion | flops 2020540416 | bytes 6160384 | tf_op jit(solution)/shard_map/dot_general | solution.py:126
  84.9 1.2 pad_maximum_fusion.5
  86.1 2.8 %collective-permute-start.7 = (bf16[344,768]{1,0:T(8,128)(2,1)}, bf16[344,768]{1,0:T(8,128)(2,1)S(1)}, u32[]{:S(2)}, u32[]{:S(2)}) collective-permute-start(bf16[344,768]{1,0:T(8,128)(2,1)} %get-tuple-element.32), channel_id=1, source_target_pairs={{0,4},{4,8},{8,12},{12,0},{1,5},{5,9},{9,13},{13,1},{2,6},{6,10},{... | collective-permute-start | bytes 1585160 | tf_op jit(solution)/shard_map/ppermute | solution.py:35
  88.9 3.3 %collective-permute-start.6 = (bf16[344,768]{1,0:T(8,128)(2,1)}, bf16[344,768]{1,0:T(8,128)(2,1)S(1)}, u32[]{:S(2)}, u32[]{:S(2)}) collective-permute-start(bf16[344,768]{1,0:T(8,128)(2,1)} %get-tuple-element.31), channel_id=1, source_target_pairs={{0,8},{4,12},{8,0},{12,4},{1,9},{5,13},{9,1},{13,5},{2,10},{6,14},... | collective-permute-start | bytes 1585160 | tf_op jit(solution)/shard_map/ppermute | solution.py:35
  92.2 4.0 %collective-permute-start.5 = (bf16[344,768]{1,0:T(8,128)(2,1)}, bf16[344,768]{1,0:T(8,128)(2,1)S(1)}, u32[]{:S(2)}, u32[]{:S(2)}) collective-permute-start(bf16[344,768]{1,0:T(8,128)(2,1)} %get-tuple-element.30), channel_id=1, source_target_pairs={{0,12},{4,0},{8,4},{12,8},{1,13},{5,1},{9,5},{13,9},{2,14},{6,2},{... | collective-permute-start | bytes 1585160 | tf_op jit(solution)/shard_map/ppermute | solution.py:35
  96.5 5.1 %collective-permute-done.7 = bf16[344,768]{1,0:T(8,128)(2,1)S(1)} collective-permute-done((bf16[344,768]{1,0:T(8,128)(2,1)}, bf16[344,768]{1,0:T(8,128)(2,1)S(1)}, u32[]{:S(2)}, u32[]{:S(2)}) %collective-permute-start.7) | collective-permute-done | bytes 528416 | tf_op jit(solution)/shard_map/ppermute | solution.py:35
  101.5 3.8 %collective-permute-done.6 = bf16[344,768]{1,0:T(8,128)(2,1)S(1)} collective-permute-done((bf16[344,768]{1,0:T(8,128)(2,1)}, bf16[344,768]{1,0:T(8,128)(2,1)S(1)}, u32[]{:S(2)}, u32[]{:S(2)}) %collective-permute-start.6) | collective-permute-done | bytes 528416 | tf_op jit(solution)/shard_map/ppermute | solution.py:35
  105.3 12.5 %collective-permute-done.5 = bf16[344,768]{1,0:T(8,128)(2,1)S(1)} collective-permute-done((bf16[344,768]{1,0:T(8,128)(2,1)}, bf16[344,768]{1,0:T(8,128)(2,1)S(1)}, u32[]{:S(2)}, u32[]{:S(2)}) %collective-permute-start.5) | collective-permute-done | bytes 528416 | tf_op jit(solution)/shard_map/ppermute | solution.py:35
  117.8 0.3 convert_add_fusion
  118.1 0.3 copy.15
  118.8 5.5 %collective-permute-start.12 = (bf16[64,768]{1,0:T(8,128)(2,1)S(1)}, bf16[64,768]{1,0:T(8,128)(2,1)S(1)}, u32[]{:S(2)}, u32[]{:S(2)}) collective-permute-start(bf16[64,768]{1,0:T(8,128)(2,1)S(1)} %bitcast.54), channel_id=1, source_target_pairs={{0,1},{1,0},{2,3},{3,2},{4,5},{5,4},{6,7},{7,6},{8,9},{9,8},{10,11... | collective-permute-start | bytes 294920 | tf_op jit(solution)/shard_map/ppermute | solution.py:44
  124.4 5.1 %collective-permute-start.10 = (bf16[208,320]{1,0:T(8,128)(2,1)S(1)}, bf16[208,320]{1,0:T(8,128)(2,1)S(1)}, u32[]{:S(2)}, u32[]{:S(2)}) collective-permute-start(bf16[208,320]{1,0:T(8,128)(2,1)S(1)} %get-tuple-element.35), channel_id=1, source_target_pairs={{0,3},{1,0},{2,1},{3,2},{4,7},{5,4},{6,5},{7,6},{8,11},{9,8},{10,9... | collective-permute-start | bytes 399368 | tf_op jit(solution)/shard_map/ppermute | solution.py:35
  129.5 1.9 collective-permute-start.8
  131.4 3.2 %collective-permute-start.9 = (bf16[208,320]{1,0:T(8,128)(2,1)S(1)}, bf16[208,320]{1,0:T(8,128)(2,1)S(1)}, u32[]{:S(2)}, u32[]{:S(2)}) collective-permute-start(bf16[208,320]{1,0:T(8,128)(2,1)S(1)} %get-tuple-element.34), channel_id=1, source_target_pairs={{0,2},{1,3},{2,0},{3,1},{4,6},{5,7},{6,4},{7,5},{8,10},{9,11},{10,... | collective-permute-start | bytes 399368 | tf_op jit(solution)/shard_map/ppermute | solution.py:35
  134.7 2.8 %collective-permute-start.13 = (bf16[128,768]{1,0:T(8,128)(2,1)S(1)}, bf16[128,768]{1,0:T(8,128)(2,1)S(1)}, u32[]{:S(2)}, u32[]{:S(2)}) collective-permute-start(bf16[128,768]{1,0:T(8,128)(2,1)S(1)} %pad_maximum_fusion.11), channel_id=1, source_target_pairs={{0,3},{1,2},{2,1},{3,0},{4,7},{5,6},{6,5},{7,4},{8,11},{9,10},{10,... | collective-permute-start | bytes 589832 | tf_op jit(solution)/shard_map/ppermute | solution.py:44
  137.5 7.1 %collective-permute-done.10 = bf16[208,320]{1,0:T(8,128)(2,1)S(1)} collective-permute-done((bf16[208,320]{1,0:T(8,128)(2,1)S(1)}, bf16[208,320]{1,0:T(8,128)(2,1)S(1)}, u32[]{:S(2)}, u32[]{:S(2)}) %collective-permute-start.10) | collective-permute-done | bytes 133152 | tf_op jit(solution)/shard_map/ppermute | solution.py:35
  144.6 3.6 %collective-permute-done.9 = bf16[208,320]{1,0:T(8,128)(2,1)S(1)} collective-permute-done((bf16[208,320]{1,0:T(8,128)(2,1)S(1)}, bf16[208,320]{1,0:T(8,128)(2,1)S(1)}, u32[]{:S(2)}, u32[]{:S(2)}) %collective-permute-start.9) | collective-permute-done | bytes 133152 | tf_op jit(solution)/shard_map/ppermute | solution.py:35
  148.8 0.2 tanh_reduce_fusion
  149.1 7.5 %collective-permute-start.11 = (bf16[192,320]{1,0:T(8,128)(2,1)S(1)}, bf16[192,320]{1,0:T(8,128)(2,1)S(1)}, u32[]{:S(2)}, u32[]{:S(2)}) collective-permute-start(bf16[192,320]{1,0:T(8,128)(2,1)S(1)} %slice.124), channel_id=1, source_target_pairs={{0,0},{1,32},{2,64},{3,96},{32,1},{33,33},{34,65},{35,97},{64,2},{... | collective-permute-start | bytes 368648 | tf_op jit(solution)/shard_map/ppermute | solution.py:161
  156.7 4.3 %psum.38 = f32[256]{0:T(256)S(1)} all-reduce(f32[256]{0:T(256)S(1)} %reshape.264), channel_id=1, replica_groups=mesh['zh'=4,'y'=4,'c'=2,'x'=4,'zl'=4] {'c'}, use_global_device_ids=true, to_apply=%region_13.14 | all-reduce | flops 256 | bytes 2048 | tf_op jit(solution)/shard_map/psum | solution.py:158
  161.1 14.6 %psum.39 = f32[1024]{0:T(1024)S(1)} all-reduce(f32[1024]{0:T(1024)S(1)} %dynamic_update_slice.11), channel_id=1, replica_groups=mesh['zh'=4,'y'=4,'c'=2,'x'=4,'zl'=4] {'zh'}, use_global_device_ids=true, to_apply=%region_14.15 | all-reduce | flops 1024 | bytes 8192 | tf_op jit(solution)/shard_map/psum | solution.py:159
  175.8 0.7 select_reduce_fusion
  176.5 0.8 add_convert_fusion
  177.3 0.5 reshape.266
  178.1 0.2 fusion.7
  178.3 14.5 %all-gather.5.cloned.1.call-done = bf16[1024,1024]{1,0:T(8,128)(2,1)} async-done(((bf16[32,1024]{1,0:T(8,128)(2,1)}), bf16[1024,1024]{1,0:T(8,128)(2,1)}) %all-gather.5.cloned.1.call-update) | async-done | bytes 2097168 | tf_op jit(solution)/shard_map/all_gather | solution.py:87
  192.7 3.0 %convolution_multiply_fusion = f32[160,1024]{1,0:T(8,128)} fusion(bf16[1024,160]{1,0:T(8,128)(2,1)S(1)} %fusion.7, bf16[1024,1024]{1,0:T(8,128)(2,1)} %all-gather.5.cloned.1.call-done), kind=kOutput, calls=%fused_computation.10 | convolution fusion | flops 335708160 | bytes 3080192 | tf_op jit(solution)/shard_map/dot_general | solution.py:171
  (97 shorter events, 3.2 us)
Async XLA Ops:
  7.2 15.4 %copy-start = (bf16[192,1024]{1,0:T(8,128)(2,1)S(1)}, bf16[192,1024]{1,0:T(8,128)(2,1)}, u32[]{:S(2)}) copy-start(bf16[192,1024]{1,0:T(8,128)(2,1)} %param.7) | copy-start | bytes 1179652
  7.2 73.6 %all-gather.3.cloned.1.call-start = ((), (), s32[]{:S(2)}) async-start(), calls=%async_computation | async-start | bytes 2949120 | tf_op jit(solution)/shard_map/all_gather | solution.py:85
  7.9 184.8 %all-gather.5.cloned.1.call-start = ((), (), s32[]{:S(2)}) async-start(), calls=%async_computation.1 | async-start | bytes 2162688 | tf_op jit(solution)/shard_map/all_gather | solution.py:87
  9.6 13.2 %copy-start.2 = (f32[320]{0:T(512)S(1)}, f32[320]{0:T(512)}, u32[]{:S(2)}) copy-start(f32[320]{0:T(512)} %param.11) | copy-start | bytes 3844
  9.6 19.9 %collective-permute-start = (f32[33,160]{1,0:T(8,128)S(1)}, f32[33,160]{1,0:T(8,128)S(1)}, u32[]{:S(2)}, u32[]{:S(2)}) collective-permute-start(f32[33,160]{1,0:T(8,128)S(1)} %fusion.12), channel_id=1, source_target_pairs={{0,0},{1,32},{2,64},{3,96},{4,128},{5,160},{6,192},{7,224},{8,256}... | collective-permute-start | bytes 63368 | tf_op jit(solution)/shard_map/ppermute | solution.py:93
  18.5 11.0 %copy-start.1 = (bf16[160,1024]{1,0:T(8,128)(2,1)S(1)}, bf16[160,1024]{1,0:T(8,128)(2,1)}, u32[]{:S(2)}) copy-start(bf16[160,1024]{1,0:T(8,128)(2,1)} %param.8) | copy-start | bytes 983044
  18.5 11.0 %collective-permute-start.1 = (bf16[32,160]{1,0:T(8,128)(2,1)S(1)}, bf16[32,160]{1,0:T(8,128)(2,1)S(1)}, u32[]{:S(2)}, u32[]{:S(2)}) collective-permute-start(bf16[32,160]{1,0:T(8,128)(2,1)S(1)} %slice_select_fusion), channel_id=1, source_target_pairs={{0,16},{1,48},{2,80},{3,112},{4,144},{5,176},{6,208},{7,240},{8,27... | collective-permute-start | bytes 30728 | tf_op jit(solution)/shard_map/ppermute | solution.py:94
  44.8 29.5 %collective-permute-start.2 = (bf16[192,1024]{1,0:T(8,128)(2,1)S(1)}, bf16[192,1024]{1,0:T(8,128)(2,1)S(1)}, u32[]{:S(2)}, u32[]{:S(2)}) collective-permute-start(bf16[192,1024]{1,0:T(8,128)(2,1)S(1)} %copy-done), channel_id=1, source_target_pairs={{0,96},{32,0},{64,32},{96,64},{1,97},{33,1},{65,33},{97,65},{2,98}... | collective-permute-start | bytes 1179656 | tf_op jit(solution)/shard_map/ppermute | solution.py:35
  46.7 27.4 %collective-permute-start.3 = (bf16[192,1024]{1,0:T(8,128)(2,1)S(1)}, bf16[192,1024]{1,0:T(8,128)(2,1)S(1)}, u32[]{:S(2)}, u32[]{:S(2)}) collective-permute-start(bf16[192,1024]{1,0:T(8,128)(2,1)S(1)} %copy-done), channel_id=1, source_target_pairs={{0,64},{32,96},{64,0},{96,32},{1,65},{33,97},{65,1},{97,33},{2,66}... | collective-permute-start | bytes 1179656 | tf_op jit(solution)/shard_map/ppermute | solution.py:35
  49.2 24.6 %collective-permute-start.4 = (bf16[192,1024]{1,0:T(8,128)(2,1)S(1)}, bf16[192,1024]{1,0:T(8,128)(2,1)S(1)}, u32[]{:S(2)}, u32[]{:S(2)}) collective-permute-start(bf16[192,1024]{1,0:T(8,128)(2,1)S(1)} %copy-done), channel_id=1, source_target_pairs={{0,32},{32,64},{64,96},{96,0},{1,33},{33,65},{65,97},{97,1},{2,34}... | collective-permute-start | bytes 1179656 | tf_op jit(solution)/shard_map/ppermute | solution.py:35
  86.1 15.4 %collective-permute-start.7 = (bf16[344,768]{1,0:T(8,128)(2,1)}, bf16[344,768]{1,0:T(8,128)(2,1)S(1)}, u32[]{:S(2)}, u32[]{:S(2)}) collective-permute-start(bf16[344,768]{1,0:T(8,128)(2,1)} %get-tuple-element.32), channel_id=1, source_target_pairs={{0,4},{4,8},{8,12},{12,0},{1,5},{5,9},{9,13},{13,1},{2,6},{6,10},{... | collective-permute-start | bytes 1585160 | tf_op jit(solution)/shard_map/ppermute | solution.py:35
  88.9 16.4 %collective-permute-start.6 = (bf16[344,768]{1,0:T(8,128)(2,1)}, bf16[344,768]{1,0:T(8,128)(2,1)S(1)}, u32[]{:S(2)}, u32[]{:S(2)}) collective-permute-start(bf16[344,768]{1,0:T(8,128)(2,1)} %get-tuple-element.31), channel_id=1, source_target_pairs={{0,8},{4,12},{8,0},{12,4},{1,9},{5,13},{9,1},{13,5},{2,10},{6,14},... | collective-permute-start | bytes 1585160 | tf_op jit(solution)/shard_map/ppermute | solution.py:35
  92.2 25.6 %collective-permute-start.5 = (bf16[344,768]{1,0:T(8,128)(2,1)}, bf16[344,768]{1,0:T(8,128)(2,1)S(1)}, u32[]{:S(2)}, u32[]{:S(2)}) collective-permute-start(bf16[344,768]{1,0:T(8,128)(2,1)} %get-tuple-element.30), channel_id=1, source_target_pairs={{0,12},{4,0},{8,4},{12,8},{1,13},{5,1},{9,5},{13,9},{2,14},{6,2},{... | collective-permute-start | bytes 1585160 | tf_op jit(solution)/shard_map/ppermute | solution.py:35
  118.8 15.9 %collective-permute-start.12 = (bf16[64,768]{1,0:T(8,128)(2,1)S(1)}, bf16[64,768]{1,0:T(8,128)(2,1)S(1)}, u32[]{:S(2)}, u32[]{:S(2)}) collective-permute-start(bf16[64,768]{1,0:T(8,128)(2,1)S(1)} %bitcast.54), channel_id=1, source_target_pairs={{0,1},{1,0},{2,3},{3,2},{4,5},{5,4},{6,7},{7,6},{8,9},{9,8},{10,11... | collective-permute-start | bytes 294920 | tf_op jit(solution)/shard_map/ppermute | solution.py:44
  124.3 51.5 %copy-start.3 = (s32[1024]{0:T(1024)S(1)}, s32[1024]{0:T(1024)}, u32[]{:S(2)}) copy-start(s32[1024]{0:T(1024)} %param.13) | copy-start | bytes 12292
  124.3 52.2 %copy-start.4 = (f32[1024]{0:T(1024)S(1)}, f32[1024]{0:T(1024)}, u32[]{:S(2)}) copy-start(f32[1024]{0:T(1024)} %param.12) | copy-start | bytes 12292
  124.4 20.2 %collective-permute-start.10 = (bf16[208,320]{1,0:T(8,128)(2,1)S(1)}, bf16[208,320]{1,0:T(8,128)(2,1)S(1)}, u32[]{:S(2)}, u32[]{:S(2)}) collective-permute-start(bf16[208,320]{1,0:T(8,128)(2,1)S(1)} %get-tuple-element.35), channel_id=1, source_target_pairs={{0,3},{1,0},{2,1},{3,2},{4,7},{5,4},{6,5},{7,6},{8,11},{9,8},{10,9... | collective-permute-start | bytes 399368 | tf_op jit(solution)/shard_map/ppermute | solution.py:35
  129.5 15.1 %collective-permute-start.8 = (bf16[208,320]{1,0:T(8,128)(2,1)S(1)}, bf16[208,320]{1,0:T(8,128)(2,1)S(1)}, u32[]{:S(2)}, u32[]{:S(2)}) collective-permute-start(bf16[208,320]{1,0:T(8,128)(2,1)S(1)} %get-tuple-element.33), channel_id=1, source_target_pairs={{0,1},{1,2},{2,3},{3,0},{4,5},{5,6},{6,7},{7,4},{8,9},{9,10},{10,1... | collective-permute-start | bytes 399368 | tf_op jit(solution)/shard_map/ppermute | solution.py:35
  131.4 16.8 %collective-permute-start.9 = (bf16[208,320]{1,0:T(8,128)(2,1)S(1)}, bf16[208,320]{1,0:T(8,128)(2,1)S(1)}, u32[]{:S(2)}, u32[]{:S(2)}) collective-permute-start(bf16[208,320]{1,0:T(8,128)(2,1)S(1)} %get-tuple-element.34), channel_id=1, source_target_pairs={{0,2},{1,3},{2,0},{3,1},{4,6},{5,7},{6,4},{7,5},{8,10},{9,11},{10,... | collective-permute-start | bytes 399368 | tf_op jit(solution)/shard_map/ppermute | solution.py:35
  134.7 42.5 %collective-permute-start.13 = (bf16[128,768]{1,0:T(8,128)(2,1)S(1)}, bf16[128,768]{1,0:T(8,128)(2,1)S(1)}, u32[]{:S(2)}, u32[]{:S(2)}) collective-permute-start(bf16[128,768]{1,0:T(8,128)(2,1)S(1)} %pad_maximum_fusion.11), channel_id=1, source_target_pairs={{0,3},{1,2},{2,1},{3,0},{4,7},{5,6},{6,5},{7,4},{8,11},{9,10},{10,... | collective-permute-start | bytes 589832 | tf_op jit(solution)/shard_map/ppermute | solution.py:44
  149.1 27.3 %collective-permute-start.11 = (bf16[192,320]{1,0:T(8,128)(2,1)S(1)}, bf16[192,320]{1,0:T(8,128)(2,1)S(1)}, u32[]{:S(2)}, u32[]{:S(2)}) collective-permute-start(bf16[192,320]{1,0:T(8,128)(2,1)S(1)} %slice.124), channel_id=1, source_target_pairs={{0,0},{1,32},{2,64},{3,96},{32,1},{33,33},{34,65},{35,97},{64,2},{... | collective-permute-start | bytes 368648 | tf_op jit(solution)/shard_map/ppermute | solution.py:161
Sparse Core Ops, SparseCore 0:
  10.1 70.6 all-gather.2
  96.6 96.0 all-gather.4

commit v17 on v16

--- a/solution.py
+++ b/solution.py
@@ -84,7 +84,8 @@
 
     weight = lax.all_gather(down_weight, ("zh", "c"), axis=0, tiled=True)
     rights, weight = lax.optimization_barrier((member_right, weight))
-    rights = lax.all_gather(rights, ("zh", "y", "c"), axis=0, tiled=True)
+    rights = lax.all_gather(rights, ("zh", "c"), axis=0, tiled=True).reshape(4, -1, width)
+    rights = lax.all_gather(rights, "y", axis=1, tiled=False)
 
     left_cols = lax.dynamic_slice(member_left, (0, (x * 4 + zl) * cols), (members, cols)).astype(f32)
     payload = jnp.concatenate([left_cols, probe[None, :]], axis=0)
@@ -169,7 +170,7 @@
     scaled = lefts.reshape(4, 4, -1, 192)[..., :block].transpose(1, 0, 2, 3)
     scaled = (fitness[:, None] * scaled.reshape(population, block).astype(f32)).astype(bf16)
     term = lax.dot_general(
-        scaled, rights, (((0,), (0,)), ((), ())),
+        scaled, rights.reshape(population, width), (((0,), (0,)), ((), ())),
         preferred_element_type=f32,
     )
     return mixed, term / jnp.sqrt(f32(population))

time: 203 us -> 189 us (0.931)
  the two profiles are of different devices: /device:TPU:67 before, /device:TPU:24 now
where the time goes in v17:
time: 189 us; the launch traced here: 186 us
  blocking collectives  76.8 us (41%)
  starting transfers between devices  51.1 us (27%)
  waiting for transfers between devices  24.8 us (13%)
  between operations  14.8 us (8%)
  matrix products  8.11 us (4%)
  other arithmetic  5.77 us (3%)
  local copies, waits for them, and re-layouts  4.87 us (3%)
    ppermute x9, starting transfers between devices, move(): return lax.ppermute(value, axis, ring(step))  30.8 us
    psum x1, blocking collectives, per_device(): direction = lax.psum(direction, 'zh')  30 us
    all_gather x1, blocking collectives, per_device(): lax.all_gather(rights, ('zh', 'c'), axis=0, tiled=True)  21 us
    psum x1, blocking collectives, per_device(): score = lax.psum(placed(score, zh, 4), 'zh')  13.3 us
    ppermute x9, waiting for transfers between devices, move(): return lax.ppermute(value, axis, ring(step))  10.9 us
    all_gather x1, waiting for transfers between devices, per_device(): weight = lax.all_gather(down_weight, ('zh', 'c'), axis=0, tiled=True)  9.31 us
    psum x1, blocking collectives, per_device(): early = lax.psum(early, 'y')  7.57 us
    ppermute x2, starting transfers between devices, joined(): got = lax.ppermute(value, axis, pairs(step))  6.74 us
  transfers between devices with their start and end apart: 16, of which 4 were waited for; matrix products, arithmetic and copies ran while one was open for 6% of the time, Pallas kernels for 0%

profile of v17, /device:TPU:24, one launch (start us, length us, event | category | flops | bytes accessed | tf_op | source)
XLA Modules:
  0.0 186.3 jit_solution(14249505400098111033)
XLA Ops:
  7.2 0.7 all-gather.3.cloned.1.call-update
  8.0 0.7 broadcast_in_dim.38
  8.7 0.8 dynamic-slice_convert_fusion
  9.6 6.3 %collective-permute-start = (f32[33,160]{1,0:T(8,128)S(1)}, f32[33,160]{1,0:T(8,128)S(1)}, u32[]{:S(2)}, u32[]{:S(2)}) collective-permute-start(f32[33,160]{1,0:T(8,128)S(1)} %fusion.14), channel_id=1, source_target_pairs={{0,0},{1,32},{2,64},{3,96},{4,128},{5,160},{6,192},{7,224},{8,256}... | collective-permute-start | bytes 63368 | tf_op jit(solution)/shard_map/ppermute | solution.py:94
  16.0 2.8 %collective-permute-start.1 = (bf16[32,160]{1,0:T(8,128)(2,1)S(1)}, bf16[32,160]{1,0:T(8,128)(2,1)S(1)}, u32[]{:S(2)}, u32[]{:S(2)}) collective-permute-start(bf16[32,160]{1,0:T(8,128)(2,1)S(1)} %slice_select_fusion), channel_id=1, source_target_pairs={{0,16},{1,48},{2,80},{3,112},{4,144},{5,176},{6,208},{7,240},{8,27... | collective-permute-start | bytes 30728 | tf_op jit(solution)/shard_map/ppermute | solution.py:95
  18.8 1.0 mul.106
  19.9 0.2 multiply_reduce_fusion
  20.1 1.0 multiply_reduce_fusion.2
  21.1 0.2 dynamic_update_slice.10
  21.4 0.2 dynamic_update_slice.9
  21.6 3.9 %collective-permute-done.1 = bf16[32,160]{1,0:T(8,128)(2,1)S(1)} collective-permute-done((bf16[32,160]{1,0:T(8,128)(2,1)S(1)}, bf16[32,160]{1,0:T(8,128)(2,1)S(1)}, u32[]{:S(2)}, u32[]{:S(2)}) %collective-permute-start.1) | collective-permute-done | bytes 10272 | tf_op jit(solution)/shard_map/ppermute | solution.py:95
  25.4 0.1 multiply_reduce_fusion.1
  25.6 2.5 %psum.35 = f32[1024]{0:T(1024)S(1)} all-reduce(f32[1024]{0:T(1024)S(1)} %multiply_reduce_fusion.1), channel_id=1, replica_groups=mesh['zh'=4,'y'=4,'c'=2,'x'=4,'zl'=4] {'c'}, use_global_device_ids=true, to_apply=%region_1.2 | all-reduce | flops 1024 | bytes 8192 | tf_op jit(solution)/shard_map/psum | solution.py:104
  28.1 7.6 %psum.36 = f32[1920]{0:T(1024)S(1)} all-reduce(f32[1920]{0:T(1024)S(1)} %pad_maximum_fusion.16), channel_id=1, replica_groups=mesh['zh'=4,'y'=4,'c'=2,'x'=4,'zl'=4] {'y'}, use_global_device_ids=true, to_apply=%region_4.5 | all-reduce | flops 1920 | bytes 15360 | tf_op jit(solution)/shard_map/psum | solution.py:106
  35.6 3.6 %collective-permute-start.2 = (bf16[192,1024]{1,0:T(8,128)(2,1)S(1)}, bf16[192,1024]{1,0:T(8,128)(2,1)S(1)}, u32[]{:S(2)}, u32[]{:S(2)}) collective-permute-start(bf16[192,1024]{1,0:T(8,128)(2,1)S(1)} %copy-done), channel_id=1, source_target_pairs={{0,96},{32,0},{64,32},{96,64},{1,97},{33,1},{65,33},{97,65},{2,98}... | collective-permute-start | bytes 1179656 | tf_op jit(solution)/shard_map/ppermute | solution.py:35
  39.2 5.2 %collective-permute-start.3 = (bf16[192,1024]{1,0:T(8,128)(2,1)S(1)}, bf16[192,1024]{1,0:T(8,128)(2,1)S(1)}, u32[]{:S(2)}, u32[]{:S(2)}) collective-permute-start(bf16[192,1024]{1,0:T(8,128)(2,1)S(1)} %copy-done), channel_id=1, source_target_pairs={{0,64},{32,96},{64,0},{96,32},{1,65},{33,97},{65,1},{97,33},{2,66}... | collective-permute-start | bytes 1179656 | tf_op jit(solution)/shard_map/ppermute | solution.py:35
  44.4 1.9 %collective-permute-start.4 = (bf16[192,1024]{1,0:T(8,128)(2,1)S(1)}, bf16[192,1024]{1,0:T(8,128)(2,1)S(1)}, u32[]{:S(2)}, u32[]{:S(2)}) collective-permute-start(bf16[192,1024]{1,0:T(8,128)(2,1)S(1)} %copy-done), channel_id=1, source_target_pairs={{0,32},{32,64},{64,96},{96,0},{1,33},{33,65},{65,97},{97,1},{2,34}... | collective-permute-start | bytes 1179656 | tf_op jit(solution)/shard_map/ppermute | solution.py:35
  46.4 30.0 %psum.37 = f32[1024]{0:T(1024)S(1)} all-reduce(f32[1024]{0:T(1024)S(1)} %split.20), channel_id=1, replica_groups=mesh['zh'=4,'y'=4,'c'=2,'x'=4,'zl'=4] {'zh'}, use_global_device_ids=true, to_apply=%region_5.6 | all-reduce | flops 1024 | bytes 8192 | tf_op jit(solution)/shard_map/psum | solution.py:111
  76.6 0.2 convolution_reduce_fusion.3
  76.8 0.2 convolution_reduce_fusion
  77.1 0.2 convolution_reduce_fusion.1
  77.3 0.2 convolution_reduce_fusion.2
  77.8 9.3 %all-gather.3.cloned.1.call-done = bf16[1280,1024]{1,0:T(8,128)(2,1)} async-done(((bf16[160,1024]{1,0:T(8,128)(2,1)}), bf16[1280,1024]{1,0:T(8,128)(2,1)}) %all-gather.3.cloned.1.call-update) | async-done | bytes 2621456 | tf_op jit(solution)/shard_map/all_gather | solution.py:85
  87.1 4.0 %convolution_convert_fusion = bf16[1280,768]{1,0:T(8,128)(2,1)S(1)} fusion(bf16[1280,1024]{1,0:T(8,128)(2,1)} %all-gather.3.cloned.1.call-done, bf16[192,1024]{1,0:T(8,128)(2,1)S(1)} %collective-permute-done.4, bf16[192,1024]{1,0:T(8,128)(2,1)S(1)} %collective-permute-done.3, bf16[192,1024]{1,0:T(8,128)(2,1)S(1)} %collective-permute-done.2, ...), kind=kOutput, calls=%fused_computation.2 | convolution fusion | flops 2020540416 | bytes 6160384 | tf_op jit(solution)/shard_map/dot_general | solution.py:127
  91.1 0.1 dynamic-slice_bitcast_fusion
  91.3 1.1 pad_maximum_fusion.5
  92.4 3.4 %collective-permute-start.7 = (bf16[344,768]{1,0:T(8,128)(2,1)}, bf16[344,768]{1,0:T(8,128)(2,1)S(1)}, u32[]{:S(2)}, u32[]{:S(2)}) collective-permute-start(bf16[344,768]{1,0:T(8,128)(2,1)} %get-tuple-element.32), channel_id=1, source_target_pairs={{0,4},{4,8},{8,12},{12,0},{1,5},{5,9},{9,13},{13,1},{2,6},{6,10},{... | collective-permute-start | bytes 1585160 | tf_op jit(solution)/shard_map/ppermute | solution.py:35
  95.7 4.7 %collective-permute-start.6 = (bf16[344,768]{1,0:T(8,128)(2,1)}, bf16[344,768]{1,0:T(8,128)(2,1)S(1)}, u32[]{:S(2)}, u32[]{:S(2)}) collective-permute-start(bf16[344,768]{1,0:T(8,128)(2,1)} %get-tuple-element.31), channel_id=1, source_target_pairs={{0,8},{4,12},{8,0},{12,4},{1,9},{5,13},{9,1},{13,5},{2,10},{6,14},... | collective-permute-start | bytes 1585160 | tf_op jit(solution)/shard_map/ppermute | solution.py:35
  100.7 2.9 %collective-permute-start.5 = (bf16[344,768]{1,0:T(8,128)(2,1)S(1)}, bf16[344,768]{1,0:T(8,128)(2,1)S(1)}, u32[]{:S(2)}, u32[]{:S(2)}) collective-permute-start(bf16[344,768]{1,0:T(8,128)(2,1)S(1)} %get-tuple-element.30), channel_id=1, source_target_pairs={{0,12},{4,0},{8,4},{12,8},{1,13},{5,1},{9,5},{13,9},{2,14},{6,2},{... | collective-permute-start | bytes 1585160 | tf_op jit(solution)/shard_map/ppermute | solution.py:35
  103.5 21.0 %all_gather.10 = bf16[256,1024]{1,0:T(8,128)(2,1)} all-gather(bf16[32,1024]{1,0:T(8,128)(2,1)S(1)} %copy-done.2), channel_id=1, replica_groups=mesh['zh'=4,'y'=4,'c'=2,'x'=4,'zl'=4] {'zh','c'}, dimensions={0}, use_global_device_ids=true | all-gather | bytes 589824 | tf_op jit(solution)/shard_map/all_gather | solution.py:87
  124.7 0.3 convert_add_fusion
  125.1 0.3 copy.17
  125.6 1.9 %collective-permute-start.12 = (bf16[64,768]{1,0:T(8,128)(2,1)S(1)}, bf16[64,768]{1,0:T(8,128)(2,1)S(1)}, u32[]{:S(2)}, u32[]{:S(2)}) collective-permute-start(bf16[64,768]{1,0:T(8,128)(2,1)S(1)} %bitcast.61), channel_id=1, source_target_pairs={{0,1},{1,0},{2,3},{3,2},{4,5},{5,4},{6,7},{7,6},{8,9},{9,8},{10,11... | collective-permute-start | bytes 294920 | tf_op jit(solution)/shard_map/ppermute | solution.py:44
  127.7 4.3 %collective-permute-start.10 = (bf16[208,320]{1,0:T(8,128)(2,1)S(1)}, bf16[208,320]{1,0:T(8,128)(2,1)S(1)}, u32[]{:S(2)}, u32[]{:S(2)}) collective-permute-start(bf16[208,320]{1,0:T(8,128)(2,1)S(1)} %get-tuple-element.35), channel_id=1, source_target_pairs={{0,3},{1,0},{2,1},{3,2},{4,7},{5,4},{6,5},{7,6},{8,11},{9,8},{10,9... | collective-permute-start | bytes 399368 | tf_op jit(solution)/shard_map/ppermute | solution.py:35
  132.1 1.9 %collective-permute-start.8 = (bf16[208,320]{1,0:T(8,128)(2,1)S(1)}, bf16[208,320]{1,0:T(8,128)(2,1)S(1)}, u32[]{:S(2)}, u32[]{:S(2)}) collective-permute-start(bf16[208,320]{1,0:T(8,128)(2,1)S(1)} %get-tuple-element.33), channel_id=1, source_target_pairs={{0,1},{1,2},{2,3},{3,0},{4,5},{5,6},{6,7},{7,4},{8,9},{9,10},{10,1... | collective-permute-start | bytes 399368 | tf_op jit(solution)/shard_map/ppermute | solution.py:35
  134.0 3.0 %collective-permute-start.9 = (bf16[208,320]{1,0:T(8,128)(2,1)S(1)}, bf16[208,320]{1,0:T(8,128)(2,1)S(1)}, u32[]{:S(2)}, u32[]{:S(2)}) collective-permute-start(bf16[208,320]{1,0:T(8,128)(2,1)S(1)} %get-tuple-element.34), channel_id=1, source_target_pairs={{0,2},{1,3},{2,0},{3,1},{4,6},{5,7},{6,4},{7,5},{8,10},{9,11},{10,... | collective-permute-start | bytes 399368 | tf_op jit(solution)/shard_map/ppermute | solution.py:35
  137.0 4.8 %collective-permute-start.13 = (bf16[128,768]{1,0:T(8,128)(2,1)S(1)}, bf16[128,768]{1,0:T(8,128)(2,1)S(1)}, u32[]{:S(2)}, u32[]{:S(2)}) collective-permute-start(bf16[128,768]{1,0:T(8,128)(2,1)S(1)} %pad_maximum_fusion.11), channel_id=1, source_target_pairs={{0,3},{1,2},{2,1},{3,0},{4,7},{5,6},{6,5},{7,4},{8,11},{9,10},{10,... | collective-permute-start | bytes 589832 | tf_op jit(solution)/shard_map/ppermute | solution.py:44
  141.9 1.0 collective-permute-done.8
  142.9 9.9 %collective-permute-done.9 = bf16[208,320]{1,0:T(8,128)(2,1)S(1)} collective-permute-done((bf16[208,320]{1,0:T(8,128)(2,1)S(1)}, bf16[208,320]{1,0:T(8,128)(2,1)S(1)}, u32[]{:S(2)}, u32[]{:S(2)}) %collective-permute-start.9) | collective-permute-done | bytes 133152 | tf_op jit(solution)/shard_map/ppermute | solution.py:35
  153.3 0.2 tanh_reduce_fusion
  153.6 4.3 %collective-permute-start.11 = (bf16[192,320]{1,0:T(8,128)(2,1)S(1)}, bf16[192,320]{1,0:T(8,128)(2,1)S(1)}, u32[]{:S(2)}, u32[]{:S(2)}) collective-permute-start(bf16[192,320]{1,0:T(8,128)(2,1)S(1)} %slice.124), channel_id=1, source_target_pairs={{0,0},{1,32},{2,64},{3,96},{32,1},{33,33},{34,65},{35,97},{64,2},{... | collective-permute-start | bytes 368648 | tf_op jit(solution)/shard_map/ppermute | solution.py:162
  158.0 2.5 %psum.38 = f32[256]{0:T(256)S(1)} all-reduce(f32[256]{0:T(256)S(1)} %reshape.269), channel_id=1, replica_groups=mesh['zh'=4,'y'=4,'c'=2,'x'=4,'zl'=4] {'c'}, use_global_device_ids=true, to_apply=%region_13.14 | all-reduce | flops 256 | bytes 2048 | tf_op jit(solution)/shard_map/psum | solution.py:159
  160.5 0.2 dynamic_update_slice.11
  160.6 13.3 %psum.39 = f32[1024]{0:T(1024)S(1)} all-reduce(f32[1024]{0:T(1024)S(1)} %dynamic_update_slice.11), channel_id=1, replica_groups=mesh['zh'=4,'y'=4,'c'=2,'x'=4,'zl'=4] {'zh'}, use_global_device_ids=true, to_apply=%region_14.15 | all-reduce | flops 1024 | bytes 8192 | tf_op jit(solution)/shard_map/psum | solution.py:160
  173.9 0.7 select_reduce_fusion
  174.8 0.8 add_convert_fusion
  175.6 0.5 reshape.271
  176.2 3.3 %fusion.7 = f32[160,1024]{1,0:T(8,128)} fusion(bf16[4,4,64,1024]{3,2,1,0:T(8,128)(2,1)} %all-gather.5.cloned.1.call-done, bf16[4,4,64,192]{3,2,1,0:T(8,128)(2,1)S(1)} %reshape.271, f32[4,4,64]{2,0,1:T(4,128)S(1)} %copy.19), kind=kOutput, calls=%fused_computation.11 | convolution fusion | flops 336199680 | bytes 3149824 | tf_op jit(solution)/shard_map/dot_general | solution.py:172
  (99 shorter events, 2.5 us)
Async XLA Ops:
  7.2 12.8 %copy-start = (bf16[192,1024]{1,0:T(8,128)(2,1)S(1)}, bf16[192,1024]{1,0:T(8,128)(2,1)}, u32[]{:S(2)}) copy-start(bf16[192,1024]{1,0:T(8,128)(2,1)} %param.7) | copy-start | bytes 1179652
  7.2 80.0 %all-gather.3.cloned.1.call-start = ((), (), s32[]{:S(2)}) async-start(), calls=%async_computation | async-start | bytes 2949120 | tf_op jit(solution)/shard_map/all_gather | solution.py:85
  7.9 168.3 %all-gather.5.cloned.1.call-start = ((), (), s32[]{:S(2)}) async-start(), calls=%async_computation.1 | async-start | bytes 2621440 | tf_op jit(solution)/shard_map/all_gather | solution.py:88
  9.6 10.5 %copy-start.3 = (f32[320]{0:T(512)S(1)}, f32[320]{0:T(512)}, u32[]{:S(2)}) copy-start(f32[320]{0:T(512)} %param.11) | copy-start | bytes 3844
  9.6 15.8 %collective-permute-start = (f32[33,160]{1,0:T(8,128)S(1)}, f32[33,160]{1,0:T(8,128)S(1)}, u32[]{:S(2)}, u32[]{:S(2)}) collective-permute-start(f32[33,160]{1,0:T(8,128)S(1)} %fusion.14), channel_id=1, source_target_pairs={{0,0},{1,32},{2,64},{3,96},{4,128},{5,160},{6,192},{7,224},{8,256}... | collective-permute-start | bytes 63368 | tf_op jit(solution)/shard_map/ppermute | solution.py:94
  16.0 9.4 %copy-start.1 = (bf16[160,1024]{1,0:T(8,128)(2,1)S(1)}, bf16[160,1024]{1,0:T(8,128)(2,1)}, u32[]{:S(2)}) copy-start(bf16[160,1024]{1,0:T(8,128)(2,1)} %param.8) | copy-start | bytes 983044
  16.0 9.4 %collective-permute-start.1 = (bf16[32,160]{1,0:T(8,128)(2,1)S(1)}, bf16[32,160]{1,0:T(8,128)(2,1)S(1)}, u32[]{:S(2)}, u32[]{:S(2)}) collective-permute-start(bf16[32,160]{1,0:T(8,128)(2,1)S(1)} %slice_select_fusion), channel_id=1, source_target_pairs={{0,16},{1,48},{2,80},{3,112},{4,144},{5,176},{6,208},{7,240},{8,27... | collective-permute-start | bytes 30728 | tf_op jit(solution)/shard_map/ppermute | solution.py:95
  35.6 41.7 %collective-permute-start.2 = (bf16[192,1024]{1,0:T(8,128)(2,1)S(1)}, bf16[192,1024]{1,0:T(8,128)(2,1)S(1)}, u32[]{:S(2)}, u32[]{:S(2)}) collective-permute-start(bf16[192,1024]{1,0:T(8,128)(2,1)S(1)} %copy-done), channel_id=1, source_target_pairs={{0,96},{32,0},{64,32},{96,64},{1,97},{33,1},{65,33},{97,65},{2,98}... | collective-permute-start | bytes 1179656 | tf_op jit(solution)/shard_map/ppermute | solution.py:35
  39.2 37.8 %collective-permute-start.3 = (bf16[192,1024]{1,0:T(8,128)(2,1)S(1)}, bf16[192,1024]{1,0:T(8,128)(2,1)S(1)}, u32[]{:S(2)}, u32[]{:S(2)}) collective-permute-start(bf16[192,1024]{1,0:T(8,128)(2,1)S(1)} %copy-done), channel_id=1, source_target_pairs={{0,64},{32,96},{64,0},{96,32},{1,65},{33,97},{65,1},{97,33},{2,66}... | collective-permute-start | bytes 1179656 | tf_op jit(solution)/shard_map/ppermute | solution.py:35
  44.4 32.4 %collective-permute-start.4 = (bf16[192,1024]{1,0:T(8,128)(2,1)S(1)}, bf16[192,1024]{1,0:T(8,128)(2,1)S(1)}, u32[]{:S(2)}, u32[]{:S(2)}) collective-permute-start(bf16[192,1024]{1,0:T(8,128)(2,1)S(1)} %copy-done), channel_id=1, source_target_pairs={{0,32},{32,64},{64,96},{96,0},{1,33},{33,65},{65,97},{97,1},{2,34}... | collective-permute-start | bytes 1179656 | tf_op jit(solution)/shard_map/ppermute | solution.py:35
  91.3 12.3 %copy-start.2 = (bf16[32,1024]{1,0:T(8,128)(2,1)S(1)}, bf16[32,1024]{1,0:T(8,128)(2,1)}, u32[]{:S(2)}) copy-start(bf16[32,1024]{1,0:T(8,128)(2,1)} %param.10) | copy-start | bytes 196612
  92.4 32.2 %collective-permute-start.7 = (bf16[344,768]{1,0:T(8,128)(2,1)}, bf16[344,768]{1,0:T(8,128)(2,1)S(1)}, u32[]{:S(2)}, u32[]{:S(2)}) collective-permute-start(bf16[344,768]{1,0:T(8,128)(2,1)} %get-tuple-element.32), channel_id=1, source_target_pairs={{0,4},{4,8},{8,12},{12,0},{1,5},{5,9},{9,13},{13,1},{2,6},{6,10},{... | collective-permute-start | bytes 1585160 | tf_op jit(solution)/shard_map/ppermute | solution.py:35
  95.7 28.9 %collective-permute-start.6 = (bf16[344,768]{1,0:T(8,128)(2,1)}, bf16[344,768]{1,0:T(8,128)(2,1)S(1)}, u32[]{:S(2)}, u32[]{:S(2)}) collective-permute-start(bf16[344,768]{1,0:T(8,128)(2,1)} %get-tuple-element.31), channel_id=1, source_target_pairs={{0,8},{4,12},{8,0},{12,4},{1,9},{5,13},{9,1},{13,5},{2,10},{6,14},... | collective-permute-start | bytes 1585160 | tf_op jit(solution)/shard_map/ppermute | solution.py:35
  100.7 23.9 %collective-permute-start.5 = (bf16[344,768]{1,0:T(8,128)(2,1)S(1)}, bf16[344,768]{1,0:T(8,128)(2,1)S(1)}, u32[]{:S(2)}, u32[]{:S(2)}) collective-permute-start(bf16[344,768]{1,0:T(8,128)(2,1)S(1)} %get-tuple-element.30), channel_id=1, source_target_pairs={{0,12},{4,0},{8,4},{12,8},{1,13},{5,1},{9,5},{13,9},{2,14},{6,2},{... | collective-permute-start | bytes 1585160 | tf_op jit(solution)/shard_map/ppermute | solution.py:35
  125.6 11.3 %collective-permute-start.12 = (bf16[64,768]{1,0:T(8,128)(2,1)S(1)}, bf16[64,768]{1,0:T(8,128)(2,1)S(1)}, u32[]{:S(2)}, u32[]{:S(2)}) collective-permute-start(bf16[64,768]{1,0:T(8,128)(2,1)S(1)} %bitcast.61), channel_id=1, source_target_pairs={{0,1},{1,0},{2,3},{3,2},{4,5},{5,4},{6,7},{7,6},{8,9},{9,8},{10,11... | collective-permute-start | bytes 294920 | tf_op jit(solution)/shard_map/ppermute | solution.py:44
  127.6 46.4 %copy-start.4 = (s32[1024]{0:T(1024)S(1)}, s32[1024]{0:T(1024)}, u32[]{:S(2)}) copy-start(s32[1024]{0:T(1024)} %param.13) | copy-start | bytes 12292
  127.6 47.0 %copy-start.5 = (f32[1024]{0:T(1024)S(1)}, f32[1024]{0:T(1024)}, u32[]{:S(2)}) copy-start(f32[1024]{0:T(1024)} %param.12) | copy-start | bytes 12292
  127.7 14.1 %collective-permute-start.10 = (bf16[208,320]{1,0:T(8,128)(2,1)S(1)}, bf16[208,320]{1,0:T(8,128)(2,1)S(1)}, u32[]{:S(2)}, u32[]{:S(2)}) collective-permute-start(bf16[208,320]{1,0:T(8,128)(2,1)S(1)} %get-tuple-element.35), channel_id=1, source_target_pairs={{0,3},{1,0},{2,1},{3,2},{4,7},{5,4},{6,5},{7,6},{8,11},{9,8},{10,9... | collective-permute-start | bytes 399368 | tf_op jit(solution)/shard_map/ppermute | solution.py:35
  132.1 10.8 %collective-permute-start.8 = (bf16[208,320]{1,0:T(8,128)(2,1)S(1)}, bf16[208,320]{1,0:T(8,128)(2,1)S(1)}, u32[]{:S(2)}, u32[]{:S(2)}) collective-permute-start(bf16[208,320]{1,0:T(8,128)(2,1)S(1)} %get-tuple-element.33), channel_id=1, source_target_pairs={{0,1},{1,2},{2,3},{3,0},{4,5},{5,6},{6,7},{7,4},{8,9},{9,10},{10,1... | collective-permute-start | bytes 399368 | tf_op jit(solution)/shard_map/ppermute | solution.py:35
  134.0 18.7 %collective-permute-start.9 = (bf16[208,320]{1,0:T(8,128)(2,1)S(1)}, bf16[208,320]{1,0:T(8,128)(2,1)S(1)}, u32[]{:S(2)}, u32[]{:S(2)}) collective-permute-start(bf16[208,320]{1,0:T(8,128)(2,1)S(1)} %get-tuple-element.34), channel_id=1, source_target_pairs={{0,2},{1,3},{2,0},{3,1},{4,6},{5,7},{6,4},{7,5},{8,10},{9,11},{10,... | collective-permute-start | bytes 399368 | tf_op jit(solution)/shard_map/ppermute | solution.py:35
  137.0 38.5 %collective-permute-start.13 = (bf16[128,768]{1,0:T(8,128)(2,1)S(1)}, bf16[128,768]{1,0:T(8,128)(2,1)S(1)}, u32[]{:S(2)}, u32[]{:S(2)}) collective-permute-start(bf16[128,768]{1,0:T(8,128)(2,1)S(1)} %pad_maximum_fusion.11), channel_id=1, source_target_pairs={{0,3},{1,2},{2,1},{3,0},{4,7},{5,6},{6,5},{7,4},{8,11},{9,10},{10,... | collective-permute-start | bytes 589832 | tf_op jit(solution)/shard_map/ppermute | solution.py:44
  153.6 21.1 %collective-permute-start.11 = (bf16[192,320]{1,0:T(8,128)(2,1)S(1)}, bf16[192,320]{1,0:T(8,128)(2,1)S(1)}, u32[]{:S(2)}, u32[]{:S(2)}) collective-permute-start(bf16[192,320]{1,0:T(8,128)(2,1)S(1)} %slice.124), channel_id=1, source_target_pairs={{0,0},{1,32},{2,64},{3,96},{32,1},{33,33},{34,65},{35,97},{64,2},{... | collective-permute-start | bytes 368648 | tf_op jit(solution)/shard_map/ppermute | solution.py:162
Sparse Core Ops, SparseCore 0:
  10.1 76.9 all-gather.2
  124.7 31.0 all-gather.4
